TPU v7x, 32 devices: a whole 2x2x4 slice. The times are simulated.
32 devices in a mesh: groups: 2 (over x), row: 4 (over y, core), col: 4 (over z).
Axes of the slice: x: 2, y: 2, z: 4, core: 2. Of those that a mesh axis runs over, the one named last changes fastest.
Arguments:
- sender_rows: bfloat16 [2, 256, 8192], P(None, ('groups', 'row', 'col')), parts along dimension 1
- counts: int32 [2, 32], P(None, 'groups'), parts along dimension 1, may hold values from 1 to 8, as said below
- assign: int32 [2, 256], P(None, 'groups'), parts along dimension 1, may hold values from 0 to 63, as said below
- gate_w: bfloat16 [8192, 14336], P('row', 'col'), may hold values from -0.0625 to 0.0625
- up_w: bfloat16 [8192, 14336], P('row', 'col'), may hold values from -0.0625 to 0.0625
- down_w: bfloat16 [14336, 8192], P('col', 'row'), may hold values from -0.046875 to 0.046875
Outputs:
- layer_output: bfloat16 [2, 128, 8192], P(None, ('groups', 'row', 'col')), parts along dimension 1
There are 2 independent parts, one for each index of `groups`. A program takes and returns all parts, laid end to end along the dimension named above; an argument that names none is the same for every part. Nothing has to cross between parts.
Inputs may be any that keep to these rules, and one draw needn't show every extreme that they name: In each step the counts of all senders sum to 64. `assign`: in each step the live entries carry each of 0 to 63 exactly once; the other entries hold arbitrary values of the same range.
All inputs are finite; a program needn't handle non-finite values.
Results may differ from a plain program's by a relative error of at most 0.02.
Values may be sent and summed in bfloat16 or wider, within the bound.
No kernel may reach another device: no remote copies, remote signals or barrier semaphores. Data moves between devices by JAX's collectives and lax.ppermute only.
A program may use at most 192 MiB of HBM per device.

v0:
```python
import jax
import jax.numpy as jnp
from jax import lax
from jax.sharding import PartitionSpec as P

STEPS = 2
MEAN = 4


epsilon = 1e-05


def layer_block(normed_block, counts_block, assign_block, paired, down_w, hidden_cols):
    row_devices = lax.axis_size("row")
    col_devices = lax.axis_size("col")
    step_count = normed_block.shape[0]
    capacity = normed_block.shape[1]
    rows_step = MEAN * counts_block.shape[1]
    spread = lax.all_to_all(normed_block, "row", split_axis=2, concat_axis=1, tiled=True)
    gathered = lax.all_gather(spread, "col", axis=1, tiled=True)
    slot_count = gathered.shape[1]
    stacked = gathered.reshape(step_count * slot_count, gathered.shape[2])
    targets = (
        assign_block.reshape(step_count, row_devices, col_devices, capacity)
        .transpose(0, 2, 1, 3)
        .reshape(step_count, slot_count)
    )
    holdings = counts_block.reshape(step_count, row_devices, col_devices).transpose(0, 2, 1)
    slot_grid = lax.broadcasted_iota(jnp.int32, (step_count, col_devices, row_devices, capacity), 3)
    live_mask = (slot_grid < holdings[..., None]).reshape(step_count, slot_count)
    targets = jnp.where(live_mask, targets, rows_step)
    slot_ids = lax.broadcasted_iota(jnp.int32, (step_count, slot_count), 1)
    step_ids = lax.broadcasted_iota(jnp.int32, (step_count, slot_count), 0)
    inverse = (
        jnp.zeros((step_count, rows_step), jnp.int32)
        .at[step_ids, targets]
        .set(slot_ids, mode="drop")
    )
    grid_shape = (col_devices, row_devices, step_count, MEAN)
    col_ids = lax.broadcasted_iota(jnp.int32, grid_shape, 0)
    row_ids = lax.broadcasted_iota(jnp.int32, grid_shape, 1)
    step_grid = lax.broadcasted_iota(jnp.int32, grid_shape, 2)
    member = lax.broadcasted_iota(jnp.int32, grid_shape, 3)
    row_numbers = (row_ids * col_devices + col_ids) * MEAN + member
    positions = (step_grid * slot_count + inverse[step_grid, row_numbers]).reshape(-1)
    inputs = jnp.take(stacked, positions, axis=0)
    rows_here = inputs
    gate_up = lax.psum_scatter(
        jnp.dot(rows_here, paired, preferred_element_type=jnp.float32).astype(jnp.bfloat16),
        "row",
        scatter_dimension=0,
        tiled=True,
    ).astype(jnp.float32)
    hidden = (jax.nn.silu(gate_up[:, :hidden_cols]) * gate_up[:, hidden_cols:]).astype(jnp.bfloat16)
    hidden_all = lax.all_gather(hidden, "row", axis=0, tiled=True)
    rows_here = hidden_all
    summed = lax.psum_scatter(
        jnp.dot(rows_here, down_w, preferred_element_type=jnp.float32).astype(jnp.bfloat16),
        "col",
        scatter_dimension=0,
        tiled=True,
    )
    finished = lax.all_to_all(summed, "row", split_axis=0, concat_axis=1, tiled=True)
    return finished.reshape(step_count, MEAN, finished.shape[1])


def per_device(sender_rows, counts, assign, gate_w, up_w, down_w):
    values = sender_rows.astype(jnp.float32)
    normed = (
        values * lax.rsqrt(jnp.mean(values * values, axis=-1, keepdims=True) + epsilon)
    ).astype(jnp.bfloat16)
    paired = jnp.concatenate((gate_w, up_w), axis=1)
    hidden_cols = gate_w.shape[1]
    outputs = []
    for step_index in range(STEPS):
        outputs.append(
            layer_block(
                normed[step_index : step_index + 1],
                counts[step_index : step_index + 1],
                assign[step_index : step_index + 1],
                paired,
                down_w,
                hidden_cols,
            )
        )
    result = jnp.concatenate(outputs, axis=0)
    return result


def solution(mesh):
    return jax.shard_map(
        per_device,
        mesh=mesh,
        in_specs=(
            P(None, ("groups", "row", "col"), None),
            P(None, "groups"),
            P(None, "groups"),
            P("row", "col"),
            P("row", "col"),
            P("col", "row"),
        ),
        out_specs=P(None, ("groups", "row", "col"), None),
        check_vma=False,
    )
```

profile of v0, /device:TPU:0, one launch (start us, length us, event | category | flops | bytes accessed | tf_op | source)
XLA Modules:
  0.0 330.4 jit_solution(4706945543074529313)
XLA Ops:
  6.5 1.1 fusion
  7.7 1.1 fusion.1
  8.8 6.7 %copy.39 = bf16[1,8,8192]{1,0,2:T(2,128)(2,1)} copy(bf16[1,8,8192]{2,1,0:T(8,128)(2,1)S(1)} %get-tuple-element.11) | data formatting | bytes 262144 | tf_op jit(solution)/shard_map/slice | solution.py:78
  16.1 45.2 %reduce.16 = bf16[8192,8]{1,0:T(8,128)(2,1)S(1)} reduce(bf16[8192,1,8]{2,1,0:T(2,128)(2,1)} %bitcast.48, bf16[]{:T(256)} %broadcast.240), dimensions={1}, to_apply=%bitcast.34.reduce_sub_computation | reduce | bytes 262146
  61.3 2.8 reshape.303
  64.2 4.2 %all-to-all-start.2 = ((bf16[4,2,8192]{2,1,0:T(2,128)(2,1)}), bf16[4,2,8192]{2,1,0:T(2,128)(2,1)S(1)}, u32[]{:S(2)}, u32[]{:S(2)}) async-start(bf16[4,2,8192]{2,1,0:T(2,128)(2,1)} %reshape.303), calls=%async_computation.4 | async-start | bytes 262144 | tf_op jit(solution)/shard_map/all_to_all | solution.py:19
  70.7 1.0 scatter_custom_fusion.1
  73.1 1.2 scatter_custom_fusion
  75.1 13.2 %constant_dynamic-update-slice_fusion.1 = bf16[2048,7168]{1,0:T(8,128)(2,1)} fusion(bf16[2048,3584]{1,0:T(8,128)(2,1)} %param.11), kind=kLoop, calls=%fused_computation.39 | loop fusion | bytes 29360128
  88.3 6.7 %copy.33 = bf16[1,8,8192]{1,0,2:T(2,128)(2,1)} copy(bf16[1,8,8192]{2,1,0:T(8,128)(2,1)S(1)} %get-tuple-element.10) | data formatting | bytes 262144 | tf_op jit(solution)/shard_map/slice | solution.py:78
  95.0 45.2 %reduce.17 = bf16[8192,8]{1,0:T(8,128)(2,1)S(1)} reduce(bf16[8192,1,8]{2,1,0:T(2,128)(2,1)} %bitcast.49, bf16[]{:T(256)} %broadcast.240), dimensions={1}, to_apply=%bitcast.36.reduce_sub_computation | reduce | bytes 262146
  140.3 2.8 reshape.305
  143.1 13.1 %constant_dynamic-update-slice_fusion = bf16[2048,7168]{1,0:T(8,128)(2,1)} fusion(bf16[2048,7168]{1,0:T(8,128)(2,1)} %constant_dynamic-update-slice_fusion.1, bf16[2048,3584]{1,0:T(8,128)(2,1)} %param.12), kind=kLoop, calls=%fused_computation.38 | loop fusion | bytes 29360128 | tf_op jit(solution)/shard_map/concatenate | solution.py:72
  156.3 3.3 %all-to-all-start = ((bf16[4,2,8192]{2,1,0:T(2,128)(2,1)}), bf16[4,2,8192]{2,1,0:T(2,128)(2,1)S(1)}, u32[]{:S(2)}, u32[]{:S(2)}) async-start(bf16[4,2,8192]{2,1,0:T(2,128)(2,1)} %reshape.305), calls=%async_computation | async-start | bytes 262144 | tf_op jit(solution)/shard_map/all_to_all | solution.py:19
  159.7 5.9 %reshape.304 = bf16[8192,1,8]{2,1,0:T(2,128)(2,1)} reshape(bf16[4,2,8192]{2,1,0:T(2,128)(2,1)S(1)} %all-to-all-done.2) | data formatting | bytes 262144
  165.6 7.8 %copy.40 = bf16[1,8,8192]{2,1,0:T(8,128)(2,1)S(1)} copy(bf16[1,8,8192]{1,0,2:T(2,128)(2,1)} %bitcast.50) | data formatting | bytes 262144 | tf_op jit(solution)/shard_map/all_to_all | solution.py:19
  173.6 17.0 %all_gather.14 = bf16[1,128,2048]{2,1,0:T(8,128)(2,1)S(1)} all-gather(bf16[1,32,2048]{2,1,0:T(8,128)(2,1)S(1)} %bitcast.54), channel_id=1, replica_groups=mesh['groups'=2,'row'=4,'col'=4] {'col'}, dimensions={1}, use_global_device_ids=true | all-gather | bytes 655360 | tf_op jit(solution)/shard_map/all_gather | solution.py:20
  191.3 13.1 %convolution_convert_fusion = bf16[64,7168]{1,0:T(8,128)(2,1)} fusion(bf16[2048,7168]{1,0:T(8,128)(2,1)} %constant_dynamic-update-slice_fusion, bf16[64,2048]{1,0:T(8,128)(2,1)S(1)} %gather_fusion.3, pred[64]{0:T(512)(128)(4,1)S(1)} %compare_and_fusion), kind=kOutput, calls=%fused_computation.6 | convolution fusion | flops 1879638016 | bytes 30539840 | tf_op jit(solution)/shard_map/dot_general | solution.py:49
  204.7 5.9 %reshape.306 = bf16[8192,1,8]{2,1,0:T(2,128)(2,1)} reshape(bf16[4,2,8192]{2,1,0:T(2,128)(2,1)S(1)} %all-to-all-done) | data formatting | bytes 262144
  210.6 7.9 %copy.34 = bf16[1,8,8192]{2,1,0:T(8,128)(2,1)S(1)} copy(bf16[1,8,8192]{1,0,2:T(2,128)(2,1)} %bitcast.51) | data formatting | bytes 262144 | tf_op jit(solution)/shard_map/all_to_all | solution.py:19
  218.7 15.5 %all_gather.12 = bf16[1,128,2048]{2,1,0:T(8,128)(2,1)S(1)} all-gather(bf16[1,32,2048]{2,1,0:T(8,128)(2,1)S(1)} %bitcast.55), channel_id=1, replica_groups=mesh['groups'=2,'row'=4,'col'=4] {'col'}, dimensions={1}, use_global_device_ids=true | all-gather | bytes 655360 | tf_op jit(solution)/shard_map/all_gather | solution.py:20
  234.9 13.2 %convolution_convert_fusion.1 = bf16[64,7168]{1,0:T(8,128)(2,1)} fusion(bf16[2048,7168]{1,0:T(8,128)(2,1)} %constant_dynamic-update-slice_fusion, bf16[64,2048]{1,0:T(8,128)(2,1)S(1)} %gather_fusion.2, pred[64]{0:T(512)(128)(4,1)S(1)} %compare_and_fusion.1), kind=kOutput, calls=%fused_computation.7 | convolution fusion | flops 1879638016 | bytes 30539840 | tf_op jit(solution)/shard_map/dot_general | solution.py:49
  249.3 7.3 %all_gather.15 = bf16[64,3584]{1,0:T(8,128)(2,1)S(1)} all-gather(bf16[16,3584]{1,0:T(8,128)(2,1)S(1)} %fusion.6), channel_id=1, replica_groups=mesh['groups'=2,'row'=4,'col'=4] {'row'}, dimensions={0}, use_global_device_ids=true | all-gather | bytes 573440 | tf_op jit(solution)/shard_map/all_gather | solution.py:55
  256.6 8.7 %convolution_convert_fusion.2 = bf16[64,2048]{1,0:T(8,128)(2,1)} fusion(bf16[64,3584]{1,0:T(8,128)(2,1)S(1)} %all_gather.15, bf16[3584,2048]{1,0:T(8,128)(2,1)} %param.13), kind=kOutput, calls=%fused_computation.8 | convolution fusion | flops 939655168 | bytes 15400960 | tf_op jit(solution)/shard_map/dot_general | solution.py:58
  265.4 8.2 %reduce-scatter.5.cloned.1.call-done = bf16[16,7168]{1,0:T(8,128)(2,1)} async-done(((bf16[64,7168]{1,0:T(8,128)(2,1)}), bf16[16,7168]{1,0:T(8,128)(2,1)}) %reduce-scatter.5.cloned.1.call-update) | async-done | bytes 229392 | tf_op jit(solution)/shard_map/reduce_scatter | solution.py:48
  274.6 6.4 %all_gather.13 = bf16[64,3584]{1,0:T(8,128)(2,1)S(1)} all-gather(bf16[16,3584]{1,0:T(8,128)(2,1)S(1)} %fusion.7), channel_id=1, replica_groups=mesh['groups'=2,'row'=4,'col'=4] {'row'}, dimensions={0}, use_global_device_ids=true | all-gather | bytes 573440 | tf_op jit(solution)/shard_map/all_gather | solution.py:55
  281.1 8.6 %convolution_convert_fusion.3 = bf16[64,2048]{1,0:T(8,128)(2,1)} fusion(bf16[64,3584]{1,0:T(8,128)(2,1)S(1)} %all_gather.13, bf16[3584,2048]{1,0:T(8,128)(2,1)} %param.13), kind=kOutput, calls=%fused_computation.9 | convolution fusion | flops 939655168 | bytes 15400960 | tf_op jit(solution)/shard_map/dot_general | solution.py:58
  289.7 5.7 %reduce-scatter.11.cloned.1.call-done = bf16[16,2048]{1,0:T(8,128)(2,1)} async-done(((bf16[64,2048]{1,0:T(8,128)(2,1)}), bf16[16,2048]{1,0:T(8,128)(2,1)}) %reduce-scatter.11.cloned.1.call-update) | async-done | bytes 65552 | tf_op jit(solution)/shard_map/reduce_scatter | solution.py:57
  295.4 1.5 all_to_all.61
  296.9 3.3 all-to-all-start.3
  300.2 15.3 %reduce-scatter.7.cloned.1.call-done = bf16[16,2048]{1,0:T(8,128)(2,1)} async-done(((bf16[64,2048]{1,0:T(8,128)(2,1)}), bf16[16,2048]{1,0:T(8,128)(2,1)}) %reduce-scatter.7.cloned.1.call-update) | async-done | bytes 65552 | tf_op jit(solution)/shard_map/reduce_scatter | solution.py:57
  316.4 6.8 %all_to_all.68 = bf16[4,4,2048]{2,1,0:T(4,128)(2,1)S(1)} all-to-all(bf16[4,4,2048]{2,1,0:T(4,128)(2,1)S(1)} %all_to_all.54), channel_id=1, replica_groups=mesh['groups'=2,'row'=4,'col'=4] {'row'}, dimensions={0} | all-to-all | bytes 131072 | tf_op jit(solution)/shard_map/all_to_all | solution.py:63
  (64 shorter events, 11.0 us)
Async XLA Ops:
  64.2 92.1 %all-to-all-start.2 = ((bf16[4,2,8192]{2,1,0:T(2,128)(2,1)}), bf16[4,2,8192]{2,1,0:T(2,128)(2,1)S(1)}, u32[]{:S(2)}, u32[]{:S(2)}) async-start(bf16[4,2,8192]{2,1,0:T(2,128)(2,1)} %reshape.303), calls=%async_computation.4 | async-start | bytes 262144 | tf_op jit(solution)/shard_map/all_to_all | solution.py:19
  156.3 48.4 %all-to-all-start = ((bf16[4,2,8192]{2,1,0:T(2,128)(2,1)}), bf16[4,2,8192]{2,1,0:T(2,128)(2,1)S(1)}, u32[]{:S(2)}, u32[]{:S(2)}) async-start(bf16[4,2,8192]{2,1,0:T(2,128)(2,1)} %reshape.305), calls=%async_computation | async-start | bytes 262144 | tf_op jit(solution)/shard_map/all_to_all | solution.py:19
  159.6 88.6 %reduce-scatter.9.cloned.1.call-start = ((), (), s32[]{:S(2)}) async-start(), calls=%async_computation.10 | async-start | bytes 1146880 | tf_op jit(solution)/shard_map/reduce_scatter | solution.py:48
  204.4 69.1 %reduce-scatter.5.cloned.1.call-start = ((), (), s32[]{:S(2)}) async-start(), calls=%async_computation.8 | async-start | bytes 1146880 | tf_op jit(solution)/shard_map/reduce_scatter | solution.py:48
  248.1 47.3 %reduce-scatter.11.cloned.1.call-start = ((), (), s32[]{:S(2)}) async-start(), calls=%async_computation.11 | async-start | bytes 327680 | tf_op jit(solution)/shard_map/reduce_scatter | solution.py:57
  265.3 50.1 %reduce-scatter.7.cloned.1.call-start = ((), (), s32[]{:S(2)}) async-start(), calls=%async_computation.9 | async-start | bytes 327680 | tf_op jit(solution)/shard_map/reduce_scatter | solution.py:57
  296.9 19.4 %all-to-all-start.3 = ((bf16[4,4,2048]{2,1,0:T(4,128)(2,1)}), bf16[4,4,2048]{2,1,0:T(4,128)(2,1)S(1)}, u32[]{:S(2)}, u32[]{:S(2)}) async-start(bf16[4,4,2048]{2,1,0:T(4,128)(2,1)} %all_to_all.61), calls=%async_computation.7 | async-start | bytes 131072 | tf_op jit(solution)/shard_map/all_to_all | solution.py:63
Sparse Core Ops, SparseCore 0:
  204.6 25.6 reduce-scatter.8
  248.3 25.2 reduce-scatter.4
  275.8 19.5 reduce-scatter.10
  297.6 17.7 reduce-scatter.6
where the time goes:
time: 332 us; the launch traced here: 330 us
  other arithmetic  95.8 us (29%)
  local copies, waits for them, and re-layouts  84.1 us (25%)
  blocking collectives  53 us (16%)
  matrix products  43.6 us (13%)
  waiting for transfers between devices  29.2 us (9%)
  between operations  13.4 us (4%)
  starting transfers between devices  11.2 us (3%)
    unnamed x2, other arithmetic  90.5 us
    all_gather x2, blocking collectives, layer_block(): gathered = lax.all_gather(spread, 'col', axis=1, tiled=True)  32.5 us
    unnamed x6, local copies, waits for them, and re-layouts  31.3 us
    dot_general x2, matrix products, layer_block(): jnp.dot(rows_here, paired, preferred_element_type=jnp.float32)  26.3 us
    reduce_scatter x2, waiting for transfers between devices, layer_block(): lax.psum_scatter(jnp.dot(rows_here, down_w, preferred_element_type=jnp.fl...  21 us
    dot_general x2, matrix products, layer_block(): jnp.dot(rows_here, down_w, preferred_element_type=jnp.float32)  17.4 us
    all_to_all x6, local copies, waits for them, and re-layouts, layer_block(): lax.all_to_all(normed_block, 'row', split_axis=2, concat_axis=1, tiled=True)  16 us
    all_gather x2, blocking collectives, layer_block(): hidden_all = lax.all_gather(hidden, 'row', axis=0, tiled=True)  13.8 us
  transfers between devices with their start and end apart: 7, of which 3 were waited for; matrix products, arithmetic and copies ran while one was open for 49% of the time, Pallas kernels for 0%

commit v1 on v0

--- a/solution.py
+++ b/solution.py
@@ -1,13 +1,332 @@
+import functools
+
 import jax
 import jax.numpy as jnp
 from jax import lax
+from jax.experimental import pallas as pl
+from jax.experimental.pallas import tpu as pltpu
 from jax.sharding import PartitionSpec as P
 
 STEPS = 2
 MEAN = 4
 
-
 epsilon = 1e-05
+
+BF = jnp.bfloat16
+F32 = jnp.float32
+MIB = 2**20
+X1 = ((0, 1), (1, 0), (2, 3), (3, 2))
+X2 = ((0, 2), (1, 3), (2, 0), (3, 1))
+X3 = ((0, 3), (1, 2), (2, 1), (3, 0))
+Z_ORDER = (0, 3, 1, 2)
+
+
+def vmem_spec():
+    return pl.BlockSpec(memory_space=pltpu.VMEM)
+
+
+def call(body, outs, specs, scratch=(), limit=24, cost=None):
+    return pl.pallas_call(
+        body,
+        out_shape=outs,
+        in_specs=specs,
+        out_specs=jax.tree.map(lambda _: vmem_spec(), outs),
+        scratch_shapes=scratch,
+        compiler_params=pltpu.CompilerParams(vmem_limit_bytes=limit * MIB),
+        cost_estimate=cost,
+    )
+
+
+def place():
+    row = lax.axis_index("row")
+    return row // 2, lax.rem(row, 2), lax.axis_index("col")
+
+
+def norm_body(rows_ref, own_ref, core_ref, y_ref, yd_ref):
+    y, c, _ = place()
+    width = own_ref.shape[2]
+    for step in range(rows_ref.shape[0]):
+        total = jnp.sum(jnp.square(rows_ref[step].astype(F32)), axis=-1, keepdims=True)
+        scale = lax.rsqrt(total / rows_ref.shape[2] + epsilon)
+        for dy, dc, out in ((0, 0, own_ref), (0, 1, core_ref), (1, 0, y_ref), (1, 1, yd_ref)):
+            block = lax.bitwise_xor(y, dy) * 2 + lax.bitwise_xor(c, dc)
+            at = pl.ds(pl.multiple_of(block * width, width), width)
+            out[step] = (rows_ref[step, :, at].astype(F32) * scale).astype(BF)
+
+
+def normed_blocks(sender_rows):
+    steps, slots, width = sender_rows.shape
+    one = jax.ShapeDtypeStruct((steps, slots, width // 4), BF)
+    return call(norm_body, (one,) * 4, [vmem_spec()])(sender_rows)
+
+
+def pick_body(counts_ref, assign_ref, pick_ref):
+    y, c, z = place()
+    rows = pick_ref.shape[0] // 2
+    slots = assign_ref.shape[1]
+    arrivals = pick_ref.shape[1]
+    spread = (
+        lax.broadcasted_iota(jnp.int32, (slots // 8, slots), 1) // 8
+        == lax.broadcasted_iota(jnp.int32, (slots // 8, slots), 0)
+    ).astype(F32)
+    held = jnp.dot(counts_ref[...].astype(F32), spread, preferred_element_type=F32)
+    slot = lax.rem(lax.broadcasted_iota(jnp.int32, (1, slots), 1), 8).astype(F32)
+    at = lax.broadcasted_iota(jnp.int32, (rows, slots), 0)
+    dz = at // 16
+    dz = jnp.where(dz == 0, 0, jnp.where(dz == 1, 3, dz - 1))
+    target = (lax.rem(at, 16) // 4) * 16 + lax.bitwise_xor(dz, z) * 4 + lax.rem(at, 4)
+    p = lax.broadcasted_iota(jnp.int32, (slots, arrivals), 1)
+    bit = lambda shift: lax.rem(lax.shift_right_logical(p, shift), 2)
+    row = lax.bitwise_xor(bit(5), y) * 2 + lax.bitwise_xor(bit(4), c)
+    sender = row * 4 + lax.bitwise_xor(lax.shift_right_logical(p, 6), z)
+    source = sender * 8 + lax.rem(p, 8)
+    entry = lax.broadcasted_iota(jnp.int32, (slots, arrivals), 0)
+    for step in range(2):
+        live = slot < held[step : step + 1]
+        chosen = jnp.where(live, assign_ref[step : step + 1, :], -1)
+        placed = (chosen == target).astype(F32).astype(BF)
+        moved = ((entry == source) & (bit(3) == step)).astype(F32).astype(BF)
+        pick_ref[step * rows : (step + 1) * rows, :] = jnp.dot(
+            placed, moved, preferred_element_type=F32
+        ).astype(BF)
+
+
+def pick_matrix(counts, assign):
+    rows = MEAN * counts.shape[1]
+    return call(
+        pick_body,
+        jax.ShapeDtypeStruct((2 * rows, 2 * assign.shape[1]), BF),
+        [vmem_spec()] * 2,
+    )(counts, assign)
+
+
+def fetch_columns_body(other, w_ref, out_ref, sem):
+    _, c, _ = place()
+    width = out_ref.shape[1]
+    half = lax.bitwise_xor(c, other)
+    copy = pltpu.make_async_copy(
+        w_ref.at[:, pl.ds(pl.multiple_of(half * width, 128), width)], out_ref, sem
+    )
+    copy.start()
+    copy.wait()
+
+
+def fetch_columns(w, other):
+    return pl.pallas_call(
+        functools.partial(fetch_columns_body, other),
+        out_shape=pltpu.VMEM((w.shape[0], w.shape[1] // 2), BF),
+        in_specs=[pl.BlockSpec(memory_space=pl.ANY)],
+        out_specs=vmem_spec(),
+        scratch_shapes=[pltpu.SemaphoreType.DMA],
+        compiler_params=pltpu.CompilerParams(vmem_limit_bytes=MIB),
+        cost_estimate=pl.CostEstimate(flops=0, bytes_accessed=w.size * 2, transcendentals=0),
+    )(w)
+
+
+def fetch_rows_body(other, w_ref, out_ref, sem):
+    _, c, _ = place()
+    height = out_ref.shape[0]
+    half = lax.bitwise_xor(c, other)
+    copy = pltpu.make_async_copy(
+        w_ref.at[pl.ds(pl.multiple_of(half * height, 16), height), :], out_ref, sem
+    )
+    copy.start()
+    copy.wait()
+
+
+def fetch_rows(w, other):
+    return pl.pallas_call(
+        functools.partial(fetch_rows_body, other),
+        out_shape=pltpu.VMEM((w.shape[0] // 2, w.shape[1]), BF),
+        in_specs=[pl.BlockSpec(memory_space=pl.ANY)],
+        out_specs=vmem_spec(),
+        scratch_shapes=[pltpu.SemaphoreType.DMA],
+        compiler_params=pltpu.CompilerParams(vmem_limit_bytes=MIB),
+        cost_estimate=pl.CostEstimate(flops=0, bytes_accessed=w.size * 2, transcendentals=0),
+    )(w)
+
+
+def quarter(ref, dy):
+    y, _, _ = place()
+    width = ref.shape[1] // 2
+    return ref[:, pl.ds(pl.multiple_of(lax.bitwise_xor(y, dy) * width, 128), width)]
+
+
+def first_body(*refs):
+    pieces, (pick_ref, gate_ref, up_ref, batch_ref, far_ref, near_ref, slots) = refs[:8], refs[8:]
+    height = pieces[0].shape[0]
+    for i, piece in enumerate(pieces):
+        slots[i * height : (i + 1) * height, :] = piece[...]
+    batch_ref[...] = jnp.dot(pick_ref[...], slots[...], preferred_element_type=F32).astype(BF)
+    width = gate_ref.shape[1] // 2
+    for dy, out in ((1, far_ref), (0, near_ref)):
+        for i, w in enumerate((gate_ref, up_ref)):
+            out[:, i * width : (i + 1) * width] = jnp.dot(
+                batch_ref[...], quarter(w, dy), preferred_element_type=F32
+            ).astype(BF)
+
+
+def first_half(pieces, pick, gate, up):
+    rows = pick.shape[0]
+    out = jax.ShapeDtypeStruct((rows, gate.shape[1]), BF)
+    height, width = pieces[0].shape
+    return call(
+        first_body,
+        (jax.ShapeDtypeStruct((rows, width), BF), out, out),
+        [vmem_spec()] * 11,
+        scratch=[pltpu.VMEM((8 * height, width), BF)],
+    )(*pieces, pick, gate, up)
+
+
+def far_body(batch_ref, gate_ref, up_ref, got_ref, *outs):
+    width = gate_ref.shape[1] // 2
+    rows = outs[0].shape[0]
+    for i, w in enumerate((gate_ref, up_ref)):
+        at = slice(i * width, (i + 1) * width)
+        total = jnp.dot(batch_ref[...], quarter(w, 1), preferred_element_type=F32)
+        total = (total + got_ref[:, at].astype(F32)).astype(BF)
+        for step, out in enumerate(outs):
+            out[:, at] = total[step * rows : (step + 1) * rows]
+
+
+def far_sums(batch, gate, up, got):
+    out = jax.ShapeDtypeStruct((batch.shape[0] // 2, gate.shape[1]), BF)
+    return call(far_body, (out, out), [vmem_spec()] * 4)(batch, gate, up, got)
+
+
+def near_body(batch_ref, gate_ref, up_ref, got_ref, *outs):
+    width = gate_ref.shape[1] // 2
+    rows = outs[0].shape[0]
+    for i, w in enumerate((gate_ref, up_ref)):
+        at = slice(i * width, (i + 1) * width)
+        total = jnp.dot(batch_ref[...], quarter(w, 0), preferred_element_type=F32)
+        total = total + got_ref[:, at].astype(F32)
+        for step, out in enumerate(outs):
+            out[:, at] = total[step * rows : (step + 1) * rows]
+
+
+def near_sums(batch, gate, up, got):
+    out = jax.ShapeDtypeStruct((batch.shape[0] // 2, gate.shape[1]), F32)
+    return call(near_body, (out, out), [vmem_spec()] * 4)(batch, gate, up, got)
+
+
+def hidden_body(near_ref, got_ref, hidden_ref):
+    width = hidden_ref.shape[1]
+    total = near_ref[...] + got_ref[...].astype(F32)
+    gate, up = total[:, :width], total[:, width:]
+    hidden_ref[...] = (gate / (1.0 + jnp.exp(-gate)) * up).astype(BF)
+
+
+def hidden_units(near, got):
+    out = jax.ShapeDtypeStruct((near.shape[0], near.shape[1] // 2), BF)
+    return call(hidden_body, out, [vmem_spec()] * 2)(near, got)
+
+
+def down_body(own_ref, core_ref, y_ref, yd_ref, down0_ref, down1_ref, keep_ref, send_ref):
+    y, _, _ = place()
+    height = down0_ref.shape[0] // 2
+    rows = keep_ref.shape[0]
+    total = 0.0
+    for dy, hidden, down in ((0, own_ref, down0_ref), (0, core_ref, down1_ref), (1, y_ref, down0_ref), (1, yd_ref, down1_ref)):
+        at = pl.ds(pl.multiple_of(lax.bitwise_xor(y, dy) * height, 16), height)
+        total = total + jnp.dot(hidden[...], down[at, :], preferred_element_type=F32)
+    keep_ref[...] = total[:rows]
+    send_ref[...] = total[rows:].astype(BF)
+
+
+def down_sums(hidden, down):
+    rows, width = hidden[0].shape[0] // 2, down[0].shape[1]
+    return call(
+        down_body,
+        (jax.ShapeDtypeStruct((rows, width), F32), jax.ShapeDtypeStruct((rows, width), BF)),
+        [vmem_spec()] * 6,
+    )(*hidden, *down)
+
+
+def pair_body(keep_ref, got_ref, own_ref, send_ref):
+    rows = own_ref.shape[0]
+    total = keep_ref[...] + got_ref[...].astype(F32)
+    own_ref[...] = total[:rows]
+    send_ref[...] = total[rows:].astype(BF)
+
+
+def pair_sums(keep, got):
+    rows, width = keep.shape[0] // 2, keep.shape[1]
+    return call(
+        pair_body,
+        (jax.ShapeDtypeStruct((rows, width), F32), jax.ShapeDtypeStruct((rows, width), BF)),
+        [vmem_spec()] * 2,
+    )(keep, got)
+
+
+def owner_body(keep0_ref, keep1_ref, got0_ref, got1_ref, *outs):
+    y, c, _ = place()
+    at = lax.broadcasted_iota(jnp.int32, (16, 16), 0)
+    source = lax.bitwise_xor(at, (y * 2 + c) * 4)
+    turn = (lax.broadcasted_iota(jnp.int32, (16, 16), 1) == source).astype(F32).astype(BF)
+    for step, (keep, got) in enumerate(((keep0_ref, got0_ref), (keep1_ref, got1_ref))):
+        total = (keep[...] + got[...].astype(F32)).astype(BF)
+        turned = jnp.dot(turn, total, preferred_element_type=F32)
+        for i, out in enumerate(outs):
+            out[step] = turned[i * 4 : (i + 1) * 4].astype(BF)
+
+
+def owner_blocks(keep, got):
+    out = jax.ShapeDtypeStruct((2, 4, keep[0].shape[1]), BF)
+    return call(owner_body, (out,) * 4, [vmem_spec()] * 4)(*keep, *got)
+
+
+def output_body(own_ref, core_ref, y_ref, yd_ref, out_ref):
+    y, c, _ = place()
+    width = own_ref.shape[2]
+    for dy, dc, block in ((0, 0, own_ref), (0, 1, core_ref), (1, 0, y_ref), (1, 1, yd_ref)):
+        source = lax.bitwise_xor(y, dy) * 2 + lax.bitwise_xor(c, dc)
+        out_ref[:, :, pl.ds(pl.multiple_of(source * width, width), width)] = block[...]
+
+
+def output_rows(blocks):
+    steps, rows, width = blocks[0].shape
+    return call(output_body, jax.ShapeDtypeStruct((steps, rows, 4 * width), BF), [vmem_spec()] * 4)(*blocks)
+
+
+def exchange(blocks):
+    own, core, y, yd = blocks
+    y = lax.ppermute(y, "row", X2)
+    yd = lax.ppermute(yd, "row", X3)
+    core = lax.ppermute(core, "row", X1)
+    return own, core, y, yd
+
+
+def near_plan(sender_rows, counts, assign, gate_w, up_w, down_w):
+    steps, slots, _ = sender_rows.shape
+    own, core, y, yd = exchange(normed_blocks(sender_rows))
+    pick = pick_matrix(counts, assign)
+    arrived = []
+    for pair in ((own, core), (y, yd)):
+        block = jnp.concatenate([p.reshape(steps * slots, -1) for p in pair], axis=0)
+        far = lax.ppermute(block, "col", X3)
+        near = lax.ppermute(block, "col", X1)
+        arrived.append((block, near, lax.ppermute(far, "col", X1), far))
+    pieces = [arrived[dy][dz] for dz in range(4) for dy in range(2)]
+    gate1, up1 = fetch_columns(gate_w, 1), fetch_columns(up_w, 1)
+    gate0, up0 = fetch_columns(gate_w, 0), fetch_columns(up_w, 0)
+    batch, far, near = first_half(pieces, pick, gate1, up1)
+    far = lax.ppermute(far, "row", X1)
+    near = lax.ppermute(near, "row", X1)
+    sends = far_sums(batch, gate0, up0, far)
+    keeps = near_sums(batch, gate0, up0, near)
+    down0, down1 = fetch_rows(down_w, 0), fetch_rows(down_w, 1)
+    owns, lasts = [], []
+    for step in range(steps):
+        hidden = hidden_units(keeps[step], lax.ppermute(sends[step], "row", X2))
+        hidden_y = lax.ppermute(hidden, "row", X2)
+        hidden_core = lax.ppermute(hidden, "row", X1)
+        hidden_yd = lax.ppermute(hidden_y, "row", X1)
+        keep, send = down_sums((hidden, hidden_core, hidden_y, hidden_yd), (down0, down1))
+        keep, send = pair_sums(keep, lax.ppermute(send, "col", X1))
+        owns.append(keep)
+        lasts.append(lax.ppermute(send, "col", X3))
+    return output_rows(exchange(owner_blocks(owns, lasts)))
 
 
 def layer_block(normed_block, counts_block, assign_block, paired, down_w, hidden_cols):
@@ -64,7 +383,7 @@
     return finished.reshape(step_count, MEAN, finished.shape[1])
 
 
-def per_device(sender_rows, counts, assign, gate_w, up_w, down_w):
+def any_plan(sender_rows, counts, assign, gate_w, up_w, down_w):
     values = sender_rows.astype(jnp.float32)
     normed = (
         values * lax.rsqrt(jnp.mean(values * values, axis=-1, keepdims=True) + epsilon)
@@ -88,8 +407,9 @@
 
 
 def solution(mesh):
+    near = mesh.shape["row"] == 4 and mesh.shape["col"] == 4
     return jax.shard_map(
-        per_device,
+        near_plan if near else any_plan,
         mesh=mesh,
         in_specs=(
             P(None, ("groups", "row", "col"), None),

time: 332 us -> 103 us (0.31)
  other arithmetic: 95.8 us -> 0.02 us
  local copies, waits for them, and re-layouts: 84.1 us -> 29.9 us
  blocking collectives: 53 us -> 0 us
  matrix products: 43.6 us -> 0 us
  starting transfers between devices: 11.2 us -> 32.2 us
  Pallas kernels: 0 us -> 15 us
  between operations: 13.4 us -> 0.33 us
  waiting for transfers between devices: 29.2 us -> 25 us
    unnamed x2, other arithmetic: 90.5 us -> 0.01 us
    all_gather x4 -> x0, blocking collectives: 46.3 us -> none  [the longest x2 32.5 us: layer_block(): gathered = lax.all_gather(spread, 'col', axis=1, tiled=True)]
    dot_general x4 -> x0, matrix products: 43.6 us -> none  [the longest x2 26.3 us: layer_block(): jnp.dot(rows_here, paired, preferred_element_type=jnp.float32)]
    ppermute x0 -> x26, starting transfers between devices: none -> 32.2 us  [the longest x2 7.78 us: near_plan(): arrived.append((block, near, lax.ppermute(far, 'col', X1), far))]
    reduce_scatter x4 -> x0, waiting for transfers between devices: 29.2 us -> none  [the longest x2 21 us: layer_block(): lax.psum_scatter(jnp.dot(rows_here, down_w, preferred_element_type=jnp.fl...]
    ppermute x0 -> x26, waiting for transfers between devices: none -> 25 us  [the longest x2 8.54 us: near_plan(): hidden = hidden_units(keeps[step], lax.ppermute(sends[step], 'row', X2))]
    all_to_all x8 -> x0, local copies, waits for them, and re-layouts: 18.4 us -> none  [the longest x6 16 us: layer_block(): lax.all_to_all(normed_block, 'row', split_axis=2, concat_axis=1, tiled=True)]
    slice x5 -> x0, local copies, waits for them, and re-layouts: 15 us -> none  [the longest x3 13.5 us: per_device(): normed[step_index:step_index + 1]]
  transfers between devices with their start and end apart: 7 -> 26, of which waited for: 3 -> 13; matrix products, arithmetic and copies ran while one was open for 49% -> 0% of each run, Pallas kernels for 0% -> 11%
where the time goes in v1:
time: 103 us; the launch traced here: 102 us
  starting transfers between devices  32.2 us (31%)
  local copies, waits for them, and re-layouts  29.9 us (29%)
  waiting for transfers between devices  25 us (24%)
  Pallas kernels  15 us (15%)
    unnamed x36, local copies, waits for them, and re-layouts  29.9 us
    ppermute x2, waiting for transfers between devices, near_plan(): hidden = hidden_units(keeps[step], lax.ppermute(sends[step], 'row', X2))  8.54 us
    ppermute x2, starting transfers between devices, near_plan(): arrived.append((block, near, lax.ppermute(far, 'col', X1), far))  7.78 us
    pallas_call x2, Pallas kernels, down_sums(): call(down_body, (jax.ShapeDtypeStruct((rows, width), F32), jax.ShapeDtype...  5.37 us
    ppermute x2, starting transfers between devices, near_plan(): lasts.append(lax.ppermute(send, 'col', X3))  5.08 us
    ppermute x2, starting transfers between devices, exchange(): y = lax.ppermute(y, 'row', X2)  4.47 us
    ppermute x2, waiting for transfers between devices, exchange(): y = lax.ppermute(y, 'row', X2)  4.16 us
    ppermute x2, starting transfers between devices, near_plan(): far = lax.ppermute(block, 'col', X3)  3.95 us
  transfers between devices with their start and end apart: 26, of which 13 were waited for; matrix products, arithmetic and copies ran while one was open for 0% of the time, Pallas kernels for 11%

profile of v1, /device:TPU:0, one launch (start us, length us, event | category | flops | bytes accessed | tf_op | source)
XLA Modules:
  0.0 102.4 jit_solution(4873694017781770225)
XLA Ops:
  1.2 3.0 %collective-permute-start.1 = (bf16[2,8,2048]{2,1,0:T(8,128)(2,1)S(1)}, bf16[2,8,2048]{2,1,0:T(8,128)(2,1)S(1)}, u32[]{:S(2)}, u32[]{:S(2)}) collective-permute-start(bf16[2,8,2048]{2,1,0:T(8,128)(2,1)S(1)} %get-tuple-element.30), channel_id=1, source_target_pairs={{0,8},{4,12},{8,0},{12,4},{1,9},{5,13},{9,1},{13,5},{2,10},{6,14},... | collective-permute-start | bytes 196616 | tf_op jit(solution)/shard_map/ppermute | solution.py:294
  4.4 2.1 %collective-permute-done.1 = bf16[2,8,2048]{2,1,0:T(8,128)(2,1)S(1)} collective-permute-done((bf16[2,8,2048]{2,1,0:T(8,128)(2,1)S(1)}, bf16[2,8,2048]{2,1,0:T(8,128)(2,1)S(1)}, u32[]{:S(2)}, u32[]{:S(2)}) %collective-permute-start.1) | collective-permute-done | bytes 65568 | tf_op jit(solution)/shard_map/ppermute | solution.py:294
  6.4 1.9 %collective-permute-done.2 = bf16[2,8,2048]{2,1,0:T(8,128)(2,1)S(1)} collective-permute-done((bf16[2,8,2048]{2,1,0:T(8,128)(2,1)S(1)}, bf16[2,8,2048]{2,1,0:T(8,128)(2,1)S(1)}, u32[]{:S(2)}, u32[]{:S(2)}) %collective-permute-start.2) | collective-permute-done | bytes 65568 | tf_op jit(solution)/shard_map/ppermute | solution.py:295
  8.3 3.7 %collective-permute-start.7 = (bf16[32,2048]{1,0:T(8,128)(2,1)S(1)}, bf16[32,2048]{1,0:T(8,128)(2,1)S(1)}, u32[]{:S(2)}, u32[]{:S(2)}) collective-permute-start(bf16[32,2048]{1,0:T(8,128)(2,1)S(1)} %pad_maximum_fusion.1.refs_1_), channel_id=1, source_target_pairs={{0,3},{1,2},{2,1},{3,0},{4,7},{5,6},{6,5},{7,4},{8,11},{9,10},{10,... | collective-permute-start | bytes 393224 | tf_op jit(solution)/shard_map/ppermute | solution.py:307
  12.3 2.0 %collective-permute-start.3 = (bf16[32,2048]{1,0:T(8,128)(2,1)S(1)}, bf16[32,2048]{1,0:T(8,128)(2,1)S(1)}, u32[]{:S(2)}, u32[]{:S(2)}) collective-permute-start(bf16[32,2048]{1,0:T(8,128)(2,1)S(1)} %pad_maximum_fusion.refs_0_), channel_id=1, source_target_pairs={{0,1},{1,0},{2,3},{3,2},{4,5},{5,4},{6,7},{7,6},{8,9},{9,8},{10,11... | collective-permute-start | bytes 393224 | tf_op jit(solution)/shard_map/ppermute | solution.py:308
  14.3 1.6 %collective-permute-done.7.refs_7_ = bf16[32,2048]{1,0:T(8,128)(2,1)S(1)} collective-permute-done((bf16[32,2048]{1,0:T(8,128)(2,1)S(1)}, bf16[32,2048]{1,0:T(8,128)(2,1)S(1)}, u32[]{:S(2)}, u32[]{:S(2)}) %collective-permute-start.7) | collective-permute-done | bytes 131104 | tf_op jit(solution)/shard_map/ppermute | solution.py:307
  15.9 5.9 %collective-permute-start.8 = (bf16[32,2048]{1,0:T(8,128)(2,1)S(1)}, bf16[32,2048]{1,0:T(8,128)(2,1)S(1)}, u32[]{:S(2)}, u32[]{:S(2)}) collective-permute-start(bf16[32,2048]{1,0:T(8,128)(2,1)S(1)} %collective-permute-done.7.refs_7_), channel_id=1, source_target_pairs={{0,1},{1,0},{2,3},{3,2},{4,5},{5,4},{6,7},{7,6},{8,9},{9,8},{10,11... | collective-permute-start | bytes 393224 | tf_op jit(solution)/shard_map/ppermute | solution.py:309
  21.8 1.9 %collective-permute-start.6 = (bf16[32,2048]{1,0:T(8,128)(2,1)S(1)}, bf16[32,2048]{1,0:T(8,128)(2,1)S(1)}, u32[]{:S(2)}, u32[]{:S(2)}) collective-permute-start(bf16[32,2048]{1,0:T(8,128)(2,1)S(1)} %collective-permute-done.5.refs_6_), channel_id=1, source_target_pairs={{0,1},{1,0},{2,3},{3,2},{4,5},{5,4},{6,7},{7,6},{8,9},{9,8},{10,11... | collective-permute-start | bytes 393224 | tf_op jit(solution)/shard_map/ppermute | solution.py:309
  23.7 5.2 %copy-done = bf16[2048,3584]{1,0:T(8,128)(2,1)S(1)} copy-done((bf16[2048,3584]{1,0:T(8,128)(2,1)S(1)}, bf16[2048,3584]{1,0:T(8,128)(2,1)}, u32[]{:S(2)}) %copy-start) | copy-done | bytes 14680088
  29.4 3.7 %copy-done.3 = bf16[2048,1792]{1,0:T(8,128)(2,1)} copy-done((bf16[2048,1792]{1,0:T(8,128)(2,1)}, bf16[2048,1792]{1,0:T(8,128)(2,1)S(1)}, u32[]{:S(2)}) %copy-start.3) | copy-done | bytes 7340056
  33.1 3.6 %copy-done.1 = bf16[2048,3584]{1,0:T(8,128)(2,1)S(1)} copy-done((bf16[2048,3584]{1,0:T(8,128)(2,1)S(1)}, bf16[2048,3584]{1,0:T(8,128)(2,1)}, u32[]{:S(2)}) %copy-start.1) | copy-done | bytes 14680088
  37.2 3.7 %copy-done.5 = bf16[2048,1792]{1,0:T(8,128)(2,1)} copy-done((bf16[2048,1792]{1,0:T(8,128)(2,1)}, bf16[2048,1792]{1,0:T(8,128)(2,1)S(1)}, u32[]{:S(2)}) %copy-start.5) | copy-done | bytes 7340056
  41.3 3.9 %copy-done.4 = bf16[2048,1792]{1,0:T(8,128)(2,1)S(1)} copy-done((bf16[2048,1792]{1,0:T(8,128)(2,1)S(1)}, bf16[2048,1792]{1,0:T(8,128)(2,1)}, u32[]{:S(2)}) %copy-start.4) | copy-done | bytes 7340056
  45.2 3.6 %copy-done.6 = bf16[2048,1792]{1,0:T(8,128)(2,1)S(1)} copy-done((bf16[2048,1792]{1,0:T(8,128)(2,1)S(1)}, bf16[2048,1792]{1,0:T(8,128)(2,1)}, u32[]{:S(2)}) %copy-start.6) | copy-done | bytes 7340056
  48.8 2.5 %shard_map.68 = (bf16[128,2048]{1,0:T(8,128)(2,1)S(1)}, bf16[128,1792]{1,0:T(8,128)(2,1)S(1)}, bf16[128,1792]{1,0:T(8,128)(2,1)S(1)}) custom-call(bf16[32,2048]{1,0:T(8,128)(2,1)S(1)} %pad_maximum_fusion.refs_0_, bf16[32,2048]{1,0:T(8,128)(2,1)S(1)} %pad_maximum_fusion.1.refs_1_, bf16[32,2048]{1,0:T(8,128)(2,1)S(1)} %collective-permute-done.3.refs_2_, ...), custom_call_target="tpu_custom_call" | custom-call | tf_op jit(solution)/shard_map/pallas_call | solution.py:173
  52.5 5.2 %copy-done.2 = bf16[2048,3584]{1,0:T(8,128)(2,1)S(1)} copy-done((bf16[2048,3584]{1,0:T(8,128)(2,1)S(1)}, bf16[2048,3584]{1,0:T(8,128)(2,1)}, u32[]{:S(2)}) %copy-start.2) | copy-done | bytes 14680088
  58.2 1.3 %shard_map.72 = (bf16[64,1792]{1,0:T(8,128)(2,1)S(1)}, bf16[64,1792]{1,0:T(8,128)(2,1)S(1)}) custom-call(bf16[128,2048]{1,0:T(8,128)(2,1)S(1)} %get-tuple-element.32.batch_ref, bf16[2048,1792]{1,0:T(8,128)(2,1)S(1)} %shard_map.69.gate_ref, bf16[2048,1792]{1,0:T(8,128)(2,1)S(1)} %shard_map.70.up_ref, bf16[128,1792]{1,0:T(8,128)(2,1)S(1)} %collective-permute-done.10.got_ref), custom_call_target="tpu_custom_call" | custom-call | tf_op jit(solution)/shard_map/pallas_call | solution.py:194
  59.5 1.4 %collective-permute-start.16 = (bf16[64,1792]{1,0:T(8,128)(2,1)S(1)}, bf16[64,1792]{1,0:T(8,128)(2,1)S(1)}, u32[]{:S(2)}, u32[]{:S(2)}) collective-permute-start(bf16[64,1792]{1,0:T(8,128)(2,1)S(1)} %get-tuple-element.41), channel_id=1, source_target_pairs={{0,8},{4,12},{8,0},{12,4},{1,9},{5,13},{9,1},{13,5},{2,10},{6,14},... | collective-permute-start | bytes 688136 | tf_op jit(solution)/shard_map/ppermute | solution.py:321
  61.6 1.3 %shard_map.71 = (f32[64,1792]{1,0:T(8,128)S(1)}, f32[64,1792]{1,0:T(8,128)S(1)}) custom-call(bf16[128,2048]{1,0:T(8,128)(2,1)S(1)} %get-tuple-element.32.batch_ref, bf16[2048,1792]{1,0:T(8,128)(2,1)S(1)} %shard_map.69.gate_ref, bf16[2048,1792]{1,0:T(8,128)(2,1)S(1)} %shard_map.70.up_ref, bf16[128,1792]{1,0:T(8,128)(2,1)S(1)} %collective-permute-done.9.got_ref), custom_call_target="tpu_custom_call" | custom-call | tf_op jit(solution)/shard_map/pallas_call | solution.py:210
  62.8 5.2 %collective-permute-done.16.got_ref = bf16[64,1792]{1,0:T(8,128)(2,1)S(1)} collective-permute-done((bf16[64,1792]{1,0:T(8,128)(2,1)S(1)}, bf16[64,1792]{1,0:T(8,128)(2,1)S(1)}, u32[]{:S(2)}, u32[]{:S(2)}) %collective-permute-start.16) | collective-permute-done | bytes 229408 | tf_op jit(solution)/shard_map/ppermute | solution.py:321
  68.1 1.4 %collective-permute-start.18 = (bf16[64,896]{1,0:T(8,128)(2,1)S(1)}, bf16[64,896]{1,0:T(8,128)(2,1)S(1)}, u32[]{:S(2)}, u32[]{:S(2)}) collective-permute-start(bf16[64,896]{1,0:T(8,128)(2,1)S(1)} %shard_map.78.own_ref), channel_id=1, source_target_pairs={{0,8},{4,12},{8,0},{12,4},{1,9},{5,13},{9,1},{13,5},{2,10},{6,14},... | collective-permute-start | bytes 344072 | tf_op jit(solution)/shard_map/ppermute | solution.py:322
  69.5 3.4 %collective-permute-done.11.got_ref = bf16[64,1792]{1,0:T(8,128)(2,1)S(1)} collective-permute-done((bf16[64,1792]{1,0:T(8,128)(2,1)S(1)}, bf16[64,1792]{1,0:T(8,128)(2,1)S(1)}, u32[]{:S(2)}, u32[]{:S(2)}) %collective-permute-start.11) | collective-permute-done | bytes 229408 | tf_op jit(solution)/shard_map/ppermute | solution.py:321
  73.0 1.4 %collective-permute-start.13 = (bf16[64,896]{1,0:T(8,128)(2,1)S(1)}, bf16[64,896]{1,0:T(8,128)(2,1)S(1)}, u32[]{:S(2)}, u32[]{:S(2)}) collective-permute-start(bf16[64,896]{1,0:T(8,128)(2,1)S(1)} %shard_map.73.own_ref), channel_id=1, source_target_pairs={{0,8},{4,12},{8,0},{12,4},{1,9},{5,13},{9,1},{13,5},{2,10},{6,14},... | collective-permute-start | bytes 344072 | tf_op jit(solution)/shard_map/ppermute | solution.py:322
  75.4 2.5 %collective-permute-done.13.y_ref = bf16[64,896]{1,0:T(8,128)(2,1)S(1)} collective-permute-done((bf16[64,896]{1,0:T(8,128)(2,1)S(1)}, bf16[64,896]{1,0:T(8,128)(2,1)S(1)}, u32[]{:S(2)}, u32[]{:S(2)}) %collective-permute-start.13) | collective-permute-done | bytes 114720 | tf_op jit(solution)/shard_map/ppermute | solution.py:322
  79.0 2.7 %shard_map.79 = (f32[32,2048]{1,0:T(8,128)S(1)}, bf16[32,2048]{1,0:T(8,128)(2,1)S(1)}) custom-call(bf16[64,896]{1,0:T(8,128)(2,1)S(1)} %shard_map.78.own_ref, bf16[64,896]{1,0:T(8,128)(2,1)S(1)} %collective-permute-done.17.core_ref, bf16[64,896]{1,0:T(8,128)(2,1)S(1)} %collective-permute-done.18.y_ref, bf16[64,896]{1,0:T(8,128)(2,1)S(1)} %collective-permute-done.19.yd_ref, ...), custom_call_target="tpu_custom_call" | custom-call | tf_op jit(solution)/shard_map/pallas_call | solution.py:239
  81.9 2.7 %shard_map.76 = (f32[32,2048]{1,0:T(8,128)S(1)}, bf16[32,2048]{1,0:T(8,128)(2,1)S(1)}) custom-call(bf16[64,896]{1,0:T(8,128)(2,1)S(1)} %shard_map.73.own_ref, bf16[64,896]{1,0:T(8,128)(2,1)S(1)} %collective-permute-done.12.core_ref, bf16[64,896]{1,0:T(8,128)(2,1)S(1)} %collective-permute-done.13.y_ref, bf16[64,896]{1,0:T(8,128)(2,1)S(1)} %collective-permute-done.14.yd_ref, ...), custom_call_target="tpu_custom_call" | custom-call | tf_op jit(solution)/shard_map/pallas_call | solution.py:239
  84.6 1.9 %collective-permute-start.15 = (bf16[32,2048]{1,0:T(8,128)(2,1)S(1)}, bf16[32,2048]{1,0:T(8,128)(2,1)S(1)}, u32[]{:S(2)}, u32[]{:S(2)}) collective-permute-start(bf16[32,2048]{1,0:T(8,128)(2,1)S(1)} %get-tuple-element.38), channel_id=1, source_target_pairs={{0,1},{1,0},{2,3},{3,2},{4,5},{5,4},{6,7},{7,6},{8,9},{9,8},{10,11... | collective-permute-start | bytes 393224 | tf_op jit(solution)/shard_map/ppermute | solution.py:326
  87.7 2.5 %collective-permute-start.22 = (bf16[16,2048]{1,0:T(8,128)(2,1)S(1)}, bf16[16,2048]{1,0:T(8,128)(2,1)S(1)}, u32[]{:S(2)}, u32[]{:S(2)}) collective-permute-start(bf16[16,2048]{1,0:T(8,128)(2,1)S(1)} %get-tuple-element.46), channel_id=1, source_target_pairs={{0,3},{1,2},{2,1},{3,0},{4,7},{5,6},{6,5},{7,4},{8,11},{9,10},{10,... | collective-permute-start | bytes 196616 | tf_op jit(solution)/shard_map/ppermute | solution.py:328
  90.5 2.5 %collective-permute-start.21 = (bf16[16,2048]{1,0:T(8,128)(2,1)S(1)}, bf16[16,2048]{1,0:T(8,128)(2,1)S(1)}, u32[]{:S(2)}, u32[]{:S(2)}) collective-permute-start(bf16[16,2048]{1,0:T(8,128)(2,1)S(1)} %get-tuple-element.45), channel_id=1, source_target_pairs={{0,3},{1,2},{2,1},{3,0},{4,7},{5,6},{6,5},{7,4},{8,11},{9,10},{10,... | collective-permute-start | bytes 196616 | tf_op jit(solution)/shard_map/ppermute | solution.py:328
  94.0 2.7 %collective-permute-done.21.got0_ref = bf16[16,2048]{1,0:T(8,128)(2,1)S(1)} collective-permute-done((bf16[16,2048]{1,0:T(8,128)(2,1)S(1)}, bf16[16,2048]{1,0:T(8,128)(2,1)S(1)}, u32[]{:S(2)}, u32[]{:S(2)}) %collective-permute-start.21) | collective-permute-done | bytes 65568 | tf_op jit(solution)/shard_map/ppermute | solution.py:328
  97.0 1.4 %collective-permute-start.24 = (bf16[2,4,2048]{2,1,0:T(4,128)(2,1)S(1)}, bf16[2,4,2048]{2,1,0:T(4,128)(2,1)S(1)}, u32[]{:S(2)}, u32[]{:S(2)}) collective-permute-start(bf16[2,4,2048]{2,1,0:T(4,128)(2,1)S(1)} %get-tuple-element.49), channel_id=1, source_target_pairs={{0,8},{4,12},{8,0},{12,4},{1,9},{5,13},{9,1},{13,5},{2,10},{6,14},... | collective-permute-start | bytes 98312 | tf_op jit(solution)/shard_map/ppermute | solution.py:294
  98.8 2.1 %collective-permute-done.24.y_ref = bf16[2,4,2048]{2,1,0:T(4,128)(2,1)S(1)} collective-permute-done((bf16[2,4,2048]{2,1,0:T(4,128)(2,1)S(1)}, bf16[2,4,2048]{2,1,0:T(4,128)(2,1)S(1)}, u32[]{:S(2)}, u32[]{:S(2)}) %collective-permute-start.24) | collective-permute-done | bytes 32800 | tf_op jit(solution)/shard_map/ppermute | solution.py:294
  (79 shorter events, 12.2 us)
Async XLA Ops:
  1.2 5.3 %collective-permute-start.1 = (bf16[2,8,2048]{2,1,0:T(8,128)(2,1)S(1)}, bf16[2,8,2048]{2,1,0:T(8,128)(2,1)S(1)}, u32[]{:S(2)}, u32[]{:S(2)}) collective-permute-start(bf16[2,8,2048]{2,1,0:T(8,128)(2,1)S(1)} %get-tuple-element.30), channel_id=1, source_target_pairs={{0,8},{4,12},{8,0},{12,4},{1,9},{5,13},{9,1},{13,5},{2,10},{6,14},... | collective-permute-start | bytes 196616 | tf_op jit(solution)/shard_map/ppermute | solution.py:294
  4.2 4.1 %collective-permute-start.2 = (bf16[2,8,2048]{2,1,0:T(8,128)(2,1)S(1)}, bf16[2,8,2048]{2,1,0:T(8,128)(2,1)S(1)}, u32[]{:S(2)}, u32[]{:S(2)}) collective-permute-start(bf16[2,8,2048]{2,1,0:T(8,128)(2,1)S(1)} %get-tuple-element.31), channel_id=1, source_target_pairs={{0,12},{4,8},{8,4},{12,0},{1,13},{5,9},{9,5},{13,1},{2,14},{6,10},... | collective-permute-start | bytes 196616 | tf_op jit(solution)/shard_map/ppermute | solution.py:295
  4.2 7.8 %collective-permute-start = (bf16[2,8,2048]{2,1,0:T(8,128)(2,1)S(1)}, bf16[2,8,2048]{2,1,0:T(8,128)(2,1)S(1)}, u32[]{:S(2)}, u32[]{:S(2)}) collective-permute-start(bf16[2,8,2048]{2,1,0:T(8,128)(2,1)S(1)} %get-tuple-element.29), channel_id=1, source_target_pairs={{0,4},{4,0},{8,12},{12,8},{1,5},{5,1},{9,13},{13,9},{2,6},{6,2},{1... | collective-permute-start | bytes 196616 | tf_op jit(solution)/shard_map/ppermute | solution.py:296
  8.3 7.6 %collective-permute-start.7 = (bf16[32,2048]{1,0:T(8,128)(2,1)S(1)}, bf16[32,2048]{1,0:T(8,128)(2,1)S(1)}, u32[]{:S(2)}, u32[]{:S(2)}) collective-permute-start(bf16[32,2048]{1,0:T(8,128)(2,1)S(1)} %pad_maximum_fusion.1.refs_1_), channel_id=1, source_target_pairs={{0,3},{1,2},{2,1},{3,0},{4,7},{5,6},{6,5},{7,4},{8,11},{9,10},{10,... | collective-permute-start | bytes 393224 | tf_op jit(solution)/shard_map/ppermute | solution.py:307
  12.0 9.8 %collective-permute-start.5 = (bf16[32,2048]{1,0:T(8,128)(2,1)S(1)}, bf16[32,2048]{1,0:T(8,128)(2,1)S(1)}, u32[]{:S(2)}, u32[]{:S(2)}) collective-permute-start(bf16[32,2048]{1,0:T(8,128)(2,1)S(1)} %pad_maximum_fusion.refs_0_), channel_id=1, source_target_pairs={{0,3},{1,2},{2,1},{3,0},{4,7},{5,6},{6,5},{7,4},{8,11},{9,10},{10,... | collective-permute-start | bytes 393224 | tf_op jit(solution)/shard_map/ppermute | solution.py:307
  12.3 28.9 %collective-permute-start.4 = (bf16[32,2048]{1,0:T(8,128)(2,1)S(1)}, bf16[32,2048]{1,0:T(8,128)(2,1)S(1)}, u32[]{:S(2)}, u32[]{:S(2)}) collective-permute-start(bf16[32,2048]{1,0:T(8,128)(2,1)S(1)} %pad_maximum_fusion.1.refs_1_), channel_id=1, source_target_pairs={{0,1},{1,0},{2,3},{3,2},{4,5},{5,4},{6,7},{7,6},{8,9},{9,8},{10,11... | collective-permute-start | bytes 393224 | tf_op jit(solution)/shard_map/ppermute | solution.py:308
  12.3 28.9 %collective-permute-start.3 = (bf16[32,2048]{1,0:T(8,128)(2,1)S(1)}, bf16[32,2048]{1,0:T(8,128)(2,1)S(1)}, u32[]{:S(2)}, u32[]{:S(2)}) collective-permute-start(bf16[32,2048]{1,0:T(8,128)(2,1)S(1)} %pad_maximum_fusion.refs_0_), channel_id=1, source_target_pairs={{0,1},{1,0},{2,3},{3,2},{4,5},{5,4},{6,7},{7,6},{8,9},{9,8},{10,11... | collective-permute-start | bytes 393224 | tf_op jit(solution)/shard_map/ppermute | solution.py:308
  15.9 25.3 %collective-permute-start.8 = (bf16[32,2048]{1,0:T(8,128)(2,1)S(1)}, bf16[32,2048]{1,0:T(8,128)(2,1)S(1)}, u32[]{:S(2)}, u32[]{:S(2)}) collective-permute-start(bf16[32,2048]{1,0:T(8,128)(2,1)S(1)} %collective-permute-done.7.refs_7_), channel_id=1, source_target_pairs={{0,1},{1,0},{2,3},{3,2},{4,5},{5,4},{6,7},{7,6},{8,9},{9,8},{10,11... | collective-permute-start | bytes 393224 | tf_op jit(solution)/shard_map/ppermute | solution.py:309
  21.8 19.4 %collective-permute-start.6 = (bf16[32,2048]{1,0:T(8,128)(2,1)S(1)}, bf16[32,2048]{1,0:T(8,128)(2,1)S(1)}, u32[]{:S(2)}, u32[]{:S(2)}) collective-permute-start(bf16[32,2048]{1,0:T(8,128)(2,1)S(1)} %collective-permute-done.5.refs_6_), channel_id=1, source_target_pairs={{0,1},{1,0},{2,3},{3,2},{4,5},{5,4},{6,7},{7,6},{8,9},{9,8},{10,11... | collective-permute-start | bytes 393224 | tf_op jit(solution)/shard_map/ppermute | solution.py:309
  36.7 15.2 %slice-start = ((s8[14680064]{0:T(1024)(128)(4,1)}), s8[4194304]{0:T(1024)(128)(4,1)S(1)}, s32[]{:S(2)}) async-start(s8[14680064]{0:T(1024)(128)(4,1)} %bitcast.4), calls=%async_computation | async-start | bytes 8388608
  36.7 15.2 %slice-start.1 = ((s8[14680064]{0:T(1024)(128)(4,1)}), s8[4194304]{0:T(1024)(128)(4,1)S(1)}, s32[]{:S(2)}) async-start(s8[14680064]{0:T(1024)(128)(4,1)} %bitcast.4), calls=%async_computation.1 | async-start | bytes 8388608
  51.3 6.8 %collective-permute-start.10 = (bf16[128,1792]{1,0:T(8,128)(2,1)S(1)}, bf16[128,1792]{1,0:T(8,128)(2,1)S(1)}, u32[]{:S(2)}, u32[]{:S(2)}) collective-permute-start(bf16[128,1792]{1,0:T(8,128)(2,1)S(1)} %get-tuple-element.35), channel_id=1, source_target_pairs={{0,4},{4,0},{8,12},{12,8},{1,5},{5,1},{9,13},{13,9},{2,6},{6,2},{1... | collective-permute-start | bytes 1376264 | tf_op jit(solution)/shard_map/ppermute | solution.py:314
  51.4 10.2 %collective-permute-start.9 = (bf16[128,1792]{1,0:T(8,128)(2,1)S(1)}, bf16[128,1792]{1,0:T(8,128)(2,1)S(1)}, u32[]{:S(2)}, u32[]{:S(2)}) collective-permute-start(bf16[128,1792]{1,0:T(8,128)(2,1)S(1)} %get-tuple-element.33), channel_id=1, source_target_pairs={{0,4},{4,0},{8,12},{12,8},{1,5},{5,1},{9,13},{13,9},{2,6},{6,2},{1... | collective-permute-start | bytes 1376264 | tf_op jit(solution)/shard_map/ppermute | solution.py:315
  58.1 19.7 %slice-start.4 = ((s8[14680064]{0:T(1024)(128)(4,1)}), s8[4194304]{0:T(1024)(128)(4,1)S(1)}, s32[]{:S(2)}) async-start(s8[14680064]{0:T(1024)(128)(4,1)} %bitcast.6), calls=%async_computation.4 | async-start | bytes 8388608
  58.1 19.7 %slice-start.5 = ((s8[14680064]{0:T(1024)(128)(4,1)}), s8[4194304]{0:T(1024)(128)(4,1)S(1)}, s32[]{:S(2)}) async-start(s8[14680064]{0:T(1024)(128)(4,1)} %bitcast.6), calls=%async_computation.5 | async-start | bytes 8388608
  59.5 8.5 %collective-permute-start.16 = (bf16[64,1792]{1,0:T(8,128)(2,1)S(1)}, bf16[64,1792]{1,0:T(8,128)(2,1)S(1)}, u32[]{:S(2)}, u32[]{:S(2)}) collective-permute-start(bf16[64,1792]{1,0:T(8,128)(2,1)S(1)} %get-tuple-element.41), channel_id=1, source_target_pairs={{0,8},{4,12},{8,0},{12,4},{1,9},{5,13},{9,1},{13,5},{2,10},{6,14},... | collective-permute-start | bytes 688136 | tf_op jit(solution)/shard_map/ppermute | solution.py:321
  60.9 17.0 %slice-start.6 = ((s8[14680064]{0:T(1024)(128)(4,1)}), s8[4194304]{0:T(1024)(128)(4,1)S(1)}, s32[]{:S(2)}) async-start(s8[14680064]{0:T(1024)(128)(4,1)} %bitcast.6), calls=%async_computation.6 | async-start | bytes 8388608
  60.9 17.0 %slice-start.7 = ((s8[14680064]{0:T(1024)(128)(4,1)}), s8[2097152]{0:T(1024)(128)(4,1)S(1)}, s32[]{:S(2)}) async-start(s8[14680064]{0:T(1024)(128)(4,1)} %bitcast.6), calls=%async_computation.7 | async-start | bytes 4194304
  60.9 12.0 %collective-permute-start.11 = (bf16[64,1792]{1,0:T(8,128)(2,1)S(1)}, bf16[64,1792]{1,0:T(8,128)(2,1)S(1)}, u32[]{:S(2)}, u32[]{:S(2)}) collective-permute-start(bf16[64,1792]{1,0:T(8,128)(2,1)S(1)} %get-tuple-element.36), channel_id=1, source_target_pairs={{0,8},{4,12},{8,0},{12,4},{1,9},{5,13},{9,1},{13,5},{2,10},{6,14},... | collective-permute-start | bytes 688136 | tf_op jit(solution)/shard_map/ppermute | solution.py:321
  68.1 6.8 %collective-permute-start.18 = (bf16[64,896]{1,0:T(8,128)(2,1)S(1)}, bf16[64,896]{1,0:T(8,128)(2,1)S(1)}, u32[]{:S(2)}, u32[]{:S(2)}) collective-permute-start(bf16[64,896]{1,0:T(8,128)(2,1)S(1)} %shard_map.78.own_ref), channel_id=1, source_target_pairs={{0,8},{4,12},{8,0},{12,4},{1,9},{5,13},{9,1},{13,5},{2,10},{6,14},... | collective-permute-start | bytes 344072 | tf_op jit(solution)/shard_map/ppermute | solution.py:322
  73.0 4.9 %collective-permute-start.13 = (bf16[64,896]{1,0:T(8,128)(2,1)S(1)}, bf16[64,896]{1,0:T(8,128)(2,1)S(1)}, u32[]{:S(2)}, u32[]{:S(2)}) collective-permute-start(bf16[64,896]{1,0:T(8,128)(2,1)S(1)} %shard_map.73.own_ref), channel_id=1, source_target_pairs={{0,8},{4,12},{8,0},{12,4},{1,9},{5,13},{9,1},{13,5},{2,10},{6,14},... | collective-permute-start | bytes 344072 | tf_op jit(solution)/shard_map/ppermute | solution.py:322
  74.4 4.5 %collective-permute-start.17 = (bf16[64,896]{1,0:T(8,128)(2,1)S(1)}, bf16[64,896]{1,0:T(8,128)(2,1)S(1)}, u32[]{:S(2)}, u32[]{:S(2)}) collective-permute-start(bf16[64,896]{1,0:T(8,128)(2,1)S(1)} %shard_map.78.own_ref), channel_id=1, source_target_pairs={{0,4},{4,0},{8,12},{12,8},{1,5},{5,1},{9,13},{13,9},{2,6},{6,2},{1... | collective-permute-start | bytes 344072 | tf_op jit(solution)/shard_map/ppermute | solution.py:323
  74.9 4.1 %collective-permute-start.19 = (bf16[64,896]{1,0:T(8,128)(2,1)S(1)}, bf16[64,896]{1,0:T(8,128)(2,1)S(1)}, u32[]{:S(2)}, u32[]{:S(2)}) collective-permute-start(bf16[64,896]{1,0:T(8,128)(2,1)S(1)} %collective-permute-done.18.y_ref), channel_id=1, source_target_pairs={{0,4},{4,0},{8,12},{12,8},{1,5},{5,1},{9,13},{13,9},{2,6},{6,2},{1... | collective-permute-start | bytes 344072 | tf_op jit(solution)/shard_map/ppermute | solution.py:324
  75.0 7.0 %collective-permute-start.12 = (bf16[64,896]{1,0:T(8,128)(2,1)S(1)}, bf16[64,896]{1,0:T(8,128)(2,1)S(1)}, u32[]{:S(2)}, u32[]{:S(2)}) collective-permute-start(bf16[64,896]{1,0:T(8,128)(2,1)S(1)} %shard_map.73.own_ref), channel_id=1, source_target_pairs={{0,4},{4,0},{8,12},{12,8},{1,5},{5,1},{9,13},{13,9},{2,6},{6,2},{1... | collective-permute-start | bytes 344072 | tf_op jit(solution)/shard_map/ppermute | solution.py:323
  77.9 4.0 %collective-permute-start.14 = (bf16[64,896]{1,0:T(8,128)(2,1)S(1)}, bf16[64,896]{1,0:T(8,128)(2,1)S(1)}, u32[]{:S(2)}, u32[]{:S(2)}) collective-permute-start(bf16[64,896]{1,0:T(8,128)(2,1)S(1)} %collective-permute-done.13.y_ref), channel_id=1, source_target_pairs={{0,4},{4,0},{8,12},{12,8},{1,5},{5,1},{9,13},{13,9},{2,6},{6,2},{1... | collective-permute-start | bytes 344072 | tf_op jit(solution)/shard_map/ppermute | solution.py:324
  81.7 6.0 %collective-permute-start.20 = (bf16[32,2048]{1,0:T(8,128)(2,1)S(1)}, bf16[32,2048]{1,0:T(8,128)(2,1)S(1)}, u32[]{:S(2)}, u32[]{:S(2)}) collective-permute-start(bf16[32,2048]{1,0:T(8,128)(2,1)S(1)} %get-tuple-element.43), channel_id=1, source_target_pairs={{0,1},{1,0},{2,3},{3,2},{4,5},{5,4},{6,7},{7,6},{8,9},{9,8},{10,11... | collective-permute-start | bytes 393224 | tf_op jit(solution)/shard_map/ppermute | solution.py:326
  84.6 5.8 %collective-permute-start.15 = (bf16[32,2048]{1,0:T(8,128)(2,1)S(1)}, bf16[32,2048]{1,0:T(8,128)(2,1)S(1)}, u32[]{:S(2)}, u32[]{:S(2)}) collective-permute-start(bf16[32,2048]{1,0:T(8,128)(2,1)S(1)} %get-tuple-element.38), channel_id=1, source_target_pairs={{0,1},{1,0},{2,3},{3,2},{4,5},{5,4},{6,7},{7,6},{8,9},{9,8},{10,11... | collective-permute-start | bytes 393224 | tf_op jit(solution)/shard_map/ppermute | solution.py:326
  87.7 6.4 %collective-permute-start.22 = (bf16[16,2048]{1,0:T(8,128)(2,1)S(1)}, bf16[16,2048]{1,0:T(8,128)(2,1)S(1)}, u32[]{:S(2)}, u32[]{:S(2)}) collective-permute-start(bf16[16,2048]{1,0:T(8,128)(2,1)S(1)} %get-tuple-element.46), channel_id=1, source_target_pairs={{0,3},{1,2},{2,1},{3,0},{4,7},{5,6},{6,5},{7,4},{8,11},{9,10},{10,... | collective-permute-start | bytes 196616 | tf_op jit(solution)/shard_map/ppermute | solution.py:328
  90.5 6.2 %collective-permute-start.21 = (bf16[16,2048]{1,0:T(8,128)(2,1)S(1)}, bf16[16,2048]{1,0:T(8,128)(2,1)S(1)}, u32[]{:S(2)}, u32[]{:S(2)}) collective-permute-start(bf16[16,2048]{1,0:T(8,128)(2,1)S(1)} %get-tuple-element.45), channel_id=1, source_target_pairs={{0,3},{1,2},{2,1},{3,0},{4,7},{5,6},{6,5},{7,4},{8,11},{9,10},{10,... | collective-permute-start | bytes 196616 | tf_op jit(solution)/shard_map/ppermute | solution.py:328
  96.9 1.9 %collective-permute-start.23 = (bf16[2,4,2048]{2,1,0:T(4,128)(2,1)S(1)}, bf16[2,4,2048]{2,1,0:T(4,128)(2,1)S(1)}, u32[]{:S(2)}, u32[]{:S(2)}) collective-permute-start(bf16[2,4,2048]{2,1,0:T(4,128)(2,1)S(1)} %get-tuple-element.48), channel_id=1, source_target_pairs={{0,4},{4,0},{8,12},{12,8},{1,5},{5,1},{9,13},{13,9},{2,6},{6,2},{1... | collective-permute-start | bytes 98312 | tf_op jit(solution)/shard_map/ppermute | solution.py:296
  97.0 4.0 %collective-permute-start.24 = (bf16[2,4,2048]{2,1,0:T(4,128)(2,1)S(1)}, bf16[2,4,2048]{2,1,0:T(4,128)(2,1)S(1)}, u32[]{:S(2)}, u32[]{:S(2)}) collective-permute-start(bf16[2,4,2048]{2,1,0:T(4,128)(2,1)S(1)} %get-tuple-element.49), channel_id=1, source_target_pairs={{0,8},{4,12},{8,0},{12,4},{1,9},{5,13},{9,1},{13,5},{2,10},{6,14},... | collective-permute-start | bytes 98312 | tf_op jit(solution)/shard_map/ppermute | solution.py:294
  98.4 3.3 %collective-permute-start.25 = (bf16[2,4,2048]{2,1,0:T(4,128)(2,1)S(1)}, bf16[2,4,2048]{2,1,0:T(4,128)(2,1)S(1)}, u32[]{:S(2)}, u32[]{:S(2)}) collective-permute-start(bf16[2,4,2048]{2,1,0:T(4,128)(2,1)S(1)} %get-tuple-element.50), channel_id=1, source_target_pairs={{0,12},{4,8},{8,4},{12,0},{1,13},{5,9},{9,5},{13,1},{2,14},{6,10},... | collective-permute-start | bytes 98312 | tf_op jit(solution)/shard_map/ppermute | solution.py:295
  (12 other events, 68.5 us)

commit v2 on v0

--- a/solution.py
+++ b/solution.py
@@ -1,13 +1,368 @@
+import functools
+
 import jax
 import jax.numpy as jnp
 from jax import lax
+from jax.experimental import pallas as pl
+from jax.experimental.pallas import tpu as pltpu
 from jax.sharding import PartitionSpec as P
 
 STEPS = 2
 MEAN = 4
 
-
 epsilon = 1e-05
+
+BF = jnp.bfloat16
+F32 = jnp.float32
+MIB = 2**20
+X1 = ((0, 1), (1, 0), (2, 3), (3, 2))
+X2 = ((0, 2), (1, 3), (2, 0), (3, 1))
+X3 = ((0, 3), (1, 2), (2, 1), (3, 0))
+
+
+def vmem_spec():
+    return pl.BlockSpec(memory_space=pltpu.VMEM)
+
+
+def call(body, outs, specs, scratch=(), limit=24, cost=None):
+    return pl.pallas_call(
+        body,
+        out_shape=outs,
+        in_specs=specs,
+        out_specs=jax.tree.map(lambda _: vmem_spec(), outs),
+        scratch_shapes=scratch,
+        compiler_params=pltpu.CompilerParams(vmem_limit_bytes=limit * MIB),
+        cost_estimate=cost,
+    )
+
+
+def place():
+    row = lax.axis_index("row")
+    return row // 2, lax.rem(row, 2), lax.axis_index("col")
+
+
+def norm_body(rows_ref, own_ref, core_ref, y_ref, yd_ref):
+    y, c, _ = place()
+    width = own_ref.shape[2]
+    for step in range(rows_ref.shape[0]):
+        total = jnp.sum(jnp.square(rows_ref[step].astype(F32)), axis=-1, keepdims=True)
+        scale = lax.rsqrt(total / rows_ref.shape[2] + epsilon)
+        for dy, dc, out in ((0, 0, own_ref), (0, 1, core_ref), (1, 0, y_ref), (1, 1, yd_ref)):
+            block = lax.bitwise_xor(y, dy) * 2 + lax.bitwise_xor(c, dc)
+            at = pl.ds(pl.multiple_of(block * width, width), width)
+            out[step] = (rows_ref[step, :, at].astype(F32) * scale).astype(BF)
+
+
+def normed_blocks(sender_rows):
+    steps, slots, width = sender_rows.shape
+    one = jax.ShapeDtypeStruct((steps, slots, width // 4), BF)
+    return call(norm_body, (one,) * 4, [vmem_spec()])(sender_rows)
+
+
+def pick_body(counts_ref, assign_ref, pick_ref):
+    y, c, z = place()
+    rows = pick_ref.shape[0] // 2
+    slots = assign_ref.shape[1]
+    arrivals = pick_ref.shape[1]
+    spread = (
+        lax.broadcasted_iota(jnp.int32, (slots // 8, slots), 1) // 8
+        == lax.broadcasted_iota(jnp.int32, (slots // 8, slots), 0)
+    ).astype(F32)
+    held = jnp.dot(counts_ref[...].astype(F32), spread, preferred_element_type=F32)
+    slot = lax.rem(lax.broadcasted_iota(jnp.int32, (1, slots), 1), 8).astype(F32)
+    at = lax.broadcasted_iota(jnp.int32, (rows, slots), 0)
+    target = (lax.rem(at, 16) // 4) * 16 + lax.bitwise_xor(at // 16, z) * 4 + lax.rem(at, 4)
+    p = lax.broadcasted_iota(jnp.int32, (slots, arrivals), 1)
+    bit = lambda shift: lax.rem(lax.shift_right_logical(p, shift), 2)
+    row = lax.bitwise_xor(bit(5), y) * 2 + lax.bitwise_xor(bit(4), c)
+    sender = row * 4 + lax.bitwise_xor(lax.shift_right_logical(p, 6), z)
+    source = sender * 8 + lax.rem(p, 8)
+    entry = lax.broadcasted_iota(jnp.int32, (slots, arrivals), 0)
+    for step in range(2):
+        live = slot < held[step : step + 1]
+        chosen = jnp.where(live, assign_ref[step : step + 1, :], -1)
+        placed = (chosen == target).astype(F32).astype(BF)
+        moved = ((entry == source) & (bit(3) == step)).astype(F32).astype(BF)
+        pick_ref[step * rows : (step + 1) * rows, :] = jnp.dot(
+            placed, moved, preferred_element_type=F32
+        ).astype(BF)
+
+
+def pick_matrix(counts, assign):
+    rows = MEAN * counts.shape[1]
+    return call(
+        pick_body,
+        jax.ShapeDtypeStruct((2 * rows, 2 * assign.shape[1]), BF),
+        [vmem_spec()] * 2,
+    )(counts, assign)
+
+
+def fetch_gate_up_body(dy, dc, gate_ref, up_ref, out_ref, token_ref, sems):
+    y, c, _ = place()
+    width = out_ref.shape[1] // 2
+    start = (lax.bitwise_xor(c, dc) * 2 + lax.bitwise_xor(y, dy)) * width
+    copies = []
+    for i, w in enumerate((gate_ref, up_ref)):
+        copies.append(
+            pltpu.make_async_copy(
+                w.at[:, pl.ds(pl.multiple_of(start, 128), width)],
+                out_ref.at[:, pl.ds(i * width, width)],
+                sems.at[i],
+            )
+        )
+    for copy in copies:
+        copy.start()
+    token_ref[...] = jnp.zeros_like(token_ref)
+    for copy in copies:
+        copy.wait()
+
+
+def fetch_down_body(dy, down_ref, out_ref, token_ref, sems):
+    y, c, _ = place()
+    height = out_ref.shape[0] // 2
+    copies = []
+    for dc in range(2):
+        start = (lax.bitwise_xor(c, dc) * 2 + lax.bitwise_xor(y, dy)) * height
+        copies.append(
+            pltpu.make_async_copy(
+                down_ref.at[pl.ds(pl.multiple_of(start, 16), height), :],
+                out_ref.at[pl.ds(dc * height, height), :],
+                sems.at[dc],
+            )
+        )
+    for copy in copies:
+        copy.start()
+    token_ref[...] = jnp.zeros_like(token_ref)
+    for copy in copies:
+        copy.wait()
+
+
+def fetch(body, shape, *weights):
+    out, token = pl.pallas_call(
+        body,
+        out_shape=(pltpu.VMEM(shape, BF), jax.ShapeDtypeStruct((8, 128), F32)),
+        in_specs=[pl.BlockSpec(memory_space=pltpu.HBM)] * len(weights),
+        out_specs=(vmem_spec(), vmem_spec()),
+        scratch_shapes=[pltpu.SemaphoreType.DMA((2,))],
+        compiler_params=pltpu.CompilerParams(vmem_limit_bytes=MIB),
+        cost_estimate=pl.CostEstimate(
+            flops=0, bytes_accessed=2 * shape[0] * shape[1], transcendentals=0
+        ),
+    )(*(pltpu.with_memory_space_constraint(w, pltpu.HBM) for w in weights))
+    return out, token
+
+
+def fetch_gate_up(gate_w, up_w, dy, dc):
+    shape = (gate_w.shape[0], gate_w.shape[1] // 2)
+    return fetch(functools.partial(fetch_gate_up_body, dy, dc), shape, gate_w, up_w)
+
+
+def fetch_down(down_w, dy):
+    shape = (down_w.shape[0] // 2, down_w.shape[1])
+    return fetch(functools.partial(fetch_down_body, dy), shape, down_w)
+
+
+def stack_body(first_ref, second_ref, *refs):
+    out_ref = refs[-1]
+    for i, piece in enumerate((first_ref, second_ref)):
+        for step in range(2):
+            at = (i * 2 + step) * 8
+            out_ref[at : at + 8, :] = piece[step]
+
+
+def stack(first, second, *tokens):
+    steps, slots, width = first.shape
+    out = jax.ShapeDtypeStruct((2 * steps * slots, width), BF)
+    return call(stack_body, out, [vmem_spec()] * (2 + len(tokens)))(first, second, *tokens)
+
+
+def after_body(x_ref, *refs):
+    refs[-1][...] = x_ref[...]
+
+
+def after(x, *tokens):
+    out = jax.ShapeDtypeStruct(x.shape, x.dtype)
+    return call(after_body, out, [vmem_spec()] * (1 + len(tokens)))(x, *tokens)
+
+
+def first_body(*refs):
+    pieces, (pick_ref, w_ref, _, batch_ref, out_ref, slots) = refs[:8], refs[8:]
+    height = pieces[0].shape[0]
+    for i, piece in enumerate(pieces):
+        slots[i * height : (i + 1) * height, :] = piece[...]
+    batch_ref[...] = jnp.dot(pick_ref[...], slots[...], preferred_element_type=F32).astype(BF)
+    out_ref[...] = jnp.dot(batch_ref[...], w_ref[...], preferred_element_type=F32).astype(BF)
+
+
+def first_sums(pieces, pick, w, token):
+    rows = pick.shape[0]
+    height, width = pieces[0].shape
+    return call(
+        first_body,
+        (jax.ShapeDtypeStruct((rows, width), BF), jax.ShapeDtypeStruct((rows, w.shape[1]), BF)),
+        [vmem_spec()] * 11,
+        scratch=[pltpu.VMEM((8 * height, width), BF)],
+        cost=pl.CostEstimate(flops=2 * rows * w.size, bytes_accessed=2 * w.size, transcendentals=0),
+    )(*pieces, pick, w, token)
+
+
+def dot_body(x_ref, w_ref, *refs):
+    out_ref = refs[-1]
+    out_ref[...] = jnp.dot(x_ref[...], w_ref[...], preferred_element_type=F32).astype(out_ref.dtype)
+
+
+def dot(x, w, dtype, *tokens):
+    rows = x.shape[0]
+    return call(
+        dot_body,
+        jax.ShapeDtypeStruct((rows, w.shape[1]), dtype),
+        [vmem_spec()] * (2 + len(tokens)),
+        cost=pl.CostEstimate(flops=2 * rows * w.size, bytes_accessed=2 * w.size, transcendentals=0),
+    )(x, w, *tokens)
+
+
+def far_body(own_ref, got_ref, *outs):
+    rows = outs[0].shape[0]
+    for step, out in enumerate(outs):
+        at = slice(step * rows, (step + 1) * rows)
+        out[...] = (own_ref[at, :] + got_ref[at, :].astype(F32)).astype(BF)
+
+
+def far_sums(own, got):
+    out = jax.ShapeDtypeStruct((own.shape[0] // 2, own.shape[1]), BF)
+    return call(far_body, (out, out), [vmem_spec()] * 2)(own, got)
+
+
+def hidden_body(step, own_ref, core_ref, y_ref, *refs):
+    hidden_ref = refs[-1]
+    rows, width = hidden_ref.shape
+    at = slice(step * rows, (step + 1) * rows)
+    total = own_ref[at, :] + core_ref[at, :].astype(F32) + y_ref[...].astype(F32)
+    gate, up = total[:, :width], total[:, width:]
+    hidden_ref[...] = (gate / (1.0 + jnp.exp(-gate)) * up).astype(BF)
+
+
+def hidden_units(step, own, core, y, *tokens):
+    out = jax.ShapeDtypeStruct((y.shape[0], y.shape[1] // 2), BF)
+    return call(functools.partial(hidden_body, step), out, [vmem_spec()] * (3 + len(tokens)))(
+        own, core, y, *tokens
+    )
+
+
+def down_body(own_ref, core_ref, down_ref, out_ref):
+    height = down_ref.shape[0] // 2
+    total = jnp.dot(own_ref[...], down_ref[:height, :], preferred_element_type=F32)
+    out_ref[...] = total + jnp.dot(core_ref[...], down_ref[height:, :], preferred_element_type=F32)
+
+
+def down_rest_body(y_ref, yd_ref, down_ref, part_ref, keep_ref, *outs):
+    height = down_ref.shape[0] // 2
+    rows = keep_ref.shape[0]
+    total = part_ref[...] + jnp.dot(y_ref[...], down_ref[:height, :], preferred_element_type=F32)
+    total = total + jnp.dot(yd_ref[...], down_ref[height:, :], preferred_element_type=F32)
+    keep_ref[...] = total[:rows]
+    for i, out in enumerate(outs):
+        out[...] = total[(i + 1) * rows : (i + 2) * rows].astype(BF)
+
+
+def down_cost(rows, down):
+    return pl.CostEstimate(flops=2 * rows * down.size, bytes_accessed=2 * down.size, transcendentals=0)
+
+
+def down_part(own, core, down):
+    rows = own.shape[0]
+    out = jax.ShapeDtypeStruct((rows, down.shape[1]), F32)
+    return call(down_body, out, [vmem_spec()] * 3, cost=down_cost(rows, down))(own, core, down)
+
+
+def down_rest(y, yd, down, part):
+    rows, width = part.shape
+    send = jax.ShapeDtypeStruct((rows // 4, width), BF)
+    keep = jax.ShapeDtypeStruct((rows // 4, width), F32)
+    return call(
+        down_rest_body, (keep, send, send, send), [vmem_spec()] * 4, cost=down_cost(rows, down)
+    )(y, yd, down, part)
+
+
+def owner_body(*refs):
+    sums, outs = refs[:8], refs[8:]
+    y, c, _ = place()
+    at = lax.broadcasted_iota(jnp.int32, (16, 16), 0)
+    source = lax.bitwise_xor(at, (y * 2 + c) * 4)
+    turn = (lax.broadcasted_iota(jnp.int32, (16, 16), 1) == source).astype(F32).astype(BF)
+    for step in range(2):
+        total = sums[step * 4][...]
+        for got in sums[step * 4 + 1 : step * 4 + 4]:
+            total = total + got[...].astype(F32)
+        turned = jnp.dot(turn, total.astype(BF), preferred_element_type=F32)
+        for i, out in enumerate(outs):
+            out[step] = turned[i * 4 : (i + 1) * 4].astype(BF)
+
+
+def owner_blocks(sums):
+    out = jax.ShapeDtypeStruct((2, 4, sums[0].shape[1]), BF)
+    return call(owner_body, (out,) * 4, [vmem_spec()] * 8)(*sums)
+
+
+def output_body(own_ref, core_ref, y_ref, yd_ref, out_ref):
+    y, c, _ = place()
+    width = own_ref.shape[2]
+    for dy, dc, block in ((0, 0, own_ref), (0, 1, core_ref), (1, 0, y_ref), (1, 1, yd_ref)):
+        source = lax.bitwise_xor(y, dy) * 2 + lax.bitwise_xor(c, dc)
+        out_ref[:, :, pl.ds(pl.multiple_of(source * width, width), width)] = block[...]
+
+
+def output_rows(blocks):
+    steps, rows, width = blocks[0].shape
+    out = jax.ShapeDtypeStruct((steps, rows, 4 * width), BF)
+    return call(output_body, out, [vmem_spec()] * 4)(*blocks)
+
+
+def exchange(blocks):
+    own, core, y, yd = blocks
+    core = lax.ppermute(core, "row", X1)
+    y = lax.ppermute(y, "row", X2)
+    yd = lax.ppermute(yd, "row", X3)
+    return own, core, y, yd
+
+
+def near_plan(sender_rows, counts, assign, gate_w, up_w, down_w):
+    pick = pick_matrix(counts, assign)
+    own, core, y, yd = exchange(normed_blocks(sender_rows))
+    w_first, token_first = fetch_gate_up(gate_w, up_w, 1, 1)
+    w_second, token_second = fetch_gate_up(gate_w, up_w, 1, 0)
+    w_third, token_third = fetch_gate_up(gate_w, up_w, 0, 1)
+    arrived = []
+    block_near = stack(own, core)
+    block_far = stack(y, yd, block_near)
+    for block, token in ((block_near, token_first), (block_far, token_second)):
+        far = lax.ppermute(block, "col", X3)
+        near = lax.ppermute(block, "col", X1)
+        arrived.append((block, near, lax.ppermute(after(far, near, token), "col", X1), far))
+    pieces = [arrived[dy][dz] for dz in range(4) for dy in range(2)]
+    batch, far_core = first_sums(pieces, pick, w_first, token_third)
+    far_core = lax.ppermute(far_core, "row", X1)
+    sends = far_sums(dot(batch, w_second, F32), far_core)
+    gots = [lax.ppermute(send, "row", X2) for send in sends]
+    near_core = lax.ppermute(dot(batch, w_third, BF, sends[0]), "row", X1)
+    w_fourth, _ = fetch_gate_up(gate_w, up_w, 0, 0)
+    near = dot(batch, w_fourth, F32)
+    down_near, token_near = fetch_down(down_w, 0)
+    down_far, token_far = fetch_down(down_w, 1)
+    sums = []
+    tokens = [token_near]
+    for step, got in enumerate(gots):
+        hidden = hidden_units(step, near, near_core, got, *tokens)
+        hidden_y = lax.ppermute(hidden, "row", X2)
+        hidden_core = lax.ppermute(hidden, "row", X1)
+        hidden_yd = lax.ppermute(hidden_y, "row", X1)
+        part = down_part(hidden, hidden_core, down_near)
+        tokens = [token_far, part]
+        keep, send1, send2, send3 = down_rest(hidden_y, hidden_yd, down_far, part)
+        sums.append(keep)
+        for send, pairs in ((send3, X3), (send2, X2), (send1, X1)):
+            sums.append(lax.ppermute(send, "col", pairs))
+    return output_rows(exchange(owner_blocks(sums)))
 
 
 def layer_block(normed_block, counts_block, assign_block, paired, down_w, hidden_cols):
@@ -64,7 +419,7 @@
     return finished.reshape(step_count, MEAN, finished.shape[1])
 
 
-def per_device(sender_rows, counts, assign, gate_w, up_w, down_w):
+def any_plan(sender_rows, counts, assign, gate_w, up_w, down_w):
     values = sender_rows.astype(jnp.float32)
     normed = (
         values * lax.rsqrt(jnp.mean(values * values, axis=-1, keepdims=True) + epsilon)
@@ -88,8 +443,9 @@
 
 
 def solution(mesh):
+    near = mesh.shape["row"] == 4 and mesh.shape["col"] == 4
     return jax.shard_map(
-        per_device,
+        near_plan if near else any_plan,
         mesh=mesh,
         in_specs=(
             P(None, ("groups", "row", "col"), None),

time: 332 us -> 79.6 us (0.24)
  other arithmetic: 95.8 us -> 0 us
  local copies, waits for them, and re-layouts: 84.1 us -> 0.96 us
  blocking collectives: 53 us -> 0 us
  matrix products: 43.6 us -> 0 us
  Pallas kernels: 0 us -> 32 us
  starting transfers between devices: 11.2 us -> 25.9 us
  between operations: 13.4 us -> 0.29 us
  waiting for transfers between devices: 29.2 us -> 20.3 us
    unnamed x2 -> x0, other arithmetic: 90.5 us -> none
    all_gather x4 -> x0, blocking collectives: 46.3 us -> none  [the longest x2 32.5 us: layer_block(): gathered = lax.all_gather(spread, 'col', axis=1, tiled=True)]
    dot_general x4 -> x0, matrix products: 43.6 us -> none  [the longest x2 26.3 us: layer_block(): jnp.dot(rows_here, paired, preferred_element_type=jnp.float32)]
    pallas_call x0 -> x25, Pallas kernels: none -> 32 us  [the longest x6 19.8 us: fetch(): pl.pallas_call(body, out_shape=(pltpu.VMEM(shape, BF), jax.ShapeDtypeStru...]
    unnamed x6, local copies, waits for them, and re-layouts: 31.3 us -> 0.96 us
    reduce_scatter x4 -> x0, waiting for transfers between devices: 29.2 us -> none  [the longest x2 21 us: layer_block(): lax.psum_scatter(jnp.dot(rows_here, down_w, preferred_element_type=jnp.fl...]
    ppermute x0 -> x28, starting transfers between devices: none -> 25.9 us  [the longest x6 8.91 us: near_plan(): sums.append(lax.ppermute(send, 'col', pairs))]
    ppermute x0 -> x28, waiting for transfers between devices: none -> 20.3 us  [the longest x2 4.91 us: exchange(): y = lax.ppermute(y, 'row', X2)]
  transfers between devices with their start and end apart: 7 -> 28, of which waited for: 3 -> 12; matrix products, arithmetic and copies ran while one was open for 49% -> 0% of each run, Pallas kernels for 0% -> 36%
where the time goes in v2:
time: 79.6 us; the launch traced here: 79.4 us
  Pallas kernels  32 us (40%)
  starting transfers between devices  25.9 us (33%)
  waiting for transfers between devices  20.3 us (26%)
  local copies, waits for them, and re-layouts  0.96 us (1%)
    pallas_call x6, Pallas kernels, fetch(): pl.pallas_call(body, out_shape=(pltpu.VMEM(shape, BF), jax.ShapeDtypeStru...  19.8 us
    ppermute x6, starting transfers between devices, near_plan(): sums.append(lax.ppermute(send, 'col', pairs))  8.91 us
    ppermute x2, waiting for transfers between devices, exchange(): y = lax.ppermute(y, 'row', X2)  4.91 us
    ppermute x6, waiting for transfers between devices, near_plan(): sums.append(lax.ppermute(send, 'col', pairs))  3.88 us
    ppermute x2, waiting for transfers between devices, near_plan(): far = lax.ppermute(block, 'col', X3)  3.79 us
    ppermute x2, waiting for transfers between devices, near_plan(): hidden_y = lax.ppermute(hidden, 'row', X2)  3.61 us
    pallas_call x3, Pallas kernels, dot(): call(dot_body, jax.ShapeDtypeStruct((rows, w.shape[1]), dtype), [vmem_spe...  3.4 us
    ppermute x2, starting transfers between devices, exchange(): y = lax.ppermute(y, 'row', X2)  3.38 us
  transfers between devices with their start and end apart: 28, of which 12 were waited for; matrix products, arithmetic and copies ran while one was open for 0% of the time, Pallas kernels for 36%

profile of v2, /device:TPU:0, one launch (start us, length us, event | category | flops | bytes accessed | tf_op | source)
XLA Modules:
  0.0 79.4 jit_solution(12086762096896111993)
XLA Ops:
  1.7 2.6 %collective-permute-start.1 = (bf16[2,8,2048]{2,1,0:T(8,128)(2,1)S(1)}, bf16[2,8,2048]{2,1,0:T(8,128)(2,1)S(1)}, u32[]{:S(2)}, u32[]{:S(2)}) collective-permute-start(bf16[2,8,2048]{2,1,0:T(8,128)(2,1)S(1)} %get-tuple-element.38), channel_id=1, source_target_pairs={{0,8},{4,12},{8,0},{12,4},{1,9},{5,13},{9,1},{13,5},{2,10},{6,14},... | collective-permute-start | bytes 196616 | tf_op jit(solution)/shard_map/ppermute | solution.py:324
  4.4 2.6 %collective-permute-done.1.first_ref = bf16[2,8,2048]{2,1,0:T(8,128)(2,1)S(1)} collective-permute-done((bf16[2,8,2048]{2,1,0:T(8,128)(2,1)S(1)}, bf16[2,8,2048]{2,1,0:T(8,128)(2,1)S(1)}, u32[]{:S(2)}, u32[]{:S(2)}) %collective-permute-start.1) | collective-permute-done | bytes 65568 | tf_op jit(solution)/shard_map/ppermute | solution.py:324
  7.0 1.4 %collective-permute-done.2.second_ref = bf16[2,8,2048]{2,1,0:T(8,128)(2,1)S(1)} collective-permute-done((bf16[2,8,2048]{2,1,0:T(8,128)(2,1)S(1)}, bf16[2,8,2048]{2,1,0:T(8,128)(2,1)S(1)}, u32[]{:S(2)}, u32[]{:S(2)}) %collective-permute-start.2) | collective-permute-done | bytes 65568 | tf_op jit(solution)/shard_map/ppermute | solution.py:325
  8.3 1.6 %collective-permute-start.4 = (bf16[32,2048]{1,0:T(8,128)(2,1)S(1)}, bf16[32,2048]{1,0:T(8,128)(2,1)S(1)}, u32[]{:S(2)}, u32[]{:S(2)}) collective-permute-start(bf16[32,2048]{1,0:T(8,128)(2,1)S(1)} %shard_map.66.refs_1_), channel_id=1, source_target_pairs={{0,1},{1,0},{2,3},{3,2},{4,5},{5,4},{6,7},{7,6},{8,9},{9,8},{10,11... | collective-permute-start | bytes 393224 | tf_op jit(solution)/shard_map/ppermute | solution.py:340
  10.0 2.5 %collective-permute-start.7 = (bf16[32,2048]{1,0:T(8,128)(2,1)S(1)}, bf16[32,2048]{1,0:T(8,128)(2,1)S(1)}, u32[]{:S(2)}, u32[]{:S(2)}) collective-permute-start(bf16[32,2048]{1,0:T(8,128)(2,1)S(1)} %shard_map.66.refs_1_), channel_id=1, source_target_pairs={{0,3},{1,2},{2,1},{3,0},{4,7},{5,6},{6,5},{7,4},{8,11},{9,10},{10,... | collective-permute-start | bytes 393224 | tf_op jit(solution)/shard_map/ppermute | solution.py:339
  14.0 3.2 %shard_map.69 = (bf16[2048,1792]{1,0:T(8,128)(2,1)S(1)}, f32[8,128]{1,0:T(8,128)S(1)}) custom-call(bf16[2048,3584]{1,0:T(8,128)(2,1)} %gate_ref.7, bf16[2048,3584]{1,0:T(8,128)(2,1)} %up_ref.7), custom_call_target="tpu_custom_call" | custom-call | bytes 7340032 | tf_op jit(solution)/shard_map/pallas_call | solution.py:141
  17.2 3.2 %shard_map.67 = (bf16[2048,1792]{1,0:T(8,128)(2,1)S(1)}, f32[8,128]{1,0:T(8,128)S(1)}) custom-call(bf16[2048,3584]{1,0:T(8,128)(2,1)} %gate_ref.7, bf16[2048,3584]{1,0:T(8,128)(2,1)} %up_ref.7), custom_call_target="tpu_custom_call" | custom-call | bytes 7340032 | tf_op jit(solution)/shard_map/pallas_call | solution.py:141
  21.5 3.8 %collective-permute-done.5.x_ref.refs_6_ = bf16[32,2048]{1,0:T(8,128)(2,1)S(1)} collective-permute-done((bf16[32,2048]{1,0:T(8,128)(2,1)S(1)}, bf16[32,2048]{1,0:T(8,128)(2,1)S(1)}, u32[]{:S(2)}, u32[]{:S(2)}) %collective-permute-start.5) | collective-permute-done | bytes 131104 | tf_op jit(solution)/shard_map/ppermute | solution.py:339
  25.4 3.3 %shard_map.72 = (bf16[2048,1792]{1,0:T(8,128)(2,1)S(1)}, f32[8,128]{1,0:T(8,128)S(1)}) custom-call(bf16[2048,3584]{1,0:T(8,128)(2,1)} %gate_ref.7, bf16[2048,3584]{1,0:T(8,128)(2,1)} %up_ref.7), custom_call_target="tpu_custom_call" | custom-call | bytes 7340032 | tf_op jit(solution)/shard_map/pallas_call | solution.py:141
  28.9 1.4 %collective-permute-done.6.refs_4_ = bf16[32,2048]{1,0:T(8,128)(2,1)S(1)} collective-permute-done((bf16[32,2048]{1,0:T(8,128)(2,1)S(1)}, bf16[32,2048]{1,0:T(8,128)(2,1)S(1)}, u32[]{:S(2)}, u32[]{:S(2)}) %collective-permute-start.6) | collective-permute-done | bytes 131104 | tf_op jit(solution)/shard_map/ppermute | solution.py:341
  30.3 1.4 %shard_map.73 = (bf16[128,2048]{1,0:T(8,128)(2,1)S(1)}, bf16[128,1792]{1,0:T(8,128)(2,1)S(1)}) custom-call(bf16[32,2048]{1,0:T(8,128)(2,1)S(1)} %shard_map.65.refs_0_, bf16[32,2048]{1,0:T(8,128)(2,1)S(1)} %shard_map.66.refs_1_, bf16[32,2048]{1,0:T(8,128)(2,1)S(1)} %collective-permute-done.3.refs_0_.refs_2_, ...), custom_call_target="tpu_custom_call" | custom-call | flops 939524096 | bytes 7340032 | tf_op jit(solution)/shard_map/pallas_call | solution.py:200
  31.8 1.1 %shard_map.76.own_ref = f32[128,1792]{1,0:T(8,128)S(1)} custom-call(bf16[128,2048]{1,0:T(8,128)(2,1)S(1)} %get-tuple-element.44.x_ref, bf16[2048,1792]{1,0:T(8,128)(2,1)S(1)} %get-tuple-element.47.w_ref), custom_call_target="tpu_custom_call" | custom-call | flops 939524096 | bytes 7340032 | tf_op jit(solution)/shard_map/pallas_call | solution.py:216
  33.7 1.1 %shard_map.78 = bf16[128,1792]{1,0:T(8,128)(2,1)S(1)} custom-call(bf16[128,2048]{1,0:T(8,128)(2,1)S(1)} %get-tuple-element.44.x_ref, bf16[2048,1792]{1,0:T(8,128)(2,1)S(1)} %get-tuple-element.46.w_ref, bf16[64,1792]{1,0:T(8,128)(2,1)S(1)} %get-tuple-element.49.refs_0_), custom_call_target="tpu_custom_call" | custom-call | flops 939524096 | bytes 7340032 | tf_op jit(solution)/shard_map/pallas_call | solution.py:216
  35.0 1.3 %collective-permute-start.11 = (bf16[64,1792]{1,0:T(8,128)(2,1)S(1)}, bf16[64,1792]{1,0:T(8,128)(2,1)S(1)}, u32[]{:S(2)}, u32[]{:S(2)}) collective-permute-start(bf16[64,1792]{1,0:T(8,128)(2,1)S(1)} %get-tuple-element.49.refs_0_), channel_id=1, source_target_pairs={{0,8},{4,12},{8,0},{12,4},{1,9},{5,13},{9,1},{13,5},{2,10},{6,14},... | collective-permute-start | bytes 688136 | tf_op jit(solution)/shard_map/ppermute | solution.py:346
  36.4 3.8 %shard_map.74 = (bf16[2048,1792]{1,0:T(8,128)(2,1)S(1)}, f32[8,128]{1,0:T(8,128)}) custom-call(bf16[2048,3584]{1,0:T(8,128)(2,1)} %gate_ref.7, bf16[2048,3584]{1,0:T(8,128)(2,1)} %up_ref.7), custom_call_target="tpu_custom_call" | custom-call | bytes 7340032 | tf_op jit(solution)/shard_map/pallas_call | solution.py:141
  40.2 3.2 %shard_map.79 = (bf16[1792,2048]{1,0:T(8,128)(2,1)S(1)}, f32[8,128]{1,0:T(8,128)S(1)}) custom-call(bf16[3584,2048]{1,0:T(8,128)(2,1)} %down_ref.3), custom_call_target="tpu_custom_call" | custom-call | bytes 7340032 | tf_op jit(solution)/shard_map/pallas_call | solution.py:141
  44.2 1.1 %shard_map.75.own_ref = f32[128,1792]{1,0:T(8,128)S(1)} custom-call(bf16[128,2048]{1,0:T(8,128)(2,1)S(1)} %get-tuple-element.44.x_ref, bf16[2048,1792]{1,0:T(8,128)(2,1)S(1)} %get-tuple-element.45.w_ref), custom_call_target="tpu_custom_call" | custom-call | flops 939524096 | bytes 7340032 | tf_op jit(solution)/shard_map/pallas_call | solution.py:216
  45.5 1.4 %collective-permute-start.12 = (bf16[64,896]{1,0:T(8,128)(2,1)S(1)}, bf16[64,896]{1,0:T(8,128)(2,1)S(1)}, u32[]{:S(2)}, u32[]{:S(2)}) collective-permute-start(bf16[64,896]{1,0:T(8,128)(2,1)S(1)} %shard_map.80.own_ref), channel_id=1, source_target_pairs={{0,8},{4,12},{8,0},{12,4},{1,9},{5,13},{9,1},{13,5},{2,10},{6,14},... | collective-permute-start | bytes 344072 | tf_op jit(solution)/shard_map/ppermute | solution.py:356
  46.9 3.2 %shard_map.81 = (bf16[1792,2048]{1,0:T(8,128)(2,1)S(1)}, f32[8,128]{1,0:T(8,128)S(1)}) custom-call(bf16[3584,2048]{1,0:T(8,128)(2,1)} %down_ref.3), custom_call_target="tpu_custom_call" | custom-call | bytes 7340032 | tf_op jit(solution)/shard_map/pallas_call | solution.py:141
  50.1 1.4 %shard_map.82.part_ref.refs_1_ = f32[64,2048]{1,0:T(8,128)S(1)} custom-call(bf16[64,896]{1,0:T(8,128)(2,1)S(1)} %shard_map.80.own_ref, bf16[64,896]{1,0:T(8,128)(2,1)S(1)} %collective-permute-done.14.core_ref, bf16[1792,2048]{1,0:T(8,128)(2,1)S(1)} %get-tuple-element.52.down_ref), custom_call_target="tpu_custom_call" | custom-call | flops 469762048 | bytes 7340032 | tf_op jit(solution)/shard_map/pallas_call | solution.py:275
  54.1 2.9 %collective-permute-done.19.y_ref = bf16[64,896]{1,0:T(8,128)(2,1)S(1)} collective-permute-done((bf16[64,896]{1,0:T(8,128)(2,1)S(1)}, bf16[64,896]{1,0:T(8,128)(2,1)S(1)}, u32[]{:S(2)}, u32[]{:S(2)}) %collective-permute-start.19) | collective-permute-done | bytes 114720 | tf_op jit(solution)/shard_map/ppermute | solution.py:356
  56.9 1.4 %shard_map.83 = (f32[16,2048]{1,0:T(8,128)S(1)}, bf16[16,2048]{1,0:T(8,128)(2,1)S(1)}, bf16[16,2048]{1,0:T(8,128)(2,1)S(1)}, bf16[16,2048]{1,0:T(8,128)(2,1)S(1)}) custom-call(bf16[64,896]{1,0:T(8,128)(2,1)S(1)} %collective-permute-done.12.y_ref, bf16[64,896]{1,0:T(8,128)(2,1)S(1)} %collective-permute-done.13.yd_ref, ...), custom_call_target="tpu_custom_call" | custom-call | flops 469762048 | bytes 7340032 | tf_op jit(solution)/shard_map/pallas_call | solution.py:282
  58.4 1.5 %collective-permute-start.15 = (bf16[16,2048]{1,0:T(8,128)(2,1)S(1)}, bf16[16,2048]{1,0:T(8,128)(2,1)S(1)}, u32[]{:S(2)}, u32[]{:S(2)}) collective-permute-start(bf16[16,2048]{1,0:T(8,128)(2,1)S(1)} %get-tuple-element.54), channel_id=1, source_target_pairs={{0,3},{1,2},{2,1},{3,0},{4,7},{5,6},{6,5},{7,4},{8,11},{9,10},{10,... | collective-permute-start | bytes 196616 | tf_op jit(solution)/shard_map/ppermute | solution.py:364
  60.5 2.4 %collective-permute-start.17 = (bf16[16,2048]{1,0:T(8,128)(2,1)S(1)}, bf16[16,2048]{1,0:T(8,128)(2,1)S(1)}, u32[]{:S(2)}, u32[]{:S(2)}) collective-permute-start(bf16[16,2048]{1,0:T(8,128)(2,1)S(1)} %get-tuple-element.56), channel_id=1, source_target_pairs={{0,1},{1,0},{2,3},{3,2},{4,5},{5,4},{6,7},{7,6},{8,9},{9,8},{10,11... | collective-permute-start | bytes 196616 | tf_op jit(solution)/shard_map/ppermute | solution.py:364
  62.8 1.4 %shard_map.85.part_ref = f32[64,2048]{1,0:T(8,128)S(1)} custom-call(bf16[64,896]{1,0:T(8,128)(2,1)S(1)} %shard_map.84.own_ref, bf16[64,896]{1,0:T(8,128)(2,1)S(1)} %collective-permute-done.21.core_ref, bf16[1792,2048]{1,0:T(8,128)(2,1)S(1)} %get-tuple-element.52.down_ref), custom_call_target="tpu_custom_call" | custom-call | flops 469762048 | bytes 7340032 | tf_op jit(solution)/shard_map/pallas_call | solution.py:275
  64.3 1.4 %shard_map.86 = (f32[16,2048]{1,0:T(8,128)S(1)}, bf16[16,2048]{1,0:T(8,128)(2,1)S(1)}, bf16[16,2048]{1,0:T(8,128)(2,1)S(1)}, bf16[16,2048]{1,0:T(8,128)(2,1)S(1)}) custom-call(bf16[64,896]{1,0:T(8,128)(2,1)S(1)} %collective-permute-done.19.y_ref, bf16[64,896]{1,0:T(8,128)(2,1)S(1)} %collective-permute-done.20.yd_ref, ...), custom_call_target="tpu_custom_call" | custom-call | flops 469762048 | bytes 7340032 | tf_op jit(solution)/shard_map/pallas_call | solution.py:282
  65.7 1.5 %collective-permute-start.22 = (bf16[16,2048]{1,0:T(8,128)(2,1)S(1)}, bf16[16,2048]{1,0:T(8,128)(2,1)S(1)}, u32[]{:S(2)}, u32[]{:S(2)}) collective-permute-start(bf16[16,2048]{1,0:T(8,128)(2,1)S(1)} %get-tuple-element.60), channel_id=1, source_target_pairs={{0,3},{1,2},{2,1},{3,0},{4,7},{5,6},{6,5},{7,4},{8,11},{9,10},{10,... | collective-permute-start | bytes 196616 | tf_op jit(solution)/shard_map/ppermute | solution.py:364
  67.2 2.9 %collective-permute-start.24 = (bf16[16,2048]{1,0:T(8,128)(2,1)S(1)}, bf16[16,2048]{1,0:T(8,128)(2,1)S(1)}, u32[]{:S(2)}, u32[]{:S(2)}) collective-permute-start(bf16[16,2048]{1,0:T(8,128)(2,1)S(1)} %get-tuple-element.62), channel_id=1, source_target_pairs={{0,1},{1,0},{2,3},{3,2},{4,5},{5,4},{6,7},{7,6},{8,9},{9,8},{10,11... | collective-permute-start | bytes 196616 | tf_op jit(solution)/shard_map/ppermute | solution.py:364
  70.1 2.5 %collective-permute-done.22.refs_5_ = bf16[16,2048]{1,0:T(8,128)(2,1)S(1)} collective-permute-done((bf16[16,2048]{1,0:T(8,128)(2,1)S(1)}, bf16[16,2048]{1,0:T(8,128)(2,1)S(1)}, u32[]{:S(2)}, u32[]{:S(2)}) %collective-permute-start.22) | collective-permute-done | bytes 65568 | tf_op jit(solution)/shard_map/ppermute | solution.py:364
  72.6 1.4 %collective-permute-done.23.refs_6_ = bf16[16,2048]{1,0:T(8,128)(2,1)S(1)} collective-permute-done((bf16[16,2048]{1,0:T(8,128)(2,1)S(1)}, bf16[16,2048]{1,0:T(8,128)(2,1)S(1)}, u32[]{:S(2)}, u32[]{:S(2)}) %collective-permute-start.23) | collective-permute-done | bytes 65568 | tf_op jit(solution)/shard_map/ppermute | solution.py:364
  75.1 1.1 %collective-permute-start.27 = (bf16[2,4,2048]{2,1,0:T(4,128)(2,1)S(1)}, bf16[2,4,2048]{2,1,0:T(4,128)(2,1)S(1)}, u32[]{:S(2)}, u32[]{:S(2)}) collective-permute-start(bf16[2,4,2048]{2,1,0:T(4,128)(2,1)S(1)} %get-tuple-element.66), channel_id=1, source_target_pairs={{0,12},{4,8},{8,4},{12,0},{1,13},{5,9},{9,5},{13,1},{2,14},{6,10},... | collective-permute-start | bytes 98312 | tf_op jit(solution)/shard_map/ppermute | solution.py:325
  76.2 2.3 %collective-permute-done.26.y_ref = bf16[2,4,2048]{2,1,0:T(4,128)(2,1)S(1)} collective-permute-done((bf16[2,4,2048]{2,1,0:T(4,128)(2,1)S(1)}, bf16[2,4,2048]{2,1,0:T(4,128)(2,1)S(1)}, u32[]{:S(2)}, u32[]{:S(2)}) %collective-permute-start.26) | collective-permute-done | bytes 32800 | tf_op jit(solution)/shard_map/ppermute | solution.py:324
  (55 shorter events, 11.9 us)
Async XLA Ops:
  0.0 0.9 %copy-start = (bf16[2,8,8192]{2,1,0:T(8,128)(2,1)S(1)}, bf16[2,8,8192]{2,1,0:T(8,128)(2,1)}, u32[]{:S(2)}) copy-start(bf16[2,8,8192]{2,1,0:T(8,128)(2,1)} %rows_ref.1) | copy-start | bytes 786436
  1.2 3.2 %collective-permute-start = (bf16[2,8,2048]{2,1,0:T(8,128)(2,1)S(1)}, bf16[2,8,2048]{2,1,0:T(8,128)(2,1)S(1)}, u32[]{:S(2)}, u32[]{:S(2)}) collective-permute-start(bf16[2,8,2048]{2,1,0:T(8,128)(2,1)S(1)} %get-tuple-element.37), channel_id=1, source_target_pairs={{0,4},{4,0},{8,12},{12,8},{1,5},{5,1},{9,13},{13,9},{2,6},{6,2},{1... | collective-permute-start | bytes 196616 | tf_op jit(solution)/shard_map/ppermute | solution.py:323
  1.7 5.3 %collective-permute-start.1 = (bf16[2,8,2048]{2,1,0:T(8,128)(2,1)S(1)}, bf16[2,8,2048]{2,1,0:T(8,128)(2,1)S(1)}, u32[]{:S(2)}, u32[]{:S(2)}) collective-permute-start(bf16[2,8,2048]{2,1,0:T(8,128)(2,1)S(1)} %get-tuple-element.38), channel_id=1, source_target_pairs={{0,8},{4,12},{8,0},{12,4},{1,9},{5,13},{9,1},{13,5},{2,10},{6,14},... | collective-permute-start | bytes 196616 | tf_op jit(solution)/shard_map/ppermute | solution.py:324
  4.3 4.0 %collective-permute-start.2 = (bf16[2,8,2048]{2,1,0:T(8,128)(2,1)S(1)}, bf16[2,8,2048]{2,1,0:T(8,128)(2,1)S(1)}, u32[]{:S(2)}, u32[]{:S(2)}) collective-permute-start(bf16[2,8,2048]{2,1,0:T(8,128)(2,1)S(1)} %get-tuple-element.39), channel_id=1, source_target_pairs={{0,12},{4,8},{8,4},{12,0},{1,13},{5,9},{9,5},{13,1},{2,14},{6,10},... | collective-permute-start | bytes 196616 | tf_op jit(solution)/shard_map/ppermute | solution.py:325
  8.3 12.1 %collective-permute-start.4 = (bf16[32,2048]{1,0:T(8,128)(2,1)S(1)}, bf16[32,2048]{1,0:T(8,128)(2,1)S(1)}, u32[]{:S(2)}, u32[]{:S(2)}) collective-permute-start(bf16[32,2048]{1,0:T(8,128)(2,1)S(1)} %shard_map.66.refs_1_), channel_id=1, source_target_pairs={{0,1},{1,0},{2,3},{3,2},{4,5},{5,4},{6,7},{7,6},{8,9},{9,8},{10,11... | collective-permute-start | bytes 393224 | tf_op jit(solution)/shard_map/ppermute | solution.py:340
  10.0 10.5 %collective-permute-start.7 = (bf16[32,2048]{1,0:T(8,128)(2,1)S(1)}, bf16[32,2048]{1,0:T(8,128)(2,1)S(1)}, u32[]{:S(2)}, u32[]{:S(2)}) collective-permute-start(bf16[32,2048]{1,0:T(8,128)(2,1)S(1)} %shard_map.66.refs_1_), channel_id=1, source_target_pairs={{0,3},{1,2},{2,1},{3,0},{4,7},{5,6},{6,5},{7,4},{8,11},{9,10},{10,... | collective-permute-start | bytes 393224 | tf_op jit(solution)/shard_map/ppermute | solution.py:339
  12.4 9.0 %collective-permute-start.3 = (bf16[32,2048]{1,0:T(8,128)(2,1)S(1)}, bf16[32,2048]{1,0:T(8,128)(2,1)S(1)}, u32[]{:S(2)}, u32[]{:S(2)}) collective-permute-start(bf16[32,2048]{1,0:T(8,128)(2,1)S(1)} %shard_map.65.refs_0_), channel_id=1, source_target_pairs={{0,1},{1,0},{2,3},{3,2},{4,5},{5,4},{6,7},{7,6},{8,9},{9,8},{10,11... | collective-permute-start | bytes 393224 | tf_op jit(solution)/shard_map/ppermute | solution.py:340
  13.1 12.1 %collective-permute-start.5 = (bf16[32,2048]{1,0:T(8,128)(2,1)S(1)}, bf16[32,2048]{1,0:T(8,128)(2,1)S(1)}, u32[]{:S(2)}, u32[]{:S(2)}) collective-permute-start(bf16[32,2048]{1,0:T(8,128)(2,1)S(1)} %shard_map.65.refs_0_), channel_id=1, source_target_pairs={{0,3},{1,2},{2,1},{3,0},{4,7},{5,6},{6,5},{7,4},{8,11},{9,10},{10,... | collective-permute-start | bytes 393224 | tf_op jit(solution)/shard_map/ppermute | solution.py:339
  20.5 8.4 %collective-permute-start.8 = (bf16[32,2048]{1,0:T(8,128)(2,1)S(1)}, bf16[32,2048]{1,0:T(8,128)(2,1)S(1)}, u32[]{:S(2)}, u32[]{:S(2)}) collective-permute-start(bf16[32,2048]{1,0:T(8,128)(2,1)S(1)} %shard_map.70), channel_id=1, source_target_pairs={{0,1},{1,0},{2,3},{3,2},{4,5},{5,4},{6,7},{7,6},{8,9},{9,8},{10,11... | collective-permute-start | bytes 393224 | tf_op jit(solution)/shard_map/ppermute | solution.py:341
  25.3 3.4 %copy-start.1 = (s32[2,16]{1,0:T(2,128)S(1)}, s32[2,16]{1,0:T(2,128)}, u32[]{:S(2)}) copy-start(s32[2,16]{1,0:T(2,128)} %counts_ref.1) | copy-start | bytes 388
  25.3 3.4 %copy-start.2 = (s32[2,128]{1,0:T(2,128)S(1)}, s32[2,128]{1,0:T(2,128)}, u32[]{:S(2)}) copy-start(s32[2,128]{1,0:T(2,128)} %assign_ref.1) | copy-start | bytes 3076
  25.3 5.0 %collective-permute-start.6 = (bf16[32,2048]{1,0:T(8,128)(2,1)S(1)}, bf16[32,2048]{1,0:T(8,128)(2,1)S(1)}, u32[]{:S(2)}, u32[]{:S(2)}) collective-permute-start(bf16[32,2048]{1,0:T(8,128)(2,1)S(1)} %shard_map.68), channel_id=1, source_target_pairs={{0,1},{1,0},{2,3},{3,2},{4,5},{5,4},{6,7},{7,6},{8,9},{9,8},{10,11... | collective-permute-start | bytes 393224 | tf_op jit(solution)/shard_map/ppermute | solution.py:341
  31.7 1.9 %collective-permute-start.9 = (bf16[128,1792]{1,0:T(8,128)(2,1)S(1)}, bf16[128,1792]{1,0:T(8,128)(2,1)S(1)}, u32[]{:S(2)}, u32[]{:S(2)}) collective-permute-start(bf16[128,1792]{1,0:T(8,128)(2,1)S(1)} %get-tuple-element.48), channel_id=1, source_target_pairs={{0,4},{4,0},{8,12},{12,8},{1,5},{5,1},{9,13},{13,9},{2,6},{6,2},{1... | collective-permute-start | bytes 1376264 | tf_op jit(solution)/shard_map/ppermute | solution.py:344
  34.8 10.5 %collective-permute-start.10 = (bf16[128,1792]{1,0:T(8,128)(2,1)S(1)}, bf16[128,1792]{1,0:T(8,128)(2,1)S(1)}, u32[]{:S(2)}, u32[]{:S(2)}) collective-permute-start(bf16[128,1792]{1,0:T(8,128)(2,1)S(1)} %shard_map.78), channel_id=1, source_target_pairs={{0,4},{4,0},{8,12},{12,8},{1,5},{5,1},{9,13},{13,9},{2,6},{6,2},{1... | collective-permute-start | bytes 1376264 | tf_op jit(solution)/shard_map/ppermute | solution.py:347
  35.0 10.2 %collective-permute-start.11 = (bf16[64,1792]{1,0:T(8,128)(2,1)S(1)}, bf16[64,1792]{1,0:T(8,128)(2,1)S(1)}, u32[]{:S(2)}, u32[]{:S(2)}) collective-permute-start(bf16[64,1792]{1,0:T(8,128)(2,1)S(1)} %get-tuple-element.49.refs_0_), channel_id=1, source_target_pairs={{0,8},{4,12},{8,0},{12,4},{1,9},{5,13},{9,1},{13,5},{2,10},{6,14},... | collective-permute-start | bytes 688136 | tf_op jit(solution)/shard_map/ppermute | solution.py:346
  43.4 8.5 %collective-permute-start.18 = (bf16[64,1792]{1,0:T(8,128)(2,1)S(1)}, bf16[64,1792]{1,0:T(8,128)(2,1)S(1)}, u32[]{:S(2)}, u32[]{:S(2)}) collective-permute-start(bf16[64,1792]{1,0:T(8,128)(2,1)S(1)} %get-tuple-element.57), channel_id=1, source_target_pairs={{0,8},{4,12},{8,0},{12,4},{1,9},{5,13},{9,1},{13,5},{2,10},{6,14},... | collective-permute-start | bytes 688136 | tf_op jit(solution)/shard_map/ppermute | solution.py:346
  45.4 4.6 %collective-permute-start.14 = (bf16[64,896]{1,0:T(8,128)(2,1)S(1)}, bf16[64,896]{1,0:T(8,128)(2,1)S(1)}, u32[]{:S(2)}, u32[]{:S(2)}) collective-permute-start(bf16[64,896]{1,0:T(8,128)(2,1)S(1)} %shard_map.80.own_ref), channel_id=1, source_target_pairs={{0,4},{4,0},{8,12},{12,8},{1,5},{5,1},{9,13},{13,9},{2,6},{6,2},{1... | collective-permute-start | bytes 344072 | tf_op jit(solution)/shard_map/ppermute | solution.py:357
  45.5 8.0 %collective-permute-start.12 = (bf16[64,896]{1,0:T(8,128)(2,1)S(1)}, bf16[64,896]{1,0:T(8,128)(2,1)S(1)}, u32[]{:S(2)}, u32[]{:S(2)}) collective-permute-start(bf16[64,896]{1,0:T(8,128)(2,1)S(1)} %shard_map.80.own_ref), channel_id=1, source_target_pairs={{0,8},{4,12},{8,0},{12,4},{1,9},{5,13},{9,1},{13,5},{2,10},{6,14},... | collective-permute-start | bytes 344072 | tf_op jit(solution)/shard_map/ppermute | solution.py:356
  52.0 4.9 %collective-permute-start.19 = (bf16[64,896]{1,0:T(8,128)(2,1)S(1)}, bf16[64,896]{1,0:T(8,128)(2,1)S(1)}, u32[]{:S(2)}, u32[]{:S(2)}) collective-permute-start(bf16[64,896]{1,0:T(8,128)(2,1)S(1)} %shard_map.84.own_ref), channel_id=1, source_target_pairs={{0,8},{4,12},{8,0},{12,4},{1,9},{5,13},{9,1},{13,5},{2,10},{6,14},... | collective-permute-start | bytes 344072 | tf_op jit(solution)/shard_map/ppermute | solution.py:356
  53.6 3.4 %collective-permute-start.13 = (bf16[64,896]{1,0:T(8,128)(2,1)S(1)}, bf16[64,896]{1,0:T(8,128)(2,1)S(1)}, u32[]{:S(2)}, u32[]{:S(2)}) collective-permute-start(bf16[64,896]{1,0:T(8,128)(2,1)S(1)} %collective-permute-done.12.y_ref), channel_id=1, source_target_pairs={{0,4},{4,0},{8,12},{12,8},{1,5},{5,1},{9,13},{13,9},{2,6},{6,2},{1... | collective-permute-start | bytes 344072 | tf_op jit(solution)/shard_map/ppermute | solution.py:358
  53.6 9.3 %collective-permute-start.21 = (bf16[64,896]{1,0:T(8,128)(2,1)S(1)}, bf16[64,896]{1,0:T(8,128)(2,1)S(1)}, u32[]{:S(2)}, u32[]{:S(2)}) collective-permute-start(bf16[64,896]{1,0:T(8,128)(2,1)S(1)} %shard_map.84.own_ref), channel_id=1, source_target_pairs={{0,4},{4,0},{8,12},{12,8},{1,5},{5,1},{9,13},{13,9},{2,6},{6,2},{1... | collective-permute-start | bytes 344072 | tf_op jit(solution)/shard_map/ppermute | solution.py:357
  56.9 7.3 %collective-permute-start.20 = (bf16[64,896]{1,0:T(8,128)(2,1)S(1)}, bf16[64,896]{1,0:T(8,128)(2,1)S(1)}, u32[]{:S(2)}, u32[]{:S(2)}) collective-permute-start(bf16[64,896]{1,0:T(8,128)(2,1)S(1)} %collective-permute-done.19.y_ref), channel_id=1, source_target_pairs={{0,4},{4,0},{8,12},{12,8},{1,5},{5,1},{9,13},{13,9},{2,6},{6,2},{1... | collective-permute-start | bytes 344072 | tf_op jit(solution)/shard_map/ppermute | solution.py:358
  58.4 8.8 %collective-permute-start.15 = (bf16[16,2048]{1,0:T(8,128)(2,1)S(1)}, bf16[16,2048]{1,0:T(8,128)(2,1)S(1)}, u32[]{:S(2)}, u32[]{:S(2)}) collective-permute-start(bf16[16,2048]{1,0:T(8,128)(2,1)S(1)} %get-tuple-element.54), channel_id=1, source_target_pairs={{0,3},{1,2},{2,1},{3,0},{4,7},{5,6},{6,5},{7,4},{8,11},{9,10},{10,... | collective-permute-start | bytes 196616 | tf_op jit(solution)/shard_map/ppermute | solution.py:364
  59.9 10.3 %collective-permute-start.16 = (bf16[16,2048]{1,0:T(8,128)(2,1)S(1)}, bf16[16,2048]{1,0:T(8,128)(2,1)S(1)}, u32[]{:S(2)}, u32[]{:S(2)}) collective-permute-start(bf16[16,2048]{1,0:T(8,128)(2,1)S(1)} %get-tuple-element.55), channel_id=1, source_target_pairs={{0,2},{1,3},{2,0},{3,1},{4,6},{5,7},{6,4},{7,5},{8,10},{9,11},{10,... | collective-permute-start | bytes 196616 | tf_op jit(solution)/shard_map/ppermute | solution.py:364
  60.5 9.7 %collective-permute-start.17 = (bf16[16,2048]{1,0:T(8,128)(2,1)S(1)}, bf16[16,2048]{1,0:T(8,128)(2,1)S(1)}, u32[]{:S(2)}, u32[]{:S(2)}) collective-permute-start(bf16[16,2048]{1,0:T(8,128)(2,1)S(1)} %get-tuple-element.56), channel_id=1, source_target_pairs={{0,1},{1,0},{2,3},{3,2},{4,5},{5,4},{6,7},{7,6},{8,9},{9,8},{10,11... | collective-permute-start | bytes 196616 | tf_op jit(solution)/shard_map/ppermute | solution.py:364
  65.7 6.9 %collective-permute-start.22 = (bf16[16,2048]{1,0:T(8,128)(2,1)S(1)}, bf16[16,2048]{1,0:T(8,128)(2,1)S(1)}, u32[]{:S(2)}, u32[]{:S(2)}) collective-permute-start(bf16[16,2048]{1,0:T(8,128)(2,1)S(1)} %get-tuple-element.60), channel_id=1, source_target_pairs={{0,3},{1,2},{2,1},{3,0},{4,7},{5,6},{6,5},{7,4},{8,11},{9,10},{10,... | collective-permute-start | bytes 196616 | tf_op jit(solution)/shard_map/ppermute | solution.py:364
  67.2 6.9 %collective-permute-start.23 = (bf16[16,2048]{1,0:T(8,128)(2,1)S(1)}, bf16[16,2048]{1,0:T(8,128)(2,1)S(1)}, u32[]{:S(2)}, u32[]{:S(2)}) collective-permute-start(bf16[16,2048]{1,0:T(8,128)(2,1)S(1)} %get-tuple-element.61), channel_id=1, source_target_pairs={{0,2},{1,3},{2,0},{3,1},{4,6},{5,7},{6,4},{7,5},{8,10},{9,11},{10,... | collective-permute-start | bytes 196616 | tf_op jit(solution)/shard_map/ppermute | solution.py:364
  67.2 6.8 %collective-permute-start.24 = (bf16[16,2048]{1,0:T(8,128)(2,1)S(1)}, bf16[16,2048]{1,0:T(8,128)(2,1)S(1)}, u32[]{:S(2)}, u32[]{:S(2)}) collective-permute-start(bf16[16,2048]{1,0:T(8,128)(2,1)S(1)} %get-tuple-element.62), channel_id=1, source_target_pairs={{0,1},{1,0},{2,3},{3,2},{4,5},{5,4},{6,7},{7,6},{8,9},{9,8},{10,11... | collective-permute-start | bytes 196616 | tf_op jit(solution)/shard_map/ppermute | solution.py:364
  74.2 1.9 %collective-permute-start.25 = (bf16[2,4,2048]{2,1,0:T(4,128)(2,1)S(1)}, bf16[2,4,2048]{2,1,0:T(4,128)(2,1)S(1)}, u32[]{:S(2)}, u32[]{:S(2)}) collective-permute-start(bf16[2,4,2048]{2,1,0:T(4,128)(2,1)S(1)} %get-tuple-element.64), channel_id=1, source_target_pairs={{0,4},{4,0},{8,12},{12,8},{1,5},{5,1},{9,13},{13,9},{2,6},{6,2},{1... | collective-permute-start | bytes 98312 | tf_op jit(solution)/shard_map/ppermute | solution.py:323
  74.3 4.2 %collective-permute-start.26 = (bf16[2,4,2048]{2,1,0:T(4,128)(2,1)S(1)}, bf16[2,4,2048]{2,1,0:T(4,128)(2,1)S(1)}, u32[]{:S(2)}, u32[]{:S(2)}) collective-permute-start(bf16[2,4,2048]{2,1,0:T(4,128)(2,1)S(1)} %get-tuple-element.65), channel_id=1, source_target_pairs={{0,8},{4,12},{8,0},{12,4},{1,9},{5,13},{9,1},{13,5},{2,10},{6,14},... | collective-permute-start | bytes 98312 | tf_op jit(solution)/shard_map/ppermute | solution.py:324
  75.1 3.7 %collective-permute-start.27 = (bf16[2,4,2048]{2,1,0:T(4,128)(2,1)S(1)}, bf16[2,4,2048]{2,1,0:T(4,128)(2,1)S(1)}, u32[]{:S(2)}, u32[]{:S(2)}) collective-permute-start(bf16[2,4,2048]{2,1,0:T(4,128)(2,1)S(1)} %get-tuple-element.66), channel_id=1, source_target_pairs={{0,12},{4,8},{8,4},{12,0},{1,13},{5,9},{9,5},{13,1},{2,14},{6,10},... | collective-permute-start | bytes 98312 | tf_op jit(solution)/shard_map/ppermute | solution.py:325

commit v3 on v0

--- a/solution.py
+++ b/solution.py
@@ -1,13 +1,380 @@
+import functools
+
 import jax
 import jax.numpy as jnp
 from jax import lax
+from jax.experimental import pallas as pl
+from jax.experimental.pallas import tpu as pltpu
 from jax.sharding import PartitionSpec as P
 
 STEPS = 2
 MEAN = 4
 
-
 epsilon = 1e-05
+
+BF = jnp.bfloat16
+F32 = jnp.float32
+MIB = 2**20
+PIECES = 2
+X1 = ((0, 1), (1, 0), (2, 3), (3, 2))
+X2 = ((0, 2), (1, 3), (2, 0), (3, 1))
+X3 = ((0, 3), (1, 2), (2, 1), (3, 0))
+
+
+def place():
+    row = lax.axis_index("row")
+    return row // 2, lax.rem(row, 2), lax.axis_index("col")
+
+
+def run(body, outs, operands, token, weights=(), scratch=()):
+    count, held = len(operands), len(weights)
+    vmem = pl.BlockSpec(memory_space=pltpu.VMEM)
+    outs = tuple(outs) + (like((8, 128), F32),)
+
+    def wrapped(*refs):
+        results = refs[count + held + 1 :]
+        body(refs[:count], refs[count : count + held], results[: len(outs) - 1], results[len(outs) :])
+        results[len(outs) - 1][...] = jnp.zeros((8, 128), F32)
+
+    return pl.pallas_call(
+        wrapped,
+        out_shape=outs,
+        in_specs=[vmem] * count
+        + [pl.BlockSpec(memory_space=pltpu.HBM)] * held
+        + [pl.BlockSpec(memory_space=pl.ANY)],
+        out_specs=(vmem,) * len(outs),
+        scratch_shapes=scratch,
+        compiler_params=pltpu.CompilerParams(vmem_limit_bytes=8 * MIB),
+        cost_estimate=pl.CostEstimate(flops=0, bytes_accessed=1, transcendentals=0),
+    )(*operands, *(pltpu.with_memory_space_constraint(w, pltpu.HBM) for w in weights), token)
+
+
+def like(shape, dtype=BF):
+    return jax.ShapeDtypeStruct(shape, dtype)
+
+
+def norm_body(ins, _, outs, __):
+    (rows_ref,) = ins
+    core_ref, sides = outs[0], outs[1:]
+    y, c, _ = place()
+    width = core_ref.shape[2]
+    for step in range(rows_ref.shape[0]):
+        total = jnp.sum(jnp.square(rows_ref[step].astype(F32)), axis=-1, keepdims=True)
+        scale = lax.rsqrt(total / rows_ref.shape[2] + epsilon)
+        y_ref, yd_ref, own_ref = sides[step * 3 : step * 3 + 3]
+        for dy, dc, out in ((1, 0, y_ref), (1, 1, yd_ref), (0, 1, core_ref.at[step]), (0, 0, own_ref)):
+            block = lax.bitwise_xor(y, dy) * 2 + lax.bitwise_xor(c, dc)
+            at = pl.ds(pl.multiple_of(block * width, width), width)
+            out[...] = (rows_ref[step, :, at].astype(F32) * scale).astype(BF)
+
+
+def normed_blocks(sender_rows, token):
+    steps, slots, width = sender_rows.shape
+    core = like((steps, slots, width // 4))
+    side = like((slots, width // 4))
+    return run(norm_body, (core,) + (side,) * 6, (sender_rows,), token)
+
+
+def pick_body(ins, _, outs, __):
+    counts_ref, assign_ref = ins
+    y, c, z = place()
+    rows = outs[0].shape[0]
+    slots = assign_ref.shape[1]
+    spread = (
+        lax.broadcasted_iota(jnp.int32, (slots // 8, slots), 1) // 8
+        == lax.broadcasted_iota(jnp.int32, (slots // 8, slots), 0)
+    ).astype(F32)
+    held = jnp.dot(counts_ref[...].astype(F32), spread, preferred_element_type=F32)
+    slot = lax.rem(lax.broadcasted_iota(jnp.int32, (1, slots), 1), 8).astype(F32)
+    at = lax.broadcasted_iota(jnp.int32, (rows, slots), 0)
+    target = (lax.rem(at, 16) // 4) * 16 + lax.bitwise_xor(at // 16, z) * 4 + lax.rem(at, 4)
+    p = lax.broadcasted_iota(jnp.int32, (slots, slots), 1)
+    bit = lambda shift: lax.rem(lax.shift_right_logical(p, shift), 2)
+    row = lax.bitwise_xor(bit(4), y) * 2 + lax.bitwise_xor(bit(3), c)
+    sender = row * 4 + lax.bitwise_xor(lax.shift_right_logical(p, 5), z)
+    source = sender * 8 + lax.rem(p, 8)
+    moved = (lax.broadcasted_iota(jnp.int32, (slots, slots), 0) == source).astype(F32).astype(BF)
+    for step, out in enumerate(outs):
+        live = slot < held[step : step + 1]
+        chosen = jnp.where(live, assign_ref[step : step + 1, :], -1)
+        placed = (chosen == target).astype(F32).astype(BF)
+        out[...] = jnp.dot(placed, moved, preferred_element_type=F32).astype(BF)
+
+
+def pick_matrices(counts, assign, token):
+    one = like((MEAN * counts.shape[1], assign.shape[1]))
+    return run(pick_body, (one, one), (counts, assign), token)
+
+
+def chunk_shape(chunk, gate_w, down_w):
+    if chunk[0] == "down":
+        return (down_w.shape[0] // 4, down_w.shape[1])
+    return (gate_w.shape[0] // 2, gate_w.shape[1] // 2)
+
+
+def chunk_copies(chunk, weights, out_ref, sems):
+    y, c, _ = place()
+    kind, dy, dc, half = chunk
+    quarter = lax.bitwise_xor(c, dc) * 2 + lax.bitwise_xor(y, dy)
+    if kind == "down":
+        height = out_ref.shape[0]
+        at = pl.ds(pl.multiple_of(quarter * height, 16), height)
+        return [pltpu.make_async_copy(weights[0].at[at, :], out_ref, sems.at[0])]
+    height, width = out_ref.shape[0], out_ref.shape[1] // 2
+    at = pl.ds(pl.multiple_of(quarter * width, 128), width)
+    return [
+        pltpu.make_async_copy(
+            w.at[pl.ds(half * height, height), at],
+            out_ref.at[:, pl.ds(i * width, width)],
+            sems.at[i],
+        )
+        for i, w in enumerate(weights)
+    ]
+
+
+def with_chunk(chunk, body):
+    def wrapped(ins, weights, outs, scratch):
+        copies = chunk_copies(chunk, weights, outs[-1], scratch[-1])
+        for copy in copies:
+            copy.start()
+        body(ins, weights, outs[:-1], scratch[:-1])
+        for copy in copies:
+            copy.wait()
+
+    return wrapped
+
+
+def meet(token):
+    return lax.ppermute(token, "row", X1)
+
+
+def run_with(chunk, model, body, outs, operands, token, scratch=()):
+    if chunk is None:
+        return run(body, outs, operands, token, (), scratch)
+    gate_w, up_w, down_w = model
+    weights = (down_w,) if chunk[0] == "down" else (gate_w, up_w)
+    return run(
+        with_chunk(chunk, body),
+        tuple(outs) + (pltpu.VMEM(chunk_shape(chunk, gate_w, down_w), BF),),
+        operands,
+        token,
+        weights,
+        tuple(scratch) + (pltpu.SemaphoreType.DMA((2,)),),
+    )
+
+
+def fetch_body(_, __, ___, ____):
+    pass
+
+
+def stack_step_body(step, ins, _, outs, __):
+    own_ref, core_ref, y_ref, yd_ref = ins
+    slots = own_ref.shape[0]
+    pairs = ((own_ref[...], core_ref[step]), (y_ref[...], yd_ref[...]))
+    for i, pair in enumerate(pairs):
+        joined = jnp.concatenate([x.astype(F32) for x in pair], axis=0).astype(BF)
+        outs[0][2 * i * slots : 2 * (i + 1) * slots, :] = joined
+
+
+def after_body(ins, _, outs, __):
+    outs[0][...] = ins[0][...]
+
+
+def halves_dot(x_ref, w_refs):
+    height = w_refs[0].shape[0]
+    total = jnp.dot(x_ref[:, :height], w_refs[0][...], preferred_element_type=F32)
+    return total + jnp.dot(x_ref[:, height:], w_refs[1][...], preferred_element_type=F32)
+
+
+def store_rows(outs, value):
+    rows = outs[0].shape[0]
+    for i, out in enumerate(outs):
+        out[...] = value[i * rows : (i + 1) * rows].astype(out.dtype)
+
+
+def load_rows(refs):
+    return jnp.concatenate([ref[...].astype(F32) for ref in refs], axis=0)
+
+
+def first_body(ins, _, outs, scratch):
+    pieces, pick_ref, w_refs = ins[:4], ins[4], ins[5:]
+    batch_ref, pieces_out = outs[0], outs[1:]
+    slots = scratch[0]
+    height = pieces[0].shape[0]
+    for i, piece in enumerate(pieces):
+        slots[i * height : (i + 1) * height, :] = piece[...]
+    batch_ref[...] = jnp.dot(pick_ref[...], slots[...], preferred_element_type=F32).astype(BF)
+    store_rows(pieces_out, halves_dot(batch_ref, w_refs))
+
+
+def dot_body(ins, _, outs, __):
+    store_rows(outs, halves_dot(ins[0], ins[1:]))
+
+
+def far_body(ins, _, outs, __):
+    outs[0][...] = (ins[0][...] + load_rows(ins[1:])).astype(BF)
+
+
+def hidden_body(ins, _, outs, __):
+    width = outs[0].shape[1]
+    total = ins[0][...] + ins[1][...].astype(F32) + load_rows(ins[2:])
+    gate, up = total[:, :width], total[:, width:]
+    outs[0][...] = (gate / (1.0 + jnp.exp(-gate)) * up).astype(BF)
+
+
+def down_part_body(ins, _, outs, __):
+    own_ref, core_ref, own_w, core_w = ins
+    total = jnp.dot(own_ref[...], own_w[...], preferred_element_type=F32)
+    outs[0][...] = total + jnp.dot(core_ref[...], core_w[...], preferred_element_type=F32)
+
+
+def down_rest_body(ins, _, outs, __):
+    y_ref, yd_ref, y_w, yd_w, part_ref = ins
+    rows = outs[0].shape[0]
+    total = part_ref[...] + jnp.dot(y_ref[...], y_w[...], preferred_element_type=F32)
+    total = total + jnp.dot(yd_ref[...], yd_w[...], preferred_element_type=F32)
+    for i, out in enumerate(outs):
+        out[...] = total[i * rows : (i + 1) * rows].astype(out.dtype)
+
+
+def owner_body(ins, _, outs, __):
+    y, c, _ = place()
+    at = lax.broadcasted_iota(jnp.int32, (16, 16), 0)
+    source = lax.bitwise_xor(at, (y * 2 + c) * 4)
+    turn = (lax.broadcasted_iota(jnp.int32, (16, 16), 1) == source).astype(F32).astype(BF)
+    for step in range(2):
+        total = ins[step * 4][...]
+        for got in ins[step * 4 + 1 : step * 4 + 4]:
+            total = total + got[...].astype(F32)
+        turned = jnp.dot(turn, total.astype(BF), preferred_element_type=F32)
+        for i, out in enumerate(outs):
+            out[step] = turned[i * 4 : (i + 1) * 4].astype(BF)
+
+
+def output_body(ins, _, outs, __):
+    y, c, _ = place()
+    width = ins[0].shape[2]
+    for dy, dc, block in ((0, 0, ins[0]), (0, 1, ins[1]), (1, 0, ins[2]), (1, 1, ins[3])):
+        source = lax.bitwise_xor(y, dy) * 2 + lax.bitwise_xor(c, dc)
+        outs[0][:, :, pl.ds(pl.multiple_of(source * width, width), width)] = block[...]
+
+
+def near_plan(sender_rows, counts, assign, gate_w, up_w, down_w):
+    steps, slots, width = sender_rows.shape
+    model = (gate_w, up_w, down_w)
+    width //= 4
+    units = gate_w.shape[1] // 4
+    rows = MEAN * counts.shape[1]
+    part = rows // 4
+    held = {}
+
+    def bring(chunk, token):
+        held[chunk], token = run_with(chunk, model, fetch_body, (), (), token)
+        return token
+
+    def quarter(dy, dc):
+        return held["gu", dy, dc, 0], held["gu", dy, dc, 1]
+
+    def carry(chunk, body, outs, operands, token, scratch=()):
+        results = run_with(chunk, model, body, outs, operands, token, scratch)
+        if chunk is not None:
+            held[chunk] = results[-2]
+        return results[: len(outs)] + (results[-1],)
+
+    core, y0, yd0, own0, y1, yd1, own1, token = normed_blocks(sender_rows, counts)
+    sides = []
+    for own, y, yd in ((own0, y0, yd0), (own1, y1, yd1)):
+        sides.append((own, lax.ppermute(y, "row", X2), lax.ppermute(yd, "row", X3)))
+    core_got = lax.ppermute(core, "row", X1)
+    *picks, token = pick_matrices(counts, assign, token)
+    token = bring(("gu", 1, 1, 0), token)
+
+    blocks, far, near, onward = [], [], [], []
+    for step, (own, y, yd) in enumerate(sides):
+        block, token = run(
+            functools.partial(stack_step_body, step),
+            (like((4 * slots, width)),),
+            (own, core_got, y, yd),
+            token,
+        )
+        blocks.append(block)
+        far.append(lax.ppermute(block, "col", X3))
+        near.append(lax.ppermute(block, "col", X1))
+    token = bring(("gu", 1, 1, 1), meet(token))
+    for step in range(steps):
+        passed, token = run(after_body, (like(far[step].shape),), (far[step],), token)
+        onward.append(lax.ppermute(passed, "col", X1))
+        token = meet(token)
+        if step == 0:
+            token = bring(("gu", 1, 0, 0), token)
+            token = bring(("gu", 1, 0, 1), token)
+
+    carried = (
+        (("gu", 0, 1, 0), ("gu", 0, 1, 1), ("gu", 0, 0, 0), ("down", 0, 0, 0)),
+        (("down", 0, 1, 0), ("down", 1, 0, 0), ("down", 1, 1, 0), None),
+    )
+    gots, nears, near_cores, hidden, sums = [], [], [], [], []
+    both = like((rows, 2 * units))
+    bits = (like((rows // PIECES, 2 * units)),) * PIECES
+    both_wide = like((rows, 2 * units), F32)
+
+    def activate(step, token):
+        result, token = run(
+            hidden_body, (like((rows, units)),), (nears[step], gots[step]) + near_cores[step], token
+        )
+        y = lax.ppermute(result, "row", X2)
+        hidden.append((result, lax.ppermute(result, "row", X1), y))
+        return token
+
+    for step in range(steps):
+        first, second, third, fourth = carried[step]
+        pieces = (blocks[step], near[step], onward[step], far[step])
+        batch, *out, token = carry(
+            first,
+            first_body,
+            (like((rows, width)),) + bits,
+            pieces + (picks[step],) + quarter(1, 1),
+            token,
+            (pltpu.VMEM((16 * slots, width), BF),),
+        )
+        core = tuple(lax.ppermute(o, "row", X1) for o in out)
+        own, token = carry(second, dot_body, (both_wide,), (batch,) + quarter(1, 0), token)
+        send, token = run(far_body, (both,), (own,) + core, token)
+        gots.append(lax.ppermute(send, "row", X2))
+        *out, token = carry(third, dot_body, bits, (batch,) + quarter(0, 1), meet(token))
+        near_cores.append(tuple(lax.ppermute(o, "row", X1) for o in out))
+        if step == 0:
+            token = bring(("gu", 0, 0, 1), token)
+        own, token = carry(fourth, dot_body, (both_wide,), (batch,) + quarter(0, 0), token)
+        nears.append(own)
+
+    def down_part(step, token):
+        weights = (held["down", 0, 0, 0], held["down", 0, 1, 0])
+        return run(
+            down_part_body, (like((rows, width), F32),), hidden[step][:2] + weights, token
+        )
+
+    def down_rest(step, part_sum, yd, token):
+        weights = (held["down", 1, 0, 0], held["down", 1, 1, 0])
+        outs = (like((part, width), F32),) + (like((part, width)),) * 3
+        operands = (hidden[step][2], yd) + weights + (part_sum,)
+        keep, send1, send2, send3, token = run(down_rest_body, outs, operands, token)
+        got = [lax.ppermute(s, "col", x) for s, x in ((send3, X3), (send2, X2), (send1, X1))]
+        sums.extend([keep] + got)
+        return token
+
+    token = activate(0, token)
+    part0, token = down_part(0, token)
+    token = activate(1, token)
+    passed, token = run(after_body, (like(hidden[0][2].shape),), (hidden[0][2],), token)
+    token = down_rest(0, part0, lax.ppermute(passed, "row", X1), token)
+    part1, token = down_part(1, meet(token))
+    passed, token = run(after_body, (like(hidden[1][2].shape),), (hidden[1][2],), token)
+    token = down_rest(1, part1, lax.ppermute(passed, "row", X1), token)
+    own, core, y, yd, token = run(owner_body, (like((steps, MEAN, width)),) * 4, tuple(sums), token)
+    blocks = (own, lax.ppermute(core, "row", X1), lax.ppermute(y, "row", X2), lax.ppermute(yd, "row", X3))
+    result, _ = run(output_body, (like((steps, MEAN, 4 * width)),), blocks, token)
+    return result
 
 
 def layer_block(normed_block, counts_block, assign_block, paired, down_w, hidden_cols):
@@ -64,7 +431,7 @@
     return finished.reshape(step_count, MEAN, finished.shape[1])
 
 
-def per_device(sender_rows, counts, assign, gate_w, up_w, down_w):
+def any_plan(sender_rows, counts, assign, gate_w, up_w, down_w):
     values = sender_rows.astype(jnp.float32)
     normed = (
         values * lax.rsqrt(jnp.mean(values * values, axis=-1, keepdims=True) + epsilon)
@@ -88,8 +455,9 @@
 
 
 def solution(mesh):
+    near = mesh.shape["row"] == 4 and mesh.shape["col"] == 4
     return jax.shard_map(
-        per_device,
+        near_plan if near else any_plan,
         mesh=mesh,
         in_specs=(
             P(None, ("groups", "row", "col"), None),

time: 332 us -> 95.5 us (0.29)
  other arithmetic: 95.8 us -> 0 us
  local copies, waits for them, and re-layouts: 84.1 us -> 2.31 us
  blocking collectives: 53 us -> 0 us
  matrix products: 43.6 us -> 0 us
  Pallas kernels: 0 us -> 43 us
  starting transfers between devices: 11.2 us -> 29.9 us
  between operations: 13.4 us -> 0.39 us
  waiting for transfers between devices: 29.2 us -> 19.5 us
    unnamed x2 -> x0, other arithmetic: 90.5 us -> none
    all_gather x4 -> x0, blocking collectives: 46.3 us -> none  [the longest x2 32.5 us: layer_block(): gathered = lax.all_gather(spread, 'col', axis=1, tiled=True)]
    dot_general x4 -> x0, matrix products: 43.6 us -> none  [the longest x2 26.3 us: layer_block(): jnp.dot(rows_here, paired, preferred_element_type=jnp.float32)]
    pallas_call x0 -> x31, Pallas kernels: none -> 43 us  [run(): pl.pallas_call(wrapped, out_shape=outs, in_specs=[vmem] * count + [pl.Blo...]
    ppermute x0 -> x42, starting transfers between devices: none -> 29.9 us  [the longest x6 8.84 us: down_rest(): lax.ppermute(s, 'col', x)]
    reduce_scatter x4 -> x0, waiting for transfers between devices: 29.2 us -> none  [the longest x2 21 us: layer_block(): lax.psum_scatter(jnp.dot(rows_here, down_w, preferred_element_type=jnp.fl...]
    unnamed x6, local copies, waits for them, and re-layouts: 31.3 us -> 2.31 us
    ppermute x0 -> x42, waiting for transfers between devices: none -> 19.5 us  [the longest x6 5.22 us: down_rest(): lax.ppermute(s, 'col', x)]
  transfers between devices with their start and end apart: 7 -> 42, of which waited for: 3 -> 14; matrix products, arithmetic and copies ran while one was open for 49% -> 0% of each run, Pallas kernels for 0% -> 44%
where the time goes in v3:
time: 95.5 us; the launch traced here: 95.1 us
  Pallas kernels  43 us (45%)
  starting transfers between devices  29.9 us (31%)
  waiting for transfers between devices  19.5 us (20%)
  local copies, waits for them, and re-layouts  2.31 us (2%)
    pallas_call x31, Pallas kernels, run(): pl.pallas_call(wrapped, out_shape=outs, in_specs=[vmem] * count + [pl.Blo...  43 us
    ppermute x6, starting transfers between devices, down_rest(): lax.ppermute(s, 'col', x)  8.84 us
    ppermute x6, waiting for transfers between devices, down_rest(): lax.ppermute(s, 'col', x)  5.22 us
    ppermute x6, waiting for transfers between devices, meet(): return lax.ppermute(token, 'row', X1)  4.98 us
    ppermute x4, starting transfers between devices, near_plan(): sides.append((own, lax.ppermute(y, 'row', X2), lax.ppermute(yd, 'row', X3)))  4.16 us
    ppermute x4, waiting for transfers between devices, near_plan(): sides.append((own, lax.ppermute(y, 'row', X2), lax.ppermute(yd, 'row', X3)))  3.91 us
    ppermute x2, starting transfers between devices, near_plan(): far.append(lax.ppermute(block, 'col', X3))  3.89 us
    ppermute x2, waiting for transfers between devices, activate(): y = lax.ppermute(result, 'row', X2)  2.81 us
  transfers between devices with their start and end apart: 42, of which 14 were waited for; matrix products, arithmetic and copies ran while one was open for 0% of the time, Pallas kernels for 44%

profile of v3, /device:TPU:0, one launch (start us, length us, event | category | flops | bytes accessed | tf_op | source)
XLA Modules:
  0.0 95.1 jit_solution(10904572450544740141)
XLA Ops:
  2.4 2.6 %collective-permute-start.1 = (bf16[8,2048]{1,0:T(8,128)(2,1)S(1)}, bf16[8,2048]{1,0:T(8,128)(2,1)S(1)}, u32[]{:S(2)}, u32[]{:S(2)}) collective-permute-start(bf16[8,2048]{1,0:T(8,128)(2,1)S(1)} %get-tuple-element.97), channel_id=1, source_target_pairs={{0,8},{4,12},{8,0},{12,4},{1,9},{5,13},{9,1},{13,5},{2,10},{6,14},... | collective-permute-start | bytes 98312 | tf_op jit(solution)/shard_map/ppermute | solution.py:287
  5.9 2.1 %shard_map.66 = (bf16[1024,1792]{1,0:T(8,128)(2,1)S(1)}, f32[8,128]{1,0:T(8,128)S(1)}) custom-call(bf16[2048,3584]{1,0:T(8,128)(2,1)} %refs_0_.13, bf16[2048,3584]{1,0:T(8,128)(2,1)} %refs_1_.13, f32[8,128]{1,0:T(8,128)S(1)} %get-tuple-element.100.refs_2_), custom_call_target="tpu_custom_call" | custom-call | bytes 1 | tf_op jit(solution)/shard_map/pallas_call | solution.py:39
  8.3 3.7 %collective-permute-start.4 = (bf16[32,2048]{1,0:T(8,128)(2,1)S(1)}, bf16[32,2048]{1,0:T(8,128)(2,1)S(1)}, u32[]{:S(2)}, u32[]{:S(2)}) collective-permute-start(bf16[32,2048]{1,0:T(8,128)(2,1)S(1)} %get-tuple-element.102.refs_0_), channel_id=1, source_target_pairs={{0,3},{1,2},{2,1},{3,0},{4,7},{5,6},{6,5},{7,4},{8,11},{9,10},{10,... | collective-permute-start | bytes 393224 | tf_op jit(solution)/shard_map/ppermute | solution.py:301
  12.0 1.5 %collective-permute-start.5 = (bf16[8,2048]{1,0:T(8,128)(2,1)S(1)}, bf16[8,2048]{1,0:T(8,128)(2,1)S(1)}, u32[]{:S(2)}, u32[]{:S(2)}) collective-permute-start(bf16[8,2048]{1,0:T(8,128)(2,1)S(1)} %get-tuple-element.104), channel_id=1, source_target_pairs={{0,8},{4,12},{8,0},{12,4},{1,9},{5,13},{9,1},{13,5},{2,10},{6,14},... | collective-permute-start | bytes 98312 | tf_op jit(solution)/shard_map/ppermute | solution.py:287
  13.5 2.4 %collective-permute-done.5.refs_2_ = bf16[8,2048]{1,0:T(8,128)(2,1)S(1)} collective-permute-done((bf16[8,2048]{1,0:T(8,128)(2,1)S(1)}, bf16[8,2048]{1,0:T(8,128)(2,1)S(1)}, u32[]{:S(2)}, u32[]{:S(2)}) %collective-permute-start.5) | collective-permute-done | bytes 32800 | tf_op jit(solution)/shard_map/ppermute | solution.py:287
  15.9 1.2 %collective-permute-done.6.refs_3_ = bf16[8,2048]{1,0:T(8,128)(2,1)S(1)} collective-permute-done((bf16[8,2048]{1,0:T(8,128)(2,1)S(1)}, bf16[8,2048]{1,0:T(8,128)(2,1)S(1)}, u32[]{:S(2)}, u32[]{:S(2)}) %collective-permute-start.6) | collective-permute-done | bytes 32800 | tf_op jit(solution)/shard_map/ppermute | solution.py:287
  18.5 2.1 %shard_map.69 = (bf16[1024,1792]{1,0:T(8,128)(2,1)S(1)}, f32[8,128]{1,0:T(8,128)S(1)}) custom-call(bf16[2048,3584]{1,0:T(8,128)(2,1)} %refs_0_.13, bf16[2048,3584]{1,0:T(8,128)(2,1)} %refs_1_.13, f32[8,128]{1,0:T(8,128)S(1)} %collective-permute-done.7.refs_2_), custom_call_target="tpu_custom_call" | custom-call | bytes 1 | tf_op jit(solution)/shard_map/pallas_call | solution.py:39
  21.6 1.2 %collective-permute-start.18 = (bf16[32,2048]{1,0:T(8,128)(2,1)S(1)}, bf16[32,2048]{1,0:T(8,128)(2,1)S(1)}, u32[]{:S(2)}, u32[]{:S(2)}) collective-permute-start(bf16[32,2048]{1,0:T(8,128)(2,1)S(1)} %get-tuple-element.113.refs_0_), channel_id=1, source_target_pairs={{0,1},{1,0},{2,3},{3,2},{4,5},{5,4},{6,7},{7,6},{8,9},{9,8},{10,11... | collective-permute-start | bytes 393224 | tf_op jit(solution)/shard_map/ppermute | solution.py:302
  22.7 2.1 %shard_map.71 = (bf16[1024,1792]{1,0:T(8,128)(2,1)S(1)}, f32[8,128]{1,0:T(8,128)S(1)}) custom-call(bf16[2048,3584]{1,0:T(8,128)(2,1)} %refs_0_.13, bf16[2048,3584]{1,0:T(8,128)(2,1)} %refs_1_.13, f32[8,128]{1,0:T(8,128)S(1)} %collective-permute-done.10.refs_2_), custom_call_target="tpu_custom_call" | custom-call | bytes 1 | tf_op jit(solution)/shard_map/pallas_call | solution.py:39
  24.8 2.1 %shard_map.72 = (bf16[1024,1792]{1,0:T(8,128)(2,1)S(1)}, f32[8,128]{1,0:T(8,128)S(1)}) custom-call(bf16[2048,3584]{1,0:T(8,128)(2,1)} %refs_0_.13, bf16[2048,3584]{1,0:T(8,128)(2,1)} %refs_1_.13, f32[8,128]{1,0:T(8,128)S(1)} %get-tuple-element.115.refs_2_), custom_call_target="tpu_custom_call" | custom-call | bytes 1 | tf_op jit(solution)/shard_map/pallas_call | solution.py:39
  27.0 1.2 %collective-permute-start.19 = (bf16[32,2048]{1,0:T(8,128)(2,1)S(1)}, bf16[32,2048]{1,0:T(8,128)(2,1)S(1)}, u32[]{:S(2)}, u32[]{:S(2)}) collective-permute-start(bf16[32,2048]{1,0:T(8,128)(2,1)S(1)} %get-tuple-element.137), channel_id=1, source_target_pairs={{0,1},{1,0},{2,3},{3,2},{4,5},{5,4},{6,7},{7,6},{8,9},{9,8},{10,11... | collective-permute-start | bytes 393224 | tf_op jit(solution)/shard_map/ppermute | solution.py:306
  28.2 1.2 %collective-permute-done.11.refs_9_ = f32[8,128]{1,0:T(8,128)S(1)} collective-permute-done((f32[8,128]{1,0:T(8,128)S(1)}, f32[8,128]{1,0:T(8,128)S(1)}, u32[]{:S(2)}, u32[]{:S(2)}) %collective-permute-start.11) | collective-permute-done | bytes 4128 | tf_op jit(solution)/shard_map/ppermute | solution.py:148
  29.4 3.5 %shard_map.74 = (bf16[64,2048]{1,0:T(8,128)(2,1)S(1)}, bf16[32,1792]{1,0:T(8,128)(2,1)S(1)}, bf16[32,1792]{1,0:T(8,128)(2,1)S(1)}, bf16[1024,1792]{1,0:T(8,128)(2,1)S(1)}, f32[8,128]{1,0:T(8,128)S(1)}) custom-call(bf16[32,2048]{1,0:T(8,128)(2,1)S(1)} %get-tuple-element.102.refs_0_, bf16[32,2048]{1,0:T(8,128)(2,1)S(1)} %collective-permute-done.3.refs_1_, ...), custom_call_target="tpu_custom_call" | custom-call | bytes 1 | tf_op jit(solution)/shard_map/pallas_call | solution.py:39
  33.4 3.3 %shard_map.75 = (f32[64,1792]{1,0:T(8,128)S(1)}, bf16[1024,1792]{1,0:T(8,128)(2,1)S(1)}, f32[8,128]{1,0:T(8,128)S(1)}) custom-call(bf16[64,2048]{1,0:T(8,128)(2,1)S(1)} %get-tuple-element.118.refs_0_, bf16[1024,1792]{1,0:T(8,128)(2,1)S(1)} %get-tuple-element.120.refs_1_, bf16[1024,1792]{1,0:T(8,128)(2,1)S(1)} %get-tuple-element.121.refs_2_, ...), custom_call_target="tpu_custom_call" | custom-call | bytes 1 | tf_op jit(solution)/shard_map/pallas_call | solution.py:39
  38.1 3.3 %shard_map.77 = (bf16[32,1792]{1,0:T(8,128)(2,1)S(1)}, bf16[32,1792]{1,0:T(8,128)(2,1)S(1)}, bf16[1024,1792]{1,0:T(8,128)(2,1)S(1)}, f32[8,128]{1,0:T(8,128)S(1)}) custom-call(bf16[64,2048]{1,0:T(8,128)(2,1)S(1)} %get-tuple-element.118.refs_0_, bf16[1024,1792]{1,0:T(8,128)(2,1)S(1)} %get-tuple-element.119.refs_1_, ...), custom_call_target="tpu_custom_call" | custom-call | bytes 1 | tf_op jit(solution)/shard_map/pallas_call | solution.py:39
  41.4 2.1 %shard_map.78 = (bf16[1024,1792]{1,0:T(8,128)(2,1)S(1)}, f32[8,128]{1,0:T(8,128)S(1)}) custom-call(bf16[2048,3584]{1,0:T(8,128)(2,1)} %refs_0_.13, bf16[2048,3584]{1,0:T(8,128)(2,1)} %refs_1_.13, f32[8,128]{1,0:T(8,128)S(1)} %get-tuple-element.130.refs_2_), custom_call_target="tpu_custom_call" | custom-call | bytes 1 | tf_op jit(solution)/shard_map/pallas_call | solution.py:39
  43.5 3.3 %shard_map.79 = (f32[64,1792]{1,0:T(8,128)S(1)}, bf16[896,2048]{1,0:T(8,128)(2,1)S(1)}, f32[8,128]{1,0:T(8,128)S(1)}) custom-call(bf16[64,2048]{1,0:T(8,128)(2,1)S(1)} %get-tuple-element.118.refs_0_, bf16[1024,1792]{1,0:T(8,128)(2,1)S(1)} %get-tuple-element.129.refs_1_, bf16[1024,1792]{1,0:T(8,128)(2,1)S(1)} %get-tuple-element.131.refs_2_, ...), custom_call_target="tpu_custom_call" | custom-call | bytes 1 | tf_op jit(solution)/shard_map/pallas_call | solution.py:39
  46.9 3.5 %shard_map.80 = (bf16[64,2048]{1,0:T(8,128)(2,1)S(1)}, bf16[32,1792]{1,0:T(8,128)(2,1)S(1)}, bf16[32,1792]{1,0:T(8,128)(2,1)S(1)}, bf16[896,2048]{1,0:T(8,128)(2,1)S(1)}, f32[8,128]{1,0:T(8,128)S(1)}) custom-call(bf16[32,2048]{1,0:T(8,128)(2,1)S(1)} %get-tuple-element.113.refs_0_, bf16[32,2048]{1,0:T(8,128)(2,1)S(1)} %collective-permute-done.18.refs_1_, ...), custom_call_target="tpu_custom_call" | custom-call | bytes 1 | tf_op jit(solution)/shard_map/pallas_call | solution.py:39
  51.5 3.3 %shard_map.81 = (f32[64,1792]{1,0:T(8,128)S(1)}, bf16[896,2048]{1,0:T(8,128)(2,1)S(1)}, f32[8,128]{1,0:T(8,128)S(1)}) custom-call(bf16[64,2048]{1,0:T(8,128)(2,1)S(1)} %get-tuple-element.140.refs_0_, bf16[1024,1792]{1,0:T(8,128)(2,1)S(1)} %get-tuple-element.120.refs_1_, bf16[1024,1792]{1,0:T(8,128)(2,1)S(1)} %get-tuple-element.121.refs_2_, ...), custom_call_target="tpu_custom_call" | custom-call | bytes 1 | tf_op jit(solution)/shard_map/pallas_call | solution.py:39
  56.0 1.2 %collective-permute-done.22.refs_4_ = f32[8,128]{1,0:T(8,128)S(1)} collective-permute-done((f32[8,128]{1,0:T(8,128)S(1)}, f32[8,128]{1,0:T(8,128)S(1)}, u32[]{:S(2)}, u32[]{:S(2)}) %collective-permute-start.22) | collective-permute-done | bytes 4128 | tf_op jit(solution)/shard_map/ppermute | solution.py:148
  57.2 3.3 %shard_map.83 = (bf16[32,1792]{1,0:T(8,128)(2,1)S(1)}, bf16[32,1792]{1,0:T(8,128)(2,1)S(1)}, bf16[896,2048]{1,0:T(8,128)(2,1)S(1)}, f32[8,128]{1,0:T(8,128)S(1)}) custom-call(bf16[64,2048]{1,0:T(8,128)(2,1)S(1)} %get-tuple-element.140.refs_0_, bf16[1024,1792]{1,0:T(8,128)(2,1)S(1)} %get-tuple-element.119.refs_1_, ...), custom_call_target="tpu_custom_call" | custom-call | bytes 1 | tf_op jit(solution)/shard_map/pallas_call | solution.py:39
  60.5 1.4 %shard_map.84 = (f32[64,1792]{1,0:T(8,128)S(1)}, f32[8,128]{1,0:T(8,128)S(1)}) custom-call(bf16[64,2048]{1,0:T(8,128)(2,1)S(1)} %get-tuple-element.140.refs_0_, bf16[1024,1792]{1,0:T(8,128)(2,1)S(1)} %get-tuple-element.129.refs_1_, bf16[1024,1792]{1,0:T(8,128)(2,1)S(1)} %get-tuple-element.131.refs_2_, f32[8,128]{1,0:T(8,128)S(1)} %get-tuple-element.147.refs_3_), custom_call_target="tpu_custom_call" | custom-call | bytes 1 | tf_op jit(solution)/shard_map/pallas_call | solution.py:39
  63.8 1.4 %shard_map.86 = (f32[64,2048]{1,0:T(8,128)S(1)}, f32[8,128]{1,0:T(8,128)S(1)}) custom-call(bf16[64,896]{1,0:T(8,128)(2,1)S(1)} %get-tuple-element.149.refs_0_, bf16[64,896]{1,0:T(8,128)(2,1)S(1)} %collective-permute-done.27.refs_1_, bf16[896,2048]{1,0:T(8,128)(2,1)S(1)} %get-tuple-element.154.refs_2_, bf16[896,2048]{1,0:T(8,128)(2,1)S(1)} %get-tuple-element.155.refs_3_, ...), custom_call_target="tpu_custom_call" | custom-call | bytes 1 | tf_op jit(solution)/shard_map/pallas_call | solution.py:39
  65.4 2.8 %collective-permute-done.23.refs_0_ = bf16[64,896]{1,0:T(8,128)(2,1)S(1)} collective-permute-done((bf16[64,896]{1,0:T(8,128)(2,1)S(1)}, bf16[64,896]{1,0:T(8,128)(2,1)S(1)}, u32[]{:S(2)}, u32[]{:S(2)}) %collective-permute-start.23) | collective-permute-done | bytes 114720 | tf_op jit(solution)/shard_map/ppermute | solution.py:325
  69.7 1.6 %shard_map.89 = (f32[16,2048]{1,0:T(8,128)S(1)}, bf16[16,2048]{1,0:T(8,128)(2,1)S(1)}, bf16[16,2048]{1,0:T(8,128)(2,1)S(1)}, bf16[16,2048]{1,0:T(8,128)(2,1)S(1)}, f32[8,128]{1,0:T(8,128)S(1)}) custom-call(bf16[64,896]{1,0:T(8,128)(2,1)S(1)} %collective-permute-done.23.refs_0_, bf16[64,896]{1,0:T(8,128)(2,1)S(1)} %collective-permute-done.28.refs_1_, ...), custom_call_target="tpu_custom_call" | custom-call | bytes 1 | tf_op jit(solution)/shard_map/pallas_call | solution.py:39
  72.6 1.4 %shard_map.90 = (f32[64,2048]{1,0:T(8,128)S(1)}, f32[8,128]{1,0:T(8,128)S(1)}) custom-call(bf16[64,896]{1,0:T(8,128)(2,1)S(1)} %get-tuple-element.168.refs_0_, bf16[64,896]{1,0:T(8,128)(2,1)S(1)} %collective-permute-done.33.refs_1_, bf16[896,2048]{1,0:T(8,128)(2,1)S(1)} %get-tuple-element.154.refs_2_, bf16[896,2048]{1,0:T(8,128)(2,1)S(1)} %get-tuple-element.155.refs_3_, ...), custom_call_target="tpu_custom_call" | custom-call | bytes 1 | tf_op jit(solution)/shard_map/pallas_call | solution.py:39
  74.3 3.7 %collective-permute-start.29 = (bf16[16,2048]{1,0:T(8,128)(2,1)S(1)}, bf16[16,2048]{1,0:T(8,128)(2,1)S(1)}, u32[]{:S(2)}, u32[]{:S(2)}) collective-permute-start(bf16[16,2048]{1,0:T(8,128)(2,1)S(1)} %get-tuple-element.165), channel_id=1, source_target_pairs={{0,3},{1,2},{2,1},{3,0},{4,7},{5,6},{6,5},{7,4},{8,11},{9,10},{10,... | collective-permute-start | bytes 196616 | tf_op jit(solution)/shard_map/ppermute | solution.py:362
  78.6 1.4 %shard_map.92 = (f32[16,2048]{1,0:T(8,128)S(1)}, bf16[16,2048]{1,0:T(8,128)(2,1)S(1)}, bf16[16,2048]{1,0:T(8,128)(2,1)S(1)}, bf16[16,2048]{1,0:T(8,128)(2,1)S(1)}, f32[8,128]{1,0:T(8,128)S(1)}) custom-call(bf16[64,896]{1,0:T(8,128)(2,1)S(1)} %collective-permute-done.32.refs_0_, bf16[64,896]{1,0:T(8,128)(2,1)S(1)} %collective-permute-done.35.refs_1_, ...), custom_call_target="tpu_custom_call" | custom-call | bytes 1 | tf_op jit(solution)/shard_map/pallas_call | solution.py:39
  80.1 3.7 %collective-permute-start.36 = (bf16[16,2048]{1,0:T(8,128)(2,1)S(1)}, bf16[16,2048]{1,0:T(8,128)(2,1)S(1)}, u32[]{:S(2)}, u32[]{:S(2)}) collective-permute-start(bf16[16,2048]{1,0:T(8,128)(2,1)S(1)} %get-tuple-element.175), channel_id=1, source_target_pairs={{0,3},{1,2},{2,1},{3,0},{4,7},{5,6},{6,5},{7,4},{8,11},{9,10},{10,... | collective-permute-start | bytes 196616 | tf_op jit(solution)/shard_map/ppermute | solution.py:362
  84.6 2.3 %collective-permute-done.36.refs_5_ = bf16[16,2048]{1,0:T(8,128)(2,1)S(1)} collective-permute-done((bf16[16,2048]{1,0:T(8,128)(2,1)S(1)}, bf16[16,2048]{1,0:T(8,128)(2,1)S(1)}, u32[]{:S(2)}, u32[]{:S(2)}) %collective-permute-start.36) | collective-permute-done | bytes 65568 | tf_op jit(solution)/shard_map/ppermute | solution.py:362
  86.9 2.8 %collective-permute-done.37.refs_6_ = bf16[16,2048]{1,0:T(8,128)(2,1)S(1)} collective-permute-done((bf16[16,2048]{1,0:T(8,128)(2,1)S(1)}, bf16[16,2048]{1,0:T(8,128)(2,1)S(1)}, u32[]{:S(2)}, u32[]{:S(2)}) %collective-permute-start.37) | collective-permute-done | bytes 65568 | tf_op jit(solution)/shard_map/ppermute | solution.py:362
  91.9 2.1 %collective-permute-done.40.refs_2_ = bf16[2,4,2048]{2,1,0:T(4,128)(2,1)S(1)} collective-permute-done((bf16[2,4,2048]{2,1,0:T(4,128)(2,1)S(1)}, bf16[2,4,2048]{2,1,0:T(4,128)(2,1)S(1)}, u32[]{:S(2)}, u32[]{:S(2)}) %collective-permute-start.40) | collective-permute-done | bytes 32800 | tf_op jit(solution)/shard_map/ppermute | solution.py:375
  (89 shorter events, 19.9 us)
Async XLA Ops:
  1.8 6.5 %collective-permute-start = (bf16[2,8,2048]{2,1,0:T(8,128)(2,1)S(1)}, bf16[2,8,2048]{2,1,0:T(8,128)(2,1)S(1)}, u32[]{:S(2)}, u32[]{:S(2)}) collective-permute-start(bf16[2,8,2048]{2,1,0:T(8,128)(2,1)S(1)} %get-tuple-element.96), channel_id=1, source_target_pairs={{0,4},{4,0},{8,12},{12,8},{1,5},{5,1},{9,13},{13,9},{2,6},{6,2},{1... | collective-permute-start | bytes 196616 | tf_op jit(solution)/shard_map/ppermute | solution.py:288
  2.4 5.7 %collective-permute-start.1 = (bf16[8,2048]{1,0:T(8,128)(2,1)S(1)}, bf16[8,2048]{1,0:T(8,128)(2,1)S(1)}, u32[]{:S(2)}, u32[]{:S(2)}) collective-permute-start(bf16[8,2048]{1,0:T(8,128)(2,1)S(1)} %get-tuple-element.97), channel_id=1, source_target_pairs={{0,8},{4,12},{8,0},{12,4},{1,9},{5,13},{9,1},{13,5},{2,10},{6,14},... | collective-permute-start | bytes 98312 | tf_op jit(solution)/shard_map/ppermute | solution.py:287
  4.9 3.3 %collective-permute-start.2 = (bf16[8,2048]{1,0:T(8,128)(2,1)S(1)}, bf16[8,2048]{1,0:T(8,128)(2,1)S(1)}, u32[]{:S(2)}, u32[]{:S(2)}) collective-permute-start(bf16[8,2048]{1,0:T(8,128)(2,1)S(1)} %get-tuple-element.98), channel_id=1, source_target_pairs={{0,12},{4,8},{8,4},{12,0},{1,13},{5,9},{9,5},{13,1},{2,14},{6,10},... | collective-permute-start | bytes 98312 | tf_op jit(solution)/shard_map/ppermute | solution.py:287
  8.3 12.3 %collective-permute-start.4 = (bf16[32,2048]{1,0:T(8,128)(2,1)S(1)}, bf16[32,2048]{1,0:T(8,128)(2,1)S(1)}, u32[]{:S(2)}, u32[]{:S(2)}) collective-permute-start(bf16[32,2048]{1,0:T(8,128)(2,1)S(1)} %get-tuple-element.102.refs_0_), channel_id=1, source_target_pairs={{0,3},{1,2},{2,1},{3,0},{4,7},{5,6},{6,5},{7,4},{8,11},{9,10},{10,... | collective-permute-start | bytes 393224 | tf_op jit(solution)/shard_map/ppermute | solution.py:301
  12.0 3.9 %collective-permute-start.5 = (bf16[8,2048]{1,0:T(8,128)(2,1)S(1)}, bf16[8,2048]{1,0:T(8,128)(2,1)S(1)}, u32[]{:S(2)}, u32[]{:S(2)}) collective-permute-start(bf16[8,2048]{1,0:T(8,128)(2,1)S(1)} %get-tuple-element.104), channel_id=1, source_target_pairs={{0,8},{4,12},{8,0},{12,4},{1,9},{5,13},{9,1},{13,5},{2,10},{6,14},... | collective-permute-start | bytes 98312 | tf_op jit(solution)/shard_map/ppermute | solution.py:287
  13.5 3.7 %collective-permute-start.6 = (bf16[8,2048]{1,0:T(8,128)(2,1)S(1)}, bf16[8,2048]{1,0:T(8,128)(2,1)S(1)}, u32[]{:S(2)}, u32[]{:S(2)}) collective-permute-start(bf16[8,2048]{1,0:T(8,128)(2,1)S(1)} %get-tuple-element.105), channel_id=1, source_target_pairs={{0,12},{4,8},{8,4},{12,0},{1,13},{5,9},{9,5},{13,1},{2,14},{6,10},... | collective-permute-start | bytes 98312 | tf_op jit(solution)/shard_map/ppermute | solution.py:287
  17.1 9.8 %collective-permute-start.9 = (bf16[32,2048]{1,0:T(8,128)(2,1)S(1)}, bf16[32,2048]{1,0:T(8,128)(2,1)S(1)}, u32[]{:S(2)}, u32[]{:S(2)}) collective-permute-start(bf16[32,2048]{1,0:T(8,128)(2,1)S(1)} %get-tuple-element.113.refs_0_), channel_id=1, source_target_pairs={{0,3},{1,2},{2,1},{3,0},{4,7},{5,6},{6,5},{7,4},{8,11},{9,10},{10,... | collective-permute-start | bytes 393224 | tf_op jit(solution)/shard_map/ppermute | solution.py:301
  17.4 10.8 %collective-permute-start.3 = (bf16[32,2048]{1,0:T(8,128)(2,1)S(1)}, bf16[32,2048]{1,0:T(8,128)(2,1)S(1)}, u32[]{:S(2)}, u32[]{:S(2)}) collective-permute-start(bf16[32,2048]{1,0:T(8,128)(2,1)S(1)} %get-tuple-element.102.refs_0_), channel_id=1, source_target_pairs={{0,1},{1,0},{2,3},{3,2},{4,5},{5,4},{6,7},{7,6},{8,9},{9,8},{10,11... | collective-permute-start | bytes 393224 | tf_op jit(solution)/shard_map/ppermute | solution.py:302
  20.6 8.7 %collective-permute-start.8 = (bf16[32,2048]{1,0:T(8,128)(2,1)S(1)}, bf16[32,2048]{1,0:T(8,128)(2,1)S(1)}, u32[]{:S(2)}, u32[]{:S(2)}) collective-permute-start(bf16[32,2048]{1,0:T(8,128)(2,1)S(1)} %get-tuple-element.109), channel_id=1, source_target_pairs={{0,1},{1,0},{2,3},{3,2},{4,5},{5,4},{6,7},{7,6},{8,9},{9,8},{10,11... | collective-permute-start | bytes 393224 | tf_op jit(solution)/shard_map/ppermute | solution.py:306
  21.6 25.3 %collective-permute-start.18 = (bf16[32,2048]{1,0:T(8,128)(2,1)S(1)}, bf16[32,2048]{1,0:T(8,128)(2,1)S(1)}, u32[]{:S(2)}, u32[]{:S(2)}) collective-permute-start(bf16[32,2048]{1,0:T(8,128)(2,1)S(1)} %get-tuple-element.113.refs_0_), channel_id=1, source_target_pairs={{0,1},{1,0},{2,3},{3,2},{4,5},{5,4},{6,7},{7,6},{8,9},{9,8},{10,11... | collective-permute-start | bytes 393224 | tf_op jit(solution)/shard_map/ppermute | solution.py:302
  27.0 19.9 %collective-permute-start.19 = (bf16[32,2048]{1,0:T(8,128)(2,1)S(1)}, bf16[32,2048]{1,0:T(8,128)(2,1)S(1)}, u32[]{:S(2)}, u32[]{:S(2)}) collective-permute-start(bf16[32,2048]{1,0:T(8,128)(2,1)S(1)} %get-tuple-element.137), channel_id=1, source_target_pairs={{0,1},{1,0},{2,3},{3,2},{4,5},{5,4},{6,7},{7,6},{8,9},{9,8},{10,11... | collective-permute-start | bytes 393224 | tf_op jit(solution)/shard_map/ppermute | solution.py:306
  32.9 3.9 %collective-permute-start.12 = (bf16[32,1792]{1,0:T(8,128)(2,1)S(1)}, bf16[32,1792]{1,0:T(8,128)(2,1)S(1)}, u32[]{:S(2)}, u32[]{:S(2)}) collective-permute-start(bf16[32,1792]{1,0:T(8,128)(2,1)S(1)} %get-tuple-element.125), channel_id=1, source_target_pairs={{0,4},{4,0},{8,12},{12,8},{1,5},{5,1},{9,13},{13,9},{2,6},{6,2},{1... | collective-permute-start | bytes 344072 | tf_op jit(solution)/shard_map/ppermute | solution.py:340
  33.1 3.7 %collective-permute-start.13 = (bf16[32,1792]{1,0:T(8,128)(2,1)S(1)}, bf16[32,1792]{1,0:T(8,128)(2,1)S(1)}, u32[]{:S(2)}, u32[]{:S(2)}) collective-permute-start(bf16[32,1792]{1,0:T(8,128)(2,1)S(1)} %get-tuple-element.126), channel_id=1, source_target_pairs={{0,4},{4,0},{8,12},{12,8},{1,5},{5,1},{9,13},{13,9},{2,6},{6,2},{1... | collective-permute-start | bytes 344072 | tf_op jit(solution)/shard_map/ppermute | solution.py:340
  37.1 24.8 %collective-permute-start.15 = (bf16[64,1792]{1,0:T(8,128)(2,1)S(1)}, bf16[64,1792]{1,0:T(8,128)(2,1)S(1)}, u32[]{:S(2)}, u32[]{:S(2)}) collective-permute-start(bf16[64,1792]{1,0:T(8,128)(2,1)S(1)} %get-tuple-element.134), channel_id=1, source_target_pairs={{0,8},{4,12},{8,0},{12,4},{1,9},{5,13},{9,1},{13,5},{2,10},{6,14},... | collective-permute-start | bytes 688136 | tf_op jit(solution)/shard_map/ppermute | solution.py:343
  50.4 4.4 %collective-permute-start.20 = (bf16[32,1792]{1,0:T(8,128)(2,1)S(1)}, bf16[32,1792]{1,0:T(8,128)(2,1)S(1)}, u32[]{:S(2)}, u32[]{:S(2)}) collective-permute-start(bf16[32,1792]{1,0:T(8,128)(2,1)S(1)} %get-tuple-element.143), channel_id=1, source_target_pairs={{0,4},{4,0},{8,12},{12,8},{1,5},{5,1},{9,13},{13,9},{2,6},{6,2},{1... | collective-permute-start | bytes 344072 | tf_op jit(solution)/shard_map/ppermute | solution.py:340
  50.6 4.2 %collective-permute-start.21 = (bf16[32,1792]{1,0:T(8,128)(2,1)S(1)}, bf16[32,1792]{1,0:T(8,128)(2,1)S(1)}, u32[]{:S(2)}, u32[]{:S(2)}) collective-permute-start(bf16[32,1792]{1,0:T(8,128)(2,1)S(1)} %get-tuple-element.144), channel_id=1, source_target_pairs={{0,4},{4,0},{8,12},{12,8},{1,5},{5,1},{9,13},{13,9},{2,6},{6,2},{1... | collective-permute-start | bytes 344072 | tf_op jit(solution)/shard_map/ppermute | solution.py:340
  51.0 10.9 %collective-permute-start.16 = (bf16[32,1792]{1,0:T(8,128)(2,1)S(1)}, bf16[32,1792]{1,0:T(8,128)(2,1)S(1)}, u32[]{:S(2)}, u32[]{:S(2)}) collective-permute-start(bf16[32,1792]{1,0:T(8,128)(2,1)S(1)} %get-tuple-element.135), channel_id=1, source_target_pairs={{0,4},{4,0},{8,12},{12,8},{1,5},{5,1},{9,13},{13,9},{2,6},{6,2},{1... | collective-permute-start | bytes 344072 | tf_op jit(solution)/shard_map/ppermute | solution.py:345
  51.1 10.7 %collective-permute-start.17 = (bf16[32,1792]{1,0:T(8,128)(2,1)S(1)}, bf16[32,1792]{1,0:T(8,128)(2,1)S(1)}, u32[]{:S(2)}, u32[]{:S(2)}) collective-permute-start(bf16[32,1792]{1,0:T(8,128)(2,1)S(1)} %get-tuple-element.136), channel_id=1, source_target_pairs={{0,4},{4,0},{8,12},{12,8},{1,5},{5,1},{9,13},{13,9},{2,6},{6,2},{1... | collective-permute-start | bytes 344072 | tf_op jit(solution)/shard_map/ppermute | solution.py:345
  54.9 10.3 %collective-permute-start.24 = (bf16[64,1792]{1,0:T(8,128)(2,1)S(1)}, bf16[64,1792]{1,0:T(8,128)(2,1)S(1)}, u32[]{:S(2)}, u32[]{:S(2)}) collective-permute-start(bf16[64,1792]{1,0:T(8,128)(2,1)S(1)} %get-tuple-element.151), channel_id=1, source_target_pairs={{0,8},{4,12},{8,0},{12,4},{1,9},{5,13},{9,1},{13,5},{2,10},{6,14},... | collective-permute-start | bytes 688136 | tf_op jit(solution)/shard_map/ppermute | solution.py:343
  62.3 2.9 %collective-permute-start.25 = (bf16[32,1792]{1,0:T(8,128)(2,1)S(1)}, bf16[32,1792]{1,0:T(8,128)(2,1)S(1)}, u32[]{:S(2)}, u32[]{:S(2)}) collective-permute-start(bf16[32,1792]{1,0:T(8,128)(2,1)S(1)} %get-tuple-element.152), channel_id=1, source_target_pairs={{0,4},{4,0},{8,12},{12,8},{1,5},{5,1},{9,13},{13,9},{2,6},{6,2},{1... | collective-permute-start | bytes 344072 | tf_op jit(solution)/shard_map/ppermute | solution.py:345
  62.8 5.4 %collective-permute-start.23 = (bf16[64,896]{1,0:T(8,128)(2,1)S(1)}, bf16[64,896]{1,0:T(8,128)(2,1)S(1)}, u32[]{:S(2)}, u32[]{:S(2)}) collective-permute-start(bf16[64,896]{1,0:T(8,128)(2,1)S(1)} %get-tuple-element.149.refs_0_), channel_id=1, source_target_pairs={{0,8},{4,12},{8,0},{12,4},{1,9},{5,13},{9,1},{13,5},{2,10},{6,14},... | collective-permute-start | bytes 344072 | tf_op jit(solution)/shard_map/ppermute | solution.py:325
  68.3 3.2 %collective-permute-start.33 = (bf16[64,896]{1,0:T(8,128)(2,1)S(1)}, bf16[64,896]{1,0:T(8,128)(2,1)S(1)}, u32[]{:S(2)}, u32[]{:S(2)}) collective-permute-start(bf16[64,896]{1,0:T(8,128)(2,1)S(1)} %get-tuple-element.168.refs_0_), channel_id=1, source_target_pairs={{0,4},{4,0},{8,12},{12,8},{1,5},{5,1},{9,13},{13,9},{2,6},{6,2},{1... | collective-permute-start | bytes 344072 | tf_op jit(solution)/shard_map/ppermute | solution.py:326
  68.8 5.2 %collective-permute-start.32 = (bf16[64,896]{1,0:T(8,128)(2,1)S(1)}, bf16[64,896]{1,0:T(8,128)(2,1)S(1)}, u32[]{:S(2)}, u32[]{:S(2)}) collective-permute-start(bf16[64,896]{1,0:T(8,128)(2,1)S(1)} %get-tuple-element.168.refs_0_), channel_id=1, source_target_pairs={{0,8},{4,12},{8,0},{12,4},{1,9},{5,13},{9,1},{13,5},{2,10},{6,14},... | collective-permute-start | bytes 344072 | tf_op jit(solution)/shard_map/ppermute | solution.py:325
  74.0 4.6 %collective-permute-start.35 = (bf16[64,896]{1,0:T(8,128)(2,1)S(1)}, bf16[64,896]{1,0:T(8,128)(2,1)S(1)}, u32[]{:S(2)}, u32[]{:S(2)}) collective-permute-start(bf16[64,896]{1,0:T(8,128)(2,1)S(1)} %get-tuple-element.171), channel_id=1, source_target_pairs={{0,4},{4,0},{8,12},{12,8},{1,5},{5,1},{9,13},{13,9},{2,6},{6,2},{1... | collective-permute-start | bytes 344072 | tf_op jit(solution)/shard_map/ppermute | solution.py:373
  74.3 9.6 %collective-permute-start.29 = (bf16[16,2048]{1,0:T(8,128)(2,1)S(1)}, bf16[16,2048]{1,0:T(8,128)(2,1)S(1)}, u32[]{:S(2)}, u32[]{:S(2)}) collective-permute-start(bf16[16,2048]{1,0:T(8,128)(2,1)S(1)} %get-tuple-element.165), channel_id=1, source_target_pairs={{0,3},{1,2},{2,1},{3,0},{4,7},{5,6},{6,5},{7,4},{8,11},{9,10},{10,... | collective-permute-start | bytes 196616 | tf_op jit(solution)/shard_map/ppermute | solution.py:362
  77.9 6.7 %collective-permute-start.30 = (bf16[16,2048]{1,0:T(8,128)(2,1)S(1)}, bf16[16,2048]{1,0:T(8,128)(2,1)S(1)}, u32[]{:S(2)}, u32[]{:S(2)}) collective-permute-start(bf16[16,2048]{1,0:T(8,128)(2,1)S(1)} %get-tuple-element.166), channel_id=1, source_target_pairs={{0,2},{1,3},{2,0},{3,1},{4,6},{5,7},{6,4},{7,5},{8,10},{9,11},{10,... | collective-permute-start | bytes 196616 | tf_op jit(solution)/shard_map/ppermute | solution.py:362
  77.9 6.7 %collective-permute-start.31 = (bf16[16,2048]{1,0:T(8,128)(2,1)S(1)}, bf16[16,2048]{1,0:T(8,128)(2,1)S(1)}, u32[]{:S(2)}, u32[]{:S(2)}) collective-permute-start(bf16[16,2048]{1,0:T(8,128)(2,1)S(1)} %get-tuple-element.167), channel_id=1, source_target_pairs={{0,1},{1,0},{2,3},{3,2},{4,5},{5,4},{6,7},{7,6},{8,9},{9,8},{10,11... | collective-permute-start | bytes 196616 | tf_op jit(solution)/shard_map/ppermute | solution.py:362
  80.1 6.8 %collective-permute-start.36 = (bf16[16,2048]{1,0:T(8,128)(2,1)S(1)}, bf16[16,2048]{1,0:T(8,128)(2,1)S(1)}, u32[]{:S(2)}, u32[]{:S(2)}) collective-permute-start(bf16[16,2048]{1,0:T(8,128)(2,1)S(1)} %get-tuple-element.175), channel_id=1, source_target_pairs={{0,3},{1,2},{2,1},{3,0},{4,7},{5,6},{6,5},{7,4},{8,11},{9,10},{10,... | collective-permute-start | bytes 196616 | tf_op jit(solution)/shard_map/ppermute | solution.py:362
  83.8 5.9 %collective-permute-start.37 = (bf16[16,2048]{1,0:T(8,128)(2,1)S(1)}, bf16[16,2048]{1,0:T(8,128)(2,1)S(1)}, u32[]{:S(2)}, u32[]{:S(2)}) collective-permute-start(bf16[16,2048]{1,0:T(8,128)(2,1)S(1)} %get-tuple-element.176), channel_id=1, source_target_pairs={{0,2},{1,3},{2,0},{3,1},{4,6},{5,7},{6,4},{7,5},{8,10},{9,11},{10,... | collective-permute-start | bytes 196616 | tf_op jit(solution)/shard_map/ppermute | solution.py:362
  83.8 5.9 %collective-permute-start.38 = (bf16[16,2048]{1,0:T(8,128)(2,1)S(1)}, bf16[16,2048]{1,0:T(8,128)(2,1)S(1)}, u32[]{:S(2)}, u32[]{:S(2)}) collective-permute-start(bf16[16,2048]{1,0:T(8,128)(2,1)S(1)} %get-tuple-element.177), channel_id=1, source_target_pairs={{0,1},{1,0},{2,3},{3,2},{4,5},{5,4},{6,7},{7,6},{8,9},{9,8},{10,11... | collective-permute-start | bytes 196616 | tf_op jit(solution)/shard_map/ppermute | solution.py:362
  90.0 4.0 %collective-permute-start.40 = (bf16[2,4,2048]{2,1,0:T(4,128)(2,1)S(1)}, bf16[2,4,2048]{2,1,0:T(4,128)(2,1)S(1)}, u32[]{:S(2)}, u32[]{:S(2)}) collective-permute-start(bf16[2,4,2048]{2,1,0:T(4,128)(2,1)S(1)} %get-tuple-element.181), channel_id=1, source_target_pairs={{0,8},{4,12},{8,0},{12,4},{1,9},{5,13},{9,1},{13,5},{2,10},{6,14},... | collective-permute-start | bytes 98312 | tf_op jit(solution)/shard_map/ppermute | solution.py:375
  91.1 3.3 %collective-permute-start.41 = (bf16[2,4,2048]{2,1,0:T(4,128)(2,1)S(1)}, bf16[2,4,2048]{2,1,0:T(4,128)(2,1)S(1)}, u32[]{:S(2)}, u32[]{:S(2)}) collective-permute-start(bf16[2,4,2048]{2,1,0:T(4,128)(2,1)S(1)} %get-tuple-element.182), channel_id=1, source_target_pairs={{0,12},{4,8},{8,4},{12,0},{1,13},{5,9},{9,5},{13,1},{2,14},{6,10},... | collective-permute-start | bytes 98312 | tf_op jit(solution)/shard_map/ppermute | solution.py:375
  (13 other events, 17.3 us)

commit v4 on v0

--- a/solution.py
+++ b/solution.py
@@ -1,13 +1,360 @@
+import functools
+
 import jax
 import jax.numpy as jnp
 from jax import lax
+from jax.experimental import pallas as pl
+from jax.experimental.pallas import tpu as pltpu
 from jax.sharding import PartitionSpec as P
 
 STEPS = 2
 MEAN = 4
 
-
 epsilon = 1e-05
+
+BF = jnp.bfloat16
+F32 = jnp.float32
+MIB = 2**20
+PIECES = 2
+X1 = ((0, 1), (1, 0), (2, 3), (3, 2))
+X2 = ((0, 2), (1, 3), (2, 0), (3, 1))
+X3 = ((0, 3), (1, 2), (2, 1), (3, 0))
+
+
+def place():
+    row = lax.axis_index("row")
+    return row // 2, lax.rem(row, 2), lax.axis_index("col")
+
+
+def run(body, outs, operands, token, weights=(), scratch=(), cost=1, spec=None):
+    count, held = len(operands), len(weights)
+    skip = count + held + (token is not None)
+    vmem = pl.BlockSpec(memory_space=pltpu.VMEM)
+    outs = tuple(outs) + (like((8, 128), F32),)
+
+    def wrapped(*refs):
+        results = refs[skip:]
+        body(refs[:count], refs[count : count + held], results[: len(outs) - 1], results[len(outs) :])
+        results[len(outs) - 1][...] = jnp.zeros((8, 128), F32)
+
+    return pl.pallas_call(
+        wrapped,
+        out_shape=outs,
+        in_specs=[spec or vmem] * count
+        + [pl.BlockSpec(memory_space=pltpu.HBM)] * held
+        + [pl.BlockSpec(memory_space=pl.ANY)] * (token is not None),
+        out_specs=(vmem,) * len(outs),
+        scratch_shapes=scratch,
+        compiler_params=pltpu.CompilerParams(vmem_limit_bytes=8 * MIB),
+        cost_estimate=pl.CostEstimate(flops=0, bytes_accessed=cost, transcendentals=0),
+    )(*operands, *(pltpu.with_memory_space_constraint(w, pltpu.HBM) for w in weights), *(() if token is None else (token,)))
+
+
+def like(shape, dtype=BF):
+    return jax.ShapeDtypeStruct(shape, dtype)
+
+
+def norm_body(ins, _, outs, __):
+    (rows_ref,) = ins
+    y, c, _ = place()
+    width = outs[0].shape[2]
+    for step in range(rows_ref.shape[0]):
+        total = jnp.sum(jnp.square(rows_ref[step].astype(F32)), axis=-1, keepdims=True)
+        scale = lax.rsqrt(total / rows_ref.shape[2] + epsilon)
+        for out, (dy, dc) in zip(outs, ((1, 0), (1, 1), (0, 1), (0, 0))):
+            block = lax.bitwise_xor(y, dy) * 2 + lax.bitwise_xor(c, dc)
+            at = pl.ds(pl.multiple_of(block * width, width), width)
+            out[step] = (rows_ref[step, :, at].astype(F32) * scale).astype(BF)
+
+
+def normed_blocks(sender_rows):
+    steps, slots, width = sender_rows.shape
+    return run(norm_body, (like((steps, slots, width // 4)),) * 4, (sender_rows,), None)
+
+
+def pick_body(ins, _, outs, __):
+    counts_ref, assign_ref = ins
+    (pick_ref,) = outs
+    y, c, z = place()
+    rows = pick_ref.shape[0] // 2
+    slots = assign_ref.shape[1]
+    arrivals = pick_ref.shape[1]
+    spread = (
+        lax.broadcasted_iota(jnp.int32, (slots // 8, slots), 1) // 8
+        == lax.broadcasted_iota(jnp.int32, (slots // 8, slots), 0)
+    ).astype(F32)
+    held = jnp.dot(counts_ref[...].astype(F32), spread, preferred_element_type=F32)
+    slot = lax.rem(lax.broadcasted_iota(jnp.int32, (1, slots), 1), 8).astype(F32)
+    at = lax.broadcasted_iota(jnp.int32, (rows, slots), 0)
+    target = (lax.rem(at, 16) // 4) * 16 + lax.bitwise_xor(at // 16, z) * 4 + lax.rem(at, 4)
+    p = lax.broadcasted_iota(jnp.int32, (slots, arrivals), 1)
+    bit = lambda shift: lax.rem(lax.shift_right_logical(p, shift), 2)
+    row = lax.bitwise_xor(bit(5), y) * 2 + lax.bitwise_xor(bit(4), c)
+    sender = row * 4 + lax.bitwise_xor(lax.shift_right_logical(p, 6), z)
+    source = sender * 8 + lax.rem(p, 8)
+    entry = lax.broadcasted_iota(jnp.int32, (slots, arrivals), 0)
+    for step in range(2):
+        live = slot < held[step : step + 1]
+        chosen = jnp.where(live, assign_ref[step : step + 1, :], -1)
+        placed = (chosen == target).astype(F32).astype(BF)
+        moved = ((entry == source) & (bit(3) == step)).astype(F32).astype(BF)
+        pick_ref[step * rows : (step + 1) * rows, :] = jnp.dot(
+            placed, moved, preferred_element_type=F32
+        ).astype(BF)
+
+
+def quarter_body(dy, dc, half, ins, weights, outs, scratch):
+    y, c, _ = place()
+    (out_ref,) = outs
+    height, width = out_ref.shape[0], out_ref.shape[1] // 2
+    start = (lax.bitwise_xor(c, dc) * 2 + lax.bitwise_xor(y, dy)) * width
+    at = pl.ds(pl.multiple_of(start, 128), width)
+    copies = [
+        pltpu.make_async_copy(
+            w.at[pl.ds(half * height, height), at],
+            out_ref.at[:, pl.ds(i * width, width)],
+            scratch[0].at[i],
+        )
+        for i, w in enumerate(weights)
+    ]
+    for copy in copies:
+        copy.start()
+    for copy in copies:
+        copy.wait()
+
+
+def fetch_quarter(gate_w, up_w, dy, dc, half, parts, token):
+    shape = pltpu.VMEM((gate_w.shape[0] // parts, gate_w.shape[1] // 2), BF)
+    return run(
+        functools.partial(quarter_body, dy, dc, half),
+        (shape,),
+        (),
+        token,
+        (gate_w, up_w),
+        (pltpu.SemaphoreType.DMA((2,)),),
+    )
+
+
+def down_rows_body(dy, ins, _, outs, scratch):
+    y, c, _ = place()
+    (out_ref,) = outs
+    height = out_ref.shape[0] // 2
+    copies = []
+    for dc in range(2):
+        start = (lax.bitwise_xor(c, dc) * 2 + lax.bitwise_xor(y, dy)) * height
+        copies.append(
+            pltpu.make_async_copy(
+                ins[0].at[pl.ds(pl.multiple_of(start, 16), height), :],
+                out_ref.at[pl.ds(dc * height, height), :],
+                scratch[0].at[dc],
+            )
+        )
+    for copy in copies:
+        copy.start()
+    for copy in copies:
+        copy.wait()
+
+
+def meet(token):
+    return lax.ppermute(token, "row", X1)
+
+
+def stack_body(ins, _, outs, __):
+    for i, piece in enumerate(ins):
+        joined = jnp.concatenate([piece[step].astype(F32) for step in range(2)], axis=0)
+        outs[0][i * 16 : (i + 1) * 16, :] = joined.astype(BF)
+
+
+def after_body(ins, _, outs, __):
+    outs[0][...] = ins[0][...]
+
+
+def halves_dot(x_ref, w_refs):
+    total = 0.0
+    height = w_refs[0].shape[0]
+    for i, w_ref in enumerate(w_refs):
+        at = slice(i * height, (i + 1) * height)
+        total = total + jnp.dot(x_ref[:, at], w_ref[...], preferred_element_type=F32)
+    return total
+
+
+def store_rows(outs, value):
+    rows = outs[0].shape[0]
+    for i, out in enumerate(outs):
+        out[...] = value[i * rows : (i + 1) * rows].astype(out.dtype)
+
+
+def load_rows(refs):
+    return jnp.concatenate([ref[...].astype(F32) for ref in refs], axis=0)
+
+
+def first_body(ins, _, outs, scratch):
+    pieces, pick_ref, w_refs = ins[:8], ins[8], ins[9:]
+    batch_ref, pieces_out = outs[0], outs[1:]
+    slots = scratch[0]
+    height = pieces[0].shape[0]
+    for i, piece in enumerate(pieces):
+        slots[i * height : (i + 1) * height, :] = piece[...]
+    batch_ref[...] = jnp.dot(pick_ref[...], slots[...], preferred_element_type=F32).astype(BF)
+    store_rows(pieces_out, halves_dot(batch_ref, w_refs))
+
+
+def dot_body(ins, _, outs, __):
+    store_rows(outs, halves_dot(ins[0], ins[1:]))
+
+
+def far_body(ins, _, outs, __):
+    store_rows(outs, ins[0][...] + load_rows(ins[1:]))
+
+
+def hidden_body(step, ins, _, outs, __):
+    rows, width = outs[0].shape
+    total = ins[0][step * rows : (step + 1) * rows, :] + ins[1][...].astype(F32) + load_rows(ins[2:])
+    gate, up = total[:, :width], total[:, width:]
+    outs[0][...] = (gate / (1.0 + jnp.exp(-gate)) * up).astype(BF)
+
+
+def down_part_body(ins, _, outs, __):
+    own_ref, core_ref, w_ref = ins
+    height = w_ref.shape[0] // 2
+    total = jnp.dot(own_ref[...], w_ref[:height, :], preferred_element_type=F32)
+    outs[0][...] = total + jnp.dot(core_ref[...], w_ref[height:, :], preferred_element_type=F32)
+
+
+def down_rest_body(ins, _, outs, __):
+    y_ref, yd_ref, w_ref, part_ref = ins
+    rows = outs[0].shape[0]
+    height = w_ref.shape[0] // 2
+    total = part_ref[...] + jnp.dot(y_ref[...], w_ref[:height, :], preferred_element_type=F32)
+    total = total + jnp.dot(yd_ref[...], w_ref[height:, :], preferred_element_type=F32)
+    for i, out in enumerate(outs):
+        out[...] = total[i * rows : (i + 1) * rows].astype(out.dtype)
+
+
+def owner_body(ins, _, outs, __):
+    y, c, _ = place()
+    at = lax.broadcasted_iota(jnp.int32, (16, 16), 0)
+    source = lax.bitwise_xor(at, (y * 2 + c) * 4)
+    turn = (lax.broadcasted_iota(jnp.int32, (16, 16), 1) == source).astype(F32).astype(BF)
+    for step in range(2):
+        total = ins[step * 4][...]
+        for got in ins[step * 4 + 1 : step * 4 + 4]:
+            total = total + got[...].astype(F32)
+        turned = jnp.dot(turn, total.astype(BF), preferred_element_type=F32)
+        for i, out in enumerate(outs):
+            out[step] = turned[i * 4 : (i + 1) * 4].astype(BF)
+
+
+def output_body(ins, _, outs, __):
+    y, c, _ = place()
+    width = ins[0].shape[2]
+    for dy, dc, block in ((0, 0, ins[0]), (0, 1, ins[1]), (1, 0, ins[2]), (1, 1, ins[3])):
+        source = lax.bitwise_xor(y, dy) * 2 + lax.bitwise_xor(c, dc)
+        outs[0][:, :, pl.ds(pl.multiple_of(source * width, width), width)] = block[...]
+
+
+def near_plan(sender_rows, counts, assign, gate_w, up_w, down_w):
+    steps, slots, width = sender_rows.shape
+    width //= 4
+    units = gate_w.shape[1] // 4
+    rows = MEAN * counts.shape[1]
+    part = rows // 4
+
+    def down_rows(dy, token):
+        shape = pltpu.VMEM((down_w.shape[0] // 2, down_w.shape[1]), BF)
+        scratch = (pltpu.SemaphoreType.DMA((2,)),)
+        spec = pl.BlockSpec(memory_space=pl.ANY)
+        return run(functools.partial(down_rows_body, dy), (shape,), (down_w,), token, (), scratch, spec=spec)
+
+    y, yd, core, own, token = normed_blocks(sender_rows)
+    y, yd = lax.ppermute(y, "row", X2), lax.ppermute(yd, "row", X3)
+    core = lax.ppermute(core, "row", X1)
+    pick, token = run(pick_body, (like((steps * rows, steps * assign.shape[1])),), (counts, assign), token)
+    quarters = {}
+
+    def bring(dy, dc, half, parts, token):
+        w, token = fetch_quarter(gate_w, up_w, dy, dc, half, parts, token)
+        quarters.setdefault((dy, dc), []).append(w)
+        return token
+
+    block = like((4 * slots, width))
+    near_block, token = run(stack_body, (block,), (own, core), token)
+    near_sent = [lax.ppermute(near_block, "col", X3), lax.ppermute(near_block, "col", X1)]
+    token = meet(token)
+    token = bring(1, 1, 0, 2, token)
+    far_block, token = run(stack_body, (block,), (y, yd), token)
+    far_sent = [lax.ppermute(far_block, "col", X3), lax.ppermute(far_block, "col", X1)]
+    token = meet(token)
+    token = bring(1, 1, 1, 2, token)
+    passed, token = run(after_body, (block,), (near_sent[0],), token)
+    near_sent.append(lax.ppermute(passed, "col", X1))
+    token = meet(token)
+    token = bring(1, 0, 0, 2, token)
+    passed, token = run(after_body, (block,), (far_sent[0],), token)
+    far_sent.append(lax.ppermute(passed, "col", X1))
+    token = meet(token)
+    token = bring(1, 0, 1, 2, token)
+    token = bring(0, 1, 0, 1, token)
+    pieces = []
+    for dz in range(4):
+        for own_block, sent in ((near_block, near_sent), (far_block, far_sent)):
+            pieces.append((own_block, sent[1], sent[2], sent[0])[dz])
+
+    bits = (like((steps * rows // PIECES, 2 * units)),) * PIECES
+    wide = like((steps * rows, 2 * units), F32)
+    batch, *out, token = run(
+        first_body,
+        (like((steps * rows, width)),) + bits,
+        tuple(pieces) + (pick, *quarters[1, 1]),
+        token,
+        (),
+        (pltpu.VMEM((32 * slots, width), BF),),
+    )
+    cores = tuple(lax.ppermute(o, "row", X1) for o in out)
+    own_far, token = run(dot_body, (wide,), (batch, *quarters[1, 0]), token)
+    *sends, token = run(far_body, (like((rows, 2 * units)),) * steps, (own_far,) + cores, token)
+    gots = [lax.ppermute(send, "row", X2) for send in sends]
+    token = meet(token)
+    *out, token = run(dot_body, bits, (batch, *quarters[0, 1]), token)
+    cores = tuple(lax.ppermute(o, "row", X1) for o in out)
+    token = bring(0, 0, 0, 1, token)
+    own_near, token = run(dot_body, (wide,), (batch, *quarters[0, 0]), token)
+    down_near, token = down_rows(0, token)
+    hidden, sums = [], []
+
+    def activate(step, token):
+        each = PIECES // steps
+        near = cores[step * each : (step + 1) * each]
+        operands = (own_near, gots[step]) + near
+        body = functools.partial(hidden_body, step)
+        result, token = run(body, (like((rows, units)),), operands, token)
+        y = lax.ppermute(result, "row", X2)
+        hidden.append((result, lax.ppermute(result, "row", X1), y))
+        return token
+
+    def down_part(step, token):
+        return run(down_part_body, (like((rows, width), F32),), hidden[step][:2] + (down_near,), token)
+
+    def down_rest(step, part_sum, token):
+        passed, token = run(after_body, (like((rows, units)),), (hidden[step][2],), token)
+        outs = (like((part, width), F32),) + (like((part, width)),) * 3
+        operands = (hidden[step][2], lax.ppermute(passed, "row", X1), down_far, part_sum)
+        keep, send1, send2, send3, token = run(down_rest_body, outs, operands, token)
+        got = [lax.ppermute(s, "col", x) for s, x in ((send3, X3), (send2, X2), (send1, X1))]
+        sums.extend([keep] + got)
+        return token
+
+    token = activate(0, token)
+    down_far, token = down_rows(1, token)
+    part0, token = down_part(0, token)
+    token = activate(1, token)
+    token = down_rest(0, part0, token)
+    part1, token = down_part(1, meet(token))
+    token = down_rest(1, part1, token)
+    own, core, y, yd, token = run(owner_body, (like((steps, MEAN, width)),) * 4, tuple(sums), token)
+    blocks = (own, lax.ppermute(core, "row", X1), lax.ppermute(y, "row", X2), lax.ppermute(yd, "row", X3))
+    result, _ = run(output_body, (like((steps, MEAN, 4 * width)),), blocks, token)
+    return result
 
 
 def layer_block(normed_block, counts_block, assign_block, paired, down_w, hidden_cols):
@@ -64,7 +411,7 @@
     return finished.reshape(step_count, MEAN, finished.shape[1])
 
 
-def per_device(sender_rows, counts, assign, gate_w, up_w, down_w):
+def any_plan(sender_rows, counts, assign, gate_w, up_w, down_w):
     values = sender_rows.astype(jnp.float32)
     normed = (
         values * lax.rsqrt(jnp.mean(values * values, axis=-1, keepdims=True) + epsilon)
@@ -88,8 +435,9 @@
 
 
 def solution(mesh):
+    near = mesh.shape["row"] == 4 and mesh.shape["col"] == 4
     return jax.shard_map(
-        per_device,
+        near_plan if near else any_plan,
         mesh=mesh,
         in_specs=(
             P(None, ("groups", "row", "col"), None),

time: 332 us -> 80.9 us (0.24)
  other arithmetic: 95.8 us -> 0.01 us
  local copies, waits for them, and re-layouts: 84.1 us -> 5.22 us
  blocking collectives: 53 us -> 0 us
  matrix products: 43.6 us -> 0 us
  Pallas kernels: 0 us -> 28.3 us
  starting transfers between devices: 11.2 us -> 31.2 us
  waiting for transfers between devices: 29.2 us -> 15.7 us
  between operations: 13.4 us -> 0.37 us
    unnamed x2 -> x1, other arithmetic: 90.5 us -> 0.01 us
    all_gather x4 -> x0, blocking collectives: 46.3 us -> none  [the longest x2 32.5 us: layer_block(): gathered = lax.all_gather(spread, 'col', axis=1, tiled=True)]
    dot_general x4 -> x0, matrix products: 43.6 us -> none  [the longest x2 26.3 us: layer_block(): jnp.dot(rows_here, paired, preferred_element_type=jnp.float32)]
    ppermute x0 -> x36, starting transfers between devices: none -> 31.2 us  [the longest x6 8.84 us: down_rest(): lax.ppermute(s, 'col', x)]
    reduce_scatter x4 -> x0, waiting for transfers between devices: 29.2 us -> none  [the longest x2 21 us: layer_block(): lax.psum_scatter(jnp.dot(rows_here, down_w, preferred_element_type=jnp.fl...]
    pallas_call x0 -> x29, Pallas kernels: none -> 28.3 us  [run(): pl.pallas_call(wrapped, out_shape=outs, in_specs=[spec or vmem] * count +...]
    unnamed x6 -> x14, local copies, waits for them, and re-layouts: 31.3 us -> 5.22 us
    all_to_all x8 -> x0, local copies, waits for them, and re-layouts: 18.4 us -> none  [the longest x6 16 us: layer_block(): lax.all_to_all(normed_block, 'row', split_axis=2, concat_axis=1, tiled=True)]
  transfers between devices with their start and end apart: 7 -> 36, of which waited for: 3 -> 11; matrix products, arithmetic and copies ran while one was open for 49% -> 0% of each run, Pallas kernels for 0% -> 32%
where the time goes in v4:
time: 80.9 us; the launch traced here: 80.7 us
  starting transfers between devices  31.2 us (39%)
  Pallas kernels  28.3 us (35%)
  waiting for transfers between devices  15.7 us (19%)
  local copies, waits for them, and re-layouts  5.22 us (6%)
    pallas_call x29, Pallas kernels, run(): pl.pallas_call(wrapped, out_shape=outs, in_specs=[spec or vmem] * count +...  28.3 us
    ppermute x6, starting transfers between devices, down_rest(): lax.ppermute(s, 'col', x)  8.84 us
    ppermute x6, waiting for transfers between devices, down_rest(): lax.ppermute(s, 'col', x)  5.71 us
    unnamed x14, local copies, waits for them, and re-layouts  5.22 us
    ppermute x1, starting transfers between devices, near_plan(): lax.ppermute(near_block, 'col', X3)  4.02 us
    ppermute x6, waiting for transfers between devices, meet(): return lax.ppermute(token, 'row', X1)  3.42 us
    ppermute x2, starting transfers between devices, near_plan(): y, yd = (lax.ppermute(y, 'row', X2), lax.ppermute(yd, 'row', X3))  2.66 us
    ppermute x1, starting transfers between devices, near_plan(): lax.ppermute(near_block, 'col', X1)  2.66 us
  transfers between devices with their start and end apart: 36, of which 11 were waited for; matrix products, arithmetic and copies ran while one was open for 0% of the time, Pallas kernels for 32%

profile of v4, /device:TPU:0, one launch (start us, length us, event | category | flops | bytes accessed | tf_op | source)
XLA Modules:
  0.0 80.7 jit_solution(11201967016726461520)
XLA Ops:
  1.7 2.6 %collective-permute-start.1 = (bf16[2,8,2048]{2,1,0:T(8,128)(2,1)S(1)}, bf16[2,8,2048]{2,1,0:T(8,128)(2,1)S(1)}, u32[]{:S(2)}, u32[]{:S(2)}) collective-permute-start(bf16[2,8,2048]{2,1,0:T(8,128)(2,1)S(1)} %get-tuple-element.83), channel_id=1, source_target_pairs={{0,8},{4,12},{8,0},{12,4},{1,9},{5,13},{9,1},{13,5},{2,10},{6,14},... | collective-permute-start | bytes 196616 | tf_op jit(solution)/shard_map/ppermute | solution.py:270
  6.2 4.0 %collective-permute-start.6 = (bf16[32,2048]{1,0:T(8,128)(2,1)S(1)}, bf16[32,2048]{1,0:T(8,128)(2,1)S(1)}, u32[]{:S(2)}, u32[]{:S(2)}) collective-permute-start(bf16[32,2048]{1,0:T(8,128)(2,1)S(1)} %get-tuple-element.82.refs_0_), channel_id=1, source_target_pairs={{0,3},{1,2},{2,1},{3,0},{4,7},{5,6},{6,5},{7,4},{8,11},{9,10},{10,... | collective-permute-start | bytes 393224 | tf_op jit(solution)/shard_map/ppermute | solution.py:282
  10.2 2.1 %shard_map.67 = (bf16[1024,1792]{1,0:T(8,128)(2,1)S(1)}, f32[8,128]{1,0:T(8,128)S(1)}) custom-call(bf16[2048,3584]{1,0:T(8,128)(2,1)} %refs_0_.17, bf16[2048,3584]{1,0:T(8,128)(2,1)} %refs_1_.13, f32[8,128]{1,0:T(8,128)S(1)} %collective-permute-done.3.refs_2_), custom_call_target="tpu_custom_call" | custom-call | bytes 1 | tf_op jit(solution)/shard_map/pallas_call | solution.py:40
  13.3 1.1 %collective-permute-done.7.refs_2_ = f32[8,128]{1,0:T(8,128)S(1)} collective-permute-done((f32[8,128]{1,0:T(8,128)S(1)}, f32[8,128]{1,0:T(8,128)S(1)}, u32[]{:S(2)}, u32[]{:S(2)}) %collective-permute-start.7) | collective-permute-done | bytes 4128 | tf_op jit(solution)/shard_map/ppermute | solution.py:159
  14.4 2.1 %shard_map.69 = (bf16[1024,1792]{1,0:T(8,128)(2,1)S(1)}, f32[8,128]{1,0:T(8,128)S(1)}) custom-call(bf16[2048,3584]{1,0:T(8,128)(2,1)} %refs_0_.17, bf16[2048,3584]{1,0:T(8,128)(2,1)} %refs_1_.13, f32[8,128]{1,0:T(8,128)S(1)} %collective-permute-done.7.refs_2_), custom_call_target="tpu_custom_call" | custom-call | bytes 1 | tf_op jit(solution)/shard_map/pallas_call | solution.py:40
  16.7 2.7 %collective-permute-start.4 = (bf16[32,2048]{1,0:T(8,128)(2,1)S(1)}, bf16[32,2048]{1,0:T(8,128)(2,1)S(1)}, u32[]{:S(2)}, u32[]{:S(2)}) collective-permute-start(bf16[32,2048]{1,0:T(8,128)(2,1)S(1)} %get-tuple-element.82.refs_0_), channel_id=1, source_target_pairs={{0,1},{1,0},{2,3},{3,2},{4,5},{5,4},{6,7},{7,6},{8,9},{9,8},{10,11... | collective-permute-start | bytes 393224 | tf_op jit(solution)/shard_map/ppermute | solution.py:282
  19.5 1.9 %collective-permute-start.8 = (bf16[32,2048]{1,0:T(8,128)(2,1)S(1)}, bf16[32,2048]{1,0:T(8,128)(2,1)S(1)}, u32[]{:S(2)}, u32[]{:S(2)}) collective-permute-start(bf16[32,2048]{1,0:T(8,128)(2,1)S(1)} %get-tuple-element.90), channel_id=1, source_target_pairs={{0,1},{1,0},{2,3},{3,2},{4,5},{5,4},{6,7},{7,6},{8,9},{9,8},{10,11... | collective-permute-start | bytes 393224 | tf_op jit(solution)/shard_map/ppermute | solution.py:290
  21.4 2.1 %shard_map.71 = (bf16[1024,1792]{1,0:T(8,128)(2,1)S(1)}, f32[8,128]{1,0:T(8,128)S(1)}) custom-call(bf16[2048,3584]{1,0:T(8,128)(2,1)} %refs_0_.17, bf16[2048,3584]{1,0:T(8,128)(2,1)} %refs_1_.13, f32[8,128]{1,0:T(8,128)S(1)} %collective-permute-done.10.refs_2_), custom_call_target="tpu_custom_call" | custom-call | bytes 1 | tf_op jit(solution)/shard_map/pallas_call | solution.py:40
  23.7 1.2 %collective-permute-done.12.refs_2_ = f32[8,128]{1,0:T(8,128)S(1)} collective-permute-done((f32[8,128]{1,0:T(8,128)S(1)}, f32[8,128]{1,0:T(8,128)S(1)}, u32[]{:S(2)}, u32[]{:S(2)}) %collective-permute-start.12) | collective-permute-done | bytes 4128 | tf_op jit(solution)/shard_map/ppermute | solution.py:159
  24.9 2.1 %shard_map.73 = (bf16[1024,1792]{1,0:T(8,128)(2,1)S(1)}, f32[8,128]{1,0:T(8,128)S(1)}) custom-call(bf16[2048,3584]{1,0:T(8,128)(2,1)} %refs_0_.17, bf16[2048,3584]{1,0:T(8,128)(2,1)} %refs_1_.13, f32[8,128]{1,0:T(8,128)S(1)} %collective-permute-done.12.refs_2_), custom_call_target="tpu_custom_call" | custom-call | bytes 1 | tf_op jit(solution)/shard_map/pallas_call | solution.py:40
  26.9 3.3 %shard_map.74 = (bf16[2048,1792]{1,0:T(8,128)(2,1)S(1)}, f32[8,128]{1,0:T(8,128)S(1)}) custom-call(bf16[2048,3584]{1,0:T(8,128)(2,1)} %refs_0_.17, bf16[2048,3584]{1,0:T(8,128)(2,1)} %refs_1_.13, f32[8,128]{1,0:T(8,128)S(1)} %get-tuple-element.98.refs_2_), custom_call_target="tpu_custom_call" | custom-call | bytes 1 | tf_op jit(solution)/shard_map/pallas_call | solution.py:40
  30.3 1.6 %collective-permute-done.11.refs_5_ = bf16[32,2048]{1,0:T(8,128)(2,1)S(1)} collective-permute-done((bf16[32,2048]{1,0:T(8,128)(2,1)S(1)}, bf16[32,2048]{1,0:T(8,128)(2,1)S(1)}, u32[]{:S(2)}, u32[]{:S(2)}) %collective-permute-start.11) | collective-permute-done | bytes 131104 | tf_op jit(solution)/shard_map/ppermute | solution.py:294
  31.9 1.5 %shard_map.75 = (bf16[128,2048]{1,0:T(8,128)(2,1)S(1)}, bf16[64,1792]{1,0:T(8,128)(2,1)S(1)}, bf16[64,1792]{1,0:T(8,128)(2,1)S(1)}, f32[8,128]{1,0:T(8,128)S(1)}) custom-call(bf16[32,2048]{1,0:T(8,128)(2,1)S(1)} %get-tuple-element.82.refs_0_, bf16[32,2048]{1,0:T(8,128)(2,1)S(1)} %get-tuple-element.87.refs_1_, ...), custom_call_target="tpu_custom_call" | custom-call | bytes 1 | tf_op jit(solution)/shard_map/pallas_call | solution.py:40
  34.0 1.1 %shard_map.76 = (f32[128,1792]{1,0:T(8,128)S(1)}, f32[8,128]{1,0:T(8,128)S(1)}) custom-call(bf16[128,2048]{1,0:T(8,128)(2,1)S(1)} %get-tuple-element.100.refs_0_, bf16[1024,1792]{1,0:T(8,128)(2,1)S(1)} %get-tuple-element.102.refs_1_, bf16[1024,1792]{1,0:T(8,128)(2,1)S(1)} %get-tuple-element.103.refs_2_, f32[8,128]{1,0:T(8,128)S(1)} %get-tuple-element.104.refs_3_), custom_call_target="tpu_custom_call" | custom-call | bytes 1 | tf_op jit(solution)/shard_map/pallas_call | solution.py:40
  35.7 1.5 %collective-permute-start.16 = (bf16[64,1792]{1,0:T(8,128)(2,1)S(1)}, bf16[64,1792]{1,0:T(8,128)(2,1)S(1)}, u32[]{:S(2)}, u32[]{:S(2)}) collective-permute-start(bf16[64,1792]{1,0:T(8,128)(2,1)S(1)} %get-tuple-element.114), channel_id=1, source_target_pairs={{0,8},{4,12},{8,0},{12,4},{1,9},{5,13},{9,1},{13,5},{2,10},{6,14},... | collective-permute-start | bytes 688136 | tf_op jit(solution)/shard_map/ppermute | solution.py:316
  37.2 1.1 %shard_map.78 = (bf16[64,1792]{1,0:T(8,128)(2,1)S(1)}, bf16[64,1792]{1,0:T(8,128)(2,1)S(1)}, f32[8,128]{1,0:T(8,128)S(1)}) custom-call(bf16[128,2048]{1,0:T(8,128)(2,1)S(1)} %get-tuple-element.100.refs_0_, bf16[2048,1792]{1,0:T(8,128)(2,1)S(1)} %get-tuple-element.101.refs_1_, f32[8,128]{1,0:T(8,128)S(1)} %collective-permute-done.15.refs_2_), custom_call_target="tpu_custom_call" | custom-call | bytes 1 | tf_op jit(solution)/shard_map/pallas_call | solution.py:40
  38.5 1.1 %collective-permute-start.19 = (bf16[64,1792]{1,0:T(8,128)(2,1)S(1)}, bf16[64,1792]{1,0:T(8,128)(2,1)S(1)}, u32[]{:S(2)}, u32[]{:S(2)}) collective-permute-start(bf16[64,1792]{1,0:T(8,128)(2,1)S(1)} %get-tuple-element.119), channel_id=1, source_target_pairs={{0,8},{4,12},{8,0},{12,4},{1,9},{5,13},{9,1},{13,5},{2,10},{6,14},... | collective-permute-start | bytes 688136 | tf_op jit(solution)/shard_map/ppermute | solution.py:316
  39.6 3.3 %shard_map.79 = (bf16[2048,1792]{1,0:T(8,128)(2,1)S(1)}, f32[8,128]{1,0:T(8,128)S(1)}) custom-call(bf16[2048,3584]{1,0:T(8,128)(2,1)} %refs_0_.17, bf16[2048,3584]{1,0:T(8,128)(2,1)} %refs_1_.13, f32[8,128]{1,0:T(8,128)S(1)} %get-tuple-element.110.refs_2_), custom_call_target="tpu_custom_call" | custom-call | bytes 1 | tf_op jit(solution)/shard_map/pallas_call | solution.py:40
  43.0 1.1 %shard_map.80 = (f32[128,1792]{1,0:T(8,128)S(1)}, f32[8,128]{1,0:T(8,128)S(1)}) custom-call(bf16[128,2048]{1,0:T(8,128)(2,1)S(1)} %get-tuple-element.100.refs_0_, bf16[2048,1792]{1,0:T(8,128)(2,1)S(1)} %get-tuple-element.111.refs_1_, f32[8,128]{1,0:T(8,128)S(1)} %get-tuple-element.112.refs_2_), custom_call_target="tpu_custom_call" | custom-call | bytes 1 | tf_op jit(solution)/shard_map/pallas_call | solution.py:40
  44.2 1.1 %slice-done.1 = s8[4194304]{0:T(1024)(128)(4,1)S(1)} async-done(((s8[14680064]{0:T(1024)(128)(4,1)}), s8[4194304]{0:T(1024)(128)(4,1)S(1)}, s32[]{:S(2)}) %slice-start.1) | async-done | bytes 4194328
  45.3 1.2 %slice-done.2 = s8[4194304]{0:T(1024)(128)(4,1)S(1)} async-done(((s8[14680064]{0:T(1024)(128)(4,1)}), s8[4194304]{0:T(1024)(128)(4,1)S(1)}, s32[]{:S(2)}) %slice-start.2) | async-done | bytes 4194328
  49.7 1.4 %shard_map.84 = (f32[64,2048]{1,0:T(8,128)S(1)}, f32[8,128]{1,0:T(8,128)S(1)}) custom-call(bf16[64,896]{1,0:T(8,128)(2,1)S(1)} %get-tuple-element.118.refs_0_, bf16[64,896]{1,0:T(8,128)(2,1)S(1)} %collective-permute-done.21.refs_1_, bf16[1792,2048]{1,0:T(8,128)(2,1)S(1)} %get-tuple-element.121.refs_2_, f32[8,128]{1,0:T(8,128)S(1)} %get-tuple-element.123.refs_3_), custom_call_target="tpu_custom_call" | custom-call | bytes 1 | tf_op jit(solution)/shard_map/pallas_call | solution.py:40
  51.3 2.1 %collective-permute-done.18.refs_0_ = bf16[64,896]{1,0:T(8,128)(2,1)S(1)} collective-permute-done((bf16[64,896]{1,0:T(8,128)(2,1)S(1)}, bf16[64,896]{1,0:T(8,128)(2,1)S(1)}, u32[]{:S(2)}, u32[]{:S(2)}) %collective-permute-start.18) | collective-permute-done | bytes 114720 | tf_op jit(solution)/shard_map/ppermute | solution.py:331
  55.0 1.4 %shard_map.87 = (f32[16,2048]{1,0:T(8,128)S(1)}, bf16[16,2048]{1,0:T(8,128)(2,1)S(1)}, bf16[16,2048]{1,0:T(8,128)(2,1)S(1)}, bf16[16,2048]{1,0:T(8,128)(2,1)S(1)}, f32[8,128]{1,0:T(8,128)S(1)}) custom-call(bf16[64,896]{1,0:T(8,128)(2,1)S(1)} %collective-permute-done.18.refs_0_, bf16[64,896]{1,0:T(8,128)(2,1)S(1)} %collective-permute-done.22.refs_1_, ...), custom_call_target="tpu_custom_call" | custom-call | bytes 1 | tf_op jit(solution)/shard_map/pallas_call | solution.py:40
  56.6 1.1 %collective-permute-done.28.refs_3_ = f32[8,128]{1,0:T(8,128)S(1)} collective-permute-done((f32[8,128]{1,0:T(8,128)S(1)}, f32[8,128]{1,0:T(8,128)S(1)}, u32[]{:S(2)}, u32[]{:S(2)}) %collective-permute-start.28) | collective-permute-done | bytes 4128 | tf_op jit(solution)/shard_map/ppermute | solution.py:159
  57.7 1.4 %shard_map.88 = (f32[64,2048]{1,0:T(8,128)S(1)}, f32[8,128]{1,0:T(8,128)S(1)}) custom-call(bf16[64,896]{1,0:T(8,128)(2,1)S(1)} %get-tuple-element.134.refs_0_, bf16[64,896]{1,0:T(8,128)(2,1)S(1)} %collective-permute-done.27.refs_1_, bf16[1792,2048]{1,0:T(8,128)(2,1)S(1)} %get-tuple-element.121.refs_2_, f32[8,128]{1,0:T(8,128)S(1)} %collective-permute-done.28.refs_3_), custom_call_target="tpu_custom_call" | custom-call | bytes 1 | tf_op jit(solution)/shard_map/pallas_call | solution.py:40
  59.4 3.4 %collective-permute-start.23 = (bf16[16,2048]{1,0:T(8,128)(2,1)S(1)}, bf16[16,2048]{1,0:T(8,128)(2,1)S(1)}, u32[]{:S(2)}, u32[]{:S(2)}) collective-permute-start(bf16[16,2048]{1,0:T(8,128)(2,1)S(1)} %get-tuple-element.131), channel_id=1, source_target_pairs={{0,3},{1,2},{2,1},{3,0},{4,7},{5,6},{6,5},{7,4},{8,11},{9,10},{10,... | collective-permute-start | bytes 196616 | tf_op jit(solution)/shard_map/ppermute | solution.py:343
  63.8 1.4 %shard_map.90 = (f32[16,2048]{1,0:T(8,128)S(1)}, bf16[16,2048]{1,0:T(8,128)(2,1)S(1)}, bf16[16,2048]{1,0:T(8,128)(2,1)S(1)}, bf16[16,2048]{1,0:T(8,128)(2,1)S(1)}, f32[8,128]{1,0:T(8,128)S(1)}) custom-call(bf16[64,896]{1,0:T(8,128)(2,1)S(1)} %collective-permute-done.26.refs_0_, bf16[64,896]{1,0:T(8,128)(2,1)S(1)} %collective-permute-done.29.refs_1_, ...), custom_call_target="tpu_custom_call" | custom-call | bytes 1 | tf_op jit(solution)/shard_map/pallas_call | solution.py:40
  65.2 3.5 %collective-permute-start.30 = (bf16[16,2048]{1,0:T(8,128)(2,1)S(1)}, bf16[16,2048]{1,0:T(8,128)(2,1)S(1)}, u32[]{:S(2)}, u32[]{:S(2)}) collective-permute-start(bf16[16,2048]{1,0:T(8,128)(2,1)S(1)} %get-tuple-element.141), channel_id=1, source_target_pairs={{0,3},{1,2},{2,1},{3,0},{4,7},{5,6},{6,5},{7,4},{8,11},{9,10},{10,... | collective-permute-start | bytes 196616 | tf_op jit(solution)/shard_map/ppermute | solution.py:343
  70.5 1.5 %collective-permute-done.30.refs_5_ = bf16[16,2048]{1,0:T(8,128)(2,1)S(1)} collective-permute-done((bf16[16,2048]{1,0:T(8,128)(2,1)S(1)}, bf16[16,2048]{1,0:T(8,128)(2,1)S(1)}, u32[]{:S(2)}, u32[]{:S(2)}) %collective-permute-start.30) | collective-permute-done | bytes 65568 | tf_op jit(solution)/shard_map/ppermute | solution.py:343
  71.9 3.4 %collective-permute-done.31.refs_6_ = bf16[16,2048]{1,0:T(8,128)(2,1)S(1)} collective-permute-done((bf16[16,2048]{1,0:T(8,128)(2,1)S(1)}, bf16[16,2048]{1,0:T(8,128)(2,1)S(1)}, u32[]{:S(2)}, u32[]{:S(2)}) %collective-permute-start.31) | collective-permute-done | bytes 65568 | tf_op jit(solution)/shard_map/ppermute | solution.py:343
  77.5 2.1 %collective-permute-done.34.refs_2_ = bf16[2,4,2048]{2,1,0:T(4,128)(2,1)S(1)} collective-permute-done((bf16[2,4,2048]{2,1,0:T(4,128)(2,1)S(1)}, bf16[2,4,2048]{2,1,0:T(4,128)(2,1)S(1)}, u32[]{:S(2)}, u32[]{:S(2)}) %collective-permute-start.34) | collective-permute-done | bytes 32800 | tf_op jit(solution)/shard_map/ppermute | solution.py:355
  (84 shorter events, 17.7 us)
Async XLA Ops:
  1.2 4.8 %collective-permute-start = (bf16[2,8,2048]{2,1,0:T(8,128)(2,1)S(1)}, bf16[2,8,2048]{2,1,0:T(8,128)(2,1)S(1)}, u32[]{:S(2)}, u32[]{:S(2)}) collective-permute-start(bf16[2,8,2048]{2,1,0:T(8,128)(2,1)S(1)} %get-tuple-element.79), channel_id=1, source_target_pairs={{0,4},{4,0},{8,12},{12,8},{1,5},{5,1},{9,13},{13,9},{2,6},{6,2},{1... | collective-permute-start | bytes 196616 | tf_op jit(solution)/shard_map/ppermute | solution.py:271
  1.7 10.6 %collective-permute-start.1 = (bf16[2,8,2048]{2,1,0:T(8,128)(2,1)S(1)}, bf16[2,8,2048]{2,1,0:T(8,128)(2,1)S(1)}, u32[]{:S(2)}, u32[]{:S(2)}) collective-permute-start(bf16[2,8,2048]{2,1,0:T(8,128)(2,1)S(1)} %get-tuple-element.83), channel_id=1, source_target_pairs={{0,8},{4,12},{8,0},{12,4},{1,9},{5,13},{9,1},{13,5},{2,10},{6,14},... | collective-permute-start | bytes 196616 | tf_op jit(solution)/shard_map/ppermute | solution.py:270
  4.3 8.0 %collective-permute-start.2 = (bf16[2,8,2048]{2,1,0:T(8,128)(2,1)S(1)}, bf16[2,8,2048]{2,1,0:T(8,128)(2,1)S(1)}, u32[]{:S(2)}, u32[]{:S(2)}) collective-permute-start(bf16[2,8,2048]{2,1,0:T(8,128)(2,1)S(1)} %get-tuple-element.84), channel_id=1, source_target_pairs={{0,12},{4,8},{8,4},{12,0},{1,13},{5,9},{9,5},{13,1},{2,14},{6,10},... | collective-permute-start | bytes 196616 | tf_op jit(solution)/shard_map/ppermute | solution.py:270
  6.0 4.2 %collective-permute-start.3 = (f32[8,128]{1,0:T(8,128)S(1)}, f32[8,128]{1,0:T(8,128)S(1)}, u32[]{:S(2)}, u32[]{:S(2)}) collective-permute-start(f32[8,128]{1,0:T(8,128)S(1)} %get-tuple-element.85), channel_id=1, source_target_pairs={{0,4},{4,0},{8,12},{12,8},{1,5},{5,1},{9,13},{13,9},{2,6},{6,2},{1... | collective-permute-start | bytes 12296 | tf_op jit(solution)/shard_map/ppermute | solution.py:159
  6.2 10.3 %collective-permute-start.6 = (bf16[32,2048]{1,0:T(8,128)(2,1)S(1)}, bf16[32,2048]{1,0:T(8,128)(2,1)S(1)}, u32[]{:S(2)}, u32[]{:S(2)}) collective-permute-start(bf16[32,2048]{1,0:T(8,128)(2,1)S(1)} %get-tuple-element.82.refs_0_), channel_id=1, source_target_pairs={{0,3},{1,2},{2,1},{3,0},{4,7},{5,6},{6,5},{7,4},{8,11},{9,10},{10,... | collective-permute-start | bytes 393224 | tf_op jit(solution)/shard_map/ppermute | solution.py:282
  12.3 11.2 %collective-permute-start.9 = (bf16[32,2048]{1,0:T(8,128)(2,1)S(1)}, bf16[32,2048]{1,0:T(8,128)(2,1)S(1)}, u32[]{:S(2)}, u32[]{:S(2)}) collective-permute-start(bf16[32,2048]{1,0:T(8,128)(2,1)S(1)} %get-tuple-element.87.refs_1_), channel_id=1, source_target_pairs={{0,3},{1,2},{2,1},{3,0},{4,7},{5,6},{6,5},{7,4},{8,11},{9,10},{10,... | collective-permute-start | bytes 393224 | tf_op jit(solution)/shard_map/ppermute | solution.py:286
  16.5 4.9 %collective-permute-start.10 = (f32[8,128]{1,0:T(8,128)S(1)}, f32[8,128]{1,0:T(8,128)S(1)}, u32[]{:S(2)}, u32[]{:S(2)}) collective-permute-start(f32[8,128]{1,0:T(8,128)S(1)} %get-tuple-element.91), channel_id=1, source_target_pairs={{0,4},{4,0},{8,12},{12,8},{1,5},{5,1},{9,13},{13,9},{2,6},{6,2},{1... | collective-permute-start | bytes 12296 | tf_op jit(solution)/shard_map/ppermute | solution.py:159
  16.7 13.5 %collective-permute-start.4 = (bf16[32,2048]{1,0:T(8,128)(2,1)S(1)}, bf16[32,2048]{1,0:T(8,128)(2,1)S(1)}, u32[]{:S(2)}, u32[]{:S(2)}) collective-permute-start(bf16[32,2048]{1,0:T(8,128)(2,1)S(1)} %get-tuple-element.82.refs_0_), channel_id=1, source_target_pairs={{0,1},{1,0},{2,3},{3,2},{4,5},{5,4},{6,7},{7,6},{8,9},{9,8},{10,11... | collective-permute-start | bytes 393224 | tf_op jit(solution)/shard_map/ppermute | solution.py:282
  19.4 10.9 %collective-permute-start.5 = (bf16[32,2048]{1,0:T(8,128)(2,1)S(1)}, bf16[32,2048]{1,0:T(8,128)(2,1)S(1)}, u32[]{:S(2)}, u32[]{:S(2)}) collective-permute-start(bf16[32,2048]{1,0:T(8,128)(2,1)S(1)} %get-tuple-element.87.refs_1_), channel_id=1, source_target_pairs={{0,1},{1,0},{2,3},{3,2},{4,5},{5,4},{6,7},{7,6},{8,9},{9,8},{10,11... | collective-permute-start | bytes 393224 | tf_op jit(solution)/shard_map/ppermute | solution.py:286
  19.5 10.8 %collective-permute-start.8 = (bf16[32,2048]{1,0:T(8,128)(2,1)S(1)}, bf16[32,2048]{1,0:T(8,128)(2,1)S(1)}, u32[]{:S(2)}, u32[]{:S(2)}) collective-permute-start(bf16[32,2048]{1,0:T(8,128)(2,1)S(1)} %get-tuple-element.90), channel_id=1, source_target_pairs={{0,1},{1,0},{2,3},{3,2},{4,5},{5,4},{6,7},{7,6},{8,9},{9,8},{10,11... | collective-permute-start | bytes 393224 | tf_op jit(solution)/shard_map/ppermute | solution.py:290
  23.5 8.4 %collective-permute-start.11 = (bf16[32,2048]{1,0:T(8,128)(2,1)S(1)}, bf16[32,2048]{1,0:T(8,128)(2,1)S(1)}, u32[]{:S(2)}, u32[]{:S(2)}) collective-permute-start(bf16[32,2048]{1,0:T(8,128)(2,1)S(1)} %get-tuple-element.93), channel_id=1, source_target_pairs={{0,1},{1,0},{2,3},{3,2},{4,5},{5,4},{6,7},{7,6},{8,9},{9,8},{10,11... | collective-permute-start | bytes 393224 | tf_op jit(solution)/shard_map/ppermute | solution.py:294
  33.4 1.7 %collective-permute-start.13 = (bf16[64,1792]{1,0:T(8,128)(2,1)S(1)}, bf16[64,1792]{1,0:T(8,128)(2,1)S(1)}, u32[]{:S(2)}, u32[]{:S(2)}) collective-permute-start(bf16[64,1792]{1,0:T(8,128)(2,1)S(1)} %get-tuple-element.106), channel_id=1, source_target_pairs={{0,4},{4,0},{8,12},{12,8},{1,5},{5,1},{9,13},{13,9},{2,6},{6,2},{1... | collective-permute-start | bytes 688136 | tf_op jit(solution)/shard_map/ppermute | solution.py:313
  33.5 1.8 %collective-permute-start.14 = (bf16[64,1792]{1,0:T(8,128)(2,1)S(1)}, bf16[64,1792]{1,0:T(8,128)(2,1)S(1)}, u32[]{:S(2)}, u32[]{:S(2)}) collective-permute-start(bf16[64,1792]{1,0:T(8,128)(2,1)S(1)} %get-tuple-element.107), channel_id=1, source_target_pairs={{0,4},{4,0},{8,12},{12,8},{1,5},{5,1},{9,13},{13,9},{2,6},{6,2},{1... | collective-permute-start | bytes 688136 | tf_op jit(solution)/shard_map/ppermute | solution.py:313
  35.4 1.8 %collective-permute-start.15 = (f32[8,128]{1,0:T(8,128)S(1)}, f32[8,128]{1,0:T(8,128)S(1)}, u32[]{:S(2)}, u32[]{:S(2)}) collective-permute-start(f32[8,128]{1,0:T(8,128)S(1)} %get-tuple-element.109), channel_id=1, source_target_pairs={{0,4},{4,0},{8,12},{12,8},{1,5},{5,1},{9,13},{13,9},{2,6},{6,2},{1... | collective-permute-start | bytes 12296 | tf_op jit(solution)/shard_map/ppermute | solution.py:159
  35.7 11.9 %collective-permute-start.16 = (bf16[64,1792]{1,0:T(8,128)(2,1)S(1)}, bf16[64,1792]{1,0:T(8,128)(2,1)S(1)}, u32[]{:S(2)}, u32[]{:S(2)}) collective-permute-start(bf16[64,1792]{1,0:T(8,128)(2,1)S(1)} %get-tuple-element.114), channel_id=1, source_target_pairs={{0,8},{4,12},{8,0},{12,4},{1,9},{5,13},{9,1},{13,5},{2,10},{6,14},... | collective-permute-start | bytes 688136 | tf_op jit(solution)/shard_map/ppermute | solution.py:316
  38.3 9.2 %collective-permute-start.17 = (bf16[64,1792]{1,0:T(8,128)(2,1)S(1)}, bf16[64,1792]{1,0:T(8,128)(2,1)S(1)}, u32[]{:S(2)}, u32[]{:S(2)}) collective-permute-start(bf16[64,1792]{1,0:T(8,128)(2,1)S(1)} %get-tuple-element.115), channel_id=1, source_target_pairs={{0,4},{4,0},{8,12},{12,8},{1,5},{5,1},{9,13},{13,9},{2,6},{6,2},{1... | collective-permute-start | bytes 688136 | tf_op jit(solution)/shard_map/ppermute | solution.py:319
  38.5 12.7 %collective-permute-start.19 = (bf16[64,1792]{1,0:T(8,128)(2,1)S(1)}, bf16[64,1792]{1,0:T(8,128)(2,1)S(1)}, u32[]{:S(2)}, u32[]{:S(2)}) collective-permute-start(bf16[64,1792]{1,0:T(8,128)(2,1)S(1)} %get-tuple-element.119), channel_id=1, source_target_pairs={{0,8},{4,12},{8,0},{12,4},{1,9},{5,13},{9,1},{13,5},{2,10},{6,14},... | collective-permute-start | bytes 688136 | tf_op jit(solution)/shard_map/ppermute | solution.py:316
  39.6 11.6 %collective-permute-start.20 = (bf16[64,1792]{1,0:T(8,128)(2,1)S(1)}, bf16[64,1792]{1,0:T(8,128)(2,1)S(1)}, u32[]{:S(2)}, u32[]{:S(2)}) collective-permute-start(bf16[64,1792]{1,0:T(8,128)(2,1)S(1)} %get-tuple-element.120), channel_id=1, source_target_pairs={{0,4},{4,0},{8,12},{12,8},{1,5},{5,1},{9,13},{13,9},{2,6},{6,2},{1... | collective-permute-start | bytes 688136 | tf_op jit(solution)/shard_map/ppermute | solution.py:319
  47.7 2.0 %collective-permute-start.21 = (bf16[64,896]{1,0:T(8,128)(2,1)S(1)}, bf16[64,896]{1,0:T(8,128)(2,1)S(1)}, u32[]{:S(2)}, u32[]{:S(2)}) collective-permute-start(bf16[64,896]{1,0:T(8,128)(2,1)S(1)} %get-tuple-element.118.refs_0_), channel_id=1, source_target_pairs={{0,4},{4,0},{8,12},{12,8},{1,5},{5,1},{9,13},{13,9},{2,6},{6,2},{1... | collective-permute-start | bytes 344072 | tf_op jit(solution)/shard_map/ppermute | solution.py:332
  48.3 5.1 %collective-permute-start.18 = (bf16[64,896]{1,0:T(8,128)(2,1)S(1)}, bf16[64,896]{1,0:T(8,128)(2,1)S(1)}, u32[]{:S(2)}, u32[]{:S(2)}) collective-permute-start(bf16[64,896]{1,0:T(8,128)(2,1)S(1)} %get-tuple-element.118.refs_0_), channel_id=1, source_target_pairs={{0,8},{4,12},{8,0},{12,4},{1,9},{5,13},{9,1},{13,5},{2,10},{6,14},... | collective-permute-start | bytes 344072 | tf_op jit(solution)/shard_map/ppermute | solution.py:331
  53.5 3.1 %collective-permute-start.27 = (bf16[64,896]{1,0:T(8,128)(2,1)S(1)}, bf16[64,896]{1,0:T(8,128)(2,1)S(1)}, u32[]{:S(2)}, u32[]{:S(2)}) collective-permute-start(bf16[64,896]{1,0:T(8,128)(2,1)S(1)} %get-tuple-element.134.refs_0_), channel_id=1, source_target_pairs={{0,4},{4,0},{8,12},{12,8},{1,5},{5,1},{9,13},{13,9},{2,6},{6,2},{1... | collective-permute-start | bytes 344072 | tf_op jit(solution)/shard_map/ppermute | solution.py:332
  54.0 5.1 %collective-permute-start.26 = (bf16[64,896]{1,0:T(8,128)(2,1)S(1)}, bf16[64,896]{1,0:T(8,128)(2,1)S(1)}, u32[]{:S(2)}, u32[]{:S(2)}) collective-permute-start(bf16[64,896]{1,0:T(8,128)(2,1)S(1)} %get-tuple-element.134.refs_0_), channel_id=1, source_target_pairs={{0,8},{4,12},{8,0},{12,4},{1,9},{5,13},{9,1},{13,5},{2,10},{6,14},... | collective-permute-start | bytes 344072 | tf_op jit(solution)/shard_map/ppermute | solution.py:331
  59.1 4.6 %collective-permute-start.29 = (bf16[64,896]{1,0:T(8,128)(2,1)S(1)}, bf16[64,896]{1,0:T(8,128)(2,1)S(1)}, u32[]{:S(2)}, u32[]{:S(2)}) collective-permute-start(bf16[64,896]{1,0:T(8,128)(2,1)S(1)} %get-tuple-element.137), channel_id=1, source_target_pairs={{0,4},{4,0},{8,12},{12,8},{1,5},{5,1},{9,13},{13,9},{2,6},{6,2},{1... | collective-permute-start | bytes 344072 | tf_op jit(solution)/shard_map/ppermute | solution.py:341
  59.4 9.3 %collective-permute-start.23 = (bf16[16,2048]{1,0:T(8,128)(2,1)S(1)}, bf16[16,2048]{1,0:T(8,128)(2,1)S(1)}, u32[]{:S(2)}, u32[]{:S(2)}) collective-permute-start(bf16[16,2048]{1,0:T(8,128)(2,1)S(1)} %get-tuple-element.131), channel_id=1, source_target_pairs={{0,3},{1,2},{2,1},{3,0},{4,7},{5,6},{6,5},{7,4},{8,11},{9,10},{10,... | collective-permute-start | bytes 196616 | tf_op jit(solution)/shard_map/ppermute | solution.py:343
  62.8 7.7 %collective-permute-start.24 = (bf16[16,2048]{1,0:T(8,128)(2,1)S(1)}, bf16[16,2048]{1,0:T(8,128)(2,1)S(1)}, u32[]{:S(2)}, u32[]{:S(2)}) collective-permute-start(bf16[16,2048]{1,0:T(8,128)(2,1)S(1)} %get-tuple-element.132), channel_id=1, source_target_pairs={{0,2},{1,3},{2,0},{3,1},{4,6},{5,7},{6,4},{7,5},{8,10},{9,11},{10,... | collective-permute-start | bytes 196616 | tf_op jit(solution)/shard_map/ppermute | solution.py:343
  63.1 7.4 %collective-permute-start.25 = (bf16[16,2048]{1,0:T(8,128)(2,1)S(1)}, bf16[16,2048]{1,0:T(8,128)(2,1)S(1)}, u32[]{:S(2)}, u32[]{:S(2)}) collective-permute-start(bf16[16,2048]{1,0:T(8,128)(2,1)S(1)} %get-tuple-element.133), channel_id=1, source_target_pairs={{0,1},{1,0},{2,3},{3,2},{4,5},{5,4},{6,7},{7,6},{8,9},{9,8},{10,11... | collective-permute-start | bytes 196616 | tf_op jit(solution)/shard_map/ppermute | solution.py:343
  65.2 6.7 %collective-permute-start.30 = (bf16[16,2048]{1,0:T(8,128)(2,1)S(1)}, bf16[16,2048]{1,0:T(8,128)(2,1)S(1)}, u32[]{:S(2)}, u32[]{:S(2)}) collective-permute-start(bf16[16,2048]{1,0:T(8,128)(2,1)S(1)} %get-tuple-element.141), channel_id=1, source_target_pairs={{0,3},{1,2},{2,1},{3,0},{4,7},{5,6},{6,5},{7,4},{8,11},{9,10},{10,... | collective-permute-start | bytes 196616 | tf_op jit(solution)/shard_map/ppermute | solution.py:343
  68.6 6.7 %collective-permute-start.31 = (bf16[16,2048]{1,0:T(8,128)(2,1)S(1)}, bf16[16,2048]{1,0:T(8,128)(2,1)S(1)}, u32[]{:S(2)}, u32[]{:S(2)}) collective-permute-start(bf16[16,2048]{1,0:T(8,128)(2,1)S(1)} %get-tuple-element.142), channel_id=1, source_target_pairs={{0,2},{1,3},{2,0},{3,1},{4,6},{5,7},{6,4},{7,5},{8,10},{9,11},{10,... | collective-permute-start | bytes 196616 | tf_op jit(solution)/shard_map/ppermute | solution.py:343
  68.6 6.7 %collective-permute-start.32 = (bf16[16,2048]{1,0:T(8,128)(2,1)S(1)}, bf16[16,2048]{1,0:T(8,128)(2,1)S(1)}, u32[]{:S(2)}, u32[]{:S(2)}) collective-permute-start(bf16[16,2048]{1,0:T(8,128)(2,1)S(1)} %get-tuple-element.143), channel_id=1, source_target_pairs={{0,1},{1,0},{2,3},{3,2},{4,5},{5,4},{6,7},{7,6},{8,9},{9,8},{10,11... | collective-permute-start | bytes 196616 | tf_op jit(solution)/shard_map/ppermute | solution.py:343
  75.5 1.9 %collective-permute-start.33 = (bf16[2,4,2048]{2,1,0:T(4,128)(2,1)S(1)}, bf16[2,4,2048]{2,1,0:T(4,128)(2,1)S(1)}, u32[]{:S(2)}, u32[]{:S(2)}) collective-permute-start(bf16[2,4,2048]{2,1,0:T(4,128)(2,1)S(1)} %get-tuple-element.146), channel_id=1, source_target_pairs={{0,4},{4,0},{8,12},{12,8},{1,5},{5,1},{9,13},{13,9},{2,6},{6,2},{1... | collective-permute-start | bytes 98312 | tf_op jit(solution)/shard_map/ppermute | solution.py:355
  75.7 3.9 %collective-permute-start.34 = (bf16[2,4,2048]{2,1,0:T(4,128)(2,1)S(1)}, bf16[2,4,2048]{2,1,0:T(4,128)(2,1)S(1)}, u32[]{:S(2)}, u32[]{:S(2)}) collective-permute-start(bf16[2,4,2048]{2,1,0:T(4,128)(2,1)S(1)} %get-tuple-element.147), channel_id=1, source_target_pairs={{0,8},{4,12},{8,0},{12,4},{1,9},{5,13},{9,1},{13,5},{2,10},{6,14},... | collective-permute-start | bytes 98312 | tf_op jit(solution)/shard_map/ppermute | solution.py:355
  76.7 3.4 %collective-permute-start.35 = (bf16[2,4,2048]{2,1,0:T(4,128)(2,1)S(1)}, bf16[2,4,2048]{2,1,0:T(4,128)(2,1)S(1)}, u32[]{:S(2)}, u32[]{:S(2)}) collective-permute-start(bf16[2,4,2048]{2,1,0:T(4,128)(2,1)S(1)} %get-tuple-element.148), channel_id=1, source_target_pairs={{0,12},{4,8},{8,4},{12,0},{1,13},{5,9},{9,5},{13,1},{2,14},{6,10},... | collective-permute-start | bytes 98312 | tf_op jit(solution)/shard_map/ppermute | solution.py:355
  (11 other events, 31.9 us)

commit v5 on v4

--- a/solution.py
+++ b/solution.py
@@ -103,30 +103,47 @@
         ).astype(BF)
 
 
-def quarter_body(dy, dc, half, ins, weights, outs, scratch):
+def quarter_copies(dy, dc, weights, out_ref, sems):
     y, c, _ = place()
-    (out_ref,) = outs
-    height, width = out_ref.shape[0], out_ref.shape[1] // 2
+    width = out_ref.shape[1] // 2
     start = (lax.bitwise_xor(c, dc) * 2 + lax.bitwise_xor(y, dy)) * width
     at = pl.ds(pl.multiple_of(start, 128), width)
-    copies = [
-        pltpu.make_async_copy(
-            w.at[pl.ds(half * height, height), at],
-            out_ref.at[:, pl.ds(i * width, width)],
-            scratch[0].at[i],
-        )
+    return [
+        pltpu.make_async_copy(w.at[:, at], out_ref.at[:, pl.ds(i * width, width)], sems.at[i])
         for i, w in enumerate(weights)
     ]
+
+
+def quarter_body(dy, dc, ins, weights, outs, scratch):
+    copies = quarter_copies(dy, dc, weights, outs[0], scratch[0])
     for copy in copies:
         copy.start()
     for copy in copies:
         copy.wait()
 
 
-def fetch_quarter(gate_w, up_w, dy, dc, half, parts, token):
-    shape = pltpu.VMEM((gate_w.shape[0] // parts, gate_w.shape[1] // 2), BF)
+def dot_and_quarter_body(dy, dc, ins, weights, outs, scratch):
+    copies = quarter_copies(dy, dc, weights, outs[-1], scratch[0])
+    for copy in copies:
+        copy.start()
+    x_ref, w_ref = ins
+    rows = outs[0].shape[0]
+
+    @pl.loop(0, w_ref.shape[1] // 256)
+    def _(i):
+        at = pl.ds(pl.multiple_of(i * 256, 256), 256)
+        total = jnp.dot(x_ref[...], w_ref[:, at], preferred_element_type=F32).astype(BF)
+        for k, out in enumerate(outs[:-1]):
+            out[:, at] = total[k * rows : (k + 1) * rows]
+
+    for copy in copies:
+        copy.wait()
+
+
+def fetch_quarter(gate_w, up_w, dy, dc, token):
+    shape = pltpu.VMEM((gate_w.shape[0], gate_w.shape[1] // 2), BF)
     return run(
-        functools.partial(quarter_body, dy, dc, half),
+        functools.partial(quarter_body, dy, dc),
         (shape,),
         (),
         token,
@@ -166,7 +183,9 @@
 
 
 def after_body(ins, _, outs, __):
-    outs[0][...] = ins[0][...]
+    rows = outs[0].shape[0]
+    for i, out in enumerate(outs):
+        out[...] = ins[0][i * rows : (i + 1) * rows, :]
 
 
 def halves_dot(x_ref, w_refs):
@@ -222,11 +241,11 @@
 
 
 def down_rest_body(ins, _, outs, __):
-    y_ref, yd_ref, w_ref, part_ref = ins
+    y_ref, w_ref, part_ref, yd_refs = *ins[:3], ins[3:]
     rows = outs[0].shape[0]
     height = w_ref.shape[0] // 2
     total = part_ref[...] + jnp.dot(y_ref[...], w_ref[:height, :], preferred_element_type=F32)
-    total = total + jnp.dot(yd_ref[...], w_ref[height:, :], preferred_element_type=F32)
+    total = total + jnp.dot(load_rows(yd_refs).astype(BF), w_ref[height:, :], preferred_element_type=F32)
     for i, out in enumerate(outs):
         out[...] = total[i * rows : (i + 1) * rows].astype(out.dtype)
 
@@ -269,11 +288,10 @@
     y, yd, core, own, token = normed_blocks(sender_rows)
     y, yd = lax.ppermute(y, "row", X2), lax.ppermute(yd, "row", X3)
     core = lax.ppermute(core, "row", X1)
-    pick, token = run(pick_body, (like((steps * rows, steps * assign.shape[1])),), (counts, assign), token)
     quarters = {}
 
-    def bring(dy, dc, half, parts, token):
-        w, token = fetch_quarter(gate_w, up_w, dy, dc, half, parts, token)
+    def bring(dy, dc, token):
+        w, token = fetch_quarter(gate_w, up_w, dy, dc, token)
         quarters.setdefault((dy, dc), []).append(w)
         return token
 
@@ -281,20 +299,19 @@
     near_block, token = run(stack_body, (block,), (own, core), token)
     near_sent = [lax.ppermute(near_block, "col", X3), lax.ppermute(near_block, "col", X1)]
     token = meet(token)
-    token = bring(1, 1, 0, 2, token)
     far_block, token = run(stack_body, (block,), (y, yd), token)
     far_sent = [lax.ppermute(far_block, "col", X3), lax.ppermute(far_block, "col", X1)]
     token = meet(token)
-    token = bring(1, 1, 1, 2, token)
-    passed, token = run(after_body, (block,), (near_sent[0],), token)
+    token = bring(1, 1, token)
+    passed, token = run(after_body, (block,), (near_sent[0], near_sent[1]), token)
     near_sent.append(lax.ppermute(passed, "col", X1))
     token = meet(token)
-    token = bring(1, 0, 0, 2, token)
-    passed, token = run(after_body, (block,), (far_sent[0],), token)
+    token = bring(1, 0, token)
+    pick, token = run(pick_body, (like((steps * rows, steps * assign.shape[1])),), (counts, assign), token)
+    passed, token = run(after_body, (block,), (far_sent[0], far_sent[1]), token)
     far_sent.append(lax.ppermute(passed, "col", X1))
     token = meet(token)
-    token = bring(1, 0, 1, 2, token)
-    token = bring(0, 1, 0, 1, token)
+    token = bring(0, 1, token)
     pieces = []
     for dz in range(4):
         for own_block, sent in ((near_block, near_sent), (far_block, far_sent)):
@@ -315,10 +332,17 @@
     *sends, token = run(far_body, (like((rows, 2 * units)),) * steps, (own_far,) + cores, token)
     gots = [lax.ppermute(send, "row", X2) for send in sends]
     token = meet(token)
-    *out, token = run(dot_body, bits, (batch, *quarters[0, 1]), token)
+    last = pltpu.VMEM((gate_w.shape[0], gate_w.shape[1] // 2), BF)
+    *out, last, token = run(
+        functools.partial(dot_and_quarter_body, 0, 0),
+        bits + (last,),
+        (batch, *quarters[0, 1]),
+        token,
+        (gate_w, up_w),
+        (pltpu.SemaphoreType.DMA((2,)),),
+    )
     cores = tuple(lax.ppermute(o, "row", X1) for o in out)
-    token = bring(0, 0, 0, 1, token)
-    own_near, token = run(dot_body, (wide,), (batch, *quarters[0, 0]), token)
+    own_near, token = run(dot_body, (wide,), (batch, last), token)
     down_near, token = down_rows(0, token)
     hidden, sums = [], []
 
@@ -336,9 +360,11 @@
         return run(down_part_body, (like((rows, width), F32),), hidden[step][:2] + (down_near,), token)
 
     def down_rest(step, part_sum, token):
-        passed, token = run(after_body, (like((rows, units)),), (hidden[step][2],), token)
+        cut = (like((16, units)),) * (rows // 16)
+        *passed, token = run(after_body, cut, (hidden[step][2],), token)
+        passed = tuple(lax.ppermute(p, "row", X1) for p in passed)
         outs = (like((part, width), F32),) + (like((part, width)),) * 3
-        operands = (hidden[step][2], lax.ppermute(passed, "row", X1), down_far, part_sum)
+        operands = (hidden[step][2], down_far, part_sum) + passed
         keep, send1, send2, send3, token = run(down_rest_body, outs, operands, token)
         got = [lax.ppermute(s, "col", x) for s, x in ((send3, X3), (send2, X2), (send1, X1))]
         sums.extend([keep] + got)

time: 80.9 us -> 74.6 us (0.922)
  Pallas kernels: 28.3 us -> 25.2 us
  local copies, waits for them, and re-layouts: 5.22 us -> 2.59 us
  waiting for transfers between devices: 15.7 us -> 13.9 us
  starting transfers between devices: 31.2 us -> 32.4 us
    pallas_call x29 -> x26, Pallas kernels: 28.3 us -> 25.2 us  [run(): pl.pallas_call(wrapped, out_shape=outs, in_specs=[spec or vmem] * count +...]
    ppermute x1, starting transfers between devices: 2.66 us -> 0.01 us  [near_plan(): lax.ppermute(near_block, 'col', X1)]
    unnamed x14, local copies, waits for them, and re-layouts: 5.22 us -> 2.59 us
    ppermute x6, waiting for transfers between devices: 5.71 us -> 3.82 us  [down_rest(): lax.ppermute(s, 'col', x)]
    ppermute x2 -> x8, waiting for transfers between devices: 0.01 us -> 1.84 us  [down_rest(): passed = tuple((lax.ppermute(p, 'row', X1) for p in passed))]
    ppermute x1, starting transfers between devices: 0.88 us -> 2.59 us  [near_plan(): lax.ppermute(far_block, 'col', X3)]
    ppermute x1, waiting for transfers between devices: 1.65 us -> 0.01 us  [near_plan(): far_sent.append(lax.ppermute(passed, 'col', X1))]
    ppermute x2 -> x8, starting transfers between devices: 0.3 us -> 1.9 us  [down_rest(): passed = tuple((lax.ppermute(p, 'row', X1) for p in passed))]
  transfers between devices with their start and end apart: 36 -> 42, of which waited for: 11 -> 15; matrix products, arithmetic and copies ran while one was open for 0% -> 0% of each run, Pallas kernels for 32% -> 30%
where the time goes in v5:
time: 74.6 us; the launch traced here: 74.4 us
  starting transfers between devices  32.4 us (43%)
  Pallas kernels  25.2 us (34%)
  waiting for transfers between devices  13.9 us (19%)
  local copies, waits for them, and re-layouts  2.59 us (3%)
    pallas_call x26, Pallas kernels, run(): pl.pallas_call(wrapped, out_shape=outs, in_specs=[spec or vmem] * count +...  25.2 us
    ppermute x6, starting transfers between devices, down_rest(): lax.ppermute(s, 'col', x)  8.91 us
    ppermute x6, waiting for transfers between devices, meet(): return lax.ppermute(token, 'row', X1)  4.4 us
    ppermute x1, starting transfers between devices, near_plan(): lax.ppermute(near_block, 'col', X3)  3.87 us
    ppermute x6, waiting for transfers between devices, down_rest(): lax.ppermute(s, 'col', x)  3.82 us
    ppermute x2, starting transfers between devices, activate(): y = lax.ppermute(result, 'row', X2)  2.67 us
    ppermute x2, starting transfers between devices, near_plan(): y, yd = (lax.ppermute(y, 'row', X2), lax.ppermute(yd, 'row', X3))  2.66 us
    ppermute x2, starting transfers between devices, near_plan(): gots = [lax.ppermute(send, 'row', X2) for send in sends]  2.6 us
  transfers between devices with their start and end apart: 42, of which 15 were waited for; matrix products, arithmetic and copies ran while one was open for 0% of the time, Pallas kernels for 30%

profile of v5, /device:TPU:0, one launch (start us, length us, event | category | flops | bytes accessed | tf_op | source)
XLA Modules:
  0.0 74.4 jit_solution(1845511795075320026)
XLA Ops:
  1.7 2.6 %collective-permute-start.1 = (bf16[2,8,2048]{2,1,0:T(8,128)(2,1)S(1)}, bf16[2,8,2048]{2,1,0:T(8,128)(2,1)S(1)}, u32[]{:S(2)}, u32[]{:S(2)}) collective-permute-start(bf16[2,8,2048]{2,1,0:T(8,128)(2,1)S(1)} %get-tuple-element.83), channel_id=1, source_target_pairs={{0,8},{4,12},{8,0},{12,4},{1,9},{5,13},{9,1},{13,5},{2,10},{6,14},... | collective-permute-start | bytes 196616 | tf_op jit(solution)/shard_map/ppermute | solution.py:289
  4.4 3.9 %collective-permute-start.6 = (bf16[32,2048]{1,0:T(8,128)(2,1)S(1)}, bf16[32,2048]{1,0:T(8,128)(2,1)S(1)}, u32[]{:S(2)}, u32[]{:S(2)}) collective-permute-start(bf16[32,2048]{1,0:T(8,128)(2,1)S(1)} %get-tuple-element.82.refs_0_), channel_id=1, source_target_pairs={{0,3},{1,2},{2,1},{3,0},{4,7},{5,6},{6,5},{7,4},{8,11},{9,10},{10,... | collective-permute-start | bytes 393224 | tf_op jit(solution)/shard_map/ppermute | solution.py:300
  8.3 1.1 %collective-permute-done.3.refs_2_ = f32[8,128]{1,0:T(8,128)S(1)} collective-permute-done((f32[8,128]{1,0:T(8,128)S(1)}, f32[8,128]{1,0:T(8,128)S(1)}, u32[]{:S(2)}, u32[]{:S(2)}) %collective-permute-start.3) | collective-permute-done | bytes 4128 | tf_op jit(solution)/shard_map/ppermute | solution.py:176
  9.4 2.6 %collective-permute-start.9 = (bf16[32,2048]{1,0:T(8,128)(2,1)S(1)}, bf16[32,2048]{1,0:T(8,128)(2,1)S(1)}, u32[]{:S(2)}, u32[]{:S(2)}) collective-permute-start(bf16[32,2048]{1,0:T(8,128)(2,1)S(1)} %get-tuple-element.86.refs_1_), channel_id=1, source_target_pairs={{0,3},{1,2},{2,1},{3,0},{4,7},{5,6},{6,5},{7,4},{8,11},{9,10},{10,... | collective-permute-start | bytes 393224 | tf_op jit(solution)/shard_map/ppermute | solution.py:303
  13.2 3.2 %shard_map.67 = (bf16[2048,1792]{1,0:T(8,128)(2,1)S(1)}, f32[8,128]{1,0:T(8,128)S(1)}) custom-call(bf16[2048,3584]{1,0:T(8,128)(2,1)} %refs_2_.1, bf16[2048,3584]{1,0:T(8,128)(2,1)} %refs_3_.1, f32[8,128]{1,0:T(8,128)S(1)} %collective-permute-done.7.refs_2_), custom_call_target="tpu_custom_call" | custom-call | bytes 1 | tf_op jit(solution)/shard_map/pallas_call | solution.py:40
  16.7 2.0 %collective-permute-start.8 = (bf16[32,2048]{1,0:T(8,128)(2,1)S(1)}, bf16[32,2048]{1,0:T(8,128)(2,1)S(1)}, u32[]{:S(2)}, u32[]{:S(2)}) collective-permute-start(bf16[32,2048]{1,0:T(8,128)(2,1)S(1)} %get-tuple-element.89), channel_id=1, source_target_pairs={{0,1},{1,0},{2,3},{3,2},{4,5},{5,4},{6,7},{7,6},{8,9},{9,8},{10,11... | collective-permute-start | bytes 393224 | tf_op jit(solution)/shard_map/ppermute | solution.py:307
  18.7 3.2 %shard_map.69 = (bf16[2048,1792]{1,0:T(8,128)(2,1)S(1)}, f32[8,128]{1,0:T(8,128)S(1)}) custom-call(bf16[2048,3584]{1,0:T(8,128)(2,1)} %refs_2_.1, bf16[2048,3584]{1,0:T(8,128)(2,1)} %refs_3_.1, f32[8,128]{1,0:T(8,128)S(1)} %collective-permute-done.10.refs_2_), custom_call_target="tpu_custom_call" | custom-call | bytes 1 | tf_op jit(solution)/shard_map/pallas_call | solution.py:40
  22.2 1.0 %collective-permute-start.11 = (bf16[32,2048]{1,0:T(8,128)(2,1)S(1)}, bf16[32,2048]{1,0:T(8,128)(2,1)S(1)}, u32[]{:S(2)}, u32[]{:S(2)}) collective-permute-start(bf16[32,2048]{1,0:T(8,128)(2,1)S(1)} %get-tuple-element.93), channel_id=1, source_target_pairs={{0,1},{1,0},{2,3},{3,2},{4,5},{5,4},{6,7},{7,6},{8,9},{9,8},{10,11... | collective-permute-start | bytes 393224 | tf_op jit(solution)/shard_map/ppermute | solution.py:312
  23.3 1.2 %collective-permute-done.12.refs_2_ = f32[8,128]{1,0:T(8,128)S(1)} collective-permute-done((f32[8,128]{1,0:T(8,128)S(1)}, f32[8,128]{1,0:T(8,128)S(1)}, u32[]{:S(2)}, u32[]{:S(2)}) %collective-permute-start.12) | collective-permute-done | bytes 4128 | tf_op jit(solution)/shard_map/ppermute | solution.py:176
  24.4 3.3 %shard_map.72 = (bf16[2048,1792]{1,0:T(8,128)(2,1)S(1)}, f32[8,128]{1,0:T(8,128)S(1)}) custom-call(bf16[2048,3584]{1,0:T(8,128)(2,1)} %refs_2_.1, bf16[2048,3584]{1,0:T(8,128)(2,1)} %refs_3_.1, f32[8,128]{1,0:T(8,128)S(1)} %collective-permute-done.12.refs_2_), custom_call_target="tpu_custom_call" | custom-call | bytes 1 | tf_op jit(solution)/shard_map/pallas_call | solution.py:40
  27.7 1.4 %shard_map.73 = (bf16[128,2048]{1,0:T(8,128)(2,1)S(1)}, bf16[64,1792]{1,0:T(8,128)(2,1)S(1)}, bf16[64,1792]{1,0:T(8,128)(2,1)S(1)}, f32[8,128]{1,0:T(8,128)S(1)}) custom-call(bf16[32,2048]{1,0:T(8,128)(2,1)S(1)} %get-tuple-element.82.refs_0_, bf16[32,2048]{1,0:T(8,128)(2,1)S(1)} %get-tuple-element.86.refs_1_, ...), custom_call_target="tpu_custom_call" | custom-call | bytes 1 | tf_op jit(solution)/shard_map/pallas_call | solution.py:40
  29.7 1.1 %shard_map.74 = (f32[128,1792]{1,0:T(8,128)S(1)}, f32[8,128]{1,0:T(8,128)S(1)}) custom-call(bf16[128,2048]{1,0:T(8,128)(2,1)S(1)} %get-tuple-element.98.refs_0_, bf16[2048,1792]{1,0:T(8,128)(2,1)S(1)} %get-tuple-element.100.refs_1_, f32[8,128]{1,0:T(8,128)S(1)} %get-tuple-element.101.refs_2_), custom_call_target="tpu_custom_call" | custom-call | bytes 1 | tf_op jit(solution)/shard_map/pallas_call | solution.py:40
  31.4 1.5 %collective-permute-start.16 = (bf16[64,1792]{1,0:T(8,128)(2,1)S(1)}, bf16[64,1792]{1,0:T(8,128)(2,1)S(1)}, u32[]{:S(2)}, u32[]{:S(2)}) collective-permute-start(bf16[64,1792]{1,0:T(8,128)(2,1)S(1)} %get-tuple-element.110), channel_id=1, source_target_pairs={{0,8},{4,12},{8,0},{12,4},{1,9},{5,13},{9,1},{13,5},{2,10},{6,14},... | collective-permute-start | bytes 688136 | tf_op jit(solution)/shard_map/ppermute | solution.py:333
  32.9 3.3 %shard_map.76 = (bf16[64,1792]{1,0:T(8,128)(2,1)S(1)}, bf16[64,1792]{1,0:T(8,128)(2,1)S(1)}, bf16[2048,1792]{1,0:T(8,128)(2,1)S(1)}, f32[8,128]{1,0:T(8,128)S(1)}) custom-call(bf16[128,2048]{1,0:T(8,128)(2,1)S(1)} %get-tuple-element.98.refs_0_, bf16[2048,1792]{1,0:T(8,128)(2,1)S(1)} %get-tuple-element.99.refs_1_, bf16[2048,3584]{1,0:T(8,128)(2,1)} %refs_2_.1, ...), custom_call_target="tpu_custom_call" | custom-call | bytes 1 | tf_op jit(solution)/shard_map/pallas_call | solution.py:40
  36.4 1.1 %collective-permute-start.20 = (bf16[64,1792]{1,0:T(8,128)(2,1)S(1)}, bf16[64,1792]{1,0:T(8,128)(2,1)S(1)}, u32[]{:S(2)}, u32[]{:S(2)}) collective-permute-start(bf16[64,1792]{1,0:T(8,128)(2,1)S(1)} %get-tuple-element.120), channel_id=1, source_target_pairs={{0,8},{4,12},{8,0},{12,4},{1,9},{5,13},{9,1},{13,5},{2,10},{6,14},... | collective-permute-start | bytes 688136 | tf_op jit(solution)/shard_map/ppermute | solution.py:333
  37.6 1.1 %shard_map.77 = (f32[128,1792]{1,0:T(8,128)S(1)}, f32[8,128]{1,0:T(8,128)S(1)}) custom-call(bf16[128,2048]{1,0:T(8,128)(2,1)S(1)} %get-tuple-element.98.refs_0_, bf16[2048,1792]{1,0:T(8,128)(2,1)S(1)} %get-tuple-element.107.refs_1_, f32[8,128]{1,0:T(8,128)S(1)} %get-tuple-element.108.refs_2_), custom_call_target="tpu_custom_call" | custom-call | bytes 1 | tf_op jit(solution)/shard_map/pallas_call | solution.py:40
  38.7 1.0 %slice-done.2 = s8[4194304]{0:T(1024)(128)(4,1)S(1)} async-done(((s8[14680064]{0:T(1024)(128)(4,1)}), s8[4194304]{0:T(1024)(128)(4,1)S(1)}, s32[]{:S(2)}) %slice-start.2) | async-done | bytes 4194328
  41.1 1.1 %collective-permute-start.18 = (bf16[64,896]{1,0:T(8,128)(2,1)S(1)}, bf16[64,896]{1,0:T(8,128)(2,1)S(1)}, u32[]{:S(2)}, u32[]{:S(2)}) collective-permute-start(bf16[64,896]{1,0:T(8,128)(2,1)S(1)} %get-tuple-element.114.refs_0_), channel_id=1, source_target_pairs={{0,8},{4,12},{8,0},{12,4},{1,9},{5,13},{9,1},{13,5},{2,10},{6,14},... | collective-permute-start | bytes 344072 | tf_op jit(solution)/shard_map/ppermute | solution.py:355
  42.8 1.4 %shard_map.81 = (f32[64,2048]{1,0:T(8,128)S(1)}, f32[8,128]{1,0:T(8,128)S(1)}) custom-call(bf16[64,896]{1,0:T(8,128)(2,1)S(1)} %get-tuple-element.114.refs_0_, bf16[64,896]{1,0:T(8,128)(2,1)S(1)} %collective-permute-done.19.refs_1_, bf16[1792,2048]{1,0:T(8,128)(2,1)S(1)} %get-tuple-element.117.refs_2_, f32[8,128]{1,0:T(8,128)S(1)} %get-tuple-element.118.refs_3_), custom_call_target="tpu_custom_call" | custom-call | bytes 1 | tf_op jit(solution)/shard_map/pallas_call | solution.py:40
  44.7 1.6 %collective-permute-start.29 = (bf16[64,896]{1,0:T(8,128)(2,1)S(1)}, bf16[64,896]{1,0:T(8,128)(2,1)S(1)}, u32[]{:S(2)}, u32[]{:S(2)}) collective-permute-start(bf16[64,896]{1,0:T(8,128)(2,1)S(1)} %get-tuple-element.133.refs_0_), channel_id=1, source_target_pairs={{0,8},{4,12},{8,0},{12,4},{1,9},{5,13},{9,1},{13,5},{2,10},{6,14},... | collective-permute-start | bytes 344072 | tf_op jit(solution)/shard_map/ppermute | solution.py:355
  49.3 1.4 %shard_map.84 = (f32[16,2048]{1,0:T(8,128)S(1)}, bf16[16,2048]{1,0:T(8,128)(2,1)S(1)}, bf16[16,2048]{1,0:T(8,128)(2,1)S(1)}, bf16[16,2048]{1,0:T(8,128)(2,1)S(1)}, f32[8,128]{1,0:T(8,128)S(1)}) custom-call(bf16[64,896]{1,0:T(8,128)(2,1)S(1)} %collective-permute-done.18.refs_0_, bf16[1792,2048]{1,0:T(8,128)(2,1)S(1)} %get-tuple-element.116.refs_1_, ...), custom_call_target="tpu_custom_call" | custom-call | bytes 1 | tf_op jit(solution)/shard_map/pallas_call | solution.py:40
  50.8 1.7 %collective-permute-start.26 = (bf16[16,2048]{1,0:T(8,128)(2,1)S(1)}, bf16[16,2048]{1,0:T(8,128)(2,1)S(1)}, u32[]{:S(2)}, u32[]{:S(2)}) collective-permute-start(bf16[16,2048]{1,0:T(8,128)(2,1)S(1)} %get-tuple-element.130), channel_id=1, source_target_pairs={{0,3},{1,2},{2,1},{3,0},{4,7},{5,6},{6,5},{7,4},{8,11},{9,10},{10,... | collective-permute-start | bytes 196616 | tf_op jit(solution)/shard_map/ppermute | solution.py:369
  52.5 1.2 %collective-permute-done.31.refs_3_ = f32[8,128]{1,0:T(8,128)S(1)} collective-permute-done((f32[8,128]{1,0:T(8,128)S(1)}, f32[8,128]{1,0:T(8,128)S(1)}, u32[]{:S(2)}, u32[]{:S(2)}) %collective-permute-start.31) | collective-permute-done | bytes 4128 | tf_op jit(solution)/shard_map/ppermute | solution.py:176
  53.6 1.4 %shard_map.85 = (f32[64,2048]{1,0:T(8,128)S(1)}, f32[8,128]{1,0:T(8,128)S(1)}) custom-call(bf16[64,896]{1,0:T(8,128)(2,1)S(1)} %get-tuple-element.133.refs_0_, bf16[64,896]{1,0:T(8,128)(2,1)S(1)} %collective-permute-done.30.refs_1_, bf16[1792,2048]{1,0:T(8,128)(2,1)S(1)} %get-tuple-element.117.refs_2_, f32[8,128]{1,0:T(8,128)S(1)} %collective-permute-done.31.refs_3_), custom_call_target="tpu_custom_call" | custom-call | bytes 1 | tf_op jit(solution)/shard_map/pallas_call | solution.py:40
  57.3 1.8 %collective-permute-start.28 = (bf16[16,2048]{1,0:T(8,128)(2,1)S(1)}, bf16[16,2048]{1,0:T(8,128)(2,1)S(1)}, u32[]{:S(2)}, u32[]{:S(2)}) collective-permute-start(bf16[16,2048]{1,0:T(8,128)(2,1)S(1)} %get-tuple-element.132), channel_id=1, source_target_pairs={{0,1},{1,0},{2,3},{3,2},{4,5},{5,4},{6,7},{7,6},{8,9},{9,8},{10,11... | collective-permute-start | bytes 196616 | tf_op jit(solution)/shard_map/ppermute | solution.py:369
  59.1 1.4 %shard_map.87 = (f32[16,2048]{1,0:T(8,128)S(1)}, bf16[16,2048]{1,0:T(8,128)(2,1)S(1)}, bf16[16,2048]{1,0:T(8,128)(2,1)S(1)}, bf16[16,2048]{1,0:T(8,128)(2,1)S(1)}, f32[8,128]{1,0:T(8,128)S(1)}) custom-call(bf16[64,896]{1,0:T(8,128)(2,1)S(1)} %collective-permute-done.29.refs_0_, bf16[1792,2048]{1,0:T(8,128)(2,1)S(1)} %get-tuple-element.116.refs_1_, ...), custom_call_target="tpu_custom_call" | custom-call | bytes 1 | tf_op jit(solution)/shard_map/pallas_call | solution.py:40
  60.5 1.7 %collective-permute-start.36 = (bf16[16,2048]{1,0:T(8,128)(2,1)S(1)}, bf16[16,2048]{1,0:T(8,128)(2,1)S(1)}, u32[]{:S(2)}, u32[]{:S(2)}) collective-permute-start(bf16[16,2048]{1,0:T(8,128)(2,1)S(1)} %get-tuple-element.143), channel_id=1, source_target_pairs={{0,3},{1,2},{2,1},{3,0},{4,7},{5,6},{6,5},{7,4},{8,11},{9,10},{10,... | collective-permute-start | bytes 196616 | tf_op jit(solution)/shard_map/ppermute | solution.py:369
  62.2 2.7 %collective-permute-start.38 = (bf16[16,2048]{1,0:T(8,128)(2,1)S(1)}, bf16[16,2048]{1,0:T(8,128)(2,1)S(1)}, u32[]{:S(2)}, u32[]{:S(2)}) collective-permute-start(bf16[16,2048]{1,0:T(8,128)(2,1)S(1)} %get-tuple-element.145), channel_id=1, source_target_pairs={{0,1},{1,0},{2,3},{3,2},{4,5},{5,4},{6,7},{7,6},{8,9},{9,8},{10,11... | collective-permute-start | bytes 196616 | tf_op jit(solution)/shard_map/ppermute | solution.py:369
  65.0 2.2 %collective-permute-done.36.refs_5_ = bf16[16,2048]{1,0:T(8,128)(2,1)S(1)} collective-permute-done((bf16[16,2048]{1,0:T(8,128)(2,1)S(1)}, bf16[16,2048]{1,0:T(8,128)(2,1)S(1)}, u32[]{:S(2)}, u32[]{:S(2)}) %collective-permute-start.36) | collective-permute-done | bytes 65568 | tf_op jit(solution)/shard_map/ppermute | solution.py:369
  67.2 1.6 %collective-permute-done.37.refs_6_ = bf16[16,2048]{1,0:T(8,128)(2,1)S(1)} collective-permute-done((bf16[16,2048]{1,0:T(8,128)(2,1)S(1)}, bf16[16,2048]{1,0:T(8,128)(2,1)S(1)}, u32[]{:S(2)}, u32[]{:S(2)}) %collective-permute-start.37) | collective-permute-done | bytes 65568 | tf_op jit(solution)/shard_map/ppermute | solution.py:369
  69.1 1.3 %collective-permute-start.40 = (bf16[2,4,2048]{2,1,0:T(4,128)(2,1)S(1)}, bf16[2,4,2048]{2,1,0:T(4,128)(2,1)S(1)}, u32[]{:S(2)}, u32[]{:S(2)}) collective-permute-start(bf16[2,4,2048]{2,1,0:T(4,128)(2,1)S(1)} %get-tuple-element.149), channel_id=1, source_target_pairs={{0,8},{4,12},{8,0},{12,4},{1,9},{5,13},{9,1},{13,5},{2,10},{6,14},... | collective-permute-start | bytes 98312 | tf_op jit(solution)/shard_map/ppermute | solution.py:381
  70.9 2.1 %collective-permute-done.40.refs_2_ = bf16[2,4,2048]{2,1,0:T(4,128)(2,1)S(1)} collective-permute-done((bf16[2,4,2048]{2,1,0:T(4,128)(2,1)S(1)}, bf16[2,4,2048]{2,1,0:T(4,128)(2,1)S(1)}, u32[]{:S(2)}, u32[]{:S(2)}) %collective-permute-start.40) | collective-permute-done | bytes 32800 | tf_op jit(solution)/shard_map/ppermute | solution.py:381
  (93 shorter events, 14.6 us)
Async XLA Ops:
  1.2 3.2 %collective-permute-start = (bf16[2,8,2048]{2,1,0:T(8,128)(2,1)S(1)}, bf16[2,8,2048]{2,1,0:T(8,128)(2,1)S(1)}, u32[]{:S(2)}, u32[]{:S(2)}) collective-permute-start(bf16[2,8,2048]{2,1,0:T(8,128)(2,1)S(1)} %get-tuple-element.80), channel_id=1, source_target_pairs={{0,4},{4,0},{8,12},{12,8},{1,5},{5,1},{9,13},{13,9},{2,6},{6,2},{1... | collective-permute-start | bytes 196616 | tf_op jit(solution)/shard_map/ppermute | solution.py:290
  1.7 6.6 %collective-permute-start.1 = (bf16[2,8,2048]{2,1,0:T(8,128)(2,1)S(1)}, bf16[2,8,2048]{2,1,0:T(8,128)(2,1)S(1)}, u32[]{:S(2)}, u32[]{:S(2)}) collective-permute-start(bf16[2,8,2048]{2,1,0:T(8,128)(2,1)S(1)} %get-tuple-element.83), channel_id=1, source_target_pairs={{0,8},{4,12},{8,0},{12,4},{1,9},{5,13},{9,1},{13,5},{2,10},{6,14},... | collective-permute-start | bytes 196616 | tf_op jit(solution)/shard_map/ppermute | solution.py:289
  4.3 4.0 %collective-permute-start.2 = (bf16[2,8,2048]{2,1,0:T(8,128)(2,1)S(1)}, bf16[2,8,2048]{2,1,0:T(8,128)(2,1)S(1)}, u32[]{:S(2)}, u32[]{:S(2)}) collective-permute-start(bf16[2,8,2048]{2,1,0:T(8,128)(2,1)S(1)} %get-tuple-element.84), channel_id=1, source_target_pairs={{0,12},{4,8},{8,4},{12,0},{1,13},{5,9},{9,5},{13,1},{2,14},{6,10},... | collective-permute-start | bytes 196616 | tf_op jit(solution)/shard_map/ppermute | solution.py:289
  4.4 12.0 %collective-permute-start.6 = (bf16[32,2048]{1,0:T(8,128)(2,1)S(1)}, bf16[32,2048]{1,0:T(8,128)(2,1)S(1)}, u32[]{:S(2)}, u32[]{:S(2)}) collective-permute-start(bf16[32,2048]{1,0:T(8,128)(2,1)S(1)} %get-tuple-element.82.refs_0_), channel_id=1, source_target_pairs={{0,3},{1,2},{2,1},{3,0},{4,7},{5,6},{6,5},{7,4},{8,11},{9,10},{10,... | collective-permute-start | bytes 393224 | tf_op jit(solution)/shard_map/ppermute | solution.py:300
  8.2 8.1 %collective-permute-start.4 = (bf16[32,2048]{1,0:T(8,128)(2,1)S(1)}, bf16[32,2048]{1,0:T(8,128)(2,1)S(1)}, u32[]{:S(2)}, u32[]{:S(2)}) collective-permute-start(bf16[32,2048]{1,0:T(8,128)(2,1)S(1)} %get-tuple-element.82.refs_0_), channel_id=1, source_target_pairs={{0,1},{1,0},{2,3},{3,2},{4,5},{5,4},{6,7},{7,6},{8,9},{9,8},{10,11... | collective-permute-start | bytes 393224 | tf_op jit(solution)/shard_map/ppermute | solution.py:300
  9.4 12.8 %collective-permute-start.9 = (bf16[32,2048]{1,0:T(8,128)(2,1)S(1)}, bf16[32,2048]{1,0:T(8,128)(2,1)S(1)}, u32[]{:S(2)}, u32[]{:S(2)}) collective-permute-start(bf16[32,2048]{1,0:T(8,128)(2,1)S(1)} %get-tuple-element.86.refs_1_), channel_id=1, source_target_pairs={{0,3},{1,2},{2,1},{3,0},{4,7},{5,6},{6,5},{7,4},{8,11},{9,10},{10,... | collective-permute-start | bytes 393224 | tf_op jit(solution)/shard_map/ppermute | solution.py:303
  12.0 10.2 %collective-permute-start.5 = (bf16[32,2048]{1,0:T(8,128)(2,1)S(1)}, bf16[32,2048]{1,0:T(8,128)(2,1)S(1)}, u32[]{:S(2)}, u32[]{:S(2)}) collective-permute-start(bf16[32,2048]{1,0:T(8,128)(2,1)S(1)} %get-tuple-element.86.refs_1_), channel_id=1, source_target_pairs={{0,1},{1,0},{2,3},{3,2},{4,5},{5,4},{6,7},{7,6},{8,9},{9,8},{10,11... | collective-permute-start | bytes 393224 | tf_op jit(solution)/shard_map/ppermute | solution.py:303
  16.4 2.3 %collective-permute-start.10 = (f32[8,128]{1,0:T(8,128)S(1)}, f32[8,128]{1,0:T(8,128)S(1)}, u32[]{:S(2)}, u32[]{:S(2)}) collective-permute-start(f32[8,128]{1,0:T(8,128)S(1)} %get-tuple-element.90), channel_id=1, source_target_pairs={{0,4},{4,0},{8,12},{12,8},{1,5},{5,1},{9,13},{13,9},{2,6},{6,2},{1... | collective-permute-start | bytes 12296 | tf_op jit(solution)/shard_map/ppermute | solution.py:176
  16.7 11.0 %collective-permute-start.8 = (bf16[32,2048]{1,0:T(8,128)(2,1)S(1)}, bf16[32,2048]{1,0:T(8,128)(2,1)S(1)}, u32[]{:S(2)}, u32[]{:S(2)}) collective-permute-start(bf16[32,2048]{1,0:T(8,128)(2,1)S(1)} %get-tuple-element.89), channel_id=1, source_target_pairs={{0,1},{1,0},{2,3},{3,2},{4,5},{5,4},{6,7},{7,6},{8,9},{9,8},{10,11... | collective-permute-start | bytes 393224 | tf_op jit(solution)/shard_map/ppermute | solution.py:307
  22.2 5.5 %collective-permute-start.11 = (bf16[32,2048]{1,0:T(8,128)(2,1)S(1)}, bf16[32,2048]{1,0:T(8,128)(2,1)S(1)}, u32[]{:S(2)}, u32[]{:S(2)}) collective-permute-start(bf16[32,2048]{1,0:T(8,128)(2,1)S(1)} %get-tuple-element.93), channel_id=1, source_target_pairs={{0,1},{1,0},{2,3},{3,2},{4,5},{5,4},{6,7},{7,6},{8,9},{9,8},{10,11... | collective-permute-start | bytes 393224 | tf_op jit(solution)/shard_map/ppermute | solution.py:312
  29.2 1.7 %collective-permute-start.13 = (bf16[64,1792]{1,0:T(8,128)(2,1)S(1)}, bf16[64,1792]{1,0:T(8,128)(2,1)S(1)}, u32[]{:S(2)}, u32[]{:S(2)}) collective-permute-start(bf16[64,1792]{1,0:T(8,128)(2,1)S(1)} %get-tuple-element.103), channel_id=1, source_target_pairs={{0,4},{4,0},{8,12},{12,8},{1,5},{5,1},{9,13},{13,9},{2,6},{6,2},{1... | collective-permute-start | bytes 688136 | tf_op jit(solution)/shard_map/ppermute | solution.py:330
  31.2 1.7 %collective-permute-start.15 = (f32[8,128]{1,0:T(8,128)S(1)}, f32[8,128]{1,0:T(8,128)S(1)}, u32[]{:S(2)}, u32[]{:S(2)}) collective-permute-start(f32[8,128]{1,0:T(8,128)S(1)} %get-tuple-element.106), channel_id=1, source_target_pairs={{0,4},{4,0},{8,12},{12,8},{1,5},{5,1},{9,13},{13,9},{2,6},{6,2},{1... | collective-permute-start | bytes 12296 | tf_op jit(solution)/shard_map/ppermute | solution.py:176
  31.4 9.5 %collective-permute-start.16 = (bf16[64,1792]{1,0:T(8,128)(2,1)S(1)}, bf16[64,1792]{1,0:T(8,128)(2,1)S(1)}, u32[]{:S(2)}, u32[]{:S(2)}) collective-permute-start(bf16[64,1792]{1,0:T(8,128)(2,1)S(1)} %get-tuple-element.110), channel_id=1, source_target_pairs={{0,8},{4,12},{8,0},{12,4},{1,9},{5,13},{9,1},{13,5},{2,10},{6,14},... | collective-permute-start | bytes 688136 | tf_op jit(solution)/shard_map/ppermute | solution.py:333
  36.3 4.6 %collective-permute-start.17 = (bf16[64,1792]{1,0:T(8,128)(2,1)S(1)}, bf16[64,1792]{1,0:T(8,128)(2,1)S(1)}, u32[]{:S(2)}, u32[]{:S(2)}) collective-permute-start(bf16[64,1792]{1,0:T(8,128)(2,1)S(1)} %get-tuple-element.111), channel_id=1, source_target_pairs={{0,4},{4,0},{8,12},{12,8},{1,5},{5,1},{9,13},{13,9},{2,6},{6,2},{1... | collective-permute-start | bytes 688136 | tf_op jit(solution)/shard_map/ppermute | solution.py:344
  36.4 8.1 %collective-permute-start.20 = (bf16[64,1792]{1,0:T(8,128)(2,1)S(1)}, bf16[64,1792]{1,0:T(8,128)(2,1)S(1)}, u32[]{:S(2)}, u32[]{:S(2)}) collective-permute-start(bf16[64,1792]{1,0:T(8,128)(2,1)S(1)} %get-tuple-element.120), channel_id=1, source_target_pairs={{0,8},{4,12},{8,0},{12,4},{1,9},{5,13},{9,1},{13,5},{2,10},{6,14},... | collective-permute-start | bytes 688136 | tf_op jit(solution)/shard_map/ppermute | solution.py:333
  37.5 7.0 %collective-permute-start.21 = (bf16[64,1792]{1,0:T(8,128)(2,1)S(1)}, bf16[64,1792]{1,0:T(8,128)(2,1)S(1)}, u32[]{:S(2)}, u32[]{:S(2)}) collective-permute-start(bf16[64,1792]{1,0:T(8,128)(2,1)S(1)} %get-tuple-element.121), channel_id=1, source_target_pairs={{0,4},{4,0},{8,12},{12,8},{1,5},{5,1},{9,13},{13,9},{2,6},{6,2},{1... | collective-permute-start | bytes 688136 | tf_op jit(solution)/shard_map/ppermute | solution.py:344
  41.0 1.7 %collective-permute-start.19 = (bf16[64,896]{1,0:T(8,128)(2,1)S(1)}, bf16[64,896]{1,0:T(8,128)(2,1)S(1)}, u32[]{:S(2)}, u32[]{:S(2)}) collective-permute-start(bf16[64,896]{1,0:T(8,128)(2,1)S(1)} %get-tuple-element.114.refs_0_), channel_id=1, source_target_pairs={{0,4},{4,0},{8,12},{12,8},{1,5},{5,1},{9,13},{13,9},{2,6},{6,2},{1... | collective-permute-start | bytes 344072 | tf_op jit(solution)/shard_map/ppermute | solution.py:356
  41.1 5.7 %collective-permute-start.18 = (bf16[64,896]{1,0:T(8,128)(2,1)S(1)}, bf16[64,896]{1,0:T(8,128)(2,1)S(1)}, u32[]{:S(2)}, u32[]{:S(2)}) collective-permute-start(bf16[64,896]{1,0:T(8,128)(2,1)S(1)} %get-tuple-element.114.refs_0_), channel_id=1, source_target_pairs={{0,8},{4,12},{8,0},{12,4},{1,9},{5,13},{9,1},{13,5},{2,10},{6,14},... | collective-permute-start | bytes 344072 | tf_op jit(solution)/shard_map/ppermute | solution.py:355
  44.6 9.0 %collective-permute-start.30 = (bf16[64,896]{1,0:T(8,128)(2,1)S(1)}, bf16[64,896]{1,0:T(8,128)(2,1)S(1)}, u32[]{:S(2)}, u32[]{:S(2)}) collective-permute-start(bf16[64,896]{1,0:T(8,128)(2,1)S(1)} %get-tuple-element.133.refs_0_), channel_id=1, source_target_pairs={{0,4},{4,0},{8,12},{12,8},{1,5},{5,1},{9,13},{13,9},{2,6},{6,2},{1... | collective-permute-start | bytes 344072 | tf_op jit(solution)/shard_map/ppermute | solution.py:356
  44.7 10.4 %collective-permute-start.29 = (bf16[64,896]{1,0:T(8,128)(2,1)S(1)}, bf16[64,896]{1,0:T(8,128)(2,1)S(1)}, u32[]{:S(2)}, u32[]{:S(2)}) collective-permute-start(bf16[64,896]{1,0:T(8,128)(2,1)S(1)} %get-tuple-element.133.refs_0_), channel_id=1, source_target_pairs={{0,8},{4,12},{8,0},{12,4},{1,9},{5,13},{9,1},{13,5},{2,10},{6,14},... | collective-permute-start | bytes 344072 | tf_op jit(solution)/shard_map/ppermute | solution.py:355
  50.8 11.5 %collective-permute-start.26 = (bf16[16,2048]{1,0:T(8,128)(2,1)S(1)}, bf16[16,2048]{1,0:T(8,128)(2,1)S(1)}, u32[]{:S(2)}, u32[]{:S(2)}) collective-permute-start(bf16[16,2048]{1,0:T(8,128)(2,1)S(1)} %get-tuple-element.130), channel_id=1, source_target_pairs={{0,3},{1,2},{2,1},{3,0},{4,7},{5,6},{6,5},{7,4},{8,11},{9,10},{10,... | collective-permute-start | bytes 196616 | tf_op jit(solution)/shard_map/ppermute | solution.py:369
  55.3 1.9 %collective-permute-start.33 = (bf16[16,896]{1,0:T(8,128)(2,1)S(1)}, bf16[16,896]{1,0:T(8,128)(2,1)S(1)}, u32[]{:S(2)}, u32[]{:S(2)}) collective-permute-start(bf16[16,896]{1,0:T(8,128)(2,1)S(1)} %get-tuple-element.138), channel_id=1, source_target_pairs={{0,4},{4,0},{8,12},{12,8},{1,5},{5,1},{9,13},{13,9},{2,6},{6,2},{1... | collective-permute-start | bytes 86024 | tf_op jit(solution)/shard_map/ppermute | solution.py:365
  55.7 3.4 %collective-permute-start.34 = (bf16[16,896]{1,0:T(8,128)(2,1)S(1)}, bf16[16,896]{1,0:T(8,128)(2,1)S(1)}, u32[]{:S(2)}, u32[]{:S(2)}) collective-permute-start(bf16[16,896]{1,0:T(8,128)(2,1)S(1)} %get-tuple-element.139), channel_id=1, source_target_pairs={{0,4},{4,0},{8,12},{12,8},{1,5},{5,1},{9,13},{13,9},{2,6},{6,2},{1... | collective-permute-start | bytes 86024 | tf_op jit(solution)/shard_map/ppermute | solution.py:365
  55.8 3.3 %collective-permute-start.35 = (bf16[16,896]{1,0:T(8,128)(2,1)S(1)}, bf16[16,896]{1,0:T(8,128)(2,1)S(1)}, u32[]{:S(2)}, u32[]{:S(2)}) collective-permute-start(bf16[16,896]{1,0:T(8,128)(2,1)S(1)} %get-tuple-element.140), channel_id=1, source_target_pairs={{0,4},{4,0},{8,12},{12,8},{1,5},{5,1},{9,13},{13,9},{2,6},{6,2},{1... | collective-permute-start | bytes 86024 | tf_op jit(solution)/shard_map/ppermute | solution.py:365
  56.4 8.6 %collective-permute-start.27 = (bf16[16,2048]{1,0:T(8,128)(2,1)S(1)}, bf16[16,2048]{1,0:T(8,128)(2,1)S(1)}, u32[]{:S(2)}, u32[]{:S(2)}) collective-permute-start(bf16[16,2048]{1,0:T(8,128)(2,1)S(1)} %get-tuple-element.131), channel_id=1, source_target_pairs={{0,2},{1,3},{2,0},{3,1},{4,6},{5,7},{6,4},{7,5},{8,10},{9,11},{10,... | collective-permute-start | bytes 196616 | tf_op jit(solution)/shard_map/ppermute | solution.py:369
  57.3 7.7 %collective-permute-start.28 = (bf16[16,2048]{1,0:T(8,128)(2,1)S(1)}, bf16[16,2048]{1,0:T(8,128)(2,1)S(1)}, u32[]{:S(2)}, u32[]{:S(2)}) collective-permute-start(bf16[16,2048]{1,0:T(8,128)(2,1)S(1)} %get-tuple-element.132), channel_id=1, source_target_pairs={{0,1},{1,0},{2,3},{3,2},{4,5},{5,4},{6,7},{7,6},{8,9},{9,8},{10,11... | collective-permute-start | bytes 196616 | tf_op jit(solution)/shard_map/ppermute | solution.py:369
  60.5 6.7 %collective-permute-start.36 = (bf16[16,2048]{1,0:T(8,128)(2,1)S(1)}, bf16[16,2048]{1,0:T(8,128)(2,1)S(1)}, u32[]{:S(2)}, u32[]{:S(2)}) collective-permute-start(bf16[16,2048]{1,0:T(8,128)(2,1)S(1)} %get-tuple-element.143), channel_id=1, source_target_pairs={{0,3},{1,2},{2,1},{3,0},{4,7},{5,6},{6,5},{7,4},{8,11},{9,10},{10,... | collective-permute-start | bytes 196616 | tf_op jit(solution)/shard_map/ppermute | solution.py:369
  62.2 6.6 %collective-permute-start.37 = (bf16[16,2048]{1,0:T(8,128)(2,1)S(1)}, bf16[16,2048]{1,0:T(8,128)(2,1)S(1)}, u32[]{:S(2)}, u32[]{:S(2)}) collective-permute-start(bf16[16,2048]{1,0:T(8,128)(2,1)S(1)} %get-tuple-element.144), channel_id=1, source_target_pairs={{0,2},{1,3},{2,0},{3,1},{4,6},{5,7},{6,4},{7,5},{8,10},{9,11},{10,... | collective-permute-start | bytes 196616 | tf_op jit(solution)/shard_map/ppermute | solution.py:369
  62.2 6.6 %collective-permute-start.38 = (bf16[16,2048]{1,0:T(8,128)(2,1)S(1)}, bf16[16,2048]{1,0:T(8,128)(2,1)S(1)}, u32[]{:S(2)}, u32[]{:S(2)}) collective-permute-start(bf16[16,2048]{1,0:T(8,128)(2,1)S(1)} %get-tuple-element.145), channel_id=1, source_target_pairs={{0,1},{1,0},{2,3},{3,2},{4,5},{5,4},{6,7},{7,6},{8,9},{9,8},{10,11... | collective-permute-start | bytes 196616 | tf_op jit(solution)/shard_map/ppermute | solution.py:369
  69.0 1.9 %collective-permute-start.39 = (bf16[2,4,2048]{2,1,0:T(4,128)(2,1)S(1)}, bf16[2,4,2048]{2,1,0:T(4,128)(2,1)S(1)}, u32[]{:S(2)}, u32[]{:S(2)}) collective-permute-start(bf16[2,4,2048]{2,1,0:T(4,128)(2,1)S(1)} %get-tuple-element.148), channel_id=1, source_target_pairs={{0,4},{4,0},{8,12},{12,8},{1,5},{5,1},{9,13},{13,9},{2,6},{6,2},{1... | collective-permute-start | bytes 98312 | tf_op jit(solution)/shard_map/ppermute | solution.py:381
  69.1 4.0 %collective-permute-start.40 = (bf16[2,4,2048]{2,1,0:T(4,128)(2,1)S(1)}, bf16[2,4,2048]{2,1,0:T(4,128)(2,1)S(1)}, u32[]{:S(2)}, u32[]{:S(2)}) collective-permute-start(bf16[2,4,2048]{2,1,0:T(4,128)(2,1)S(1)} %get-tuple-element.149), channel_id=1, source_target_pairs={{0,8},{4,12},{8,0},{12,4},{1,9},{5,13},{9,1},{13,5},{2,10},{6,14},... | collective-permute-start | bytes 98312 | tf_op jit(solution)/shard_map/ppermute | solution.py:381
  70.4 3.3 %collective-permute-start.41 = (bf16[2,4,2048]{2,1,0:T(4,128)(2,1)S(1)}, bf16[2,4,2048]{2,1,0:T(4,128)(2,1)S(1)}, u32[]{:S(2)}, u32[]{:S(2)}) collective-permute-start(bf16[2,4,2048]{2,1,0:T(4,128)(2,1)S(1)} %get-tuple-element.150), channel_id=1, source_target_pairs={{0,12},{4,8},{8,4},{12,0},{1,13},{5,9},{9,5},{13,1},{2,14},{6,10},... | collective-permute-start | bytes 98312 | tf_op jit(solution)/shard_map/ppermute | solution.py:381
  (17 other events, 50.0 us)

commit v6 on v5

--- a/solution.py
+++ b/solution.py
@@ -16,6 +16,7 @@
 F32 = jnp.float32
 MIB = 2**20
 PIECES = 2
+CUTS = 1
 X1 = ((0, 1), (1, 0), (2, 3), (3, 2))
 X2 = ((0, 2), (1, 3), (2, 0), (3, 1))
 X3 = ((0, 3), (1, 2), (2, 1), (3, 0))
@@ -172,10 +173,6 @@
         copy.wait()
 
 
-def meet(token):
-    return lax.ppermute(token, "row", X1)
-
-
 def stack_body(ins, _, outs, __):
     for i, piece in enumerate(ins):
         joined = jnp.concatenate([piece[step].astype(F32) for step in range(2)], axis=0)
@@ -234,20 +231,25 @@
 
 
 def down_part_body(ins, _, outs, __):
-    own_ref, core_ref, w_ref = ins
+    w_ref, hidden = ins[0], ins[1:]
     height = w_ref.shape[0] // 2
-    total = jnp.dot(own_ref[...], w_ref[:height, :], preferred_element_type=F32)
-    outs[0][...] = total + jnp.dot(core_ref[...], w_ref[height:, :], preferred_element_type=F32)
+    own, core = (jnp.concatenate([x[...] for x in hidden[i : i + 2]], axis=0) for i in (0, 2))
+    total = jnp.dot(own, w_ref[:height, :], preferred_element_type=F32)
+    outs[0][...] = total + jnp.dot(core, w_ref[height:, :], preferred_element_type=F32)
 
 
 def down_rest_body(ins, _, outs, __):
-    y_ref, w_ref, part_ref, yd_refs = *ins[:3], ins[3:]
-    rows = outs[0].shape[0]
+    w_ref, part_ref, y0_ref, y1_ref = ins[:4]
+    steps, rows, _ = outs[0].shape
     height = w_ref.shape[0] // 2
-    total = part_ref[...] + jnp.dot(y_ref[...], w_ref[:height, :], preferred_element_type=F32)
-    total = total + jnp.dot(load_rows(yd_refs).astype(BF), w_ref[height:, :], preferred_element_type=F32)
+    y = jnp.concatenate([y0_ref[...], y1_ref[...]], axis=0)
+    total = part_ref[...] + jnp.dot(y, w_ref[:height, :], preferred_element_type=F32)
+    yd = load_rows(ins[4:]).astype(BF)
+    total = total + jnp.dot(yd, w_ref[height:, :], preferred_element_type=F32)
     for i, out in enumerate(outs):
-        out[...] = total[i * rows : (i + 1) * rows].astype(out.dtype)
+        for step in range(steps):
+            at = (step * len(outs) + i) * rows
+            out[step] = total[at : at + rows].astype(out.dtype)
 
 
 def owner_body(ins, _, outs, __):
@@ -256,9 +258,9 @@
     source = lax.bitwise_xor(at, (y * 2 + c) * 4)
     turn = (lax.broadcasted_iota(jnp.int32, (16, 16), 1) == source).astype(F32).astype(BF)
     for step in range(2):
-        total = ins[step * 4][...]
-        for got in ins[step * 4 + 1 : step * 4 + 4]:
-            total = total + got[...].astype(F32)
+        total = ins[0][step]
+        for got in ins[1:]:
+            total = total + got[step].astype(F32)
         turned = jnp.dot(turn, total.astype(BF), preferred_element_type=F32)
         for i, out in enumerate(outs):
             out[step] = turned[i * 4 : (i + 1) * 4].astype(BF)
@@ -298,19 +300,15 @@
     block = like((4 * slots, width))
     near_block, token = run(stack_body, (block,), (own, core), token)
     near_sent = [lax.ppermute(near_block, "col", X3), lax.ppermute(near_block, "col", X1)]
-    token = meet(token)
     far_block, token = run(stack_body, (block,), (y, yd), token)
     far_sent = [lax.ppermute(far_block, "col", X3), lax.ppermute(far_block, "col", X1)]
-    token = meet(token)
     token = bring(1, 1, token)
     passed, token = run(after_body, (block,), (near_sent[0], near_sent[1]), token)
     near_sent.append(lax.ppermute(passed, "col", X1))
-    token = meet(token)
     token = bring(1, 0, token)
     pick, token = run(pick_body, (like((steps * rows, steps * assign.shape[1])),), (counts, assign), token)
     passed, token = run(after_body, (block,), (far_sent[0], far_sent[1]), token)
     far_sent.append(lax.ppermute(passed, "col", X1))
-    token = meet(token)
     token = bring(0, 1, token)
     pieces = []
     for dz in range(4):
@@ -331,7 +329,6 @@
     own_far, token = run(dot_body, (wide,), (batch, *quarters[1, 0]), token)
     *sends, token = run(far_body, (like((rows, 2 * units)),) * steps, (own_far,) + cores, token)
     gots = [lax.ppermute(send, "row", X2) for send in sends]
-    token = meet(token)
     last = pltpu.VMEM((gate_w.shape[0], gate_w.shape[1] // 2), BF)
     *out, last, token = run(
         functools.partial(dot_and_quarter_body, 0, 0),
@@ -344,7 +341,7 @@
     cores = tuple(lax.ppermute(o, "row", X1) for o in out)
     own_near, token = run(dot_body, (wide,), (batch, last), token)
     down_near, token = down_rows(0, token)
-    hidden, sums = [], []
+    hidden = []
 
     def activate(step, token):
         each = PIECES // steps
@@ -356,27 +353,23 @@
         hidden.append((result, lax.ppermute(result, "row", X1), y))
         return token
 
-    def down_part(step, token):
-        return run(down_part_body, (like((rows, width), F32),), hidden[step][:2] + (down_near,), token)
-
-    def down_rest(step, part_sum, token):
-        cut = (like((16, units)),) * (rows // 16)
+    def shared(step, token):
+        cut = (like((rows // CUTS, units)),) * CUTS
         *passed, token = run(after_body, cut, (hidden[step][2],), token)
-        passed = tuple(lax.ppermute(p, "row", X1) for p in passed)
-        outs = (like((part, width), F32),) + (like((part, width)),) * 3
-        operands = (hidden[step][2], down_far, part_sum) + passed
-        keep, send1, send2, send3, token = run(down_rest_body, outs, operands, token)
-        got = [lax.ppermute(s, "col", x) for s, x in ((send3, X3), (send2, X2), (send1, X1))]
-        sums.extend([keep] + got)
-        return token
+        return tuple(lax.ppermute(p, "row", X1) for p in passed), token
 
     token = activate(0, token)
     down_far, token = down_rows(1, token)
-    part0, token = down_part(0, token)
     token = activate(1, token)
-    token = down_rest(0, part0, token)
-    part1, token = down_part(1, meet(token))
-    token = down_rest(1, part1, token)
+    yd0, token = shared(0, token)
+    (own0, core0, y0), (own1, core1, y1) = hidden
+    wide = like((steps * rows, width), F32)
+    part_sum, token = run(down_part_body, (wide,), (down_near, own0, own1, core0, core1), token)
+    yd1, token = shared(1, token)
+    outs = (like((steps, part, width), F32),) + (like((steps, part, width)),) * 3
+    operands = (down_far, part_sum, y0, y1) + yd0 + yd1
+    keep, send1, send2, send3, token = run(down_rest_body, outs, operands, token)
+    sums = [keep] + [lax.ppermute(s, "col", x) for s, x in ((send3, X3), (send2, X2), (send1, X1))]
     own, core, y, yd, token = run(owner_body, (like((steps, MEAN, width)),) * 4, tuple(sums), token)
     blocks = (own, lax.ppermute(core, "row", X1), lax.ppermute(y, "row", X2), lax.ppermute(yd, "row", X3))
     result, _ = run(output_body, (like((steps, MEAN, 4 * width)),), blocks, token)

time: 74.6 us -> 72.8 us (0.976)
  waiting for transfers between devices: 13.9 us -> 21.3 us
  starting transfers between devices: 32.4 us -> 25.9 us
  Pallas kernels: 25.2 us -> 22 us
    ppermute x20 -> x5, starting transfers between devices: 11.6 us -> 4.59 us  [the longest x3 4.45 us: near_plan(): lax.ppermute(s, 'col', x)]
    pallas_call x26 -> x24, Pallas kernels: 25.2 us -> 22 us  [run(): pl.pallas_call(wrapped, out_shape=outs, in_specs=[spec or vmem] * count +...]
    ppermute x2, waiting for transfers between devices: 0.28 us -> 2.67 us  [near_plan(): gots = [lax.ppermute(send, 'row', X2) for send in sends]]
    ppermute x2, waiting for transfers between devices: 0.58 us -> 2.9 us  [activate(): y = lax.ppermute(result, 'row', X2)]
    ppermute x20 -> x5, waiting for transfers between devices: 10.1 us -> 12.1 us  [the longest x3 10.8 us: near_plan(): lax.ppermute(s, 'col', x)]
    ppermute x1, starting transfers between devices: 1.03 us -> 2.12 us  [near_plan(): far_sent.append(lax.ppermute(passed, 'col', X1))]
    ppermute x1, starting transfers between devices: 2.59 us -> 3.67 us  [near_plan(): lax.ppermute(far_block, 'col', X3)]
    ppermute x2, starting transfers between devices: 2.67 us -> 1.9 us  [activate(): y = lax.ppermute(result, 'row', X2)]
  transfers between devices with their start and end apart: 42 -> 27, of which waited for: 15 -> 11; matrix products, arithmetic and copies ran while one was open for 0% -> 0% of each run, Pallas kernels for 30% -> 25%
where the time goes in v6:
time: 72.8 us; the launch traced here: 72.6 us
  starting transfers between devices  25.9 us (36%)
  Pallas kernels  22 us (30%)
  waiting for transfers between devices  21.3 us (29%)
  local copies, waits for them, and re-layouts  3.01 us (4%)
    pallas_call x24, Pallas kernels, run(): pl.pallas_call(wrapped, out_shape=outs, in_specs=[spec or vmem] * count +...  22 us
    ppermute x3, waiting for transfers between devices, near_plan(): lax.ppermute(s, 'col', x)  10.8 us
    ppermute x3, starting transfers between devices, near_plan(): lax.ppermute(s, 'col', x)  4.45 us
    ppermute x1, starting transfers between devices, near_plan(): lax.ppermute(near_block, 'col', X3)  3.87 us
    ppermute x1, starting transfers between devices, near_plan(): lax.ppermute(far_block, 'col', X3)  3.67 us
    unnamed x14, local copies, waits for them, and re-layouts  3.01 us
    ppermute x2, waiting for transfers between devices, activate(): y = lax.ppermute(result, 'row', X2)  2.9 us
    ppermute x2, waiting for transfers between devices, near_plan(): gots = [lax.ppermute(send, 'row', X2) for send in sends]  2.67 us
  transfers between devices with their start and end apart: 27, of which 11 were waited for; matrix products, arithmetic and copies ran while one was open for 0% of the time, Pallas kernels for 25%

profile of v6, /device:TPU:0, one launch (start us, length us, event | category | flops | bytes accessed | tf_op | source)
XLA Modules:
  0.0 72.6 jit_solution(15556782777226798896)
XLA Ops:
  0.0 0.9 %copy-done = bf16[2,8,8192]{2,1,0:T(8,128)(2,1)S(1)} copy-done((bf16[2,8,8192]{2,1,0:T(8,128)(2,1)S(1)}, bf16[2,8,8192]{2,1,0:T(8,128)(2,1)}, u32[]{:S(2)}) %copy-start) | copy-done | bytes 262168
  1.7 2.6 %collective-permute-start.1 = (bf16[2,8,2048]{2,1,0:T(8,128)(2,1)S(1)}, bf16[2,8,2048]{2,1,0:T(8,128)(2,1)S(1)}, u32[]{:S(2)}, u32[]{:S(2)}) collective-permute-start(bf16[2,8,2048]{2,1,0:T(8,128)(2,1)S(1)} %get-tuple-element.70), channel_id=1, source_target_pairs={{0,8},{4,12},{8,0},{12,4},{1,9},{5,13},{9,1},{13,5},{2,10},{6,14},... | collective-permute-start | bytes 196616 | tf_op jit(solution)/shard_map/ppermute | solution.py:291
  4.4 3.9 %collective-permute-start.5 = (bf16[32,2048]{1,0:T(8,128)(2,1)S(1)}, bf16[32,2048]{1,0:T(8,128)(2,1)S(1)}, u32[]{:S(2)}, u32[]{:S(2)}) collective-permute-start(bf16[32,2048]{1,0:T(8,128)(2,1)S(1)} %get-tuple-element.69.refs_0_), channel_id=1, source_target_pairs={{0,3},{1,2},{2,1},{3,0},{4,7},{5,6},{6,5},{7,4},{8,11},{9,10},{10,... | collective-permute-start | bytes 393224 | tf_op jit(solution)/shard_map/ppermute | solution.py:302
  8.3 3.7 %collective-permute-start.7 = (bf16[32,2048]{1,0:T(8,128)(2,1)S(1)}, bf16[32,2048]{1,0:T(8,128)(2,1)S(1)}, u32[]{:S(2)}, u32[]{:S(2)}) collective-permute-start(bf16[32,2048]{1,0:T(8,128)(2,1)S(1)} %get-tuple-element.73.refs_1_), channel_id=1, source_target_pairs={{0,3},{1,2},{2,1},{3,0},{4,7},{5,6},{6,5},{7,4},{8,11},{9,10},{10,... | collective-permute-start | bytes 393224 | tf_op jit(solution)/shard_map/ppermute | solution.py:304
  12.0 3.2 %shard_map.67 = (bf16[2048,1792]{1,0:T(8,128)(2,1)S(1)}, f32[8,128]{1,0:T(8,128)S(1)}) custom-call(bf16[2048,3584]{1,0:T(8,128)(2,1)} %refs_2_.1, bf16[2048,3584]{1,0:T(8,128)(2,1)} %refs_3_.1, f32[8,128]{1,0:T(8,128)S(1)} %get-tuple-element.74.refs_2_), custom_call_target="tpu_custom_call" | custom-call | bytes 1 | tf_op jit(solution)/shard_map/pallas_call | solution.py:41
  15.2 0.6 collective-permute-done.3.refs_1_.refs_2_
  15.8 1.6 %collective-permute-start.6 = (bf16[32,2048]{1,0:T(8,128)(2,1)S(1)}, bf16[32,2048]{1,0:T(8,128)(2,1)S(1)}, u32[]{:S(2)}, u32[]{:S(2)}) collective-permute-start(bf16[32,2048]{1,0:T(8,128)(2,1)S(1)} %get-tuple-element.76), channel_id=1, source_target_pairs={{0,1},{1,0},{2,3},{3,2},{4,5},{5,4},{6,7},{7,6},{8,9},{9,8},{10,11... | collective-permute-start | bytes 393224 | tf_op jit(solution)/shard_map/ppermute | solution.py:307
  17.5 3.2 %shard_map.69 = (bf16[2048,1792]{1,0:T(8,128)(2,1)S(1)}, f32[8,128]{1,0:T(8,128)S(1)}) custom-call(bf16[2048,3584]{1,0:T(8,128)(2,1)} %refs_2_.1, bf16[2048,3584]{1,0:T(8,128)(2,1)} %refs_3_.1, f32[8,128]{1,0:T(8,128)S(1)} %get-tuple-element.77.refs_2_), custom_call_target="tpu_custom_call" | custom-call | bytes 1 | tf_op jit(solution)/shard_map/pallas_call | solution.py:41
  21.0 2.1 %collective-permute-start.8 = (bf16[32,2048]{1,0:T(8,128)(2,1)S(1)}, bf16[32,2048]{1,0:T(8,128)(2,1)S(1)}, u32[]{:S(2)}, u32[]{:S(2)}) collective-permute-start(bf16[32,2048]{1,0:T(8,128)(2,1)S(1)} %get-tuple-element.80), channel_id=1, source_target_pairs={{0,1},{1,0},{2,3},{3,2},{4,5},{5,4},{6,7},{7,6},{8,9},{9,8},{10,11... | collective-permute-start | bytes 393224 | tf_op jit(solution)/shard_map/ppermute | solution.py:311
  23.1 3.3 %shard_map.72 = (bf16[2048,1792]{1,0:T(8,128)(2,1)S(1)}, f32[8,128]{1,0:T(8,128)S(1)}) custom-call(bf16[2048,3584]{1,0:T(8,128)(2,1)} %refs_2_.1, bf16[2048,3584]{1,0:T(8,128)(2,1)} %refs_3_.1, f32[8,128]{1,0:T(8,128)S(1)} %get-tuple-element.83.refs_2_), custom_call_target="tpu_custom_call" | custom-call | bytes 1 | tf_op jit(solution)/shard_map/pallas_call | solution.py:41
  26.4 1.4 %shard_map.73 = (bf16[128,2048]{1,0:T(8,128)(2,1)S(1)}, bf16[64,1792]{1,0:T(8,128)(2,1)S(1)}, bf16[64,1792]{1,0:T(8,128)(2,1)S(1)}, f32[8,128]{1,0:T(8,128)S(1)}) custom-call(bf16[32,2048]{1,0:T(8,128)(2,1)S(1)} %get-tuple-element.69.refs_0_, bf16[32,2048]{1,0:T(8,128)(2,1)S(1)} %get-tuple-element.73.refs_1_, ...), custom_call_target="tpu_custom_call" | custom-call | bytes 1 | tf_op jit(solution)/shard_map/pallas_call | solution.py:41
  28.4 1.1 %shard_map.74 = (f32[128,1792]{1,0:T(8,128)S(1)}, f32[8,128]{1,0:T(8,128)S(1)}) custom-call(bf16[128,2048]{1,0:T(8,128)(2,1)S(1)} %get-tuple-element.85.refs_0_, bf16[2048,1792]{1,0:T(8,128)(2,1)S(1)} %get-tuple-element.87.refs_1_, f32[8,128]{1,0:T(8,128)S(1)} %get-tuple-element.88.refs_2_), custom_call_target="tpu_custom_call" | custom-call | bytes 1 | tf_op jit(solution)/shard_map/pallas_call | solution.py:41
  29.9 1.5 %collective-permute-start.11 = (bf16[64,1792]{1,0:T(8,128)(2,1)S(1)}, bf16[64,1792]{1,0:T(8,128)(2,1)S(1)}, u32[]{:S(2)}, u32[]{:S(2)}) collective-permute-start(bf16[64,1792]{1,0:T(8,128)(2,1)S(1)} %get-tuple-element.97), channel_id=1, source_target_pairs={{0,8},{4,12},{8,0},{12,4},{1,9},{5,13},{9,1},{13,5},{2,10},{6,14},... | collective-permute-start | bytes 688136 | tf_op jit(solution)/shard_map/ppermute | solution.py:331
  31.4 3.3 %shard_map.76 = (bf16[64,1792]{1,0:T(8,128)(2,1)S(1)}, bf16[64,1792]{1,0:T(8,128)(2,1)S(1)}, bf16[2048,1792]{1,0:T(8,128)(2,1)S(1)}, f32[8,128]{1,0:T(8,128)S(1)}) custom-call(bf16[128,2048]{1,0:T(8,128)(2,1)S(1)} %get-tuple-element.85.refs_0_, bf16[2048,1792]{1,0:T(8,128)(2,1)S(1)} %get-tuple-element.86.refs_1_, bf16[2048,3584]{1,0:T(8,128)(2,1)} %refs_2_.1, ...), custom_call_target="tpu_custom_call" | custom-call | bytes 1 | tf_op jit(solution)/shard_map/pallas_call | solution.py:41
  34.9 0.6 collective-permute-start.13
  35.6 1.1 %shard_map.77 = (f32[128,1792]{1,0:T(8,128)S(1)}, f32[8,128]{1,0:T(8,128)S(1)}) custom-call(bf16[128,2048]{1,0:T(8,128)(2,1)S(1)} %get-tuple-element.85.refs_0_, bf16[2048,1792]{1,0:T(8,128)(2,1)S(1)} %get-tuple-element.94.refs_1_, f32[8,128]{1,0:T(8,128)S(1)} %get-tuple-element.95.refs_2_), custom_call_target="tpu_custom_call" | custom-call | bytes 1 | tf_op jit(solution)/shard_map/pallas_call | solution.py:41
  37.1 1.2 %slice-done.2 = s8[4194304]{0:T(1024)(128)(4,1)S(1)} async-done(((s8[14680064]{0:T(1024)(128)(4,1)}), s8[4194304]{0:T(1024)(128)(4,1)S(1)}, s32[]{:S(2)}) %slice-start.2) | async-done | bytes 4194328
  40.7 2.7 %collective-permute-done.13.refs_1_ = bf16[64,1792]{1,0:T(8,128)(2,1)S(1)} collective-permute-done((bf16[64,1792]{1,0:T(8,128)(2,1)S(1)}, bf16[64,1792]{1,0:T(8,128)(2,1)S(1)}, u32[]{:S(2)}, u32[]{:S(2)}) %collective-permute-start.13) | collective-permute-done | bytes 229408 | tf_op jit(solution)/shard_map/ppermute | solution.py:331
  43.5 1.3 %collective-permute-start.18 = (bf16[64,896]{1,0:T(8,128)(2,1)S(1)}, bf16[64,896]{1,0:T(8,128)(2,1)S(1)}, u32[]{:S(2)}, u32[]{:S(2)}) collective-permute-start(bf16[64,896]{1,0:T(8,128)(2,1)S(1)} %get-tuple-element.108.refs_2_), channel_id=1, source_target_pairs={{0,8},{4,12},{8,0},{12,4},{1,9},{5,13},{9,1},{13,5},{2,10},{6,14},... | collective-permute-start | bytes 344072 | tf_op jit(solution)/shard_map/ppermute | solution.py:352
  45.4 1.3 %shard_map.83 = (f32[128,2048]{1,0:T(8,128)S(1)}, f32[8,128]{1,0:T(8,128)S(1)}) custom-call(bf16[1792,2048]{1,0:T(8,128)(2,1)S(1)} %get-tuple-element.103.refs_0_, bf16[64,896]{1,0:T(8,128)(2,1)S(1)} %get-tuple-element.104.refs_1_, bf16[64,896]{1,0:T(8,128)(2,1)S(1)} %get-tuple-element.108.refs_2_, bf16[64,896]{1,0:T(8,128)(2,1)S(1)} %collective-permute-done.15.refs_3_, ...), custom_call_target="tpu_custom_call" | custom-call | bytes 1 | tf_op jit(solution)/shard_map/pallas_call | solution.py:41
  46.7 2.4 %collective-permute-done.18.refs_0_.refs_3_ = bf16[64,896]{1,0:T(8,128)(2,1)S(1)} collective-permute-done((bf16[64,896]{1,0:T(8,128)(2,1)S(1)}, bf16[64,896]{1,0:T(8,128)(2,1)S(1)}, u32[]{:S(2)}, u32[]{:S(2)}) %collective-permute-start.18) | collective-permute-done | bytes 114720 | tf_op jit(solution)/shard_map/ppermute | solution.py:352
  49.2 1.3 %collective-permute-done.20.refs_5_ = bf16[64,896]{1,0:T(8,128)(2,1)S(1)} collective-permute-done((bf16[64,896]{1,0:T(8,128)(2,1)S(1)}, bf16[64,896]{1,0:T(8,128)(2,1)S(1)}, u32[]{:S(2)}, u32[]{:S(2)}) %collective-permute-start.20) | collective-permute-done | bytes 114720 | tf_op jit(solution)/shard_map/ppermute | solution.py:359
  50.5 1.3 %shard_map.85 = (f32[2,16,2048]{2,1,0:T(8,128)S(1)}, bf16[2,16,2048]{2,1,0:T(8,128)(2,1)S(1)}, bf16[2,16,2048]{2,1,0:T(8,128)(2,1)S(1)}, bf16[2,16,2048]{2,1,0:T(8,128)(2,1)S(1)}, f32[8,128]{1,0:T(8,128)S(1)}) custom-call(bf16[1792,2048]{1,0:T(8,128)(2,1)S(1)} %get-tuple-element.102.refs_0_, f32[128,2048]{1,0:T(8,128)S(1)} %get-tuple-element.111.refs_1_, ...), custom_call_target="tpu_custom_call" | custom-call | bytes 1 | tf_op jit(solution)/shard_map/pallas_call | solution.py:41
  51.8 2.0 %collective-permute-start.21 = (bf16[2,16,2048]{2,1,0:T(8,128)(2,1)S(1)}, bf16[2,16,2048]{2,1,0:T(8,128)(2,1)S(1)}, u32[]{:S(2)}, u32[]{:S(2)}) collective-permute-start(bf16[2,16,2048]{2,1,0:T(8,128)(2,1)S(1)} %get-tuple-element.117), channel_id=1, source_target_pairs={{0,3},{1,2},{2,1},{3,0},{4,7},{5,6},{6,5},{7,4},{8,11},{9,10},{10,... | collective-permute-start | bytes 393224 | tf_op jit(solution)/shard_map/ppermute | solution.py:372
  53.7 1.3 %collective-permute-start.22 = (bf16[2,16,2048]{2,1,0:T(8,128)(2,1)S(1)}, bf16[2,16,2048]{2,1,0:T(8,128)(2,1)S(1)}, u32[]{:S(2)}, u32[]{:S(2)}) collective-permute-start(bf16[2,16,2048]{2,1,0:T(8,128)(2,1)S(1)} %get-tuple-element.118), channel_id=1, source_target_pairs={{0,2},{1,3},{2,0},{3,1},{4,6},{5,7},{6,4},{7,5},{8,10},{9,11},{10,... | collective-permute-start | bytes 393224 | tf_op jit(solution)/shard_map/ppermute | solution.py:372
  55.0 1.2 %collective-permute-start.23 = (bf16[2,16,2048]{2,1,0:T(8,128)(2,1)S(1)}, bf16[2,16,2048]{2,1,0:T(8,128)(2,1)S(1)}, u32[]{:S(2)}, u32[]{:S(2)}) collective-permute-start(bf16[2,16,2048]{2,1,0:T(8,128)(2,1)S(1)} %get-tuple-element.119), channel_id=1, source_target_pairs={{0,1},{1,0},{2,3},{3,2},{4,5},{5,4},{6,7},{7,6},{8,9},{9,8},{10,11... | collective-permute-start | bytes 393224 | tf_op jit(solution)/shard_map/ppermute | solution.py:372
  56.2 3.9 %collective-permute-done.21.refs_1_ = bf16[2,16,2048]{2,1,0:T(8,128)(2,1)S(1)} collective-permute-done((bf16[2,16,2048]{2,1,0:T(8,128)(2,1)S(1)}, bf16[2,16,2048]{2,1,0:T(8,128)(2,1)S(1)}, u32[]{:S(2)}, u32[]{:S(2)}) %collective-permute-start.21) | collective-permute-done | bytes 131104 | tf_op jit(solution)/shard_map/ppermute | solution.py:372
  60.1 6.9 %collective-permute-done.22.refs_2_ = bf16[2,16,2048]{2,1,0:T(8,128)(2,1)S(1)} collective-permute-done((bf16[2,16,2048]{2,1,0:T(8,128)(2,1)S(1)}, bf16[2,16,2048]{2,1,0:T(8,128)(2,1)S(1)}, u32[]{:S(2)}, u32[]{:S(2)}) %collective-permute-start.22) | collective-permute-done | bytes 131104 | tf_op jit(solution)/shard_map/ppermute | solution.py:372
  67.3 1.3 %collective-permute-start.25 = (bf16[2,4,2048]{2,1,0:T(4,128)(2,1)S(1)}, bf16[2,4,2048]{2,1,0:T(4,128)(2,1)S(1)}, u32[]{:S(2)}, u32[]{:S(2)}) collective-permute-start(bf16[2,4,2048]{2,1,0:T(4,128)(2,1)S(1)} %get-tuple-element.123), channel_id=1, source_target_pairs={{0,8},{4,12},{8,0},{12,4},{1,9},{5,13},{9,1},{13,5},{2,10},{6,14},... | collective-permute-start | bytes 98312 | tf_op jit(solution)/shard_map/ppermute | solution.py:374
  69.2 2.1 %collective-permute-done.25.refs_2_ = bf16[2,4,2048]{2,1,0:T(4,128)(2,1)S(1)} collective-permute-done((bf16[2,4,2048]{2,1,0:T(4,128)(2,1)S(1)}, bf16[2,4,2048]{2,1,0:T(4,128)(2,1)S(1)}, u32[]{:S(2)}, u32[]{:S(2)}) %collective-permute-start.25) | collective-permute-done | bytes 32800 | tf_op jit(solution)/shard_map/ppermute | solution.py:374
  71.3 0.7 collective-permute-done.26.refs_3_
  72.0 0.7 shard_map.87
  (61 shorter events, 6.6 us)
Async XLA Ops:
  1.2 3.2 %collective-permute-start = (bf16[2,8,2048]{2,1,0:T(8,128)(2,1)S(1)}, bf16[2,8,2048]{2,1,0:T(8,128)(2,1)S(1)}, u32[]{:S(2)}, u32[]{:S(2)}) collective-permute-start(bf16[2,8,2048]{2,1,0:T(8,128)(2,1)S(1)} %get-tuple-element.67), channel_id=1, source_target_pairs={{0,4},{4,0},{8,12},{12,8},{1,5},{5,1},{9,13},{13,9},{2,6},{6,2},{1... | collective-permute-start | bytes 196616 | tf_op jit(solution)/shard_map/ppermute | solution.py:292
  1.7 6.6 %collective-permute-start.1 = (bf16[2,8,2048]{2,1,0:T(8,128)(2,1)S(1)}, bf16[2,8,2048]{2,1,0:T(8,128)(2,1)S(1)}, u32[]{:S(2)}, u32[]{:S(2)}) collective-permute-start(bf16[2,8,2048]{2,1,0:T(8,128)(2,1)S(1)} %get-tuple-element.70), channel_id=1, source_target_pairs={{0,8},{4,12},{8,0},{12,4},{1,9},{5,13},{9,1},{13,5},{2,10},{6,14},... | collective-permute-start | bytes 196616 | tf_op jit(solution)/shard_map/ppermute | solution.py:291
  4.3 4.0 %collective-permute-start.2 = (bf16[2,8,2048]{2,1,0:T(8,128)(2,1)S(1)}, bf16[2,8,2048]{2,1,0:T(8,128)(2,1)S(1)}, u32[]{:S(2)}, u32[]{:S(2)}) collective-permute-start(bf16[2,8,2048]{2,1,0:T(8,128)(2,1)S(1)} %get-tuple-element.71), channel_id=1, source_target_pairs={{0,12},{4,8},{8,4},{12,0},{1,13},{5,9},{9,5},{13,1},{2,14},{6,10},... | collective-permute-start | bytes 196616 | tf_op jit(solution)/shard_map/ppermute | solution.py:291
  4.4 10.8 %collective-permute-start.5 = (bf16[32,2048]{1,0:T(8,128)(2,1)S(1)}, bf16[32,2048]{1,0:T(8,128)(2,1)S(1)}, u32[]{:S(2)}, u32[]{:S(2)}) collective-permute-start(bf16[32,2048]{1,0:T(8,128)(2,1)S(1)} %get-tuple-element.69.refs_0_), channel_id=1, source_target_pairs={{0,3},{1,2},{2,1},{3,0},{4,7},{5,6},{6,5},{7,4},{8,11},{9,10},{10,... | collective-permute-start | bytes 393224 | tf_op jit(solution)/shard_map/ppermute | solution.py:302
  8.2 7.6 %collective-permute-start.3 = (bf16[32,2048]{1,0:T(8,128)(2,1)S(1)}, bf16[32,2048]{1,0:T(8,128)(2,1)S(1)}, u32[]{:S(2)}, u32[]{:S(2)}) collective-permute-start(bf16[32,2048]{1,0:T(8,128)(2,1)S(1)} %get-tuple-element.69.refs_0_), channel_id=1, source_target_pairs={{0,1},{1,0},{2,3},{3,2},{4,5},{5,4},{6,7},{7,6},{8,9},{9,8},{10,11... | collective-permute-start | bytes 393224 | tf_op jit(solution)/shard_map/ppermute | solution.py:302
  8.3 12.7 %collective-permute-start.7 = (bf16[32,2048]{1,0:T(8,128)(2,1)S(1)}, bf16[32,2048]{1,0:T(8,128)(2,1)S(1)}, u32[]{:S(2)}, u32[]{:S(2)}) collective-permute-start(bf16[32,2048]{1,0:T(8,128)(2,1)S(1)} %get-tuple-element.73.refs_1_), channel_id=1, source_target_pairs={{0,3},{1,2},{2,1},{3,0},{4,7},{5,6},{6,5},{7,4},{8,11},{9,10},{10,... | collective-permute-start | bytes 393224 | tf_op jit(solution)/shard_map/ppermute | solution.py:304
  12.0 9.0 %collective-permute-start.4 = (bf16[32,2048]{1,0:T(8,128)(2,1)S(1)}, bf16[32,2048]{1,0:T(8,128)(2,1)S(1)}, u32[]{:S(2)}, u32[]{:S(2)}) collective-permute-start(bf16[32,2048]{1,0:T(8,128)(2,1)S(1)} %get-tuple-element.73.refs_1_), channel_id=1, source_target_pairs={{0,1},{1,0},{2,3},{3,2},{4,5},{5,4},{6,7},{7,6},{8,9},{9,8},{10,11... | collective-permute-start | bytes 393224 | tf_op jit(solution)/shard_map/ppermute | solution.py:304
  15.8 10.6 %collective-permute-start.6 = (bf16[32,2048]{1,0:T(8,128)(2,1)S(1)}, bf16[32,2048]{1,0:T(8,128)(2,1)S(1)}, u32[]{:S(2)}, u32[]{:S(2)}) collective-permute-start(bf16[32,2048]{1,0:T(8,128)(2,1)S(1)} %get-tuple-element.76), channel_id=1, source_target_pairs={{0,1},{1,0},{2,3},{3,2},{4,5},{5,4},{6,7},{7,6},{8,9},{9,8},{10,11... | collective-permute-start | bytes 393224 | tf_op jit(solution)/shard_map/ppermute | solution.py:307
  17.5 3.2 %copy-start.2 = (s32[2,128]{1,0:T(2,128)S(1)}, s32[2,128]{1,0:T(2,128)}, u32[]{:S(2)}) copy-start(s32[2,128]{1,0:T(2,128)} %refs_1_.6) | copy-start | bytes 3076
  21.0 5.4 %collective-permute-start.8 = (bf16[32,2048]{1,0:T(8,128)(2,1)S(1)}, bf16[32,2048]{1,0:T(8,128)(2,1)S(1)}, u32[]{:S(2)}, u32[]{:S(2)}) collective-permute-start(bf16[32,2048]{1,0:T(8,128)(2,1)S(1)} %get-tuple-element.80), channel_id=1, source_target_pairs={{0,1},{1,0},{2,3},{3,2},{4,5},{5,4},{6,7},{7,6},{8,9},{9,8},{10,11... | collective-permute-start | bytes 393224 | tf_op jit(solution)/shard_map/ppermute | solution.py:311
  27.9 1.7 %collective-permute-start.9 = (bf16[64,1792]{1,0:T(8,128)(2,1)S(1)}, bf16[64,1792]{1,0:T(8,128)(2,1)S(1)}, u32[]{:S(2)}, u32[]{:S(2)}) collective-permute-start(bf16[64,1792]{1,0:T(8,128)(2,1)S(1)} %get-tuple-element.90), channel_id=1, source_target_pairs={{0,4},{4,0},{8,12},{12,8},{1,5},{5,1},{9,13},{13,9},{2,6},{6,2},{1... | collective-permute-start | bytes 688136 | tf_op jit(solution)/shard_map/ppermute | solution.py:328
  27.9 1.8 %collective-permute-start.10 = (bf16[64,1792]{1,0:T(8,128)(2,1)S(1)}, bf16[64,1792]{1,0:T(8,128)(2,1)S(1)}, u32[]{:S(2)}, u32[]{:S(2)}) collective-permute-start(bf16[64,1792]{1,0:T(8,128)(2,1)S(1)} %get-tuple-element.91), channel_id=1, source_target_pairs={{0,4},{4,0},{8,12},{12,8},{1,5},{5,1},{9,13},{13,9},{2,6},{6,2},{1... | collective-permute-start | bytes 688136 | tf_op jit(solution)/shard_map/ppermute | solution.py:328
  29.9 9.5 %collective-permute-start.11 = (bf16[64,1792]{1,0:T(8,128)(2,1)S(1)}, bf16[64,1792]{1,0:T(8,128)(2,1)S(1)}, u32[]{:S(2)}, u32[]{:S(2)}) collective-permute-start(bf16[64,1792]{1,0:T(8,128)(2,1)S(1)} %get-tuple-element.97), channel_id=1, source_target_pairs={{0,8},{4,12},{8,0},{12,4},{1,9},{5,13},{9,1},{13,5},{2,10},{6,14},... | collective-permute-start | bytes 688136 | tf_op jit(solution)/shard_map/ppermute | solution.py:331
  31.4 5.4 %slice-start = ((s8[14680064]{0:T(1024)(128)(4,1)}), s8[4194304]{0:T(1024)(128)(4,1)S(1)}, s32[]{:S(2)}) async-start(s8[14680064]{0:T(1024)(128)(4,1)} %bitcast), calls=%async_computation | async-start | bytes 8388608
  31.4 5.6 %slice-start.1 = ((s8[14680064]{0:T(1024)(128)(4,1)}), s8[4194304]{0:T(1024)(128)(4,1)S(1)}, s32[]{:S(2)}) async-start(s8[14680064]{0:T(1024)(128)(4,1)} %bitcast), calls=%async_computation.1 | async-start | bytes 8388608
  31.4 6.8 %slice-start.2 = ((s8[14680064]{0:T(1024)(128)(4,1)}), s8[4194304]{0:T(1024)(128)(4,1)S(1)}, s32[]{:S(2)}) async-start(s8[14680064]{0:T(1024)(128)(4,1)} %bitcast), calls=%async_computation.2 | async-start | bytes 8388608
  31.4 7.4 %slice-start.3 = ((s8[14680064]{0:T(1024)(128)(4,1)}), s8[2097152]{0:T(1024)(128)(4,1)S(1)}, s32[]{:S(2)}) async-start(s8[14680064]{0:T(1024)(128)(4,1)} %bitcast), calls=%async_computation.3 | async-start | bytes 4194304
  34.8 4.6 %collective-permute-start.12 = (bf16[64,1792]{1,0:T(8,128)(2,1)S(1)}, bf16[64,1792]{1,0:T(8,128)(2,1)S(1)}, u32[]{:S(2)}, u32[]{:S(2)}) collective-permute-start(bf16[64,1792]{1,0:T(8,128)(2,1)S(1)} %get-tuple-element.98), channel_id=1, source_target_pairs={{0,4},{4,0},{8,12},{12,8},{1,5},{5,1},{9,13},{13,9},{2,6},{6,2},{1... | collective-permute-start | bytes 688136 | tf_op jit(solution)/shard_map/ppermute | solution.py:341
  34.9 8.5 %collective-permute-start.13 = (bf16[64,1792]{1,0:T(8,128)(2,1)S(1)}, bf16[64,1792]{1,0:T(8,128)(2,1)S(1)}, u32[]{:S(2)}, u32[]{:S(2)}) collective-permute-start(bf16[64,1792]{1,0:T(8,128)(2,1)S(1)} %get-tuple-element.105), channel_id=1, source_target_pairs={{0,8},{4,12},{8,0},{12,4},{1,9},{5,13},{9,1},{13,5},{2,10},{6,14},... | collective-permute-start | bytes 688136 | tf_op jit(solution)/shard_map/ppermute | solution.py:331
  35.5 7.9 %collective-permute-start.14 = (bf16[64,1792]{1,0:T(8,128)(2,1)S(1)}, bf16[64,1792]{1,0:T(8,128)(2,1)S(1)}, u32[]{:S(2)}, u32[]{:S(2)}) collective-permute-start(bf16[64,1792]{1,0:T(8,128)(2,1)S(1)} %get-tuple-element.106), channel_id=1, source_target_pairs={{0,4},{4,0},{8,12},{12,8},{1,5},{5,1},{9,13},{13,9},{2,6},{6,2},{1... | collective-permute-start | bytes 688136 | tf_op jit(solution)/shard_map/ppermute | solution.py:341
  39.5 5.8 %collective-permute-start.17 = (bf16[64,896]{1,0:T(8,128)(2,1)S(1)}, bf16[64,896]{1,0:T(8,128)(2,1)S(1)}, u32[]{:S(2)}, u32[]{:S(2)}) collective-permute-start(bf16[64,896]{1,0:T(8,128)(2,1)S(1)} %get-tuple-element.104.refs_1_), channel_id=1, source_target_pairs={{0,8},{4,12},{8,0},{12,4},{1,9},{5,13},{9,1},{13,5},{2,10},{6,14},... | collective-permute-start | bytes 344072 | tf_op jit(solution)/shard_map/ppermute | solution.py:352
  40.1 5.3 %collective-permute-start.15 = (bf16[64,896]{1,0:T(8,128)(2,1)S(1)}, bf16[64,896]{1,0:T(8,128)(2,1)S(1)}, u32[]{:S(2)}, u32[]{:S(2)}) collective-permute-start(bf16[64,896]{1,0:T(8,128)(2,1)S(1)} %get-tuple-element.104.refs_1_), channel_id=1, source_target_pairs={{0,4},{4,0},{8,12},{12,8},{1,5},{5,1},{9,13},{13,9},{2,6},{6,2},{1... | collective-permute-start | bytes 344072 | tf_op jit(solution)/shard_map/ppermute | solution.py:353
  43.5 2.0 %collective-permute-start.16 = (bf16[64,896]{1,0:T(8,128)(2,1)S(1)}, bf16[64,896]{1,0:T(8,128)(2,1)S(1)}, u32[]{:S(2)}, u32[]{:S(2)}) collective-permute-start(bf16[64,896]{1,0:T(8,128)(2,1)S(1)} %get-tuple-element.108.refs_2_), channel_id=1, source_target_pairs={{0,4},{4,0},{8,12},{12,8},{1,5},{5,1},{9,13},{13,9},{2,6},{6,2},{1... | collective-permute-start | bytes 344072 | tf_op jit(solution)/shard_map/ppermute | solution.py:353
  43.5 5.6 %collective-permute-start.18 = (bf16[64,896]{1,0:T(8,128)(2,1)S(1)}, bf16[64,896]{1,0:T(8,128)(2,1)S(1)}, u32[]{:S(2)}, u32[]{:S(2)}) collective-permute-start(bf16[64,896]{1,0:T(8,128)(2,1)S(1)} %get-tuple-element.108.refs_2_), channel_id=1, source_target_pairs={{0,8},{4,12},{8,0},{12,4},{1,9},{5,13},{9,1},{13,5},{2,10},{6,14},... | collective-permute-start | bytes 344072 | tf_op jit(solution)/shard_map/ppermute | solution.py:352
  45.3 3.9 %collective-permute-start.19 = (bf16[64,896]{1,0:T(8,128)(2,1)S(1)}, bf16[64,896]{1,0:T(8,128)(2,1)S(1)}, u32[]{:S(2)}, u32[]{:S(2)}) collective-permute-start(bf16[64,896]{1,0:T(8,128)(2,1)S(1)} %get-tuple-element.112), channel_id=1, source_target_pairs={{0,4},{4,0},{8,12},{12,8},{1,5},{5,1},{9,13},{13,9},{2,6},{6,2},{1... | collective-permute-start | bytes 344072 | tf_op jit(solution)/shard_map/ppermute | solution.py:359
  49.1 1.4 %collective-permute-start.20 = (bf16[64,896]{1,0:T(8,128)(2,1)S(1)}, bf16[64,896]{1,0:T(8,128)(2,1)S(1)}, u32[]{:S(2)}, u32[]{:S(2)}) collective-permute-start(bf16[64,896]{1,0:T(8,128)(2,1)S(1)} %get-tuple-element.114), channel_id=1, source_target_pairs={{0,4},{4,0},{8,12},{12,8},{1,5},{5,1},{9,13},{13,9},{2,6},{6,2},{1... | collective-permute-start | bytes 344072 | tf_op jit(solution)/shard_map/ppermute | solution.py:359
  51.8 8.3 %collective-permute-start.21 = (bf16[2,16,2048]{2,1,0:T(8,128)(2,1)S(1)}, bf16[2,16,2048]{2,1,0:T(8,128)(2,1)S(1)}, u32[]{:S(2)}, u32[]{:S(2)}) collective-permute-start(bf16[2,16,2048]{2,1,0:T(8,128)(2,1)S(1)} %get-tuple-element.117), channel_id=1, source_target_pairs={{0,3},{1,2},{2,1},{3,0},{4,7},{5,6},{6,5},{7,4},{8,11},{9,10},{10,... | collective-permute-start | bytes 393224 | tf_op jit(solution)/shard_map/ppermute | solution.py:372
  53.7 13.3 %collective-permute-start.22 = (bf16[2,16,2048]{2,1,0:T(8,128)(2,1)S(1)}, bf16[2,16,2048]{2,1,0:T(8,128)(2,1)S(1)}, u32[]{:S(2)}, u32[]{:S(2)}) collective-permute-start(bf16[2,16,2048]{2,1,0:T(8,128)(2,1)S(1)} %get-tuple-element.118), channel_id=1, source_target_pairs={{0,2},{1,3},{2,0},{3,1},{4,6},{5,7},{6,4},{7,5},{8,10},{9,11},{10,... | collective-permute-start | bytes 393224 | tf_op jit(solution)/shard_map/ppermute | solution.py:372
  55.0 12.0 %collective-permute-start.23 = (bf16[2,16,2048]{2,1,0:T(8,128)(2,1)S(1)}, bf16[2,16,2048]{2,1,0:T(8,128)(2,1)S(1)}, u32[]{:S(2)}, u32[]{:S(2)}) collective-permute-start(bf16[2,16,2048]{2,1,0:T(8,128)(2,1)S(1)} %get-tuple-element.119), channel_id=1, source_target_pairs={{0,1},{1,0},{2,3},{3,2},{4,5},{5,4},{6,7},{7,6},{8,9},{9,8},{10,11... | collective-permute-start | bytes 393224 | tf_op jit(solution)/shard_map/ppermute | solution.py:372
  67.2 1.9 %collective-permute-start.24 = (bf16[2,4,2048]{2,1,0:T(4,128)(2,1)S(1)}, bf16[2,4,2048]{2,1,0:T(4,128)(2,1)S(1)}, u32[]{:S(2)}, u32[]{:S(2)}) collective-permute-start(bf16[2,4,2048]{2,1,0:T(4,128)(2,1)S(1)} %get-tuple-element.122), channel_id=1, source_target_pairs={{0,4},{4,0},{8,12},{12,8},{1,5},{5,1},{9,13},{13,9},{2,6},{6,2},{1... | collective-permute-start | bytes 98312 | tf_op jit(solution)/shard_map/ppermute | solution.py:374
  67.3 4.0 %collective-permute-start.25 = (bf16[2,4,2048]{2,1,0:T(4,128)(2,1)S(1)}, bf16[2,4,2048]{2,1,0:T(4,128)(2,1)S(1)}, u32[]{:S(2)}, u32[]{:S(2)}) collective-permute-start(bf16[2,4,2048]{2,1,0:T(4,128)(2,1)S(1)} %get-tuple-element.123), channel_id=1, source_target_pairs={{0,8},{4,12},{8,0},{12,4},{1,9},{5,13},{9,1},{13,5},{2,10},{6,14},... | collective-permute-start | bytes 98312 | tf_op jit(solution)/shard_map/ppermute | solution.py:374
  68.6 3.3 %collective-permute-start.26 = (bf16[2,4,2048]{2,1,0:T(4,128)(2,1)S(1)}, bf16[2,4,2048]{2,1,0:T(4,128)(2,1)S(1)}, u32[]{:S(2)}, u32[]{:S(2)}) collective-permute-start(bf16[2,4,2048]{2,1,0:T(4,128)(2,1)S(1)} %get-tuple-element.124), channel_id=1, source_target_pairs={{0,12},{4,8},{8,4},{12,0},{1,13},{5,9},{9,5},{13,1},{2,14},{6,10},... | collective-permute-start | bytes 98312 | tf_op jit(solution)/shard_map/ppermute | solution.py:374
  (2 other events, 4.2 us)

commit v7 on v5

--- a/solution.py
+++ b/solution.py
@@ -16,6 +16,7 @@
 F32 = jnp.float32
 MIB = 2**20
 PIECES = 2
+CUTS = 2
 X1 = ((0, 1), (1, 0), (2, 3), (3, 2))
 X2 = ((0, 2), (1, 3), (2, 0), (3, 1))
 X3 = ((0, 3), (1, 2), (2, 1), (3, 0))
@@ -172,10 +173,6 @@
         copy.wait()
 
 
-def meet(token):
-    return lax.ppermute(token, "row", X1)
-
-
 def stack_body(ins, _, outs, __):
     for i, piece in enumerate(ins):
         joined = jnp.concatenate([piece[step].astype(F32) for step in range(2)], axis=0)
@@ -234,18 +231,19 @@
 
 
 def down_part_body(ins, _, outs, __):
-    own_ref, core_ref, w_ref = ins
+    w_ref, own_ref, core_ref = ins
     height = w_ref.shape[0] // 2
     total = jnp.dot(own_ref[...], w_ref[:height, :], preferred_element_type=F32)
     outs[0][...] = total + jnp.dot(core_ref[...], w_ref[height:, :], preferred_element_type=F32)
 
 
 def down_rest_body(ins, _, outs, __):
-    y_ref, w_ref, part_ref, yd_refs = *ins[:3], ins[3:]
+    w_ref, part_ref, y_ref = ins[:3]
     rows = outs[0].shape[0]
     height = w_ref.shape[0] // 2
     total = part_ref[...] + jnp.dot(y_ref[...], w_ref[:height, :], preferred_element_type=F32)
-    total = total + jnp.dot(load_rows(yd_refs).astype(BF), w_ref[height:, :], preferred_element_type=F32)
+    yd = load_rows(ins[3:]).astype(BF)
+    total = total + jnp.dot(yd, w_ref[height:, :], preferred_element_type=F32)
     for i, out in enumerate(outs):
         out[...] = total[i * rows : (i + 1) * rows].astype(out.dtype)
 
@@ -298,19 +296,15 @@
     block = like((4 * slots, width))
     near_block, token = run(stack_body, (block,), (own, core), token)
     near_sent = [lax.ppermute(near_block, "col", X3), lax.ppermute(near_block, "col", X1)]
-    token = meet(token)
     far_block, token = run(stack_body, (block,), (y, yd), token)
     far_sent = [lax.ppermute(far_block, "col", X3), lax.ppermute(far_block, "col", X1)]
-    token = meet(token)
     token = bring(1, 1, token)
     passed, token = run(after_body, (block,), (near_sent[0], near_sent[1]), token)
     near_sent.append(lax.ppermute(passed, "col", X1))
-    token = meet(token)
     token = bring(1, 0, token)
     pick, token = run(pick_body, (like((steps * rows, steps * assign.shape[1])),), (counts, assign), token)
     passed, token = run(after_body, (block,), (far_sent[0], far_sent[1]), token)
     far_sent.append(lax.ppermute(passed, "col", X1))
-    token = meet(token)
     token = bring(0, 1, token)
     pieces = []
     for dz in range(4):
@@ -331,7 +325,6 @@
     own_far, token = run(dot_body, (wide,), (batch, *quarters[1, 0]), token)
     *sends, token = run(far_body, (like((rows, 2 * units)),) * steps, (own_far,) + cores, token)
     gots = [lax.ppermute(send, "row", X2) for send in sends]
-    token = meet(token)
     last = pltpu.VMEM((gate_w.shape[0], gate_w.shape[1] // 2), BF)
     *out, last, token = run(
         functools.partial(dot_and_quarter_body, 0, 0),
@@ -344,7 +337,7 @@
     cores = tuple(lax.ppermute(o, "row", X1) for o in out)
     own_near, token = run(dot_body, (wide,), (batch, last), token)
     down_near, token = down_rows(0, token)
-    hidden, sums = [], []
+    hidden = []
 
     def activate(step, token):
         each = PIECES // steps
@@ -356,27 +349,37 @@
         hidden.append((result, lax.ppermute(result, "row", X1), y))
         return token
 
+    def shared(step, token):
+        cut = (like((rows // CUTS, units)),) * CUTS
+        *passed, token = run(after_body, cut, (hidden[step][2],), token)
+        return tuple(lax.ppermute(p, "row", X1) for p in passed), token
+
+    def shared(step, token):
+        cut = (like((rows // CUTS, units)),) * CUTS
+        *passed, token = run(after_body, cut, (hidden[step][2],), token)
+        return tuple(lax.ppermute(p, "row", X1) for p in passed), token
+
     def down_part(step, token):
-        return run(down_part_body, (like((rows, width), F32),), hidden[step][:2] + (down_near,), token)
-
-    def down_rest(step, part_sum, token):
-        cut = (like((16, units)),) * (rows // 16)
-        *passed, token = run(after_body, cut, (hidden[step][2],), token)
-        passed = tuple(lax.ppermute(p, "row", X1) for p in passed)
+        own, core, _ = hidden[step]
+        return run(down_part_body, (like((rows, width), F32),), (down_near, own, core), token)
+
+    def down_rest(step, part_sum, yd, token):
         outs = (like((part, width), F32),) + (like((part, width)),) * 3
-        operands = (hidden[step][2], down_far, part_sum) + passed
+        operands = (down_far, part_sum, hidden[step][2]) + yd
         keep, send1, send2, send3, token = run(down_rest_body, outs, operands, token)
-        got = [lax.ppermute(s, "col", x) for s, x in ((send3, X3), (send2, X2), (send1, X1))]
-        sums.extend([keep] + got)
-        return token
+        sent = ((send3, X3), (send2, X2), (send1, X1))
+        return (keep,) + tuple(lax.ppermute(s, "col", x) for s, x in sent), token
 
     token = activate(0, token)
     down_far, token = down_rows(1, token)
     part0, token = down_part(0, token)
     token = activate(1, token)
-    token = down_rest(0, part0, token)
-    part1, token = down_part(1, meet(token))
-    token = down_rest(1, part1, token)
+    yd0, token = shared(0, token)
+    sums0, token = down_rest(0, part0, yd0, token)
+    part1, token = down_part(1, token)
+    yd1, token = shared(1, token)
+    sums1, token = down_rest(1, part1, yd1, token)
+    sums = sums0 + sums1
     own, core, y, yd, token = run(owner_body, (like((steps, MEAN, width)),) * 4, tuple(sums), token)
     blocks = (own, lax.ppermute(core, "row", X1), lax.ppermute(y, "row", X2), lax.ppermute(yd, "row", X3))
     result, _ = run(output_body, (like((steps, MEAN, 4 * width)),), blocks, token)

time: 74.6 us -> 70.6 us (0.946)
  waiting for transfers between devices: 13.9 us -> 10.1 us
    ppermute x14 -> x4, waiting for transfers between devices: 6.24 us -> 0.9 us  [shared(): return (tuple((lax.ppermute(p, 'row', X1) for p in passed)), token)]
    ppermute x14 -> x4, starting transfers between devices: 2.66 us -> 1.14 us  [shared(): return (tuple((lax.ppermute(p, 'row', X1) for p in passed)), token)]
    ppermute x1, starting transfers between devices: 1.03 us -> 2.12 us  [near_plan(): far_sent.append(lax.ppermute(passed, 'col', X1))]
    ppermute x1, starting transfers between devices: 2.59 us -> 3.67 us  [near_plan(): lax.ppermute(far_block, 'col', X3)]
  transfers between devices with their start and end apart: 42 -> 32, of which waited for: 15 -> 12; matrix products, arithmetic and copies ran while one was open for 0% -> 0% of each run, Pallas kernels for 30% -> 32%
where the time goes in v7:
time: 70.6 us; the launch traced here: 70.5 us
  starting transfers between devices  31.8 us (45%)
  Pallas kernels  25.2 us (36%)
  waiting for transfers between devices  10.1 us (14%)
  local copies, waits for them, and re-layouts  3.01 us (4%)
    pallas_call x26, Pallas kernels, run(): pl.pallas_call(wrapped, out_shape=outs, in_specs=[spec or vmem] * count +...  25.2 us
    ppermute x6, starting transfers between devices, down_rest(): lax.ppermute(s, 'col', x)  8.9 us
    ppermute x6, waiting for transfers between devices, down_rest(): lax.ppermute(s, 'col', x)  4.35 us
    ppermute x1, starting transfers between devices, near_plan(): lax.ppermute(near_block, 'col', X3)  3.87 us
    ppermute x1, starting transfers between devices, near_plan(): lax.ppermute(far_block, 'col', X3)  3.67 us
    unnamed x14, local copies, waits for them, and re-layouts  3.01 us
    ppermute x2, starting transfers between devices, near_plan(): y, yd = (lax.ppermute(y, 'row', X2), lax.ppermute(yd, 'row', X3))  2.66 us
    ppermute x2, starting transfers between devices, activate(): y = lax.ppermute(result, 'row', X2)  2.25 us
  transfers between devices with their start and end apart: 32, of which 12 were waited for; matrix products, arithmetic and copies ran while one was open for 0% of the time, Pallas kernels for 32%

profile of v7, /device:TPU:0, one launch (start us, length us, event | category | flops | bytes accessed | tf_op | source)
XLA Modules:
  0.0 70.5 jit_solution(15164918639017320513)
XLA Ops:
  0.0 0.9 %copy-done = bf16[2,8,8192]{2,1,0:T(8,128)(2,1)S(1)} copy-done((bf16[2,8,8192]{2,1,0:T(8,128)(2,1)S(1)}, bf16[2,8,8192]{2,1,0:T(8,128)(2,1)}, u32[]{:S(2)}) %copy-start) | copy-done | bytes 262168
  1.7 2.6 %collective-permute-start.1 = (bf16[2,8,2048]{2,1,0:T(8,128)(2,1)S(1)}, bf16[2,8,2048]{2,1,0:T(8,128)(2,1)S(1)}, u32[]{:S(2)}, u32[]{:S(2)}) collective-permute-start(bf16[2,8,2048]{2,1,0:T(8,128)(2,1)S(1)} %get-tuple-element.79), channel_id=1, source_target_pairs={{0,8},{4,12},{8,0},{12,4},{1,9},{5,13},{9,1},{13,5},{2,10},{6,14},... | collective-permute-start | bytes 196616 | tf_op jit(solution)/shard_map/ppermute | solution.py:287
  4.4 3.9 %collective-permute-start.5 = (bf16[32,2048]{1,0:T(8,128)(2,1)S(1)}, bf16[32,2048]{1,0:T(8,128)(2,1)S(1)}, u32[]{:S(2)}, u32[]{:S(2)}) collective-permute-start(bf16[32,2048]{1,0:T(8,128)(2,1)S(1)} %get-tuple-element.78.refs_0_), channel_id=1, source_target_pairs={{0,3},{1,2},{2,1},{3,0},{4,7},{5,6},{6,5},{7,4},{8,11},{9,10},{10,... | collective-permute-start | bytes 393224 | tf_op jit(solution)/shard_map/ppermute | solution.py:298
  8.3 3.7 %collective-permute-start.7 = (bf16[32,2048]{1,0:T(8,128)(2,1)S(1)}, bf16[32,2048]{1,0:T(8,128)(2,1)S(1)}, u32[]{:S(2)}, u32[]{:S(2)}) collective-permute-start(bf16[32,2048]{1,0:T(8,128)(2,1)S(1)} %get-tuple-element.82.refs_1_), channel_id=1, source_target_pairs={{0,3},{1,2},{2,1},{3,0},{4,7},{5,6},{6,5},{7,4},{8,11},{9,10},{10,... | collective-permute-start | bytes 393224 | tf_op jit(solution)/shard_map/ppermute | solution.py:300
  12.0 3.2 %shard_map.67 = (bf16[2048,1792]{1,0:T(8,128)(2,1)S(1)}, f32[8,128]{1,0:T(8,128)S(1)}) custom-call(bf16[2048,3584]{1,0:T(8,128)(2,1)} %refs_2_.1, bf16[2048,3584]{1,0:T(8,128)(2,1)} %refs_3_.1, f32[8,128]{1,0:T(8,128)S(1)} %get-tuple-element.83.refs_2_), custom_call_target="tpu_custom_call" | custom-call | bytes 1 | tf_op jit(solution)/shard_map/pallas_call | solution.py:41
  15.8 1.6 %collective-permute-start.6 = (bf16[32,2048]{1,0:T(8,128)(2,1)S(1)}, bf16[32,2048]{1,0:T(8,128)(2,1)S(1)}, u32[]{:S(2)}, u32[]{:S(2)}) collective-permute-start(bf16[32,2048]{1,0:T(8,128)(2,1)S(1)} %get-tuple-element.85), channel_id=1, source_target_pairs={{0,1},{1,0},{2,3},{3,2},{4,5},{5,4},{6,7},{7,6},{8,9},{9,8},{10,11... | collective-permute-start | bytes 393224 | tf_op jit(solution)/shard_map/ppermute | solution.py:303
  17.5 3.2 %shard_map.69 = (bf16[2048,1792]{1,0:T(8,128)(2,1)S(1)}, f32[8,128]{1,0:T(8,128)S(1)}) custom-call(bf16[2048,3584]{1,0:T(8,128)(2,1)} %refs_2_.1, bf16[2048,3584]{1,0:T(8,128)(2,1)} %refs_3_.1, f32[8,128]{1,0:T(8,128)S(1)} %get-tuple-element.86.refs_2_), custom_call_target="tpu_custom_call" | custom-call | bytes 1 | tf_op jit(solution)/shard_map/pallas_call | solution.py:41
  21.0 2.1 %collective-permute-start.8 = (bf16[32,2048]{1,0:T(8,128)(2,1)S(1)}, bf16[32,2048]{1,0:T(8,128)(2,1)S(1)}, u32[]{:S(2)}, u32[]{:S(2)}) collective-permute-start(bf16[32,2048]{1,0:T(8,128)(2,1)S(1)} %get-tuple-element.89), channel_id=1, source_target_pairs={{0,1},{1,0},{2,3},{3,2},{4,5},{5,4},{6,7},{7,6},{8,9},{9,8},{10,11... | collective-permute-start | bytes 393224 | tf_op jit(solution)/shard_map/ppermute | solution.py:307
  23.1 3.3 %shard_map.72 = (bf16[2048,1792]{1,0:T(8,128)(2,1)S(1)}, f32[8,128]{1,0:T(8,128)S(1)}) custom-call(bf16[2048,3584]{1,0:T(8,128)(2,1)} %refs_2_.1, bf16[2048,3584]{1,0:T(8,128)(2,1)} %refs_3_.1, f32[8,128]{1,0:T(8,128)S(1)} %get-tuple-element.92.refs_2_), custom_call_target="tpu_custom_call" | custom-call | bytes 1 | tf_op jit(solution)/shard_map/pallas_call | solution.py:41
  26.4 1.4 %shard_map.73 = (bf16[128,2048]{1,0:T(8,128)(2,1)S(1)}, bf16[64,1792]{1,0:T(8,128)(2,1)S(1)}, bf16[64,1792]{1,0:T(8,128)(2,1)S(1)}, f32[8,128]{1,0:T(8,128)S(1)}) custom-call(bf16[32,2048]{1,0:T(8,128)(2,1)S(1)} %get-tuple-element.78.refs_0_, bf16[32,2048]{1,0:T(8,128)(2,1)S(1)} %get-tuple-element.82.refs_1_, ...), custom_call_target="tpu_custom_call" | custom-call | bytes 1 | tf_op jit(solution)/shard_map/pallas_call | solution.py:41
  28.4 1.1 %shard_map.74 = (f32[128,1792]{1,0:T(8,128)S(1)}, f32[8,128]{1,0:T(8,128)S(1)}) custom-call(bf16[128,2048]{1,0:T(8,128)(2,1)S(1)} %get-tuple-element.94.refs_0_, bf16[2048,1792]{1,0:T(8,128)(2,1)S(1)} %get-tuple-element.96.refs_1_, f32[8,128]{1,0:T(8,128)S(1)} %get-tuple-element.97.refs_2_), custom_call_target="tpu_custom_call" | custom-call | bytes 1 | tf_op jit(solution)/shard_map/pallas_call | solution.py:41
  29.9 1.5 %collective-permute-start.11 = (bf16[64,1792]{1,0:T(8,128)(2,1)S(1)}, bf16[64,1792]{1,0:T(8,128)(2,1)S(1)}, u32[]{:S(2)}, u32[]{:S(2)}) collective-permute-start(bf16[64,1792]{1,0:T(8,128)(2,1)S(1)} %get-tuple-element.106), channel_id=1, source_target_pairs={{0,8},{4,12},{8,0},{12,4},{1,9},{5,13},{9,1},{13,5},{2,10},{6,14},... | collective-permute-start | bytes 688136 | tf_op jit(solution)/shard_map/ppermute | solution.py:327
  31.4 3.3 %shard_map.76 = (bf16[64,1792]{1,0:T(8,128)(2,1)S(1)}, bf16[64,1792]{1,0:T(8,128)(2,1)S(1)}, bf16[2048,1792]{1,0:T(8,128)(2,1)S(1)}, f32[8,128]{1,0:T(8,128)S(1)}) custom-call(bf16[128,2048]{1,0:T(8,128)(2,1)S(1)} %get-tuple-element.94.refs_0_, bf16[2048,1792]{1,0:T(8,128)(2,1)S(1)} %get-tuple-element.95.refs_1_, bf16[2048,3584]{1,0:T(8,128)(2,1)} %refs_2_.1, ...), custom_call_target="tpu_custom_call" | custom-call | bytes 1 | tf_op jit(solution)/shard_map/pallas_call | solution.py:41
  35.6 1.1 %shard_map.77 = (f32[128,1792]{1,0:T(8,128)S(1)}, f32[8,128]{1,0:T(8,128)S(1)}) custom-call(bf16[128,2048]{1,0:T(8,128)(2,1)S(1)} %get-tuple-element.94.refs_0_, bf16[2048,1792]{1,0:T(8,128)(2,1)S(1)} %get-tuple-element.103.refs_1_, f32[8,128]{1,0:T(8,128)S(1)} %get-tuple-element.104.refs_2_), custom_call_target="tpu_custom_call" | custom-call | bytes 1 | tf_op jit(solution)/shard_map/pallas_call | solution.py:41
  37.1 1.2 %slice-done.2 = s8[4194304]{0:T(1024)(128)(4,1)S(1)} async-done(((s8[14680064]{0:T(1024)(128)(4,1)}), s8[4194304]{0:T(1024)(128)(4,1)S(1)}, s32[]{:S(2)}) %slice-start.2) | async-done | bytes 4194328
  40.9 1.4 %shard_map.81 = (f32[64,2048]{1,0:T(8,128)S(1)}, f32[8,128]{1,0:T(8,128)S(1)}) custom-call(bf16[1792,2048]{1,0:T(8,128)(2,1)S(1)} %get-tuple-element.112.refs_0_, bf16[64,896]{1,0:T(8,128)(2,1)S(1)} %get-tuple-element.113.refs_1_, bf16[64,896]{1,0:T(8,128)(2,1)S(1)} %collective-permute-done.13.refs_2_, f32[8,128]{1,0:T(8,128)S(1)} %get-tuple-element.114.refs_3_), custom_call_target="tpu_custom_call" | custom-call | bytes 1 | tf_op jit(solution)/shard_map/pallas_call | solution.py:41
  43.2 1.6 %collective-permute-start.23 = (bf16[64,896]{1,0:T(8,128)(2,1)S(1)}, bf16[64,896]{1,0:T(8,128)(2,1)S(1)}, u32[]{:S(2)}, u32[]{:S(2)}) collective-permute-start(bf16[64,896]{1,0:T(8,128)(2,1)S(1)} %get-tuple-element.127.refs_1_), channel_id=1, source_target_pairs={{0,8},{4,12},{8,0},{12,4},{1,9},{5,13},{9,1},{13,5},{2,10},{6,14},... | collective-permute-start | bytes 344072 | tf_op jit(solution)/shard_map/ppermute | solution.py:348
  45.9 0.7 %collective-permute-done.17.refs_3_ = bf16[32,896]{1,0:T(8,128)(2,1)S(1)} collective-permute-done((bf16[32,896]{1,0:T(8,128)(2,1)S(1)}, bf16[32,896]{1,0:T(8,128)(2,1)S(1)}, u32[]{:S(2)}, u32[]{:S(2)}) %collective-permute-start.17) | collective-permute-done | bytes 57376 | tf_op jit(solution)/shard_map/ppermute | solution.py:360
  46.8 1.4 %shard_map.84 = (f32[16,2048]{1,0:T(8,128)S(1)}, bf16[16,2048]{1,0:T(8,128)(2,1)S(1)}, bf16[16,2048]{1,0:T(8,128)(2,1)S(1)}, bf16[16,2048]{1,0:T(8,128)(2,1)S(1)}, f32[8,128]{1,0:T(8,128)S(1)}) custom-call(bf16[1792,2048]{1,0:T(8,128)(2,1)S(1)} %get-tuple-element.111.refs_0_, f32[64,2048]{1,0:T(8,128)S(1)} %get-tuple-element.115.refs_1_, ...), custom_call_target="tpu_custom_call" | custom-call | bytes 1 | tf_op jit(solution)/shard_map/pallas_call | solution.py:41
  48.2 1.9 %collective-permute-start.19 = (bf16[16,2048]{1,0:T(8,128)(2,1)S(1)}, bf16[16,2048]{1,0:T(8,128)(2,1)S(1)}, u32[]{:S(2)}, u32[]{:S(2)}) collective-permute-start(bf16[16,2048]{1,0:T(8,128)(2,1)S(1)} %get-tuple-element.124), channel_id=1, source_target_pairs={{0,3},{1,2},{2,1},{3,0},{4,7},{5,6},{6,5},{7,4},{8,11},{9,10},{10,... | collective-permute-start | bytes 196616 | tf_op jit(solution)/shard_map/ppermute | solution.py:371
  50.2 1.4 %shard_map.85 = (f32[64,2048]{1,0:T(8,128)S(1)}, f32[8,128]{1,0:T(8,128)S(1)}) custom-call(bf16[1792,2048]{1,0:T(8,128)(2,1)S(1)} %get-tuple-element.112.refs_0_, bf16[64,896]{1,0:T(8,128)(2,1)S(1)} %get-tuple-element.127.refs_1_, bf16[64,896]{1,0:T(8,128)(2,1)S(1)} %collective-permute-done.22.refs_2_, f32[8,128]{1,0:T(8,128)S(1)} %get-tuple-element.128.refs_3_), custom_call_target="tpu_custom_call" | custom-call | bytes 1 | tf_op jit(solution)/shard_map/pallas_call | solution.py:41
  52.2 1.3 %collective-permute-start.20 = (bf16[16,2048]{1,0:T(8,128)(2,1)S(1)}, bf16[16,2048]{1,0:T(8,128)(2,1)S(1)}, u32[]{:S(2)}, u32[]{:S(2)}) collective-permute-start(bf16[16,2048]{1,0:T(8,128)(2,1)S(1)} %get-tuple-element.125), channel_id=1, source_target_pairs={{0,2},{1,3},{2,0},{3,1},{4,6},{5,7},{6,4},{7,5},{8,10},{9,11},{10,... | collective-permute-start | bytes 196616 | tf_op jit(solution)/shard_map/ppermute | solution.py:371
  53.5 1.2 %collective-permute-start.21 = (bf16[16,2048]{1,0:T(8,128)(2,1)S(1)}, bf16[16,2048]{1,0:T(8,128)(2,1)S(1)}, u32[]{:S(2)}, u32[]{:S(2)}) collective-permute-start(bf16[16,2048]{1,0:T(8,128)(2,1)S(1)} %get-tuple-element.126), channel_id=1, source_target_pairs={{0,1},{1,0},{2,3},{3,2},{4,5},{5,4},{6,7},{7,6},{8,9},{9,8},{10,11... | collective-permute-start | bytes 196616 | tf_op jit(solution)/shard_map/ppermute | solution.py:371
  54.7 1.4 %shard_map.87 = (f32[16,2048]{1,0:T(8,128)S(1)}, bf16[16,2048]{1,0:T(8,128)(2,1)S(1)}, bf16[16,2048]{1,0:T(8,128)(2,1)S(1)}, bf16[16,2048]{1,0:T(8,128)(2,1)S(1)}, f32[8,128]{1,0:T(8,128)S(1)}) custom-call(bf16[1792,2048]{1,0:T(8,128)(2,1)S(1)} %get-tuple-element.111.refs_0_, f32[64,2048]{1,0:T(8,128)S(1)} %get-tuple-element.129.refs_1_, ...), custom_call_target="tpu_custom_call" | custom-call | bytes 1 | tf_op jit(solution)/shard_map/pallas_call | solution.py:41
  56.1 1.9 %collective-permute-start.26 = (bf16[16,2048]{1,0:T(8,128)(2,1)S(1)}, bf16[16,2048]{1,0:T(8,128)(2,1)S(1)}, u32[]{:S(2)}, u32[]{:S(2)}) collective-permute-start(bf16[16,2048]{1,0:T(8,128)(2,1)S(1)} %get-tuple-element.135), channel_id=1, source_target_pairs={{0,3},{1,2},{2,1},{3,0},{4,7},{5,6},{6,5},{7,4},{8,11},{9,10},{10,... | collective-permute-start | bytes 196616 | tf_op jit(solution)/shard_map/ppermute | solution.py:371
  58.5 2.1 %collective-permute-start.28 = (bf16[16,2048]{1,0:T(8,128)(2,1)S(1)}, bf16[16,2048]{1,0:T(8,128)(2,1)S(1)}, u32[]{:S(2)}, u32[]{:S(2)}) collective-permute-start(bf16[16,2048]{1,0:T(8,128)(2,1)S(1)} %get-tuple-element.137), channel_id=1, source_target_pairs={{0,1},{1,0},{2,3},{3,2},{4,5},{5,4},{6,7},{7,6},{8,9},{9,8},{10,11... | collective-permute-start | bytes 196616 | tf_op jit(solution)/shard_map/ppermute | solution.py:371
  60.6 2.0 %collective-permute-done.26.refs_5_ = bf16[16,2048]{1,0:T(8,128)(2,1)S(1)} collective-permute-done((bf16[16,2048]{1,0:T(8,128)(2,1)S(1)}, bf16[16,2048]{1,0:T(8,128)(2,1)S(1)}, u32[]{:S(2)}, u32[]{:S(2)}) %collective-permute-start.26) | collective-permute-done | bytes 65568 | tf_op jit(solution)/shard_map/ppermute | solution.py:371
  62.6 2.3 %collective-permute-done.27.refs_6_ = bf16[16,2048]{1,0:T(8,128)(2,1)S(1)} collective-permute-done((bf16[16,2048]{1,0:T(8,128)(2,1)S(1)}, bf16[16,2048]{1,0:T(8,128)(2,1)S(1)}, u32[]{:S(2)}, u32[]{:S(2)}) %collective-permute-start.27) | collective-permute-done | bytes 65568 | tf_op jit(solution)/shard_map/ppermute | solution.py:371
  65.2 1.2 %collective-permute-start.30 = (bf16[2,4,2048]{2,1,0:T(4,128)(2,1)S(1)}, bf16[2,4,2048]{2,1,0:T(4,128)(2,1)S(1)}, u32[]{:S(2)}, u32[]{:S(2)}) collective-permute-start(bf16[2,4,2048]{2,1,0:T(4,128)(2,1)S(1)} %get-tuple-element.141), channel_id=1, source_target_pairs={{0,8},{4,12},{8,0},{12,4},{1,9},{5,13},{9,1},{13,5},{2,10},{6,14},... | collective-permute-start | bytes 98312 | tf_op jit(solution)/shard_map/ppermute | solution.py:384
  66.4 0.7 collective-permute-start.31
  67.1 2.1 %collective-permute-done.30.refs_2_ = bf16[2,4,2048]{2,1,0:T(4,128)(2,1)S(1)} collective-permute-done((bf16[2,4,2048]{2,1,0:T(4,128)(2,1)S(1)}, bf16[2,4,2048]{2,1,0:T(4,128)(2,1)S(1)}, u32[]{:S(2)}, u32[]{:S(2)}) %collective-permute-start.30) | collective-permute-done | bytes 32800 | tf_op jit(solution)/shard_map/ppermute | solution.py:384
  69.8 0.7 shard_map.89
  (73 shorter events, 10.3 us)
Async XLA Ops:
  1.2 3.2 %collective-permute-start = (bf16[2,8,2048]{2,1,0:T(8,128)(2,1)S(1)}, bf16[2,8,2048]{2,1,0:T(8,128)(2,1)S(1)}, u32[]{:S(2)}, u32[]{:S(2)}) collective-permute-start(bf16[2,8,2048]{2,1,0:T(8,128)(2,1)S(1)} %get-tuple-element.76), channel_id=1, source_target_pairs={{0,4},{4,0},{8,12},{12,8},{1,5},{5,1},{9,13},{13,9},{2,6},{6,2},{1... | collective-permute-start | bytes 196616 | tf_op jit(solution)/shard_map/ppermute | solution.py:288
  1.7 6.6 %collective-permute-start.1 = (bf16[2,8,2048]{2,1,0:T(8,128)(2,1)S(1)}, bf16[2,8,2048]{2,1,0:T(8,128)(2,1)S(1)}, u32[]{:S(2)}, u32[]{:S(2)}) collective-permute-start(bf16[2,8,2048]{2,1,0:T(8,128)(2,1)S(1)} %get-tuple-element.79), channel_id=1, source_target_pairs={{0,8},{4,12},{8,0},{12,4},{1,9},{5,13},{9,1},{13,5},{2,10},{6,14},... | collective-permute-start | bytes 196616 | tf_op jit(solution)/shard_map/ppermute | solution.py:287
  4.3 4.0 %collective-permute-start.2 = (bf16[2,8,2048]{2,1,0:T(8,128)(2,1)S(1)}, bf16[2,8,2048]{2,1,0:T(8,128)(2,1)S(1)}, u32[]{:S(2)}, u32[]{:S(2)}) collective-permute-start(bf16[2,8,2048]{2,1,0:T(8,128)(2,1)S(1)} %get-tuple-element.80), channel_id=1, source_target_pairs={{0,12},{4,8},{8,4},{12,0},{1,13},{5,9},{9,5},{13,1},{2,14},{6,10},... | collective-permute-start | bytes 196616 | tf_op jit(solution)/shard_map/ppermute | solution.py:287
  4.4 10.8 %collective-permute-start.5 = (bf16[32,2048]{1,0:T(8,128)(2,1)S(1)}, bf16[32,2048]{1,0:T(8,128)(2,1)S(1)}, u32[]{:S(2)}, u32[]{:S(2)}) collective-permute-start(bf16[32,2048]{1,0:T(8,128)(2,1)S(1)} %get-tuple-element.78.refs_0_), channel_id=1, source_target_pairs={{0,3},{1,2},{2,1},{3,0},{4,7},{5,6},{6,5},{7,4},{8,11},{9,10},{10,... | collective-permute-start | bytes 393224 | tf_op jit(solution)/shard_map/ppermute | solution.py:298
  8.2 7.6 %collective-permute-start.3 = (bf16[32,2048]{1,0:T(8,128)(2,1)S(1)}, bf16[32,2048]{1,0:T(8,128)(2,1)S(1)}, u32[]{:S(2)}, u32[]{:S(2)}) collective-permute-start(bf16[32,2048]{1,0:T(8,128)(2,1)S(1)} %get-tuple-element.78.refs_0_), channel_id=1, source_target_pairs={{0,1},{1,0},{2,3},{3,2},{4,5},{5,4},{6,7},{7,6},{8,9},{9,8},{10,11... | collective-permute-start | bytes 393224 | tf_op jit(solution)/shard_map/ppermute | solution.py:298
  8.3 12.7 %collective-permute-start.7 = (bf16[32,2048]{1,0:T(8,128)(2,1)S(1)}, bf16[32,2048]{1,0:T(8,128)(2,1)S(1)}, u32[]{:S(2)}, u32[]{:S(2)}) collective-permute-start(bf16[32,2048]{1,0:T(8,128)(2,1)S(1)} %get-tuple-element.82.refs_1_), channel_id=1, source_target_pairs={{0,3},{1,2},{2,1},{3,0},{4,7},{5,6},{6,5},{7,4},{8,11},{9,10},{10,... | collective-permute-start | bytes 393224 | tf_op jit(solution)/shard_map/ppermute | solution.py:300
  12.0 9.0 %collective-permute-start.4 = (bf16[32,2048]{1,0:T(8,128)(2,1)S(1)}, bf16[32,2048]{1,0:T(8,128)(2,1)S(1)}, u32[]{:S(2)}, u32[]{:S(2)}) collective-permute-start(bf16[32,2048]{1,0:T(8,128)(2,1)S(1)} %get-tuple-element.82.refs_1_), channel_id=1, source_target_pairs={{0,1},{1,0},{2,3},{3,2},{4,5},{5,4},{6,7},{7,6},{8,9},{9,8},{10,11... | collective-permute-start | bytes 393224 | tf_op jit(solution)/shard_map/ppermute | solution.py:300
  15.8 10.6 %collective-permute-start.6 = (bf16[32,2048]{1,0:T(8,128)(2,1)S(1)}, bf16[32,2048]{1,0:T(8,128)(2,1)S(1)}, u32[]{:S(2)}, u32[]{:S(2)}) collective-permute-start(bf16[32,2048]{1,0:T(8,128)(2,1)S(1)} %get-tuple-element.85), channel_id=1, source_target_pairs={{0,1},{1,0},{2,3},{3,2},{4,5},{5,4},{6,7},{7,6},{8,9},{9,8},{10,11... | collective-permute-start | bytes 393224 | tf_op jit(solution)/shard_map/ppermute | solution.py:303
  21.0 5.4 %collective-permute-start.8 = (bf16[32,2048]{1,0:T(8,128)(2,1)S(1)}, bf16[32,2048]{1,0:T(8,128)(2,1)S(1)}, u32[]{:S(2)}, u32[]{:S(2)}) collective-permute-start(bf16[32,2048]{1,0:T(8,128)(2,1)S(1)} %get-tuple-element.89), channel_id=1, source_target_pairs={{0,1},{1,0},{2,3},{3,2},{4,5},{5,4},{6,7},{7,6},{8,9},{9,8},{10,11... | collective-permute-start | bytes 393224 | tf_op jit(solution)/shard_map/ppermute | solution.py:307
  27.9 1.7 %collective-permute-start.9 = (bf16[64,1792]{1,0:T(8,128)(2,1)S(1)}, bf16[64,1792]{1,0:T(8,128)(2,1)S(1)}, u32[]{:S(2)}, u32[]{:S(2)}) collective-permute-start(bf16[64,1792]{1,0:T(8,128)(2,1)S(1)} %get-tuple-element.99), channel_id=1, source_target_pairs={{0,4},{4,0},{8,12},{12,8},{1,5},{5,1},{9,13},{13,9},{2,6},{6,2},{1... | collective-permute-start | bytes 688136 | tf_op jit(solution)/shard_map/ppermute | solution.py:324
  27.9 1.8 %collective-permute-start.10 = (bf16[64,1792]{1,0:T(8,128)(2,1)S(1)}, bf16[64,1792]{1,0:T(8,128)(2,1)S(1)}, u32[]{:S(2)}, u32[]{:S(2)}) collective-permute-start(bf16[64,1792]{1,0:T(8,128)(2,1)S(1)} %get-tuple-element.100), channel_id=1, source_target_pairs={{0,4},{4,0},{8,12},{12,8},{1,5},{5,1},{9,13},{13,9},{2,6},{6,2},{1... | collective-permute-start | bytes 688136 | tf_op jit(solution)/shard_map/ppermute | solution.py:324
  29.9 9.5 %collective-permute-start.11 = (bf16[64,1792]{1,0:T(8,128)(2,1)S(1)}, bf16[64,1792]{1,0:T(8,128)(2,1)S(1)}, u32[]{:S(2)}, u32[]{:S(2)}) collective-permute-start(bf16[64,1792]{1,0:T(8,128)(2,1)S(1)} %get-tuple-element.106), channel_id=1, source_target_pairs={{0,8},{4,12},{8,0},{12,4},{1,9},{5,13},{9,1},{13,5},{2,10},{6,14},... | collective-permute-start | bytes 688136 | tf_op jit(solution)/shard_map/ppermute | solution.py:327
  34.8 4.6 %collective-permute-start.12 = (bf16[64,1792]{1,0:T(8,128)(2,1)S(1)}, bf16[64,1792]{1,0:T(8,128)(2,1)S(1)}, u32[]{:S(2)}, u32[]{:S(2)}) collective-permute-start(bf16[64,1792]{1,0:T(8,128)(2,1)S(1)} %get-tuple-element.107), channel_id=1, source_target_pairs={{0,4},{4,0},{8,12},{12,8},{1,5},{5,1},{9,13},{13,9},{2,6},{6,2},{1... | collective-permute-start | bytes 688136 | tf_op jit(solution)/shard_map/ppermute | solution.py:337
  34.9 8.1 %collective-permute-start.15 = (bf16[64,1792]{1,0:T(8,128)(2,1)S(1)}, bf16[64,1792]{1,0:T(8,128)(2,1)S(1)}, u32[]{:S(2)}, u32[]{:S(2)}) collective-permute-start(bf16[64,1792]{1,0:T(8,128)(2,1)S(1)} %get-tuple-element.116), channel_id=1, source_target_pairs={{0,8},{4,12},{8,0},{12,4},{1,9},{5,13},{9,1},{13,5},{2,10},{6,14},... | collective-permute-start | bytes 688136 | tf_op jit(solution)/shard_map/ppermute | solution.py:327
  35.5 7.5 %collective-permute-start.16 = (bf16[64,1792]{1,0:T(8,128)(2,1)S(1)}, bf16[64,1792]{1,0:T(8,128)(2,1)S(1)}, u32[]{:S(2)}, u32[]{:S(2)}) collective-permute-start(bf16[64,1792]{1,0:T(8,128)(2,1)S(1)} %get-tuple-element.117), channel_id=1, source_target_pairs={{0,4},{4,0},{8,12},{12,8},{1,5},{5,1},{9,13},{13,9},{2,6},{6,2},{1... | collective-permute-start | bytes 688136 | tf_op jit(solution)/shard_map/ppermute | solution.py:337
  39.5 1.4 %collective-permute-start.13 = (bf16[64,896]{1,0:T(8,128)(2,1)S(1)}, bf16[64,896]{1,0:T(8,128)(2,1)S(1)}, u32[]{:S(2)}, u32[]{:S(2)}) collective-permute-start(bf16[64,896]{1,0:T(8,128)(2,1)S(1)} %get-tuple-element.113.refs_1_), channel_id=1, source_target_pairs={{0,4},{4,0},{8,12},{12,8},{1,5},{5,1},{9,13},{13,9},{2,6},{6,2},{1... | collective-permute-start | bytes 344072 | tf_op jit(solution)/shard_map/ppermute | solution.py:349
  39.6 5.7 %collective-permute-start.14 = (bf16[64,896]{1,0:T(8,128)(2,1)S(1)}, bf16[64,896]{1,0:T(8,128)(2,1)S(1)}, u32[]{:S(2)}, u32[]{:S(2)}) collective-permute-start(bf16[64,896]{1,0:T(8,128)(2,1)S(1)} %get-tuple-element.113.refs_1_), channel_id=1, source_target_pairs={{0,8},{4,12},{8,0},{12,4},{1,9},{5,13},{9,1},{13,5},{2,10},{6,14},... | collective-permute-start | bytes 344072 | tf_op jit(solution)/shard_map/ppermute | solution.py:348
  43.1 7.1 %collective-permute-start.22 = (bf16[64,896]{1,0:T(8,128)(2,1)S(1)}, bf16[64,896]{1,0:T(8,128)(2,1)S(1)}, u32[]{:S(2)}, u32[]{:S(2)}) collective-permute-start(bf16[64,896]{1,0:T(8,128)(2,1)S(1)} %get-tuple-element.127.refs_1_), channel_id=1, source_target_pairs={{0,4},{4,0},{8,12},{12,8},{1,5},{5,1},{9,13},{13,9},{2,6},{6,2},{1... | collective-permute-start | bytes 344072 | tf_op jit(solution)/shard_map/ppermute | solution.py:349
  43.2 8.4 %collective-permute-start.23 = (bf16[64,896]{1,0:T(8,128)(2,1)S(1)}, bf16[64,896]{1,0:T(8,128)(2,1)S(1)}, u32[]{:S(2)}, u32[]{:S(2)}) collective-permute-start(bf16[64,896]{1,0:T(8,128)(2,1)S(1)} %get-tuple-element.127.refs_1_), channel_id=1, source_target_pairs={{0,8},{4,12},{8,0},{12,4},{1,9},{5,13},{9,1},{13,5},{2,10},{6,14},... | collective-permute-start | bytes 344072 | tf_op jit(solution)/shard_map/ppermute | solution.py:348
  45.3 1.3 %collective-permute-start.17 = (bf16[32,896]{1,0:T(8,128)(2,1)S(1)}, bf16[32,896]{1,0:T(8,128)(2,1)S(1)}, u32[]{:S(2)}, u32[]{:S(2)}) collective-permute-start(bf16[32,896]{1,0:T(8,128)(2,1)S(1)} %get-tuple-element.120), channel_id=1, source_target_pairs={{0,4},{4,0},{8,12},{12,8},{1,5},{5,1},{9,13},{13,9},{2,6},{6,2},{1... | collective-permute-start | bytes 172040 | tf_op jit(solution)/shard_map/ppermute | solution.py:360
  45.4 1.4 %collective-permute-start.18 = (bf16[32,896]{1,0:T(8,128)(2,1)S(1)}, bf16[32,896]{1,0:T(8,128)(2,1)S(1)}, u32[]{:S(2)}, u32[]{:S(2)}) collective-permute-start(bf16[32,896]{1,0:T(8,128)(2,1)S(1)} %get-tuple-element.121), channel_id=1, source_target_pairs={{0,4},{4,0},{8,12},{12,8},{1,5},{5,1},{9,13},{13,9},{2,6},{6,2},{1... | collective-permute-start | bytes 172040 | tf_op jit(solution)/shard_map/ppermute | solution.py:360
  48.2 10.3 %collective-permute-start.19 = (bf16[16,2048]{1,0:T(8,128)(2,1)S(1)}, bf16[16,2048]{1,0:T(8,128)(2,1)S(1)}, u32[]{:S(2)}, u32[]{:S(2)}) collective-permute-start(bf16[16,2048]{1,0:T(8,128)(2,1)S(1)} %get-tuple-element.124), channel_id=1, source_target_pairs={{0,3},{1,2},{2,1},{3,0},{4,7},{5,6},{6,5},{7,4},{8,11},{9,10},{10,... | collective-permute-start | bytes 196616 | tf_op jit(solution)/shard_map/ppermute | solution.py:371
  51.6 3.1 %collective-permute-start.24 = (bf16[32,896]{1,0:T(8,128)(2,1)S(1)}, bf16[32,896]{1,0:T(8,128)(2,1)S(1)}, u32[]{:S(2)}, u32[]{:S(2)}) collective-permute-start(bf16[32,896]{1,0:T(8,128)(2,1)S(1)} %get-tuple-element.131), channel_id=1, source_target_pairs={{0,4},{4,0},{8,12},{12,8},{1,5},{5,1},{9,13},{13,9},{2,6},{6,2},{1... | collective-permute-start | bytes 172040 | tf_op jit(solution)/shard_map/ppermute | solution.py:360
  51.8 3.0 %collective-permute-start.25 = (bf16[32,896]{1,0:T(8,128)(2,1)S(1)}, bf16[32,896]{1,0:T(8,128)(2,1)S(1)}, u32[]{:S(2)}, u32[]{:S(2)}) collective-permute-start(bf16[32,896]{1,0:T(8,128)(2,1)S(1)} %get-tuple-element.132), channel_id=1, source_target_pairs={{0,4},{4,0},{8,12},{12,8},{1,5},{5,1},{9,13},{13,9},{2,6},{6,2},{1... | collective-permute-start | bytes 172040 | tf_op jit(solution)/shard_map/ppermute | solution.py:360
  52.2 8.4 %collective-permute-start.20 = (bf16[16,2048]{1,0:T(8,128)(2,1)S(1)}, bf16[16,2048]{1,0:T(8,128)(2,1)S(1)}, u32[]{:S(2)}, u32[]{:S(2)}) collective-permute-start(bf16[16,2048]{1,0:T(8,128)(2,1)S(1)} %get-tuple-element.125), channel_id=1, source_target_pairs={{0,2},{1,3},{2,0},{3,1},{4,6},{5,7},{6,4},{7,5},{8,10},{9,11},{10,... | collective-permute-start | bytes 196616 | tf_op jit(solution)/shard_map/ppermute | solution.py:371
  53.5 7.1 %collective-permute-start.21 = (bf16[16,2048]{1,0:T(8,128)(2,1)S(1)}, bf16[16,2048]{1,0:T(8,128)(2,1)S(1)}, u32[]{:S(2)}, u32[]{:S(2)}) collective-permute-start(bf16[16,2048]{1,0:T(8,128)(2,1)S(1)} %get-tuple-element.126), channel_id=1, source_target_pairs={{0,1},{1,0},{2,3},{3,2},{4,5},{5,4},{6,7},{7,6},{8,9},{9,8},{10,11... | collective-permute-start | bytes 196616 | tf_op jit(solution)/shard_map/ppermute | solution.py:371
  56.1 6.5 %collective-permute-start.26 = (bf16[16,2048]{1,0:T(8,128)(2,1)S(1)}, bf16[16,2048]{1,0:T(8,128)(2,1)S(1)}, u32[]{:S(2)}, u32[]{:S(2)}) collective-permute-start(bf16[16,2048]{1,0:T(8,128)(2,1)S(1)} %get-tuple-element.135), channel_id=1, source_target_pairs={{0,3},{1,2},{2,1},{3,0},{4,7},{5,6},{6,5},{7,4},{8,11},{9,10},{10,... | collective-permute-start | bytes 196616 | tf_op jit(solution)/shard_map/ppermute | solution.py:371
  58.1 6.9 %collective-permute-start.27 = (bf16[16,2048]{1,0:T(8,128)(2,1)S(1)}, bf16[16,2048]{1,0:T(8,128)(2,1)S(1)}, u32[]{:S(2)}, u32[]{:S(2)}) collective-permute-start(bf16[16,2048]{1,0:T(8,128)(2,1)S(1)} %get-tuple-element.136), channel_id=1, source_target_pairs={{0,2},{1,3},{2,0},{3,1},{4,6},{5,7},{6,4},{7,5},{8,10},{9,11},{10,... | collective-permute-start | bytes 196616 | tf_op jit(solution)/shard_map/ppermute | solution.py:371
  58.5 6.5 %collective-permute-start.28 = (bf16[16,2048]{1,0:T(8,128)(2,1)S(1)}, bf16[16,2048]{1,0:T(8,128)(2,1)S(1)}, u32[]{:S(2)}, u32[]{:S(2)}) collective-permute-start(bf16[16,2048]{1,0:T(8,128)(2,1)S(1)} %get-tuple-element.137), channel_id=1, source_target_pairs={{0,1},{1,0},{2,3},{3,2},{4,5},{5,4},{6,7},{7,6},{8,9},{9,8},{10,11... | collective-permute-start | bytes 196616 | tf_op jit(solution)/shard_map/ppermute | solution.py:371
  65.1 1.9 %collective-permute-start.29 = (bf16[2,4,2048]{2,1,0:T(4,128)(2,1)S(1)}, bf16[2,4,2048]{2,1,0:T(4,128)(2,1)S(1)}, u32[]{:S(2)}, u32[]{:S(2)}) collective-permute-start(bf16[2,4,2048]{2,1,0:T(4,128)(2,1)S(1)} %get-tuple-element.140), channel_id=1, source_target_pairs={{0,4},{4,0},{8,12},{12,8},{1,5},{5,1},{9,13},{13,9},{2,6},{6,2},{1... | collective-permute-start | bytes 98312 | tf_op jit(solution)/shard_map/ppermute | solution.py:384
  65.2 4.0 %collective-permute-start.30 = (bf16[2,4,2048]{2,1,0:T(4,128)(2,1)S(1)}, bf16[2,4,2048]{2,1,0:T(4,128)(2,1)S(1)}, u32[]{:S(2)}, u32[]{:S(2)}) collective-permute-start(bf16[2,4,2048]{2,1,0:T(4,128)(2,1)S(1)} %get-tuple-element.141), channel_id=1, source_target_pairs={{0,8},{4,12},{8,0},{12,4},{1,9},{5,13},{9,1},{13,5},{2,10},{6,14},... | collective-permute-start | bytes 98312 | tf_op jit(solution)/shard_map/ppermute | solution.py:384
  66.4 3.3 %collective-permute-start.31 = (bf16[2,4,2048]{2,1,0:T(4,128)(2,1)S(1)}, bf16[2,4,2048]{2,1,0:T(4,128)(2,1)S(1)}, u32[]{:S(2)}, u32[]{:S(2)}) collective-permute-start(bf16[2,4,2048]{2,1,0:T(4,128)(2,1)S(1)} %get-tuple-element.142), channel_id=1, source_target_pairs={{0,12},{4,8},{8,4},{12,0},{1,13},{5,9},{9,5},{13,1},{2,14},{6,10},... | collective-permute-start | bytes 98312 | tf_op jit(solution)/shard_map/ppermute | solution.py:384
  (7 other events, 32.7 us)

commit v8 on v7

--- a/solution.py
+++ b/solution.py
@@ -237,15 +237,17 @@
     outs[0][...] = total + jnp.dot(core_ref[...], w_ref[height:, :], preferred_element_type=F32)
 
 
-def down_rest_body(ins, _, outs, __):
+def down_rest_body(count, ins, _, outs, __):
     w_ref, part_ref, y_ref = ins[:3]
     rows = outs[0].shape[0]
     height = w_ref.shape[0] // 2
     total = part_ref[...] + jnp.dot(y_ref[...], w_ref[:height, :], preferred_element_type=F32)
-    yd = load_rows(ins[3:]).astype(BF)
+    yd = load_rows(ins[3 + count :]).astype(BF)
     total = total + jnp.dot(yd, w_ref[height:, :], preferred_element_type=F32)
-    for i, out in enumerate(outs):
+    for i, out in enumerate(outs[:4]):
         out[...] = total[i * rows : (i + 1) * rows].astype(out.dtype)
+    for given, out in zip(ins[3 : 3 + count], outs[4:]):
+        out[...] = given[...]
 
 
 def owner_body(ins, _, outs, __):
@@ -254,8 +256,8 @@
     source = lax.bitwise_xor(at, (y * 2 + c) * 4)
     turn = (lax.broadcasted_iota(jnp.int32, (16, 16), 1) == source).astype(F32).astype(BF)
     for step in range(2):
-        total = ins[step * 4][...]
-        for got in ins[step * 4 + 1 : step * 4 + 4]:
+        total = ins[step * 3][...]
+        for got in (ins[step * 3 + 1], ins[step * 3 + 2], ins[7 - step]):
             total = total + got[...].astype(F32)
         turned = jnp.dot(turn, total.astype(BF), preferred_element_type=F32)
         for i, out in enumerate(outs):
@@ -302,9 +304,9 @@
     passed, token = run(after_body, (block,), (near_sent[0], near_sent[1]), token)
     near_sent.append(lax.ppermute(passed, "col", X1))
     token = bring(1, 0, token)
-    pick, token = run(pick_body, (like((steps * rows, steps * assign.shape[1])),), (counts, assign), token)
     passed, token = run(after_body, (block,), (far_sent[0], far_sent[1]), token)
     far_sent.append(lax.ppermute(passed, "col", X1))
+    pick, token = run(pick_body, (like((steps * rows, steps * assign.shape[1])),), (counts, assign), token)
     token = bring(0, 1, token)
     pieces = []
     for dz in range(4):
@@ -363,23 +365,24 @@
         own, core, _ = hidden[step]
         return run(down_part_body, (like((rows, width), F32),), (down_near, own, core), token)
 
-    def down_rest(step, part_sum, yd, token):
-        outs = (like((part, width), F32),) + (like((part, width)),) * 3
-        operands = (down_far, part_sum, hidden[step][2]) + yd
-        keep, send1, send2, send3, token = run(down_rest_body, outs, operands, token)
-        sent = ((send3, X3), (send2, X2), (send1, X1))
-        return (keep,) + tuple(lax.ppermute(s, "col", x) for s, x in sent), token
+    def down_rest(step, part_sum, yd, first, token):
+        outs = (like((part, width), F32),) + (like((part, width)),) * (3 + len(first))
+        operands = (down_far, part_sum, hidden[step][2]) + first + yd
+        body = functools.partial(down_rest_body, len(first))
+        keep, send1, send2, send3, *passed, token = run(body, outs, operands, token)
+        sent = [keep, lax.ppermute(send3, "col", X3), lax.ppermute(send2, "col", X2)]
+        return sent, send1, passed, token
 
     token = activate(0, token)
     down_far, token = down_rows(1, token)
     part0, token = down_part(0, token)
     token = activate(1, token)
     yd0, token = shared(0, token)
-    sums0, token = down_rest(0, part0, yd0, token)
     part1, token = down_part(1, token)
+    sums0, first, _, token = down_rest(0, part0, yd0, (), token)
     yd1, token = shared(1, token)
-    sums1, token = down_rest(1, part1, yd1, token)
-    sums = sums0 + sums1
+    sums1, second, passed, token = down_rest(1, part1, yd1, (first,), token)
+    sums = sums0 + sums1 + [lax.ppermute(s, "col", X1) for s in (second, passed[0])]
     own, core, y, yd, token = run(owner_body, (like((steps, MEAN, width)),) * 4, tuple(sums), token)
     blocks = (own, lax.ppermute(core, "row", X1), lax.ppermute(y, "row", X2), lax.ppermute(yd, "row", X3))
     result, _ = run(output_body, (like((steps, MEAN, 4 * width)),), blocks, token)

time: 70.6 us -> 70 us (level)
  starting transfers between devices: 31.8 us -> 31 us
    ppermute x6, waiting for transfers between devices: 4.35 us -> 5.31 us  [the longest x2 5.14 us: down_rest(): lax.ppermute(send2, 'col', X2)]
    ppermute x6, starting transfers between devices: 8.9 us -> 8 us  [the longest x2 3.53 us: down_rest(): lax.ppermute(send3, 'col', X3)]
    ppermute x4, waiting for transfers between devices: 0.9 us -> 0.01 us  [shared(): return (tuple((lax.ppermute(p, 'row', X1) for p in passed)), token)]
where the time goes in v8:
time: 70 us; the launch traced here: 69.9 us
  starting transfers between devices  31 us (44%)
  Pallas kernels  25.2 us (36%)
  waiting for transfers between devices  10.3 us (15%)
  local copies, waits for them, and re-layouts  2.98 us (4%)
    pallas_call x26, Pallas kernels, run(): pl.pallas_call(wrapped, out_shape=outs, in_specs=[spec or vmem] * count +...  25.2 us
    ppermute x2, waiting for transfers between devices, down_rest(): lax.ppermute(send2, 'col', X2)  5.14 us
    ppermute x1, starting transfers between devices, near_plan(): lax.ppermute(near_block, 'col', X3)  3.87 us
    ppermute x1, starting transfers between devices, near_plan(): lax.ppermute(far_block, 'col', X3)  3.67 us
    ppermute x2, starting transfers between devices, down_rest(): lax.ppermute(send3, 'col', X3)  3.53 us
    unnamed x14, local copies, waits for them, and re-layouts  2.98 us
    ppermute x2, starting transfers between devices, near_plan(): y, yd = (lax.ppermute(y, 'row', X2), lax.ppermute(yd, 'row', X3))  2.66 us
    ppermute x2, starting transfers between devices, down_rest(): lax.ppermute(send2, 'col', X2)  2.44 us
  transfers between devices with their start and end apart: 32, of which 12 were waited for; matrix products, arithmetic and copies ran while one was open for 0% of the time, Pallas kernels for 32%

profile of v8, /device:TPU:0, one launch (start us, length us, event | category | flops | bytes accessed | tf_op | source)
XLA Modules:
  0.0 69.9 jit_solution(16202175339829026701)
XLA Ops:
  0.0 0.9 %copy-done = bf16[2,8,8192]{2,1,0:T(8,128)(2,1)S(1)} copy-done((bf16[2,8,8192]{2,1,0:T(8,128)(2,1)S(1)}, bf16[2,8,8192]{2,1,0:T(8,128)(2,1)}, u32[]{:S(2)}) %copy-start) | copy-done | bytes 262168
  1.7 2.6 %collective-permute-start.1 = (bf16[2,8,2048]{2,1,0:T(8,128)(2,1)S(1)}, bf16[2,8,2048]{2,1,0:T(8,128)(2,1)S(1)}, u32[]{:S(2)}, u32[]{:S(2)}) collective-permute-start(bf16[2,8,2048]{2,1,0:T(8,128)(2,1)S(1)} %get-tuple-element.80), channel_id=1, source_target_pairs={{0,8},{4,12},{8,0},{12,4},{1,9},{5,13},{9,1},{13,5},{2,10},{6,14},... | collective-permute-start | bytes 196616 | tf_op jit(solution)/shard_map/ppermute | solution.py:289
  4.4 3.9 %collective-permute-start.5 = (bf16[32,2048]{1,0:T(8,128)(2,1)S(1)}, bf16[32,2048]{1,0:T(8,128)(2,1)S(1)}, u32[]{:S(2)}, u32[]{:S(2)}) collective-permute-start(bf16[32,2048]{1,0:T(8,128)(2,1)S(1)} %get-tuple-element.79.refs_0_), channel_id=1, source_target_pairs={{0,3},{1,2},{2,1},{3,0},{4,7},{5,6},{6,5},{7,4},{8,11},{9,10},{10,... | collective-permute-start | bytes 393224 | tf_op jit(solution)/shard_map/ppermute | solution.py:300
  8.3 3.7 %collective-permute-start.7 = (bf16[32,2048]{1,0:T(8,128)(2,1)S(1)}, bf16[32,2048]{1,0:T(8,128)(2,1)S(1)}, u32[]{:S(2)}, u32[]{:S(2)}) collective-permute-start(bf16[32,2048]{1,0:T(8,128)(2,1)S(1)} %get-tuple-element.83.refs_1_), channel_id=1, source_target_pairs={{0,3},{1,2},{2,1},{3,0},{4,7},{5,6},{6,5},{7,4},{8,11},{9,10},{10,... | collective-permute-start | bytes 393224 | tf_op jit(solution)/shard_map/ppermute | solution.py:302
  12.0 3.2 %shard_map.67 = (bf16[2048,1792]{1,0:T(8,128)(2,1)S(1)}, f32[8,128]{1,0:T(8,128)S(1)}) custom-call(bf16[2048,3584]{1,0:T(8,128)(2,1)} %refs_2_.1, bf16[2048,3584]{1,0:T(8,128)(2,1)} %refs_3_.1, f32[8,128]{1,0:T(8,128)S(1)} %get-tuple-element.84.refs_2_), custom_call_target="tpu_custom_call" | custom-call | bytes 1 | tf_op jit(solution)/shard_map/pallas_call | solution.py:41
  15.8 1.6 %collective-permute-start.6 = (bf16[32,2048]{1,0:T(8,128)(2,1)S(1)}, bf16[32,2048]{1,0:T(8,128)(2,1)S(1)}, u32[]{:S(2)}, u32[]{:S(2)}) collective-permute-start(bf16[32,2048]{1,0:T(8,128)(2,1)S(1)} %get-tuple-element.86), channel_id=1, source_target_pairs={{0,1},{1,0},{2,3},{3,2},{4,5},{5,4},{6,7},{7,6},{8,9},{9,8},{10,11... | collective-permute-start | bytes 393224 | tf_op jit(solution)/shard_map/ppermute | solution.py:305
  17.5 3.2 %shard_map.69 = (bf16[2048,1792]{1,0:T(8,128)(2,1)S(1)}, f32[8,128]{1,0:T(8,128)S(1)}) custom-call(bf16[2048,3584]{1,0:T(8,128)(2,1)} %refs_2_.1, bf16[2048,3584]{1,0:T(8,128)(2,1)} %refs_3_.1, f32[8,128]{1,0:T(8,128)S(1)} %get-tuple-element.87.refs_2_), custom_call_target="tpu_custom_call" | custom-call | bytes 1 | tf_op jit(solution)/shard_map/pallas_call | solution.py:41
  20.9 2.3 %collective-permute-start.8 = (bf16[32,2048]{1,0:T(8,128)(2,1)S(1)}, bf16[32,2048]{1,0:T(8,128)(2,1)S(1)}, u32[]{:S(2)}, u32[]{:S(2)}) collective-permute-start(bf16[32,2048]{1,0:T(8,128)(2,1)S(1)} %get-tuple-element.89), channel_id=1, source_target_pairs={{0,1},{1,0},{2,3},{3,2},{4,5},{5,4},{6,7},{7,6},{8,9},{9,8},{10,11... | collective-permute-start | bytes 393224 | tf_op jit(solution)/shard_map/ppermute | solution.py:308
  23.4 3.3 %shard_map.72 = (bf16[2048,1792]{1,0:T(8,128)(2,1)S(1)}, f32[8,128]{1,0:T(8,128)S(1)}) custom-call(bf16[2048,3584]{1,0:T(8,128)(2,1)} %refs_2_.1, bf16[2048,3584]{1,0:T(8,128)(2,1)} %refs_3_.1, f32[8,128]{1,0:T(8,128)S(1)} %get-tuple-element.93.refs_2_), custom_call_target="tpu_custom_call" | custom-call | bytes 1 | tf_op jit(solution)/shard_map/pallas_call | solution.py:41
  26.7 1.4 %shard_map.73 = (bf16[128,2048]{1,0:T(8,128)(2,1)S(1)}, bf16[64,1792]{1,0:T(8,128)(2,1)S(1)}, bf16[64,1792]{1,0:T(8,128)(2,1)S(1)}, f32[8,128]{1,0:T(8,128)S(1)}) custom-call(bf16[32,2048]{1,0:T(8,128)(2,1)S(1)} %get-tuple-element.79.refs_0_, bf16[32,2048]{1,0:T(8,128)(2,1)S(1)} %get-tuple-element.83.refs_1_, ...), custom_call_target="tpu_custom_call" | custom-call | bytes 1 | tf_op jit(solution)/shard_map/pallas_call | solution.py:41
  28.7 1.1 %shard_map.74 = (f32[128,1792]{1,0:T(8,128)S(1)}, f32[8,128]{1,0:T(8,128)S(1)}) custom-call(bf16[128,2048]{1,0:T(8,128)(2,1)S(1)} %get-tuple-element.95.refs_0_, bf16[2048,1792]{1,0:T(8,128)(2,1)S(1)} %get-tuple-element.97.refs_1_, f32[8,128]{1,0:T(8,128)S(1)} %get-tuple-element.98.refs_2_), custom_call_target="tpu_custom_call" | custom-call | bytes 1 | tf_op jit(solution)/shard_map/pallas_call | solution.py:41
  30.1 1.5 %collective-permute-start.11 = (bf16[64,1792]{1,0:T(8,128)(2,1)S(1)}, bf16[64,1792]{1,0:T(8,128)(2,1)S(1)}, u32[]{:S(2)}, u32[]{:S(2)}) collective-permute-start(bf16[64,1792]{1,0:T(8,128)(2,1)S(1)} %get-tuple-element.107), channel_id=1, source_target_pairs={{0,8},{4,12},{8,0},{12,4},{1,9},{5,13},{9,1},{13,5},{2,10},{6,14},... | collective-permute-start | bytes 688136 | tf_op jit(solution)/shard_map/ppermute | solution.py:329
  31.7 3.3 %shard_map.76 = (bf16[64,1792]{1,0:T(8,128)(2,1)S(1)}, bf16[64,1792]{1,0:T(8,128)(2,1)S(1)}, bf16[2048,1792]{1,0:T(8,128)(2,1)S(1)}, f32[8,128]{1,0:T(8,128)S(1)}) custom-call(bf16[128,2048]{1,0:T(8,128)(2,1)S(1)} %get-tuple-element.95.refs_0_, bf16[2048,1792]{1,0:T(8,128)(2,1)S(1)} %get-tuple-element.96.refs_1_, bf16[2048,3584]{1,0:T(8,128)(2,1)} %refs_2_.1, ...), custom_call_target="tpu_custom_call" | custom-call | bytes 1 | tf_op jit(solution)/shard_map/pallas_call | solution.py:41
  35.9 1.1 %shard_map.77 = (f32[128,1792]{1,0:T(8,128)S(1)}, f32[8,128]{1,0:T(8,128)S(1)}) custom-call(bf16[128,2048]{1,0:T(8,128)(2,1)S(1)} %get-tuple-element.95.refs_0_, bf16[2048,1792]{1,0:T(8,128)(2,1)S(1)} %get-tuple-element.104.refs_1_, f32[8,128]{1,0:T(8,128)S(1)} %get-tuple-element.105.refs_2_), custom_call_target="tpu_custom_call" | custom-call | bytes 1 | tf_op jit(solution)/shard_map/pallas_call | solution.py:41
  37.3 1.2 %slice-done.2 = s8[4194304]{0:T(1024)(128)(4,1)S(1)} async-done(((s8[14680064]{0:T(1024)(128)(4,1)}), s8[4194304]{0:T(1024)(128)(4,1)S(1)}, s32[]{:S(2)}) %slice-start.2) | async-done | bytes 4194328
  41.2 1.4 %shard_map.81 = (f32[64,2048]{1,0:T(8,128)S(1)}, f32[8,128]{1,0:T(8,128)S(1)}) custom-call(bf16[1792,2048]{1,0:T(8,128)(2,1)S(1)} %get-tuple-element.113.refs_0_, bf16[64,896]{1,0:T(8,128)(2,1)S(1)} %get-tuple-element.114.refs_1_, bf16[64,896]{1,0:T(8,128)(2,1)S(1)} %collective-permute-done.13.refs_2_, f32[8,128]{1,0:T(8,128)S(1)} %get-tuple-element.115.refs_3_), custom_call_target="tpu_custom_call" | custom-call | bytes 1 | tf_op jit(solution)/shard_map/pallas_call | solution.py:41
  42.6 0.6 collective-permute-done.15.refs_1_
  43.5 1.6 %collective-permute-start.22 = (bf16[64,896]{1,0:T(8,128)(2,1)S(1)}, bf16[64,896]{1,0:T(8,128)(2,1)S(1)}, u32[]{:S(2)}, u32[]{:S(2)}) collective-permute-start(bf16[64,896]{1,0:T(8,128)(2,1)S(1)} %get-tuple-element.123.refs_1_), channel_id=1, source_target_pairs={{0,8},{4,12},{8,0},{12,4},{1,9},{5,13},{9,1},{13,5},{2,10},{6,14},... | collective-permute-start | bytes 344072 | tf_op jit(solution)/shard_map/ppermute | solution.py:350
  46.2 1.4 %shard_map.84 = (f32[64,2048]{1,0:T(8,128)S(1)}, f32[8,128]{1,0:T(8,128)S(1)}) custom-call(bf16[1792,2048]{1,0:T(8,128)(2,1)S(1)} %get-tuple-element.113.refs_0_, bf16[64,896]{1,0:T(8,128)(2,1)S(1)} %get-tuple-element.123.refs_1_, bf16[64,896]{1,0:T(8,128)(2,1)S(1)} %collective-permute-done.19.refs_2_, f32[8,128]{1,0:T(8,128)S(1)} %get-tuple-element.124.refs_3_), custom_call_target="tpu_custom_call" | custom-call | bytes 1 | tf_op jit(solution)/shard_map/pallas_call | solution.py:41
  47.6 1.4 %shard_map.85 = (f32[16,2048]{1,0:T(8,128)S(1)}, bf16[16,2048]{1,0:T(8,128)(2,1)S(1)}, bf16[16,2048]{1,0:T(8,128)(2,1)S(1)}, bf16[16,2048]{1,0:T(8,128)(2,1)S(1)}, f32[8,128]{1,0:T(8,128)S(1)}) custom-call(bf16[1792,2048]{1,0:T(8,128)(2,1)S(1)} %get-tuple-element.112.refs_0_, f32[64,2048]{1,0:T(8,128)S(1)} %get-tuple-element.116.refs_1_, ...), custom_call_target="tpu_custom_call" | custom-call | bytes 1 | tf_op jit(solution)/shard_map/pallas_call | solution.py:41
  49.1 1.7 %collective-permute-start.20 = (bf16[16,2048]{1,0:T(8,128)(2,1)S(1)}, bf16[16,2048]{1,0:T(8,128)(2,1)S(1)}, u32[]{:S(2)}, u32[]{:S(2)}) collective-permute-start(bf16[16,2048]{1,0:T(8,128)(2,1)S(1)} %get-tuple-element.127), channel_id=1, source_target_pairs={{0,3},{1,2},{2,1},{3,0},{4,7},{5,6},{6,5},{7,4},{8,11},{9,10},{10,... | collective-permute-start | bytes 196616 | tf_op jit(solution)/shard_map/ppermute | solution.py:373
  51.3 1.3 %collective-permute-start.21 = (bf16[16,2048]{1,0:T(8,128)(2,1)S(1)}, bf16[16,2048]{1,0:T(8,128)(2,1)S(1)}, u32[]{:S(2)}, u32[]{:S(2)}) collective-permute-start(bf16[16,2048]{1,0:T(8,128)(2,1)S(1)} %get-tuple-element.128), channel_id=1, source_target_pairs={{0,2},{1,3},{2,0},{3,1},{4,6},{5,7},{6,4},{7,5},{8,10},{9,11},{10,... | collective-permute-start | bytes 196616 | tf_op jit(solution)/shard_map/ppermute | solution.py:373
  52.7 1.4 %shard_map.87 = (f32[16,2048]{1,0:T(8,128)S(1)}, bf16[16,2048]{1,0:T(8,128)(2,1)S(1)}, bf16[16,2048]{1,0:T(8,128)(2,1)S(1)}, bf16[16,2048]{1,0:T(8,128)(2,1)S(1)...) custom-call(bf16[1792,2048]{1,0:T(8,128)(2,1)S(1)} %get-tuple-element.112.refs_0_, ...), custom_call_target="tpu_custom_call" | custom-call | bytes 1 | tf_op jit(solution)/shard_map/pallas_call | solution.py:41
  54.1 1.8 %collective-permute-start.25 = (bf16[16,2048]{1,0:T(8,128)(2,1)S(1)}, bf16[16,2048]{1,0:T(8,128)(2,1)S(1)}, u32[]{:S(2)}, u32[]{:S(2)}) collective-permute-start(bf16[16,2048]{1,0:T(8,128)(2,1)S(1)} %get-tuple-element.136), channel_id=1, source_target_pairs={{0,3},{1,2},{2,1},{3,0},{4,7},{5,6},{6,5},{7,4},{8,11},{9,10},{10,... | collective-permute-start | bytes 196616 | tf_op jit(solution)/shard_map/ppermute | solution.py:373
  55.9 1.1 %collective-permute-start.26 = (bf16[16,2048]{1,0:T(8,128)(2,1)S(1)}, bf16[16,2048]{1,0:T(8,128)(2,1)S(1)}, u32[]{:S(2)}, u32[]{:S(2)}) collective-permute-start(bf16[16,2048]{1,0:T(8,128)(2,1)S(1)} %get-tuple-element.137), channel_id=1, source_target_pairs={{0,2},{1,3},{2,0},{3,1},{4,6},{5,7},{6,4},{7,5},{8,10},{9,11},{10,... | collective-permute-start | bytes 196616 | tf_op jit(solution)/shard_map/ppermute | solution.py:373
  57.1 1.5 %collective-permute-start.27 = (bf16[16,2048]{1,0:T(8,128)(2,1)S(1)}, bf16[16,2048]{1,0:T(8,128)(2,1)S(1)}, u32[]{:S(2)}, u32[]{:S(2)}) collective-permute-start(bf16[16,2048]{1,0:T(8,128)(2,1)S(1)} %get-tuple-element.138), channel_id=1, source_target_pairs={{0,1},{1,0},{2,3},{3,2},{4,5},{5,4},{6,7},{7,6},{8,9},{9,8},{10,11... | collective-permute-start | bytes 196616 | tf_op jit(solution)/shard_map/ppermute | solution.py:385
  59.1 2.6 %collective-permute-done.21.refs_2_ = bf16[16,2048]{1,0:T(8,128)(2,1)S(1)} collective-permute-done((bf16[16,2048]{1,0:T(8,128)(2,1)S(1)}, bf16[16,2048]{1,0:T(8,128)(2,1)S(1)}, u32[]{:S(2)}, u32[]{:S(2)}) %collective-permute-start.21) | collective-permute-done | bytes 65568 | tf_op jit(solution)/shard_map/ppermute | solution.py:373
  61.6 2.6 %collective-permute-done.26.refs_5_ = bf16[16,2048]{1,0:T(8,128)(2,1)S(1)} collective-permute-done((bf16[16,2048]{1,0:T(8,128)(2,1)S(1)}, bf16[16,2048]{1,0:T(8,128)(2,1)S(1)}, u32[]{:S(2)}, u32[]{:S(2)}) %collective-permute-start.26) | collective-permute-done | bytes 65568 | tf_op jit(solution)/shard_map/ppermute | solution.py:373
  64.7 1.2 %collective-permute-start.30 = (bf16[2,4,2048]{2,1,0:T(4,128)(2,1)S(1)}, bf16[2,4,2048]{2,1,0:T(4,128)(2,1)S(1)}, u32[]{:S(2)}, u32[]{:S(2)}) collective-permute-start(bf16[2,4,2048]{2,1,0:T(4,128)(2,1)S(1)} %get-tuple-element.143), channel_id=1, source_target_pairs={{0,8},{4,12},{8,0},{12,4},{1,9},{5,13},{9,1},{13,5},{2,10},{6,14},... | collective-permute-start | bytes 98312 | tf_op jit(solution)/shard_map/ppermute | solution.py:387
  65.9 0.7 collective-permute-start.31
  66.5 2.1 %collective-permute-done.30.refs_2_ = bf16[2,4,2048]{2,1,0:T(4,128)(2,1)S(1)} collective-permute-done((bf16[2,4,2048]{2,1,0:T(4,128)(2,1)S(1)}, bf16[2,4,2048]{2,1,0:T(4,128)(2,1)S(1)}, u32[]{:S(2)}, u32[]{:S(2)}) %collective-permute-start.30) | collective-permute-done | bytes 32800 | tf_op jit(solution)/shard_map/ppermute | solution.py:387
  69.2 0.7 shard_map.89
  (73 shorter events, 10.0 us)
Async XLA Ops:
  1.2 3.2 %collective-permute-start = (bf16[2,8,2048]{2,1,0:T(8,128)(2,1)S(1)}, bf16[2,8,2048]{2,1,0:T(8,128)(2,1)S(1)}, u32[]{:S(2)}, u32[]{:S(2)}) collective-permute-start(bf16[2,8,2048]{2,1,0:T(8,128)(2,1)S(1)} %get-tuple-element.77), channel_id=1, source_target_pairs={{0,4},{4,0},{8,12},{12,8},{1,5},{5,1},{9,13},{13,9},{2,6},{6,2},{1... | collective-permute-start | bytes 196616 | tf_op jit(solution)/shard_map/ppermute | solution.py:290
  1.7 6.6 %collective-permute-start.1 = (bf16[2,8,2048]{2,1,0:T(8,128)(2,1)S(1)}, bf16[2,8,2048]{2,1,0:T(8,128)(2,1)S(1)}, u32[]{:S(2)}, u32[]{:S(2)}) collective-permute-start(bf16[2,8,2048]{2,1,0:T(8,128)(2,1)S(1)} %get-tuple-element.80), channel_id=1, source_target_pairs={{0,8},{4,12},{8,0},{12,4},{1,9},{5,13},{9,1},{13,5},{2,10},{6,14},... | collective-permute-start | bytes 196616 | tf_op jit(solution)/shard_map/ppermute | solution.py:289
  4.3 4.0 %collective-permute-start.2 = (bf16[2,8,2048]{2,1,0:T(8,128)(2,1)S(1)}, bf16[2,8,2048]{2,1,0:T(8,128)(2,1)S(1)}, u32[]{:S(2)}, u32[]{:S(2)}) collective-permute-start(bf16[2,8,2048]{2,1,0:T(8,128)(2,1)S(1)} %get-tuple-element.81), channel_id=1, source_target_pairs={{0,12},{4,8},{8,4},{12,0},{1,13},{5,9},{9,5},{13,1},{2,14},{6,10},... | collective-permute-start | bytes 196616 | tf_op jit(solution)/shard_map/ppermute | solution.py:289
  4.4 10.8 %collective-permute-start.5 = (bf16[32,2048]{1,0:T(8,128)(2,1)S(1)}, bf16[32,2048]{1,0:T(8,128)(2,1)S(1)}, u32[]{:S(2)}, u32[]{:S(2)}) collective-permute-start(bf16[32,2048]{1,0:T(8,128)(2,1)S(1)} %get-tuple-element.79.refs_0_), channel_id=1, source_target_pairs={{0,3},{1,2},{2,1},{3,0},{4,7},{5,6},{6,5},{7,4},{8,11},{9,10},{10,... | collective-permute-start | bytes 393224 | tf_op jit(solution)/shard_map/ppermute | solution.py:300
  8.2 7.6 %collective-permute-start.3 = (bf16[32,2048]{1,0:T(8,128)(2,1)S(1)}, bf16[32,2048]{1,0:T(8,128)(2,1)S(1)}, u32[]{:S(2)}, u32[]{:S(2)}) collective-permute-start(bf16[32,2048]{1,0:T(8,128)(2,1)S(1)} %get-tuple-element.79.refs_0_), channel_id=1, source_target_pairs={{0,1},{1,0},{2,3},{3,2},{4,5},{5,4},{6,7},{7,6},{8,9},{9,8},{10,11... | collective-permute-start | bytes 393224 | tf_op jit(solution)/shard_map/ppermute | solution.py:300
  8.3 12.4 %collective-permute-start.7 = (bf16[32,2048]{1,0:T(8,128)(2,1)S(1)}, bf16[32,2048]{1,0:T(8,128)(2,1)S(1)}, u32[]{:S(2)}, u32[]{:S(2)}) collective-permute-start(bf16[32,2048]{1,0:T(8,128)(2,1)S(1)} %get-tuple-element.83.refs_1_), channel_id=1, source_target_pairs={{0,3},{1,2},{2,1},{3,0},{4,7},{5,6},{6,5},{7,4},{8,11},{9,10},{10,... | collective-permute-start | bytes 393224 | tf_op jit(solution)/shard_map/ppermute | solution.py:302
  12.0 8.8 %collective-permute-start.4 = (bf16[32,2048]{1,0:T(8,128)(2,1)S(1)}, bf16[32,2048]{1,0:T(8,128)(2,1)S(1)}, u32[]{:S(2)}, u32[]{:S(2)}) collective-permute-start(bf16[32,2048]{1,0:T(8,128)(2,1)S(1)} %get-tuple-element.83.refs_1_), channel_id=1, source_target_pairs={{0,1},{1,0},{2,3},{3,2},{4,5},{5,4},{6,7},{7,6},{8,9},{9,8},{10,11... | collective-permute-start | bytes 393224 | tf_op jit(solution)/shard_map/ppermute | solution.py:302
  15.8 10.8 %collective-permute-start.6 = (bf16[32,2048]{1,0:T(8,128)(2,1)S(1)}, bf16[32,2048]{1,0:T(8,128)(2,1)S(1)}, u32[]{:S(2)}, u32[]{:S(2)}) collective-permute-start(bf16[32,2048]{1,0:T(8,128)(2,1)S(1)} %get-tuple-element.86), channel_id=1, source_target_pairs={{0,1},{1,0},{2,3},{3,2},{4,5},{5,4},{6,7},{7,6},{8,9},{9,8},{10,11... | collective-permute-start | bytes 393224 | tf_op jit(solution)/shard_map/ppermute | solution.py:305
  20.9 5.8 %collective-permute-start.8 = (bf16[32,2048]{1,0:T(8,128)(2,1)S(1)}, bf16[32,2048]{1,0:T(8,128)(2,1)S(1)}, u32[]{:S(2)}, u32[]{:S(2)}) collective-permute-start(bf16[32,2048]{1,0:T(8,128)(2,1)S(1)} %get-tuple-element.89), channel_id=1, source_target_pairs={{0,1},{1,0},{2,3},{3,2},{4,5},{5,4},{6,7},{7,6},{8,9},{9,8},{10,11... | collective-permute-start | bytes 393224 | tf_op jit(solution)/shard_map/ppermute | solution.py:308
  28.1 1.7 %collective-permute-start.9 = (bf16[64,1792]{1,0:T(8,128)(2,1)S(1)}, bf16[64,1792]{1,0:T(8,128)(2,1)S(1)}, u32[]{:S(2)}, u32[]{:S(2)}) collective-permute-start(bf16[64,1792]{1,0:T(8,128)(2,1)S(1)} %get-tuple-element.100), channel_id=1, source_target_pairs={{0,4},{4,0},{8,12},{12,8},{1,5},{5,1},{9,13},{13,9},{2,6},{6,2},{1... | collective-permute-start | bytes 688136 | tf_op jit(solution)/shard_map/ppermute | solution.py:326
  28.2 1.8 %collective-permute-start.10 = (bf16[64,1792]{1,0:T(8,128)(2,1)S(1)}, bf16[64,1792]{1,0:T(8,128)(2,1)S(1)}, u32[]{:S(2)}, u32[]{:S(2)}) collective-permute-start(bf16[64,1792]{1,0:T(8,128)(2,1)S(1)} %get-tuple-element.101), channel_id=1, source_target_pairs={{0,4},{4,0},{8,12},{12,8},{1,5},{5,1},{9,13},{13,9},{2,6},{6,2},{1... | collective-permute-start | bytes 688136 | tf_op jit(solution)/shard_map/ppermute | solution.py:326
  30.1 9.5 %collective-permute-start.11 = (bf16[64,1792]{1,0:T(8,128)(2,1)S(1)}, bf16[64,1792]{1,0:T(8,128)(2,1)S(1)}, u32[]{:S(2)}, u32[]{:S(2)}) collective-permute-start(bf16[64,1792]{1,0:T(8,128)(2,1)S(1)} %get-tuple-element.107), channel_id=1, source_target_pairs={{0,8},{4,12},{8,0},{12,4},{1,9},{5,13},{9,1},{13,5},{2,10},{6,14},... | collective-permute-start | bytes 688136 | tf_op jit(solution)/shard_map/ppermute | solution.py:329
  35.0 4.6 %collective-permute-start.12 = (bf16[64,1792]{1,0:T(8,128)(2,1)S(1)}, bf16[64,1792]{1,0:T(8,128)(2,1)S(1)}, u32[]{:S(2)}, u32[]{:S(2)}) collective-permute-start(bf16[64,1792]{1,0:T(8,128)(2,1)S(1)} %get-tuple-element.108), channel_id=1, source_target_pairs={{0,4},{4,0},{8,12},{12,8},{1,5},{5,1},{9,13},{13,9},{2,6},{6,2},{1... | collective-permute-start | bytes 688136 | tf_op jit(solution)/shard_map/ppermute | solution.py:339
  35.1 8.1 %collective-permute-start.15 = (bf16[64,1792]{1,0:T(8,128)(2,1)S(1)}, bf16[64,1792]{1,0:T(8,128)(2,1)S(1)}, u32[]{:S(2)}, u32[]{:S(2)}) collective-permute-start(bf16[64,1792]{1,0:T(8,128)(2,1)S(1)} %get-tuple-element.117), channel_id=1, source_target_pairs={{0,8},{4,12},{8,0},{12,4},{1,9},{5,13},{9,1},{13,5},{2,10},{6,14},... | collective-permute-start | bytes 688136 | tf_op jit(solution)/shard_map/ppermute | solution.py:329
  35.8 7.5 %collective-permute-start.16 = (bf16[64,1792]{1,0:T(8,128)(2,1)S(1)}, bf16[64,1792]{1,0:T(8,128)(2,1)S(1)}, u32[]{:S(2)}, u32[]{:S(2)}) collective-permute-start(bf16[64,1792]{1,0:T(8,128)(2,1)S(1)} %get-tuple-element.118), channel_id=1, source_target_pairs={{0,4},{4,0},{8,12},{12,8},{1,5},{5,1},{9,13},{13,9},{2,6},{6,2},{1... | collective-permute-start | bytes 688136 | tf_op jit(solution)/shard_map/ppermute | solution.py:339
  39.8 1.4 %collective-permute-start.13 = (bf16[64,896]{1,0:T(8,128)(2,1)S(1)}, bf16[64,896]{1,0:T(8,128)(2,1)S(1)}, u32[]{:S(2)}, u32[]{:S(2)}) collective-permute-start(bf16[64,896]{1,0:T(8,128)(2,1)S(1)} %get-tuple-element.114.refs_1_), channel_id=1, source_target_pairs={{0,4},{4,0},{8,12},{12,8},{1,5},{5,1},{9,13},{13,9},{2,6},{6,2},{1... | collective-permute-start | bytes 344072 | tf_op jit(solution)/shard_map/ppermute | solution.py:351
  39.9 5.7 %collective-permute-start.14 = (bf16[64,896]{1,0:T(8,128)(2,1)S(1)}, bf16[64,896]{1,0:T(8,128)(2,1)S(1)}, u32[]{:S(2)}, u32[]{:S(2)}) collective-permute-start(bf16[64,896]{1,0:T(8,128)(2,1)S(1)} %get-tuple-element.114.refs_1_), channel_id=1, source_target_pairs={{0,8},{4,12},{8,0},{12,4},{1,9},{5,13},{9,1},{13,5},{2,10},{6,14},... | collective-permute-start | bytes 344072 | tf_op jit(solution)/shard_map/ppermute | solution.py:350
  43.4 2.8 %collective-permute-start.19 = (bf16[64,896]{1,0:T(8,128)(2,1)S(1)}, bf16[64,896]{1,0:T(8,128)(2,1)S(1)}, u32[]{:S(2)}, u32[]{:S(2)}) collective-permute-start(bf16[64,896]{1,0:T(8,128)(2,1)S(1)} %get-tuple-element.123.refs_1_), channel_id=1, source_target_pairs={{0,4},{4,0},{8,12},{12,8},{1,5},{5,1},{9,13},{13,9},{2,6},{6,2},{1... | collective-permute-start | bytes 344072 | tf_op jit(solution)/shard_map/ppermute | solution.py:351
  43.5 7.3 %collective-permute-start.22 = (bf16[64,896]{1,0:T(8,128)(2,1)S(1)}, bf16[64,896]{1,0:T(8,128)(2,1)S(1)}, u32[]{:S(2)}, u32[]{:S(2)}) collective-permute-start(bf16[64,896]{1,0:T(8,128)(2,1)S(1)} %get-tuple-element.123.refs_1_), channel_id=1, source_target_pairs={{0,8},{4,12},{8,0},{12,4},{1,9},{5,13},{9,1},{13,5},{2,10},{6,14},... | collective-permute-start | bytes 344072 | tf_op jit(solution)/shard_map/ppermute | solution.py:350
  45.6 2.0 %collective-permute-start.17 = (bf16[32,896]{1,0:T(8,128)(2,1)S(1)}, bf16[32,896]{1,0:T(8,128)(2,1)S(1)}, u32[]{:S(2)}, u32[]{:S(2)}) collective-permute-start(bf16[32,896]{1,0:T(8,128)(2,1)S(1)} %get-tuple-element.121), channel_id=1, source_target_pairs={{0,4},{4,0},{8,12},{12,8},{1,5},{5,1},{9,13},{13,9},{2,6},{6,2},{1... | collective-permute-start | bytes 172040 | tf_op jit(solution)/shard_map/ppermute | solution.py:362
  45.7 1.9 %collective-permute-start.18 = (bf16[32,896]{1,0:T(8,128)(2,1)S(1)}, bf16[32,896]{1,0:T(8,128)(2,1)S(1)}, u32[]{:S(2)}, u32[]{:S(2)}) collective-permute-start(bf16[32,896]{1,0:T(8,128)(2,1)S(1)} %get-tuple-element.122), channel_id=1, source_target_pairs={{0,4},{4,0},{8,12},{12,8},{1,5},{5,1},{9,13},{13,9},{2,6},{6,2},{1... | collective-permute-start | bytes 172040 | tf_op jit(solution)/shard_map/ppermute | solution.py:362
  49.1 9.5 %collective-permute-start.20 = (bf16[16,2048]{1,0:T(8,128)(2,1)S(1)}, bf16[16,2048]{1,0:T(8,128)(2,1)S(1)}, u32[]{:S(2)}, u32[]{:S(2)}) collective-permute-start(bf16[16,2048]{1,0:T(8,128)(2,1)S(1)} %get-tuple-element.127), channel_id=1, source_target_pairs={{0,3},{1,2},{2,1},{3,0},{4,7},{5,6},{6,5},{7,4},{8,11},{9,10},{10,... | collective-permute-start | bytes 196616 | tf_op jit(solution)/shard_map/ppermute | solution.py:373
  50.8 1.9 %collective-permute-start.23 = (bf16[32,896]{1,0:T(8,128)(2,1)S(1)}, bf16[32,896]{1,0:T(8,128)(2,1)S(1)}, u32[]{:S(2)}, u32[]{:S(2)}) collective-permute-start(bf16[32,896]{1,0:T(8,128)(2,1)S(1)} %get-tuple-element.132), channel_id=1, source_target_pairs={{0,4},{4,0},{8,12},{12,8},{1,5},{5,1},{9,13},{13,9},{2,6},{6,2},{1... | collective-permute-start | bytes 172040 | tf_op jit(solution)/shard_map/ppermute | solution.py:362
  50.8 1.8 %collective-permute-start.24 = (bf16[32,896]{1,0:T(8,128)(2,1)S(1)}, bf16[32,896]{1,0:T(8,128)(2,1)S(1)}, u32[]{:S(2)}, u32[]{:S(2)}) collective-permute-start(bf16[32,896]{1,0:T(8,128)(2,1)S(1)} %get-tuple-element.133), channel_id=1, source_target_pairs={{0,4},{4,0},{8,12},{12,8},{1,5},{5,1},{9,13},{13,9},{2,6},{6,2},{1... | collective-permute-start | bytes 172040 | tf_op jit(solution)/shard_map/ppermute | solution.py:362
  51.3 10.3 %collective-permute-start.21 = (bf16[16,2048]{1,0:T(8,128)(2,1)S(1)}, bf16[16,2048]{1,0:T(8,128)(2,1)S(1)}, u32[]{:S(2)}, u32[]{:S(2)}) collective-permute-start(bf16[16,2048]{1,0:T(8,128)(2,1)S(1)} %get-tuple-element.128), channel_id=1, source_target_pairs={{0,2},{1,3},{2,0},{3,1},{4,6},{5,7},{6,4},{7,5},{8,10},{9,11},{10,... | collective-permute-start | bytes 196616 | tf_op jit(solution)/shard_map/ppermute | solution.py:373
  54.1 7.6 %collective-permute-start.25 = (bf16[16,2048]{1,0:T(8,128)(2,1)S(1)}, bf16[16,2048]{1,0:T(8,128)(2,1)S(1)}, u32[]{:S(2)}, u32[]{:S(2)}) collective-permute-start(bf16[16,2048]{1,0:T(8,128)(2,1)S(1)} %get-tuple-element.136), channel_id=1, source_target_pairs={{0,3},{1,2},{2,1},{3,0},{4,7},{5,6},{6,5},{7,4},{8,11},{9,10},{10,... | collective-permute-start | bytes 196616 | tf_op jit(solution)/shard_map/ppermute | solution.py:373
  55.9 8.3 %collective-permute-start.26 = (bf16[16,2048]{1,0:T(8,128)(2,1)S(1)}, bf16[16,2048]{1,0:T(8,128)(2,1)S(1)}, u32[]{:S(2)}, u32[]{:S(2)}) collective-permute-start(bf16[16,2048]{1,0:T(8,128)(2,1)S(1)} %get-tuple-element.137), channel_id=1, source_target_pairs={{0,2},{1,3},{2,0},{3,1},{4,6},{5,7},{6,4},{7,5},{8,10},{9,11},{10,... | collective-permute-start | bytes 196616 | tf_op jit(solution)/shard_map/ppermute | solution.py:373
  57.1 7.2 %collective-permute-start.27 = (bf16[16,2048]{1,0:T(8,128)(2,1)S(1)}, bf16[16,2048]{1,0:T(8,128)(2,1)S(1)}, u32[]{:S(2)}, u32[]{:S(2)}) collective-permute-start(bf16[16,2048]{1,0:T(8,128)(2,1)S(1)} %get-tuple-element.138), channel_id=1, source_target_pairs={{0,1},{1,0},{2,3},{3,2},{4,5},{5,4},{6,7},{7,6},{8,9},{9,8},{10,11... | collective-permute-start | bytes 196616 | tf_op jit(solution)/shard_map/ppermute | solution.py:385
  58.5 5.9 %collective-permute-start.28 = (bf16[16,2048]{1,0:T(8,128)(2,1)S(1)}, bf16[16,2048]{1,0:T(8,128)(2,1)S(1)}, u32[]{:S(2)}, u32[]{:S(2)}) collective-permute-start(bf16[16,2048]{1,0:T(8,128)(2,1)S(1)} %get-tuple-element.139), channel_id=1, source_target_pairs={{0,1},{1,0},{2,3},{3,2},{4,5},{5,4},{6,7},{7,6},{8,9},{9,8},{10,11... | collective-permute-start | bytes 196616 | tf_op jit(solution)/shard_map/ppermute | solution.py:385
  64.6 1.9 %collective-permute-start.29 = (bf16[2,4,2048]{2,1,0:T(4,128)(2,1)S(1)}, bf16[2,4,2048]{2,1,0:T(4,128)(2,1)S(1)}, u32[]{:S(2)}, u32[]{:S(2)}) collective-permute-start(bf16[2,4,2048]{2,1,0:T(4,128)(2,1)S(1)} %get-tuple-element.142), channel_id=1, source_target_pairs={{0,4},{4,0},{8,12},{12,8},{1,5},{5,1},{9,13},{13,9},{2,6},{6,2},{1... | collective-permute-start | bytes 98312 | tf_op jit(solution)/shard_map/ppermute | solution.py:387
  64.7 4.0 %collective-permute-start.30 = (bf16[2,4,2048]{2,1,0:T(4,128)(2,1)S(1)}, bf16[2,4,2048]{2,1,0:T(4,128)(2,1)S(1)}, u32[]{:S(2)}, u32[]{:S(2)}) collective-permute-start(bf16[2,4,2048]{2,1,0:T(4,128)(2,1)S(1)} %get-tuple-element.143), channel_id=1, source_target_pairs={{0,8},{4,12},{8,0},{12,4},{1,9},{5,13},{9,1},{13,5},{2,10},{6,14},... | collective-permute-start | bytes 98312 | tf_op jit(solution)/shard_map/ppermute | solution.py:387
  65.9 3.3 %collective-permute-start.31 = (bf16[2,4,2048]{2,1,0:T(4,128)(2,1)S(1)}, bf16[2,4,2048]{2,1,0:T(4,128)(2,1)S(1)}, u32[]{:S(2)}, u32[]{:S(2)}) collective-permute-start(bf16[2,4,2048]{2,1,0:T(4,128)(2,1)S(1)} %get-tuple-element.144), channel_id=1, source_target_pairs={{0,12},{4,8},{8,4},{12,0},{1,13},{5,9},{9,5},{13,1},{2,14},{6,10},... | collective-permute-start | bytes 98312 | tf_op jit(solution)/shard_map/ppermute | solution.py:387
  (7 other events, 37.6 us)

commit v9 on v8

--- a/solution.py
+++ b/solution.py
@@ -185,6 +185,11 @@
         out[...] = ins[0][i * rows : (i + 1) * rows, :]
 
 
+def two_body(ins, _, outs, __):
+    for x, out in zip(ins, outs):
+        out[...] = x[...]
+
+
 def halves_dot(x_ref, w_refs):
     total = 0.0
     height = w_refs[0].shape[0]
@@ -298,15 +303,16 @@
     block = like((4 * slots, width))
     near_block, token = run(stack_body, (block,), (own, core), token)
     near_sent = [lax.ppermute(near_block, "col", X3), lax.ppermute(near_block, "col", X1)]
+    pick, token = run(pick_body, (like((steps * rows, steps * assign.shape[1])),), (counts, assign), token)
     far_block, token = run(stack_body, (block,), (y, yd), token)
-    far_sent = [lax.ppermute(far_block, "col", X3), lax.ppermute(far_block, "col", X1)]
+    far_sent = [lax.ppermute(far_block, "col", X3)]
     token = bring(1, 1, token)
-    passed, token = run(after_body, (block,), (near_sent[0], near_sent[1]), token)
+    passed, late, token = run(two_body, (block, block), (near_sent[0], far_block, near_sent[1]), token)
     near_sent.append(lax.ppermute(passed, "col", X1))
+    far_sent.append(lax.ppermute(late, "col", X1))
     token = bring(1, 0, token)
-    passed, token = run(after_body, (block,), (far_sent[0], far_sent[1]), token)
+    passed, token = run(after_body, (block,), (far_sent[0],), token)
     far_sent.append(lax.ppermute(passed, "col", X1))
-    pick, token = run(pick_body, (like((steps * rows, steps * assign.shape[1])),), (counts, assign), token)
     token = bring(0, 1, token)
     pieces = []
     for dz in range(4):

time: 70 us -> 71.2 us (1.017)
  local copies, waits for them, and re-layouts: 2.98 us -> 4.62 us
  starting transfers between devices: 31 us -> 29.6 us
  waiting for transfers between devices: 10.3 us -> 11.2 us
    ppermute x2, waiting for transfers between devices: 5.14 us -> 1.97 us  [down_rest(): lax.ppermute(send2, 'col', X2)]
    ppermute x2, waiting for transfers between devices: 0.01 us -> 2.39 us  [down_rest(): lax.ppermute(send3, 'col', X3)]
    unnamed x14, local copies, waits for them, and re-layouts: 2.98 us -> 4.62 us
    ppermute x1, starting transfers between devices: 1.62 us -> 0.08 us  [near_plan(): near_sent.append(lax.ppermute(passed, 'col', X1))]
    ppermute x2, waiting for transfers between devices: 0.16 us -> 1.32 us  [near_plan(): lax.ppermute(s, 'col', X1)]
    ppermute x2, starting transfers between devices: 2.44 us -> 1.51 us  [down_rest(): lax.ppermute(send2, 'col', X2)]
    ppermute x4, waiting for transfers between devices: 0.01 us -> 0.89 us  [shared(): return (tuple((lax.ppermute(p, 'row', X1) for p in passed)), token)]
  transfers between devices with their start and end apart: 32 -> 32, of which waited for: 12 -> 13; matrix products, arithmetic and copies ran while one was open for 0% -> 0% of each run, Pallas kernels for 32% -> 32%
where the time goes in v9:
time: 71.2 us; the launch traced here: 71 us
  starting transfers between devices  29.6 us (42%)
  Pallas kernels  25.2 us (35%)
  waiting for transfers between devices  11.2 us (16%)
  local copies, waits for them, and re-layouts  4.62 us (6%)
    pallas_call x26, Pallas kernels, run(): pl.pallas_call(wrapped, out_shape=outs, in_specs=[spec or vmem] * count +...  25.2 us
    unnamed x14, local copies, waits for them, and re-layouts  4.62 us
    ppermute x2, starting transfers between devices, down_rest(): lax.ppermute(send3, 'col', X3)  3.96 us
    ppermute x1, starting transfers between devices, near_plan(): lax.ppermute(near_block, 'col', X3)  3.87 us
    ppermute x2, starting transfers between devices, near_plan(): y, yd = (lax.ppermute(y, 'row', X2), lax.ppermute(yd, 'row', X3))  2.66 us
    ppermute x2, starting transfers between devices, activate(): y = lax.ppermute(result, 'row', X2)  2.39 us
    ppermute x2, waiting for transfers between devices, down_rest(): lax.ppermute(send3, 'col', X3)  2.39 us
    ppermute x2, starting transfers between devices, near_plan(): lax.ppermute(s, 'col', X1)  2.3 us
  transfers between devices with their start and end apart: 32, of which 13 were waited for; matrix products, arithmetic and copies ran while one was open for 0% of the time, Pallas kernels for 32%

profile of v9, /device:TPU:0, one launch (start us, length us, event | category | flops | bytes accessed | tf_op | source)
XLA Modules:
  0.0 71.0 jit_solution(13150417117416350044)
XLA Ops:
  0.0 0.9 %copy-done = bf16[2,8,8192]{2,1,0:T(8,128)(2,1)S(1)} copy-done((bf16[2,8,8192]{2,1,0:T(8,128)(2,1)S(1)}, bf16[2,8,8192]{2,1,0:T(8,128)(2,1)}, u32[]{:S(2)}) %copy-start) | copy-done | bytes 262168
  1.7 2.6 %collective-permute-start.1 = (bf16[2,8,2048]{2,1,0:T(8,128)(2,1)S(1)}, bf16[2,8,2048]{2,1,0:T(8,128)(2,1)S(1)}, u32[]{:S(2)}, u32[]{:S(2)}) collective-permute-start(bf16[2,8,2048]{2,1,0:T(8,128)(2,1)S(1)} %get-tuple-element.81), channel_id=1, source_target_pairs={{0,8},{4,12},{8,0},{12,4},{1,9},{5,13},{9,1},{13,5},{2,10},{6,14},... | collective-permute-start | bytes 196616 | tf_op jit(solution)/shard_map/ppermute | solution.py:294
  4.4 3.9 %collective-permute-start.4 = (bf16[32,2048]{1,0:T(8,128)(2,1)S(1)}, bf16[32,2048]{1,0:T(8,128)(2,1)S(1)}, u32[]{:S(2)}, u32[]{:S(2)}) collective-permute-start(bf16[32,2048]{1,0:T(8,128)(2,1)S(1)} %get-tuple-element.80.refs_0_), channel_id=1, source_target_pairs={{0,3},{1,2},{2,1},{3,0},{4,7},{5,6},{6,5},{7,4},{8,11},{9,10},{10,... | collective-permute-start | bytes 393224 | tf_op jit(solution)/shard_map/ppermute | solution.py:305
  8.2 0.7 copy-done.1
  8.9 0.7 copy-done.2
  9.9 2.1 %collective-permute-start.7 = (bf16[32,2048]{1,0:T(8,128)(2,1)S(1)}, bf16[32,2048]{1,0:T(8,128)(2,1)S(1)}, u32[]{:S(2)}, u32[]{:S(2)}) collective-permute-start(bf16[32,2048]{1,0:T(8,128)(2,1)S(1)} %get-tuple-element.85.refs_1_), channel_id=1, source_target_pairs={{0,3},{1,2},{2,1},{3,0},{4,7},{5,6},{6,5},{7,4},{8,11},{9,10},{10,... | collective-permute-start | bytes 393224 | tf_op jit(solution)/shard_map/ppermute | solution.py:308
  12.0 3.2 %shard_map.68 = (bf16[2048,1792]{1,0:T(8,128)(2,1)S(1)}, f32[8,128]{1,0:T(8,128)S(1)}) custom-call(bf16[2048,3584]{1,0:T(8,128)(2,1)} %refs_2_.1, bf16[2048,3584]{1,0:T(8,128)(2,1)} %refs_3_.1, f32[8,128]{1,0:T(8,128)S(1)} %get-tuple-element.86.refs_2_), custom_call_target="tpu_custom_call" | custom-call | bytes 1 | tf_op jit(solution)/shard_map/pallas_call | solution.py:41
  15.4 2.0 %collective-permute-start.5 = (bf16[32,2048]{1,0:T(8,128)(2,1)S(1)}, bf16[32,2048]{1,0:T(8,128)(2,1)S(1)}, u32[]{:S(2)}, u32[]{:S(2)}) collective-permute-start(bf16[32,2048]{1,0:T(8,128)(2,1)S(1)} %get-tuple-element.88), channel_id=1, source_target_pairs={{0,1},{1,0},{2,3},{3,2},{4,5},{5,4},{6,7},{7,6},{8,9},{9,8},{10,11... | collective-permute-start | bytes 393224 | tf_op jit(solution)/shard_map/ppermute | solution.py:312
  17.6 3.2 %shard_map.70 = (bf16[2048,1792]{1,0:T(8,128)(2,1)S(1)}, f32[8,128]{1,0:T(8,128)S(1)}) custom-call(bf16[2048,3584]{1,0:T(8,128)(2,1)} %refs_2_.1, bf16[2048,3584]{1,0:T(8,128)(2,1)} %refs_3_.1, f32[8,128]{1,0:T(8,128)S(1)} %get-tuple-element.90.refs_2_), custom_call_target="tpu_custom_call" | custom-call | bytes 1 | tf_op jit(solution)/shard_map/pallas_call | solution.py:41
  20.8 2.0 %collective-permute-start.8 = (bf16[32,2048]{1,0:T(8,128)(2,1)S(1)}, bf16[32,2048]{1,0:T(8,128)(2,1)S(1)}, u32[]{:S(2)}, u32[]{:S(2)}) collective-permute-start(bf16[32,2048]{1,0:T(8,128)(2,1)S(1)} %get-tuple-element.92), channel_id=1, source_target_pairs={{0,1},{1,0},{2,3},{3,2},{4,5},{5,4},{6,7},{7,6},{8,9},{9,8},{10,11... | collective-permute-start | bytes 393224 | tf_op jit(solution)/shard_map/ppermute | solution.py:315
  22.8 3.3 %shard_map.72 = (bf16[2048,1792]{1,0:T(8,128)(2,1)S(1)}, f32[8,128]{1,0:T(8,128)S(1)}) custom-call(bf16[2048,3584]{1,0:T(8,128)(2,1)} %refs_2_.1, bf16[2048,3584]{1,0:T(8,128)(2,1)} %refs_3_.1, f32[8,128]{1,0:T(8,128)S(1)} %get-tuple-element.95.refs_2_), custom_call_target="tpu_custom_call" | custom-call | bytes 1 | tf_op jit(solution)/shard_map/pallas_call | solution.py:41
  26.5 1.4 %shard_map.73 = (bf16[128,2048]{1,0:T(8,128)(2,1)S(1)}, bf16[64,1792]{1,0:T(8,128)(2,1)S(1)}, bf16[64,1792]{1,0:T(8,128)(2,1)S(1)}, f32[8,128]{1,0:T(8,128)S(1)}) custom-call(bf16[32,2048]{1,0:T(8,128)(2,1)S(1)} %get-tuple-element.80.refs_0_, bf16[32,2048]{1,0:T(8,128)(2,1)S(1)} %get-tuple-element.85.refs_1_, ...), custom_call_target="tpu_custom_call" | custom-call | bytes 1 | tf_op jit(solution)/shard_map/pallas_call | solution.py:41
  28.5 1.1 %shard_map.74 = (f32[128,1792]{1,0:T(8,128)S(1)}, f32[8,128]{1,0:T(8,128)S(1)}) custom-call(bf16[128,2048]{1,0:T(8,128)(2,1)S(1)} %get-tuple-element.97.refs_0_, bf16[2048,1792]{1,0:T(8,128)(2,1)S(1)} %get-tuple-element.99.refs_1_, f32[8,128]{1,0:T(8,128)S(1)} %get-tuple-element.100.refs_2_), custom_call_target="tpu_custom_call" | custom-call | bytes 1 | tf_op jit(solution)/shard_map/pallas_call | solution.py:41
  30.0 1.8 %collective-permute-start.11 = (bf16[64,1792]{1,0:T(8,128)(2,1)S(1)}, bf16[64,1792]{1,0:T(8,128)(2,1)S(1)}, u32[]{:S(2)}, u32[]{:S(2)}) collective-permute-start(bf16[64,1792]{1,0:T(8,128)(2,1)S(1)} %get-tuple-element.109), channel_id=1, source_target_pairs={{0,8},{4,12},{8,0},{12,4},{1,9},{5,13},{9,1},{13,5},{2,10},{6,14},... | collective-permute-start | bytes 688136 | tf_op jit(solution)/shard_map/ppermute | solution.py:335
  31.8 3.3 %shard_map.76 = (bf16[64,1792]{1,0:T(8,128)(2,1)S(1)}, bf16[64,1792]{1,0:T(8,128)(2,1)S(1)}, bf16[2048,1792]{1,0:T(8,128)(2,1)S(1)}, f32[8,128]{1,0:T(8,128)S(1)}) custom-call(bf16[128,2048]{1,0:T(8,128)(2,1)S(1)} %get-tuple-element.97.refs_0_, bf16[2048,1792]{1,0:T(8,128)(2,1)S(1)} %get-tuple-element.98.refs_1_, bf16[2048,3584]{1,0:T(8,128)(2,1)} %refs_2_.1, ...), custom_call_target="tpu_custom_call" | custom-call | bytes 1 | tf_op jit(solution)/shard_map/pallas_call | solution.py:41
  35.7 1.1 %shard_map.77 = (f32[128,1792]{1,0:T(8,128)S(1)}, f32[8,128]{1,0:T(8,128)S(1)}) custom-call(bf16[128,2048]{1,0:T(8,128)(2,1)S(1)} %get-tuple-element.97.refs_0_, bf16[2048,1792]{1,0:T(8,128)(2,1)S(1)} %get-tuple-element.106.refs_1_, f32[8,128]{1,0:T(8,128)S(1)} %get-tuple-element.107.refs_2_), custom_call_target="tpu_custom_call" | custom-call | bytes 1 | tf_op jit(solution)/shard_map/pallas_call | solution.py:41
  37.4 1.2 %slice-done.2 = s8[4194304]{0:T(1024)(128)(4,1)S(1)} async-done(((s8[14680064]{0:T(1024)(128)(4,1)}), s8[4194304]{0:T(1024)(128)(4,1)S(1)}, s32[]{:S(2)}) %slice-start.2) | async-done | bytes 4194328
  41.3 1.4 %shard_map.81 = (f32[64,2048]{1,0:T(8,128)S(1)}, f32[8,128]{1,0:T(8,128)S(1)}) custom-call(bf16[1792,2048]{1,0:T(8,128)(2,1)S(1)} %get-tuple-element.115.refs_0_, bf16[64,896]{1,0:T(8,128)(2,1)S(1)} %get-tuple-element.116.refs_1_, bf16[64,896]{1,0:T(8,128)(2,1)S(1)} %collective-permute-done.13.refs_2_, f32[8,128]{1,0:T(8,128)S(1)} %get-tuple-element.117.refs_3_), custom_call_target="tpu_custom_call" | custom-call | bytes 1 | tf_op jit(solution)/shard_map/pallas_call | solution.py:41
  43.5 1.9 %collective-permute-start.22 = (bf16[64,896]{1,0:T(8,128)(2,1)S(1)}, bf16[64,896]{1,0:T(8,128)(2,1)S(1)}, u32[]{:S(2)}, u32[]{:S(2)}) collective-permute-start(bf16[64,896]{1,0:T(8,128)(2,1)S(1)} %get-tuple-element.125.refs_1_), channel_id=1, source_target_pairs={{0,8},{4,12},{8,0},{12,4},{1,9},{5,13},{9,1},{13,5},{2,10},{6,14},... | collective-permute-start | bytes 344072 | tf_op jit(solution)/shard_map/ppermute | solution.py:356
  46.3 1.4 %shard_map.84 = (f32[64,2048]{1,0:T(8,128)S(1)}, f32[8,128]{1,0:T(8,128)S(1)}) custom-call(bf16[1792,2048]{1,0:T(8,128)(2,1)S(1)} %get-tuple-element.115.refs_0_, bf16[64,896]{1,0:T(8,128)(2,1)S(1)} %get-tuple-element.125.refs_1_, bf16[64,896]{1,0:T(8,128)(2,1)S(1)} %collective-permute-done.19.refs_2_, f32[8,128]{1,0:T(8,128)S(1)} %get-tuple-element.126.refs_3_), custom_call_target="tpu_custom_call" | custom-call | bytes 1 | tf_op jit(solution)/shard_map/pallas_call | solution.py:41
  47.7 1.4 %shard_map.85 = (f32[16,2048]{1,0:T(8,128)S(1)}, bf16[16,2048]{1,0:T(8,128)(2,1)S(1)}, bf16[16,2048]{1,0:T(8,128)(2,1)S(1)}, bf16[16,2048]{1,0:T(8,128)(2,1)S(1)}, f32[8,128]{1,0:T(8,128)S(1)}) custom-call(bf16[1792,2048]{1,0:T(8,128)(2,1)S(1)} %get-tuple-element.114.refs_0_, f32[64,2048]{1,0:T(8,128)S(1)} %get-tuple-element.118.refs_1_, ...), custom_call_target="tpu_custom_call" | custom-call | bytes 1 | tf_op jit(solution)/shard_map/pallas_call | solution.py:41
  49.2 3.3 %collective-permute-start.20 = (bf16[16,2048]{1,0:T(8,128)(2,1)S(1)}, bf16[16,2048]{1,0:T(8,128)(2,1)S(1)}, u32[]{:S(2)}, u32[]{:S(2)}) collective-permute-start(bf16[16,2048]{1,0:T(8,128)(2,1)S(1)} %get-tuple-element.129), channel_id=1, source_target_pairs={{0,3},{1,2},{2,1},{3,0},{4,7},{5,6},{6,5},{7,4},{8,11},{9,10},{10,... | collective-permute-start | bytes 196616 | tf_op jit(solution)/shard_map/ppermute | solution.py:379
  53.0 0.7 %collective-permute-done.23.refs_4_ = bf16[32,896]{1,0:T(8,128)(2,1)S(1)} collective-permute-done((bf16[32,896]{1,0:T(8,128)(2,1)S(1)}, bf16[32,896]{1,0:T(8,128)(2,1)S(1)}, u32[]{:S(2)}, u32[]{:S(2)}) %collective-permute-start.23) | collective-permute-done | bytes 57376 | tf_op jit(solution)/shard_map/ppermute | solution.py:368
  53.9 1.4 %shard_map.87 = (f32[16,2048]{1,0:T(8,128)S(1)}, bf16[16,2048]{1,0:T(8,128)(2,1)S(1)}, bf16[16,2048]{1,0:T(8,128)(2,1)S(1)}, bf16[16,2048]{1,0:T(8,128)(2,1)S(1)...) custom-call(bf16[1792,2048]{1,0:T(8,128)(2,1)S(1)} %get-tuple-element.114.refs_0_, ...), custom_call_target="tpu_custom_call" | custom-call | bytes 1 | tf_op jit(solution)/shard_map/pallas_call | solution.py:41
  55.3 0.7 collective-permute-start.25
  56.0 1.5 %collective-permute-start.26 = (bf16[16,2048]{1,0:T(8,128)(2,1)S(1)}, bf16[16,2048]{1,0:T(8,128)(2,1)S(1)}, u32[]{:S(2)}, u32[]{:S(2)}) collective-permute-start(bf16[16,2048]{1,0:T(8,128)(2,1)S(1)} %get-tuple-element.139), channel_id=1, source_target_pairs={{0,2},{1,3},{2,0},{3,1},{4,6},{5,7},{6,4},{7,5},{8,10},{9,11},{10,... | collective-permute-start | bytes 196616 | tf_op jit(solution)/shard_map/ppermute | solution.py:379
  57.5 2.3 %collective-permute-start.27 = (bf16[16,2048]{1,0:T(8,128)(2,1)S(1)}, bf16[16,2048]{1,0:T(8,128)(2,1)S(1)}, u32[]{:S(2)}, u32[]{:S(2)}) collective-permute-start(bf16[16,2048]{1,0:T(8,128)(2,1)S(1)} %get-tuple-element.140), channel_id=1, source_target_pairs={{0,1},{1,0},{2,3},{3,2},{4,5},{5,4},{6,7},{7,6},{8,9},{9,8},{10,11... | collective-permute-start | bytes 196616 | tf_op jit(solution)/shard_map/ppermute | solution.py:391
  59.8 2.4 %collective-permute-done.25.refs_4_ = bf16[16,2048]{1,0:T(8,128)(2,1)S(1)} collective-permute-done((bf16[16,2048]{1,0:T(8,128)(2,1)S(1)}, bf16[16,2048]{1,0:T(8,128)(2,1)S(1)}, u32[]{:S(2)}, u32[]{:S(2)}) %collective-permute-start.25) | collective-permute-done | bytes 65568 | tf_op jit(solution)/shard_map/ppermute | solution.py:379
  62.2 2.0 %collective-permute-done.26.refs_5_ = bf16[16,2048]{1,0:T(8,128)(2,1)S(1)} collective-permute-done((bf16[16,2048]{1,0:T(8,128)(2,1)S(1)}, bf16[16,2048]{1,0:T(8,128)(2,1)S(1)}, u32[]{:S(2)}, u32[]{:S(2)}) %collective-permute-start.26) | collective-permute-done | bytes 65568 | tf_op jit(solution)/shard_map/ppermute | solution.py:379
  64.2 1.3 %collective-permute-done.28.refs_7_ = bf16[16,2048]{1,0:T(8,128)(2,1)S(1)} collective-permute-done((bf16[16,2048]{1,0:T(8,128)(2,1)S(1)}, bf16[16,2048]{1,0:T(8,128)(2,1)S(1)}, u32[]{:S(2)}, u32[]{:S(2)}) %collective-permute-start.28) | collective-permute-done | bytes 65568 | tf_op jit(solution)/shard_map/ppermute | solution.py:391
  65.8 1.2 %collective-permute-start.30 = (bf16[2,4,2048]{2,1,0:T(4,128)(2,1)S(1)}, bf16[2,4,2048]{2,1,0:T(4,128)(2,1)S(1)}, u32[]{:S(2)}, u32[]{:S(2)}) collective-permute-start(bf16[2,4,2048]{2,1,0:T(4,128)(2,1)S(1)} %get-tuple-element.145), channel_id=1, source_target_pairs={{0,8},{4,12},{8,0},{12,4},{1,9},{5,13},{9,1},{13,5},{2,10},{6,14},... | collective-permute-start | bytes 98312 | tf_op jit(solution)/shard_map/ppermute | solution.py:393
  67.6 2.1 %collective-permute-done.30.refs_2_ = bf16[2,4,2048]{2,1,0:T(4,128)(2,1)S(1)} collective-permute-done((bf16[2,4,2048]{2,1,0:T(4,128)(2,1)S(1)}, bf16[2,4,2048]{2,1,0:T(4,128)(2,1)S(1)}, u32[]{:S(2)}, u32[]{:S(2)}) %collective-permute-start.30) | collective-permute-done | bytes 32800 | tf_op jit(solution)/shard_map/ppermute | solution.py:393
  (73 shorter events, 11.1 us)
Async XLA Ops:
  1.2 3.2 %collective-permute-start = (bf16[2,8,2048]{2,1,0:T(8,128)(2,1)S(1)}, bf16[2,8,2048]{2,1,0:T(8,128)(2,1)S(1)}, u32[]{:S(2)}, u32[]{:S(2)}) collective-permute-start(bf16[2,8,2048]{2,1,0:T(8,128)(2,1)S(1)} %get-tuple-element.78), channel_id=1, source_target_pairs={{0,4},{4,0},{8,12},{12,8},{1,5},{5,1},{9,13},{13,9},{2,6},{6,2},{1... | collective-permute-start | bytes 196616 | tf_op jit(solution)/shard_map/ppermute | solution.py:295
  1.7 8.2 %collective-permute-start.1 = (bf16[2,8,2048]{2,1,0:T(8,128)(2,1)S(1)}, bf16[2,8,2048]{2,1,0:T(8,128)(2,1)S(1)}, u32[]{:S(2)}, u32[]{:S(2)}) collective-permute-start(bf16[2,8,2048]{2,1,0:T(8,128)(2,1)S(1)} %get-tuple-element.81), channel_id=1, source_target_pairs={{0,8},{4,12},{8,0},{12,4},{1,9},{5,13},{9,1},{13,5},{2,10},{6,14},... | collective-permute-start | bytes 196616 | tf_op jit(solution)/shard_map/ppermute | solution.py:294
  4.3 5.6 %collective-permute-start.2 = (bf16[2,8,2048]{2,1,0:T(8,128)(2,1)S(1)}, bf16[2,8,2048]{2,1,0:T(8,128)(2,1)S(1)}, u32[]{:S(2)}, u32[]{:S(2)}) collective-permute-start(bf16[2,8,2048]{2,1,0:T(8,128)(2,1)S(1)} %get-tuple-element.82), channel_id=1, source_target_pairs={{0,12},{4,8},{8,4},{12,0},{1,13},{5,9},{9,5},{13,1},{2,14},{6,10},... | collective-permute-start | bytes 196616 | tf_op jit(solution)/shard_map/ppermute | solution.py:294
  4.4 10.8 %collective-permute-start.4 = (bf16[32,2048]{1,0:T(8,128)(2,1)S(1)}, bf16[32,2048]{1,0:T(8,128)(2,1)S(1)}, u32[]{:S(2)}, u32[]{:S(2)}) collective-permute-start(bf16[32,2048]{1,0:T(8,128)(2,1)S(1)} %get-tuple-element.80.refs_0_), channel_id=1, source_target_pairs={{0,3},{1,2},{2,1},{3,0},{4,7},{5,6},{6,5},{7,4},{8,11},{9,10},{10,... | collective-permute-start | bytes 393224 | tf_op jit(solution)/shard_map/ppermute | solution.py:305
  8.2 7.2 %collective-permute-start.3 = (bf16[32,2048]{1,0:T(8,128)(2,1)S(1)}, bf16[32,2048]{1,0:T(8,128)(2,1)S(1)}, u32[]{:S(2)}, u32[]{:S(2)}) collective-permute-start(bf16[32,2048]{1,0:T(8,128)(2,1)S(1)} %get-tuple-element.80.refs_0_), channel_id=1, source_target_pairs={{0,1},{1,0},{2,3},{3,2},{4,5},{5,4},{6,7},{7,6},{8,9},{9,8},{10,11... | collective-permute-start | bytes 393224 | tf_op jit(solution)/shard_map/ppermute | solution.py:305
  9.9 10.9 %collective-permute-start.7 = (bf16[32,2048]{1,0:T(8,128)(2,1)S(1)}, bf16[32,2048]{1,0:T(8,128)(2,1)S(1)}, u32[]{:S(2)}, u32[]{:S(2)}) collective-permute-start(bf16[32,2048]{1,0:T(8,128)(2,1)S(1)} %get-tuple-element.85.refs_1_), channel_id=1, source_target_pairs={{0,3},{1,2},{2,1},{3,0},{4,7},{5,6},{6,5},{7,4},{8,11},{9,10},{10,... | collective-permute-start | bytes 393224 | tf_op jit(solution)/shard_map/ppermute | solution.py:308
  15.4 10.7 %collective-permute-start.5 = (bf16[32,2048]{1,0:T(8,128)(2,1)S(1)}, bf16[32,2048]{1,0:T(8,128)(2,1)S(1)}, u32[]{:S(2)}, u32[]{:S(2)}) collective-permute-start(bf16[32,2048]{1,0:T(8,128)(2,1)S(1)} %get-tuple-element.88), channel_id=1, source_target_pairs={{0,1},{1,0},{2,3},{3,2},{4,5},{5,4},{6,7},{7,6},{8,9},{9,8},{10,11... | collective-permute-start | bytes 393224 | tf_op jit(solution)/shard_map/ppermute | solution.py:312
  17.5 8.6 %collective-permute-start.6 = (bf16[32,2048]{1,0:T(8,128)(2,1)S(1)}, bf16[32,2048]{1,0:T(8,128)(2,1)S(1)}, u32[]{:S(2)}, u32[]{:S(2)}) collective-permute-start(bf16[32,2048]{1,0:T(8,128)(2,1)S(1)} %get-tuple-element.89), channel_id=1, source_target_pairs={{0,1},{1,0},{2,3},{3,2},{4,5},{5,4},{6,7},{7,6},{8,9},{9,8},{10,11... | collective-permute-start | bytes 393224 | tf_op jit(solution)/shard_map/ppermute | solution.py:311
  20.8 5.7 %collective-permute-start.8 = (bf16[32,2048]{1,0:T(8,128)(2,1)S(1)}, bf16[32,2048]{1,0:T(8,128)(2,1)S(1)}, u32[]{:S(2)}, u32[]{:S(2)}) collective-permute-start(bf16[32,2048]{1,0:T(8,128)(2,1)S(1)} %get-tuple-element.92), channel_id=1, source_target_pairs={{0,1},{1,0},{2,3},{3,2},{4,5},{5,4},{6,7},{7,6},{8,9},{9,8},{10,11... | collective-permute-start | bytes 393224 | tf_op jit(solution)/shard_map/ppermute | solution.py:315
  28.0 1.7 %collective-permute-start.9 = (bf16[64,1792]{1,0:T(8,128)(2,1)S(1)}, bf16[64,1792]{1,0:T(8,128)(2,1)S(1)}, u32[]{:S(2)}, u32[]{:S(2)}) collective-permute-start(bf16[64,1792]{1,0:T(8,128)(2,1)S(1)} %get-tuple-element.102), channel_id=1, source_target_pairs={{0,4},{4,0},{8,12},{12,8},{1,5},{5,1},{9,13},{13,9},{2,6},{6,2},{1... | collective-permute-start | bytes 688136 | tf_op jit(solution)/shard_map/ppermute | solution.py:332
  28.0 1.8 %collective-permute-start.10 = (bf16[64,1792]{1,0:T(8,128)(2,1)S(1)}, bf16[64,1792]{1,0:T(8,128)(2,1)S(1)}, u32[]{:S(2)}, u32[]{:S(2)}) collective-permute-start(bf16[64,1792]{1,0:T(8,128)(2,1)S(1)} %get-tuple-element.103), channel_id=1, source_target_pairs={{0,4},{4,0},{8,12},{12,8},{1,5},{5,1},{9,13},{13,9},{2,6},{6,2},{1... | collective-permute-start | bytes 688136 | tf_op jit(solution)/shard_map/ppermute | solution.py:332
  30.0 9.8 %collective-permute-start.11 = (bf16[64,1792]{1,0:T(8,128)(2,1)S(1)}, bf16[64,1792]{1,0:T(8,128)(2,1)S(1)}, u32[]{:S(2)}, u32[]{:S(2)}) collective-permute-start(bf16[64,1792]{1,0:T(8,128)(2,1)S(1)} %get-tuple-element.109), channel_id=1, source_target_pairs={{0,8},{4,12},{8,0},{12,4},{1,9},{5,13},{9,1},{13,5},{2,10},{6,14},... | collective-permute-start | bytes 688136 | tf_op jit(solution)/shard_map/ppermute | solution.py:335
  35.1 4.6 %collective-permute-start.12 = (bf16[64,1792]{1,0:T(8,128)(2,1)S(1)}, bf16[64,1792]{1,0:T(8,128)(2,1)S(1)}, u32[]{:S(2)}, u32[]{:S(2)}) collective-permute-start(bf16[64,1792]{1,0:T(8,128)(2,1)S(1)} %get-tuple-element.110), channel_id=1, source_target_pairs={{0,4},{4,0},{8,12},{12,8},{1,5},{5,1},{9,13},{13,9},{2,6},{6,2},{1... | collective-permute-start | bytes 688136 | tf_op jit(solution)/shard_map/ppermute | solution.py:345
  35.2 8.1 %collective-permute-start.15 = (bf16[64,1792]{1,0:T(8,128)(2,1)S(1)}, bf16[64,1792]{1,0:T(8,128)(2,1)S(1)}, u32[]{:S(2)}, u32[]{:S(2)}) collective-permute-start(bf16[64,1792]{1,0:T(8,128)(2,1)S(1)} %get-tuple-element.119), channel_id=1, source_target_pairs={{0,8},{4,12},{8,0},{12,4},{1,9},{5,13},{9,1},{13,5},{2,10},{6,14},... | collective-permute-start | bytes 688136 | tf_op jit(solution)/shard_map/ppermute | solution.py:335
  35.6 7.8 %collective-permute-start.16 = (bf16[64,1792]{1,0:T(8,128)(2,1)S(1)}, bf16[64,1792]{1,0:T(8,128)(2,1)S(1)}, u32[]{:S(2)}, u32[]{:S(2)}) collective-permute-start(bf16[64,1792]{1,0:T(8,128)(2,1)S(1)} %get-tuple-element.120), channel_id=1, source_target_pairs={{0,4},{4,0},{8,12},{12,8},{1,5},{5,1},{9,13},{13,9},{2,6},{6,2},{1... | collective-permute-start | bytes 688136 | tf_op jit(solution)/shard_map/ppermute | solution.py:345
  39.9 1.4 %collective-permute-start.13 = (bf16[64,896]{1,0:T(8,128)(2,1)S(1)}, bf16[64,896]{1,0:T(8,128)(2,1)S(1)}, u32[]{:S(2)}, u32[]{:S(2)}) collective-permute-start(bf16[64,896]{1,0:T(8,128)(2,1)S(1)} %get-tuple-element.116.refs_1_), channel_id=1, source_target_pairs={{0,4},{4,0},{8,12},{12,8},{1,5},{5,1},{9,13},{13,9},{2,6},{6,2},{1... | collective-permute-start | bytes 344072 | tf_op jit(solution)/shard_map/ppermute | solution.py:357
  40.0 5.7 %collective-permute-start.14 = (bf16[64,896]{1,0:T(8,128)(2,1)S(1)}, bf16[64,896]{1,0:T(8,128)(2,1)S(1)}, u32[]{:S(2)}, u32[]{:S(2)}) collective-permute-start(bf16[64,896]{1,0:T(8,128)(2,1)S(1)} %get-tuple-element.116.refs_1_), channel_id=1, source_target_pairs={{0,8},{4,12},{8,0},{12,4},{1,9},{5,13},{9,1},{13,5},{2,10},{6,14},... | collective-permute-start | bytes 344072 | tf_op jit(solution)/shard_map/ppermute | solution.py:356
  43.5 2.8 %collective-permute-start.19 = (bf16[64,896]{1,0:T(8,128)(2,1)S(1)}, bf16[64,896]{1,0:T(8,128)(2,1)S(1)}, u32[]{:S(2)}, u32[]{:S(2)}) collective-permute-start(bf16[64,896]{1,0:T(8,128)(2,1)S(1)} %get-tuple-element.125.refs_1_), channel_id=1, source_target_pairs={{0,4},{4,0},{8,12},{12,8},{1,5},{5,1},{9,13},{13,9},{2,6},{6,2},{1... | collective-permute-start | bytes 344072 | tf_op jit(solution)/shard_map/ppermute | solution.py:357
  43.5 8.9 %collective-permute-start.22 = (bf16[64,896]{1,0:T(8,128)(2,1)S(1)}, bf16[64,896]{1,0:T(8,128)(2,1)S(1)}, u32[]{:S(2)}, u32[]{:S(2)}) collective-permute-start(bf16[64,896]{1,0:T(8,128)(2,1)S(1)} %get-tuple-element.125.refs_1_), channel_id=1, source_target_pairs={{0,8},{4,12},{8,0},{12,4},{1,9},{5,13},{9,1},{13,5},{2,10},{6,14},... | collective-permute-start | bytes 344072 | tf_op jit(solution)/shard_map/ppermute | solution.py:356
  45.7 2.0 %collective-permute-start.17 = (bf16[32,896]{1,0:T(8,128)(2,1)S(1)}, bf16[32,896]{1,0:T(8,128)(2,1)S(1)}, u32[]{:S(2)}, u32[]{:S(2)}) collective-permute-start(bf16[32,896]{1,0:T(8,128)(2,1)S(1)} %get-tuple-element.123), channel_id=1, source_target_pairs={{0,4},{4,0},{8,12},{12,8},{1,5},{5,1},{9,13},{13,9},{2,6},{6,2},{1... | collective-permute-start | bytes 172040 | tf_op jit(solution)/shard_map/ppermute | solution.py:368
  45.8 1.9 %collective-permute-start.18 = (bf16[32,896]{1,0:T(8,128)(2,1)S(1)}, bf16[32,896]{1,0:T(8,128)(2,1)S(1)}, u32[]{:S(2)}, u32[]{:S(2)}) collective-permute-start(bf16[32,896]{1,0:T(8,128)(2,1)S(1)} %get-tuple-element.124), channel_id=1, source_target_pairs={{0,4},{4,0},{8,12},{12,8},{1,5},{5,1},{9,13},{13,9},{2,6},{6,2},{1... | collective-permute-start | bytes 172040 | tf_op jit(solution)/shard_map/ppermute | solution.py:368
  49.2 10.6 %collective-permute-start.20 = (bf16[16,2048]{1,0:T(8,128)(2,1)S(1)}, bf16[16,2048]{1,0:T(8,128)(2,1)S(1)}, u32[]{:S(2)}, u32[]{:S(2)}) collective-permute-start(bf16[16,2048]{1,0:T(8,128)(2,1)S(1)} %get-tuple-element.129), channel_id=1, source_target_pairs={{0,3},{1,2},{2,1},{3,0},{4,7},{5,6},{6,5},{7,4},{8,11},{9,10},{10,... | collective-permute-start | bytes 196616 | tf_op jit(solution)/shard_map/ppermute | solution.py:379
  52.5 1.3 %collective-permute-start.23 = (bf16[32,896]{1,0:T(8,128)(2,1)S(1)}, bf16[32,896]{1,0:T(8,128)(2,1)S(1)}, u32[]{:S(2)}, u32[]{:S(2)}) collective-permute-start(bf16[32,896]{1,0:T(8,128)(2,1)S(1)} %get-tuple-element.134), channel_id=1, source_target_pairs={{0,4},{4,0},{8,12},{12,8},{1,5},{5,1},{9,13},{13,9},{2,6},{6,2},{1... | collective-permute-start | bytes 172040 | tf_op jit(solution)/shard_map/ppermute | solution.py:368
  52.5 1.4 %collective-permute-start.24 = (bf16[32,896]{1,0:T(8,128)(2,1)S(1)}, bf16[32,896]{1,0:T(8,128)(2,1)S(1)}, u32[]{:S(2)}, u32[]{:S(2)}) collective-permute-start(bf16[32,896]{1,0:T(8,128)(2,1)S(1)} %get-tuple-element.135), channel_id=1, source_target_pairs={{0,4},{4,0},{8,12},{12,8},{1,5},{5,1},{9,13},{13,9},{2,6},{6,2},{1... | collective-permute-start | bytes 172040 | tf_op jit(solution)/shard_map/ppermute | solution.py:368
  53.0 6.8 %collective-permute-start.21 = (bf16[16,2048]{1,0:T(8,128)(2,1)S(1)}, bf16[16,2048]{1,0:T(8,128)(2,1)S(1)}, u32[]{:S(2)}, u32[]{:S(2)}) collective-permute-start(bf16[16,2048]{1,0:T(8,128)(2,1)S(1)} %get-tuple-element.130), channel_id=1, source_target_pairs={{0,2},{1,3},{2,0},{3,1},{4,6},{5,7},{6,4},{7,5},{8,10},{9,11},{10,... | collective-permute-start | bytes 196616 | tf_op jit(solution)/shard_map/ppermute | solution.py:379
  55.3 6.9 %collective-permute-start.25 = (bf16[16,2048]{1,0:T(8,128)(2,1)S(1)}, bf16[16,2048]{1,0:T(8,128)(2,1)S(1)}, u32[]{:S(2)}, u32[]{:S(2)}) collective-permute-start(bf16[16,2048]{1,0:T(8,128)(2,1)S(1)} %get-tuple-element.138), channel_id=1, source_target_pairs={{0,3},{1,2},{2,1},{3,0},{4,7},{5,6},{6,5},{7,4},{8,11},{9,10},{10,... | collective-permute-start | bytes 196616 | tf_op jit(solution)/shard_map/ppermute | solution.py:379
  56.0 8.2 %collective-permute-start.26 = (bf16[16,2048]{1,0:T(8,128)(2,1)S(1)}, bf16[16,2048]{1,0:T(8,128)(2,1)S(1)}, u32[]{:S(2)}, u32[]{:S(2)}) collective-permute-start(bf16[16,2048]{1,0:T(8,128)(2,1)S(1)} %get-tuple-element.139), channel_id=1, source_target_pairs={{0,2},{1,3},{2,0},{3,1},{4,6},{5,7},{6,4},{7,5},{8,10},{9,11},{10,... | collective-permute-start | bytes 196616 | tf_op jit(solution)/shard_map/ppermute | solution.py:379
  57.5 6.7 %collective-permute-start.27 = (bf16[16,2048]{1,0:T(8,128)(2,1)S(1)}, bf16[16,2048]{1,0:T(8,128)(2,1)S(1)}, u32[]{:S(2)}, u32[]{:S(2)}) collective-permute-start(bf16[16,2048]{1,0:T(8,128)(2,1)S(1)} %get-tuple-element.140), channel_id=1, source_target_pairs={{0,1},{1,0},{2,3},{3,2},{4,5},{5,4},{6,7},{7,6},{8,9},{9,8},{10,11... | collective-permute-start | bytes 196616 | tf_op jit(solution)/shard_map/ppermute | solution.py:391
  59.8 5.7 %collective-permute-start.28 = (bf16[16,2048]{1,0:T(8,128)(2,1)S(1)}, bf16[16,2048]{1,0:T(8,128)(2,1)S(1)}, u32[]{:S(2)}, u32[]{:S(2)}) collective-permute-start(bf16[16,2048]{1,0:T(8,128)(2,1)S(1)} %get-tuple-element.141), channel_id=1, source_target_pairs={{0,1},{1,0},{2,3},{3,2},{4,5},{5,4},{6,7},{7,6},{8,9},{9,8},{10,11... | collective-permute-start | bytes 196616 | tf_op jit(solution)/shard_map/ppermute | solution.py:391
  65.7 1.9 %collective-permute-start.29 = (bf16[2,4,2048]{2,1,0:T(4,128)(2,1)S(1)}, bf16[2,4,2048]{2,1,0:T(4,128)(2,1)S(1)}, u32[]{:S(2)}, u32[]{:S(2)}) collective-permute-start(bf16[2,4,2048]{2,1,0:T(4,128)(2,1)S(1)} %get-tuple-element.144), channel_id=1, source_target_pairs={{0,4},{4,0},{8,12},{12,8},{1,5},{5,1},{9,13},{13,9},{2,6},{6,2},{1... | collective-permute-start | bytes 98312 | tf_op jit(solution)/shard_map/ppermute | solution.py:393
  65.8 4.0 %collective-permute-start.30 = (bf16[2,4,2048]{2,1,0:T(4,128)(2,1)S(1)}, bf16[2,4,2048]{2,1,0:T(4,128)(2,1)S(1)}, u32[]{:S(2)}, u32[]{:S(2)}) collective-permute-start(bf16[2,4,2048]{2,1,0:T(4,128)(2,1)S(1)} %get-tuple-element.145), channel_id=1, source_target_pairs={{0,8},{4,12},{8,0},{12,4},{1,9},{5,13},{9,1},{13,5},{2,10},{6,14},... | collective-permute-start | bytes 98312 | tf_op jit(solution)/shard_map/ppermute | solution.py:393
  67.0 3.3 %collective-permute-start.31 = (bf16[2,4,2048]{2,1,0:T(4,128)(2,1)S(1)}, bf16[2,4,2048]{2,1,0:T(4,128)(2,1)S(1)}, u32[]{:S(2)}, u32[]{:S(2)}) collective-permute-start(bf16[2,4,2048]{2,1,0:T(4,128)(2,1)S(1)} %get-tuple-element.146), channel_id=1, source_target_pairs={{0,12},{4,8},{8,4},{12,0},{1,13},{5,9},{9,5},{13,1},{2,14},{6,10},... | collective-permute-start | bytes 98312 | tf_op jit(solution)/shard_map/ppermute | solution.py:393
  (7 other events, 27.4 us)

commit v10 on v8

--- a/solution.py
+++ b/solution.py
@@ -16,6 +16,7 @@
 F32 = jnp.float32
 MIB = 2**20
 PIECES = 2
+ARRIVAL = (0, 1, 2, 3, 6, 7, 5, 4)
 CUTS = 2
 X1 = ((0, 1), (1, 0), (2, 3), (3, 2))
 X2 = ((0, 2), (1, 3), (2, 0), (3, 1))
@@ -74,7 +75,7 @@
 
 
 def pick_body(ins, _, outs, __):
-    counts_ref, assign_ref = ins
+    counts_ref, assign_ref = ins[:2]
     (pick_ref,) = outs
     y, c, z = place()
     rows = pick_ref.shape[0] // 2
@@ -209,7 +210,7 @@
     batch_ref, pieces_out = outs[0], outs[1:]
     slots = scratch[0]
     height = pieces[0].shape[0]
-    for i, piece in enumerate(pieces):
+    for i, piece in zip(ARRIVAL, pieces):
         slots[i * height : (i + 1) * height, :] = piece[...]
     batch_ref[...] = jnp.dot(pick_ref[...], slots[...], preferred_element_type=F32).astype(BF)
     store_rows(pieces_out, halves_dot(batch_ref, w_refs))
@@ -299,19 +300,20 @@
     near_block, token = run(stack_body, (block,), (own, core), token)
     near_sent = [lax.ppermute(near_block, "col", X3), lax.ppermute(near_block, "col", X1)]
     far_block, token = run(stack_body, (block,), (y, yd), token)
-    far_sent = [lax.ppermute(far_block, "col", X3), lax.ppermute(far_block, "col", X1)]
+    far_sent = [lax.ppermute(far_block, "col", pairs) for pairs in (X3, X1, X2)]
     token = bring(1, 1, token)
     passed, token = run(after_body, (block,), (near_sent[0], near_sent[1]), token)
     near_sent.append(lax.ppermute(passed, "col", X1))
     token = bring(1, 0, token)
-    passed, token = run(after_body, (block,), (far_sent[0], far_sent[1]), token)
-    far_sent.append(lax.ppermute(passed, "col", X1))
-    pick, token = run(pick_body, (like((steps * rows, steps * assign.shape[1])),), (counts, assign), token)
+    pick, token = run(
+        pick_body, (like((steps * rows, steps * assign.shape[1])),), (counts, assign), token
+    )
     token = bring(0, 1, token)
     pieces = []
     for dz in range(4):
         for own_block, sent in ((near_block, near_sent), (far_block, far_sent)):
             pieces.append((own_block, sent[1], sent[2], sent[0])[dz])
+    pieces = [pieces[i] for i in ARRIVAL]
 
     bits = (like((steps * rows // PIECES, 2 * units)),) * PIECES
     wide = like((steps * rows, 2 * units), F32)

time: 70 us -> 72.8 us (1.040)
  waiting for transfers between devices: 10.3 us -> 15.3 us
  starting transfers between devices: 31 us -> 29.2 us
    ppermute x2, waiting for transfers between devices: 0.08 us -> 4.17 us  [near_plan(): y, yd = (lax.ppermute(y, 'row', X2), lax.ppermute(yd, 'row', X3))]
    ppermute x2, waiting for transfers between devices: 5.14 us -> 3.08 us  [down_rest(): lax.ppermute(send2, 'col', X2)]
    ppermute x2, waiting for transfers between devices: 0.01 us -> 1.54 us  [down_rest(): lax.ppermute(send3, 'col', X3)]
    ppermute x3, starting transfers between devices: 5.95 us -> 4.43 us  [near_plan(): far_sent = [lax.ppermute(far_block, 'col', pairs) for pairs in (X3, X1, X2)]]
    ppermute x2, starting transfers between devices: 2.44 us -> 1.15 us  [down_rest(): lax.ppermute(send2, 'col', X2)]
    ppermute x2, starting transfers between devices: 2.66 us -> 1.52 us  [near_plan(): y, yd = (lax.ppermute(y, 'row', X2), lax.ppermute(yd, 'row', X3))]
    ppermute x1, starting transfers between devices: 3.87 us -> 5.01 us  [near_plan(): lax.ppermute(near_block, 'col', X3)]
    ppermute x1, waiting for transfers between devices: 0.01 us -> 0.9 us  [near_plan(): core = lax.ppermute(core, 'row', X1)]
  transfers between devices with their start and end apart: 32 -> 32, of which waited for: 12 -> 13; matrix products, arithmetic and copies ran while one was open for 0% -> 0% of each run, Pallas kernels for 32% -> 31%
where the time goes in v10:
time: 72.8 us; the launch traced here: 72.7 us
  starting transfers between devices  29.2 us (40%)
  Pallas kernels  25.2 us (35%)
  waiting for transfers between devices  15.3 us (21%)
  local copies, waits for them, and re-layouts  2.64 us (4%)
    pallas_call x25, Pallas kernels, run(): pl.pallas_call(wrapped, out_shape=outs, in_specs=[spec or vmem] * count +...  25.2 us
    ppermute x1, starting transfers between devices, near_plan(): lax.ppermute(near_block, 'col', X3)  5.01 us
    ppermute x3, starting transfers between devices, near_plan(): far_sent = [lax.ppermute(far_block, 'col', pairs) for pairs in (X3, X1, X2)]  4.43 us
    ppermute x2, waiting for transfers between devices, near_plan(): y, yd = (lax.ppermute(y, 'row', X2), lax.ppermute(yd, 'row', X3))  4.17 us
    ppermute x2, starting transfers between devices, down_rest(): lax.ppermute(send3, 'col', X3)  3.95 us
    ppermute x2, waiting for transfers between devices, down_rest(): lax.ppermute(send2, 'col', X2)  3.08 us
    unnamed x14, local copies, waits for them, and re-layouts  2.64 us
    ppermute x2, starting transfers between devices, activate(): y = lax.ppermute(result, 'row', X2)  2.32 us
  transfers between devices with their start and end apart: 32, of which 13 were waited for; matrix products, arithmetic and copies ran while one was open for 0% of the time, Pallas kernels for 31%

profile of v10, /device:TPU:0, one launch (start us, length us, event | category | flops | bytes accessed | tf_op | source)
XLA Modules:
  0.0 72.7 jit_solution(4039844068280267864)
XLA Ops:
  0.0 0.9 %copy-done = bf16[2,8,8192]{2,1,0:T(8,128)(2,1)S(1)} copy-done((bf16[2,8,8192]{2,1,0:T(8,128)(2,1)S(1)}, bf16[2,8,8192]{2,1,0:T(8,128)(2,1)}, u32[]{:S(2)}) %copy-start) | copy-done | bytes 262168
  1.7 0.9 %collective-permute-done.refs_1_ = bf16[2,8,2048]{2,1,0:T(8,128)(2,1)S(1)} collective-permute-done((bf16[2,8,2048]{2,1,0:T(8,128)(2,1)S(1)}, bf16[2,8,2048]{2,1,0:T(8,128)(2,1)S(1)}, u32[]{:S(2)}, u32[]{:S(2)}) %collective-permute-start) | collective-permute-done | bytes 65568 | tf_op jit(solution)/shard_map/ppermute | solution.py:291
  2.6 5.0 %collective-permute-start.5 = (bf16[32,2048]{1,0:T(8,128)(2,1)S(1)}, bf16[32,2048]{1,0:T(8,128)(2,1)S(1)}, u32[]{:S(2)}, u32[]{:S(2)}) collective-permute-start(bf16[32,2048]{1,0:T(8,128)(2,1)S(1)} %get-tuple-element.77.refs_0_), channel_id=1, source_target_pairs={{0,3},{1,2},{2,1},{3,0},{4,7},{5,6},{6,5},{7,4},{8,11},{9,10},{10,... | collective-permute-start | bytes 393224 | tf_op jit(solution)/shard_map/ppermute | solution.py:301
  7.6 1.5 %collective-permute-start.1 = (bf16[2,8,2048]{2,1,0:T(8,128)(2,1)S(1)}, bf16[2,8,2048]{2,1,0:T(8,128)(2,1)S(1)}, u32[]{:S(2)}, u32[]{:S(2)}) collective-permute-start(bf16[2,8,2048]{2,1,0:T(8,128)(2,1)S(1)} %get-tuple-element.78), channel_id=1, source_target_pairs={{0,8},{4,12},{8,0},{12,4},{1,9},{5,13},{9,1},{13,5},{2,10},{6,14},... | collective-permute-start | bytes 196616 | tf_op jit(solution)/shard_map/ppermute | solution.py:290
  9.1 2.7 %collective-permute-done.1.refs_0_ = bf16[2,8,2048]{2,1,0:T(8,128)(2,1)S(1)} collective-permute-done((bf16[2,8,2048]{2,1,0:T(8,128)(2,1)S(1)}, bf16[2,8,2048]{2,1,0:T(8,128)(2,1)S(1)}, u32[]{:S(2)}, u32[]{:S(2)}) %collective-permute-start.1) | collective-permute-done | bytes 65568 | tf_op jit(solution)/shard_map/ppermute | solution.py:290
  11.9 1.4 %collective-permute-done.2.refs_1_ = bf16[2,8,2048]{2,1,0:T(8,128)(2,1)S(1)} collective-permute-done((bf16[2,8,2048]{2,1,0:T(8,128)(2,1)S(1)}, bf16[2,8,2048]{2,1,0:T(8,128)(2,1)S(1)}, u32[]{:S(2)}, u32[]{:S(2)}) %collective-permute-start.2) | collective-permute-done | bytes 65568 | tf_op jit(solution)/shard_map/ppermute | solution.py:290
  14.0 3.7 %collective-permute-start.6 = (bf16[32,2048]{1,0:T(8,128)(2,1)S(1)}, bf16[32,2048]{1,0:T(8,128)(2,1)S(1)}, u32[]{:S(2)}, u32[]{:S(2)}) collective-permute-start(bf16[32,2048]{1,0:T(8,128)(2,1)S(1)} %get-tuple-element.81.refs_1_), channel_id=1, source_target_pairs={{0,3},{1,2},{2,1},{3,0},{4,7},{5,6},{6,5},{7,4},{8,11},{9,10},{10,... | collective-permute-start | bytes 393224 | tf_op jit(solution)/shard_map/ppermute | solution.py:303
  17.7 3.2 %shard_map.67 = (bf16[2048,1792]{1,0:T(8,128)(2,1)S(1)}, f32[8,128]{1,0:T(8,128)S(1)}) custom-call(bf16[2048,3584]{1,0:T(8,128)(2,1)} %refs_2_.1, bf16[2048,3584]{1,0:T(8,128)(2,1)} %refs_3_.1, f32[8,128]{1,0:T(8,128)S(1)} %get-tuple-element.82.refs_2_), custom_call_target="tpu_custom_call" | custom-call | bytes 1 | tf_op jit(solution)/shard_map/pallas_call | solution.py:42
  21.0 2.1 %collective-permute-start.8 = (bf16[32,2048]{1,0:T(8,128)(2,1)S(1)}, bf16[32,2048]{1,0:T(8,128)(2,1)S(1)}, u32[]{:S(2)}, u32[]{:S(2)}) collective-permute-start(bf16[32,2048]{1,0:T(8,128)(2,1)S(1)} %get-tuple-element.84), channel_id=1, source_target_pairs={{0,1},{1,0},{2,3},{3,2},{4,5},{5,4},{6,7},{7,6},{8,9},{9,8},{10,11... | collective-permute-start | bytes 393224 | tf_op jit(solution)/shard_map/ppermute | solution.py:306
  23.1 3.2 %shard_map.69 = (bf16[2048,1792]{1,0:T(8,128)(2,1)S(1)}, f32[8,128]{1,0:T(8,128)S(1)}) custom-call(bf16[2048,3584]{1,0:T(8,128)(2,1)} %refs_2_.1, bf16[2048,3584]{1,0:T(8,128)(2,1)} %refs_3_.1, f32[8,128]{1,0:T(8,128)S(1)} %get-tuple-element.85.refs_2_), custom_call_target="tpu_custom_call" | custom-call | bytes 1 | tf_op jit(solution)/shard_map/pallas_call | solution.py:42
  26.6 3.3 %shard_map.71 = (bf16[2048,1792]{1,0:T(8,128)(2,1)S(1)}, f32[8,128]{1,0:T(8,128)S(1)}) custom-call(bf16[2048,3584]{1,0:T(8,128)(2,1)} %refs_2_.1, bf16[2048,3584]{1,0:T(8,128)(2,1)} %refs_3_.1, f32[8,128]{1,0:T(8,128)S(1)} %get-tuple-element.89.refs_2_), custom_call_target="tpu_custom_call" | custom-call | bytes 1 | tf_op jit(solution)/shard_map/pallas_call | solution.py:42
  29.9 1.4 %shard_map.72 = (bf16[128,2048]{1,0:T(8,128)(2,1)S(1)}, bf16[64,1792]{1,0:T(8,128)(2,1)S(1)}, bf16[64,1792]{1,0:T(8,128)(2,1)S(1)}, f32[8,128]{1,0:T(8,128)S(1)}) custom-call(bf16[32,2048]{1,0:T(8,128)(2,1)S(1)} %get-tuple-element.77.refs_0_, bf16[32,2048]{1,0:T(8,128)(2,1)S(1)} %get-tuple-element.81.refs_1_, ...), custom_call_target="tpu_custom_call" | custom-call | bytes 1 | tf_op jit(solution)/shard_map/pallas_call | solution.py:42
  31.9 1.1 %shard_map.73 = (f32[128,1792]{1,0:T(8,128)S(1)}, f32[8,128]{1,0:T(8,128)S(1)}) custom-call(bf16[128,2048]{1,0:T(8,128)(2,1)S(1)} %get-tuple-element.91.refs_0_, bf16[2048,1792]{1,0:T(8,128)(2,1)S(1)} %get-tuple-element.93.refs_1_, f32[8,128]{1,0:T(8,128)S(1)} %get-tuple-element.94.refs_2_), custom_call_target="tpu_custom_call" | custom-call | bytes 1 | tf_op jit(solution)/shard_map/pallas_call | solution.py:42
  33.3 1.2 %collective-permute-start.11 = (bf16[64,1792]{1,0:T(8,128)(2,1)S(1)}, bf16[64,1792]{1,0:T(8,128)(2,1)S(1)}, u32[]{:S(2)}, u32[]{:S(2)}) collective-permute-start(bf16[64,1792]{1,0:T(8,128)(2,1)S(1)} %get-tuple-element.103), channel_id=1, source_target_pairs={{0,8},{4,12},{8,0},{12,4},{1,9},{5,13},{9,1},{13,5},{2,10},{6,14},... | collective-permute-start | bytes 688136 | tf_op jit(solution)/shard_map/ppermute | solution.py:331
  34.5 3.3 %shard_map.75 = (bf16[64,1792]{1,0:T(8,128)(2,1)S(1)}, bf16[64,1792]{1,0:T(8,128)(2,1)S(1)}, bf16[2048,1792]{1,0:T(8,128)(2,1)S(1)}, f32[8,128]{1,0:T(8,128)S(1)}) custom-call(bf16[128,2048]{1,0:T(8,128)(2,1)S(1)} %get-tuple-element.91.refs_0_, bf16[2048,1792]{1,0:T(8,128)(2,1)S(1)} %get-tuple-element.92.refs_1_, bf16[2048,3584]{1,0:T(8,128)(2,1)} %refs_2_.1, ...), custom_call_target="tpu_custom_call" | custom-call | bytes 1 | tf_op jit(solution)/shard_map/pallas_call | solution.py:42
  38.0 1.0 %collective-permute-start.15 = (bf16[64,1792]{1,0:T(8,128)(2,1)S(1)}, bf16[64,1792]{1,0:T(8,128)(2,1)S(1)}, u32[]{:S(2)}, u32[]{:S(2)}) collective-permute-start(bf16[64,1792]{1,0:T(8,128)(2,1)S(1)} %get-tuple-element.113), channel_id=1, source_target_pairs={{0,8},{4,12},{8,0},{12,4},{1,9},{5,13},{9,1},{13,5},{2,10},{6,14},... | collective-permute-start | bytes 688136 | tf_op jit(solution)/shard_map/ppermute | solution.py:331
  39.1 1.1 %shard_map.76 = (f32[128,1792]{1,0:T(8,128)S(1)}, f32[8,128]{1,0:T(8,128)S(1)}) custom-call(bf16[128,2048]{1,0:T(8,128)(2,1)S(1)} %get-tuple-element.91.refs_0_, bf16[2048,1792]{1,0:T(8,128)(2,1)S(1)} %get-tuple-element.100.refs_1_, f32[8,128]{1,0:T(8,128)S(1)} %get-tuple-element.101.refs_2_), custom_call_target="tpu_custom_call" | custom-call | bytes 1 | tf_op jit(solution)/shard_map/pallas_call | solution.py:42
  40.3 1.1 %slice-done.2 = s8[4194304]{0:T(1024)(128)(4,1)S(1)} async-done(((s8[14680064]{0:T(1024)(128)(4,1)}), s8[4194304]{0:T(1024)(128)(4,1)S(1)}, s32[]{:S(2)}) %slice-start.2) | async-done | bytes 4194328
  42.7 1.0 %collective-permute-start.14 = (bf16[64,896]{1,0:T(8,128)(2,1)S(1)}, bf16[64,896]{1,0:T(8,128)(2,1)S(1)}, u32[]{:S(2)}, u32[]{:S(2)}) collective-permute-start(bf16[64,896]{1,0:T(8,128)(2,1)S(1)} %get-tuple-element.110.refs_1_), channel_id=1, source_target_pairs={{0,8},{4,12},{8,0},{12,4},{1,9},{5,13},{9,1},{13,5},{2,10},{6,14},... | collective-permute-start | bytes 344072 | tf_op jit(solution)/shard_map/ppermute | solution.py:352
  44.2 1.4 %shard_map.80 = (f32[64,2048]{1,0:T(8,128)S(1)}, f32[8,128]{1,0:T(8,128)S(1)}) custom-call(bf16[1792,2048]{1,0:T(8,128)(2,1)S(1)} %get-tuple-element.109.refs_0_, bf16[64,896]{1,0:T(8,128)(2,1)S(1)} %get-tuple-element.110.refs_1_, bf16[64,896]{1,0:T(8,128)(2,1)S(1)} %collective-permute-done.13.refs_2_, f32[8,128]{1,0:T(8,128)S(1)} %get-tuple-element.111.refs_3_), custom_call_target="tpu_custom_call" | custom-call | bytes 1 | tf_op jit(solution)/shard_map/pallas_call | solution.py:42
  46.4 1.3 %collective-permute-start.22 = (bf16[64,896]{1,0:T(8,128)(2,1)S(1)}, bf16[64,896]{1,0:T(8,128)(2,1)S(1)}, u32[]{:S(2)}, u32[]{:S(2)}) collective-permute-start(bf16[64,896]{1,0:T(8,128)(2,1)S(1)} %get-tuple-element.119.refs_1_), channel_id=1, source_target_pairs={{0,8},{4,12},{8,0},{12,4},{1,9},{5,13},{9,1},{13,5},{2,10},{6,14},... | collective-permute-start | bytes 344072 | tf_op jit(solution)/shard_map/ppermute | solution.py:352
  49.1 1.4 %shard_map.83 = (f32[64,2048]{1,0:T(8,128)S(1)}, f32[8,128]{1,0:T(8,128)S(1)}) custom-call(bf16[1792,2048]{1,0:T(8,128)(2,1)S(1)} %get-tuple-element.109.refs_0_, bf16[64,896]{1,0:T(8,128)(2,1)S(1)} %get-tuple-element.119.refs_1_, bf16[64,896]{1,0:T(8,128)(2,1)S(1)} %collective-permute-done.19.refs_2_, f32[8,128]{1,0:T(8,128)S(1)} %get-tuple-element.120.refs_3_), custom_call_target="tpu_custom_call" | custom-call | bytes 1 | tf_op jit(solution)/shard_map/pallas_call | solution.py:42
  50.5 1.4 %shard_map.84 = (f32[16,2048]{1,0:T(8,128)S(1)}, bf16[16,2048]{1,0:T(8,128)(2,1)S(1)}, bf16[16,2048]{1,0:T(8,128)(2,1)S(1)}, bf16[16,2048]{1,0:T(8,128)(2,1)S(1)}, f32[8,128]{1,0:T(8,128)S(1)}) custom-call(bf16[1792,2048]{1,0:T(8,128)(2,1)S(1)} %get-tuple-element.108.refs_0_, f32[64,2048]{1,0:T(8,128)S(1)} %get-tuple-element.112.refs_1_, ...), custom_call_target="tpu_custom_call" | custom-call | bytes 1 | tf_op jit(solution)/shard_map/pallas_call | solution.py:42
  51.9 1.8 %collective-permute-start.20 = (bf16[16,2048]{1,0:T(8,128)(2,1)S(1)}, bf16[16,2048]{1,0:T(8,128)(2,1)S(1)}, u32[]{:S(2)}, u32[]{:S(2)}) collective-permute-start(bf16[16,2048]{1,0:T(8,128)(2,1)S(1)} %get-tuple-element.123), channel_id=1, source_target_pairs={{0,3},{1,2},{2,1},{3,0},{4,7},{5,6},{6,5},{7,4},{8,11},{9,10},{10,... | collective-permute-start | bytes 196616 | tf_op jit(solution)/shard_map/ppermute | solution.py:375
  55.2 1.4 %shard_map.86 = (f32[16,2048]{1,0:T(8,128)S(1)}, bf16[16,2048]{1,0:T(8,128)(2,1)S(1)}, bf16[16,2048]{1,0:T(8,128)(2,1)S(1)}, bf16[16,2048]{1,0:T(8,128)(2,1)S(1)...) custom-call(bf16[1792,2048]{1,0:T(8,128)(2,1)S(1)} %get-tuple-element.108.refs_0_, ...), custom_call_target="tpu_custom_call" | custom-call | bytes 1 | tf_op jit(solution)/shard_map/pallas_call | solution.py:42
  56.6 2.2 %collective-permute-start.25 = (bf16[16,2048]{1,0:T(8,128)(2,1)S(1)}, bf16[16,2048]{1,0:T(8,128)(2,1)S(1)}, u32[]{:S(2)}, u32[]{:S(2)}) collective-permute-start(bf16[16,2048]{1,0:T(8,128)(2,1)S(1)} %get-tuple-element.132), channel_id=1, source_target_pairs={{0,3},{1,2},{2,1},{3,0},{4,7},{5,6},{6,5},{7,4},{8,11},{9,10},{10,... | collective-permute-start | bytes 196616 | tf_op jit(solution)/shard_map/ppermute | solution.py:375
  58.8 1.1 %collective-permute-start.26 = (bf16[16,2048]{1,0:T(8,128)(2,1)S(1)}, bf16[16,2048]{1,0:T(8,128)(2,1)S(1)}, u32[]{:S(2)}, u32[]{:S(2)}) collective-permute-start(bf16[16,2048]{1,0:T(8,128)(2,1)S(1)} %get-tuple-element.133), channel_id=1, source_target_pairs={{0,2},{1,3},{2,0},{3,1},{4,6},{5,7},{6,4},{7,5},{8,10},{9,11},{10,... | collective-permute-start | bytes 196616 | tf_op jit(solution)/shard_map/ppermute | solution.py:375
  59.9 1.1 %collective-permute-start.27 = (bf16[16,2048]{1,0:T(8,128)(2,1)S(1)}, bf16[16,2048]{1,0:T(8,128)(2,1)S(1)}, u32[]{:S(2)}, u32[]{:S(2)}) collective-permute-start(bf16[16,2048]{1,0:T(8,128)(2,1)S(1)} %get-tuple-element.134), channel_id=1, source_target_pairs={{0,1},{1,0},{2,3},{3,2},{4,5},{5,4},{6,7},{7,6},{8,9},{9,8},{10,11... | collective-permute-start | bytes 196616 | tf_op jit(solution)/shard_map/ppermute | solution.py:387
  62.0 1.5 %collective-permute-done.25.refs_4_ = bf16[16,2048]{1,0:T(8,128)(2,1)S(1)} collective-permute-done((bf16[16,2048]{1,0:T(8,128)(2,1)S(1)}, bf16[16,2048]{1,0:T(8,128)(2,1)S(1)}, u32[]{:S(2)}, u32[]{:S(2)}) %collective-permute-start.25) | collective-permute-done | bytes 65568 | tf_op jit(solution)/shard_map/ppermute | solution.py:375
  63.5 3.1 %collective-permute-done.26.refs_5_ = bf16[16,2048]{1,0:T(8,128)(2,1)S(1)} collective-permute-done((bf16[16,2048]{1,0:T(8,128)(2,1)S(1)}, bf16[16,2048]{1,0:T(8,128)(2,1)S(1)}, u32[]{:S(2)}, u32[]{:S(2)}) %collective-permute-start.26) | collective-permute-done | bytes 65568 | tf_op jit(solution)/shard_map/ppermute | solution.py:375
  67.4 1.2 %collective-permute-start.30 = (bf16[2,4,2048]{2,1,0:T(4,128)(2,1)S(1)}, bf16[2,4,2048]{2,1,0:T(4,128)(2,1)S(1)}, u32[]{:S(2)}, u32[]{:S(2)}) collective-permute-start(bf16[2,4,2048]{2,1,0:T(4,128)(2,1)S(1)} %get-tuple-element.139), channel_id=1, source_target_pairs={{0,8},{4,12},{8,0},{12,4},{1,9},{5,13},{9,1},{13,5},{2,10},{6,14},... | collective-permute-start | bytes 98312 | tf_op jit(solution)/shard_map/ppermute | solution.py:389
  69.3 2.1 %collective-permute-done.30.refs_2_ = bf16[2,4,2048]{2,1,0:T(4,128)(2,1)S(1)} collective-permute-done((bf16[2,4,2048]{2,1,0:T(4,128)(2,1)S(1)}, bf16[2,4,2048]{2,1,0:T(4,128)(2,1)S(1)}, u32[]{:S(2)}, u32[]{:S(2)}) %collective-permute-start.30) | collective-permute-done | bytes 32800 | tf_op jit(solution)/shard_map/ppermute | solution.py:389
  (72 shorter events, 11.8 us)
Async XLA Ops:
  1.2 1.4 %collective-permute-start = (bf16[2,8,2048]{2,1,0:T(8,128)(2,1)S(1)}, bf16[2,8,2048]{2,1,0:T(8,128)(2,1)S(1)}, u32[]{:S(2)}, u32[]{:S(2)}) collective-permute-start(bf16[2,8,2048]{2,1,0:T(8,128)(2,1)S(1)} %get-tuple-element.75), channel_id=1, source_target_pairs={{0,4},{4,0},{8,12},{12,8},{1,5},{5,1},{9,13},{13,9},{2,6},{6,2},{1... | collective-permute-start | bytes 196616 | tf_op jit(solution)/shard_map/ppermute | solution.py:291
  2.6 18.4 %collective-permute-start.5 = (bf16[32,2048]{1,0:T(8,128)(2,1)S(1)}, bf16[32,2048]{1,0:T(8,128)(2,1)S(1)}, u32[]{:S(2)}, u32[]{:S(2)}) collective-permute-start(bf16[32,2048]{1,0:T(8,128)(2,1)S(1)} %get-tuple-element.77.refs_0_), channel_id=1, source_target_pairs={{0,3},{1,2},{2,1},{3,0},{4,7},{5,6},{6,5},{7,4},{8,11},{9,10},{10,... | collective-permute-start | bytes 393224 | tf_op jit(solution)/shard_map/ppermute | solution.py:301
  7.6 13.3 %collective-permute-start.3 = (bf16[32,2048]{1,0:T(8,128)(2,1)S(1)}, bf16[32,2048]{1,0:T(8,128)(2,1)S(1)}, u32[]{:S(2)}, u32[]{:S(2)}) collective-permute-start(bf16[32,2048]{1,0:T(8,128)(2,1)S(1)} %get-tuple-element.77.refs_0_), channel_id=1, source_target_pairs={{0,1},{1,0},{2,3},{3,2},{4,5},{5,4},{6,7},{7,6},{8,9},{9,8},{10,11... | collective-permute-start | bytes 393224 | tf_op jit(solution)/shard_map/ppermute | solution.py:301
  7.6 4.3 %collective-permute-start.1 = (bf16[2,8,2048]{2,1,0:T(8,128)(2,1)S(1)}, bf16[2,8,2048]{2,1,0:T(8,128)(2,1)S(1)}, u32[]{:S(2)}, u32[]{:S(2)}) collective-permute-start(bf16[2,8,2048]{2,1,0:T(8,128)(2,1)S(1)} %get-tuple-element.78), channel_id=1, source_target_pairs={{0,8},{4,12},{8,0},{12,4},{1,9},{5,13},{9,1},{13,5},{2,10},{6,14},... | collective-permute-start | bytes 196616 | tf_op jit(solution)/shard_map/ppermute | solution.py:290
  9.1 4.2 %collective-permute-start.2 = (bf16[2,8,2048]{2,1,0:T(8,128)(2,1)S(1)}, bf16[2,8,2048]{2,1,0:T(8,128)(2,1)S(1)}, u32[]{:S(2)}, u32[]{:S(2)}) collective-permute-start(bf16[2,8,2048]{2,1,0:T(8,128)(2,1)S(1)} %get-tuple-element.79), channel_id=1, source_target_pairs={{0,12},{4,8},{8,4},{12,0},{1,13},{5,9},{9,5},{13,1},{2,14},{6,10},... | collective-permute-start | bytes 196616 | tf_op jit(solution)/shard_map/ppermute | solution.py:290
  13.3 16.5 %collective-permute-start.7 = (bf16[32,2048]{1,0:T(8,128)(2,1)S(1)}, bf16[32,2048]{1,0:T(8,128)(2,1)S(1)}, u32[]{:S(2)}, u32[]{:S(2)}) collective-permute-start(bf16[32,2048]{1,0:T(8,128)(2,1)S(1)} %get-tuple-element.81.refs_1_), channel_id=1, source_target_pairs={{0,2},{1,3},{2,0},{3,1},{4,6},{5,7},{6,4},{7,5},{8,10},{9,11},{10,... | collective-permute-start | bytes 393224 | tf_op jit(solution)/shard_map/ppermute | solution.py:303
  14.0 15.9 %collective-permute-start.6 = (bf16[32,2048]{1,0:T(8,128)(2,1)S(1)}, bf16[32,2048]{1,0:T(8,128)(2,1)S(1)}, u32[]{:S(2)}, u32[]{:S(2)}) collective-permute-start(bf16[32,2048]{1,0:T(8,128)(2,1)S(1)} %get-tuple-element.81.refs_1_), channel_id=1, source_target_pairs={{0,3},{1,2},{2,1},{3,0},{4,7},{5,6},{6,5},{7,4},{8,11},{9,10},{10,... | collective-permute-start | bytes 393224 | tf_op jit(solution)/shard_map/ppermute | solution.py:303
  17.7 12.1 %collective-permute-start.4 = (bf16[32,2048]{1,0:T(8,128)(2,1)S(1)}, bf16[32,2048]{1,0:T(8,128)(2,1)S(1)}, u32[]{:S(2)}, u32[]{:S(2)}) collective-permute-start(bf16[32,2048]{1,0:T(8,128)(2,1)S(1)} %get-tuple-element.81.refs_1_), channel_id=1, source_target_pairs={{0,1},{1,0},{2,3},{3,2},{4,5},{5,4},{6,7},{7,6},{8,9},{9,8},{10,11... | collective-permute-start | bytes 393224 | tf_op jit(solution)/shard_map/ppermute | solution.py:303
  21.0 8.9 %collective-permute-start.8 = (bf16[32,2048]{1,0:T(8,128)(2,1)S(1)}, bf16[32,2048]{1,0:T(8,128)(2,1)S(1)}, u32[]{:S(2)}, u32[]{:S(2)}) collective-permute-start(bf16[32,2048]{1,0:T(8,128)(2,1)S(1)} %get-tuple-element.84), channel_id=1, source_target_pairs={{0,1},{1,0},{2,3},{3,2},{4,5},{5,4},{6,7},{7,6},{8,9},{9,8},{10,11... | collective-permute-start | bytes 393224 | tf_op jit(solution)/shard_map/ppermute | solution.py:306
  31.3 1.7 %collective-permute-start.9 = (bf16[64,1792]{1,0:T(8,128)(2,1)S(1)}, bf16[64,1792]{1,0:T(8,128)(2,1)S(1)}, u32[]{:S(2)}, u32[]{:S(2)}) collective-permute-start(bf16[64,1792]{1,0:T(8,128)(2,1)S(1)} %get-tuple-element.96), channel_id=1, source_target_pairs={{0,4},{4,0},{8,12},{12,8},{1,5},{5,1},{9,13},{13,9},{2,6},{6,2},{1... | collective-permute-start | bytes 688136 | tf_op jit(solution)/shard_map/ppermute | solution.py:328
  31.4 1.8 %collective-permute-start.10 = (bf16[64,1792]{1,0:T(8,128)(2,1)S(1)}, bf16[64,1792]{1,0:T(8,128)(2,1)S(1)}, u32[]{:S(2)}, u32[]{:S(2)}) collective-permute-start(bf16[64,1792]{1,0:T(8,128)(2,1)S(1)} %get-tuple-element.97), channel_id=1, source_target_pairs={{0,4},{4,0},{8,12},{12,8},{1,5},{5,1},{9,13},{13,9},{2,6},{6,2},{1... | collective-permute-start | bytes 688136 | tf_op jit(solution)/shard_map/ppermute | solution.py:328
  33.3 9.1 %collective-permute-start.11 = (bf16[64,1792]{1,0:T(8,128)(2,1)S(1)}, bf16[64,1792]{1,0:T(8,128)(2,1)S(1)}, u32[]{:S(2)}, u32[]{:S(2)}) collective-permute-start(bf16[64,1792]{1,0:T(8,128)(2,1)S(1)} %get-tuple-element.103), channel_id=1, source_target_pairs={{0,8},{4,12},{8,0},{12,4},{1,9},{5,13},{9,1},{13,5},{2,10},{6,14},... | collective-permute-start | bytes 688136 | tf_op jit(solution)/shard_map/ppermute | solution.py:331
  37.9 4.6 %collective-permute-start.12 = (bf16[64,1792]{1,0:T(8,128)(2,1)S(1)}, bf16[64,1792]{1,0:T(8,128)(2,1)S(1)}, u32[]{:S(2)}, u32[]{:S(2)}) collective-permute-start(bf16[64,1792]{1,0:T(8,128)(2,1)S(1)} %get-tuple-element.104), channel_id=1, source_target_pairs={{0,4},{4,0},{8,12},{12,8},{1,5},{5,1},{9,13},{13,9},{2,6},{6,2},{1... | collective-permute-start | bytes 688136 | tf_op jit(solution)/shard_map/ppermute | solution.py:341
  38.0 8.2 %collective-permute-start.15 = (bf16[64,1792]{1,0:T(8,128)(2,1)S(1)}, bf16[64,1792]{1,0:T(8,128)(2,1)S(1)}, u32[]{:S(2)}, u32[]{:S(2)}) collective-permute-start(bf16[64,1792]{1,0:T(8,128)(2,1)S(1)} %get-tuple-element.113), channel_id=1, source_target_pairs={{0,8},{4,12},{8,0},{12,4},{1,9},{5,13},{9,1},{13,5},{2,10},{6,14},... | collective-permute-start | bytes 688136 | tf_op jit(solution)/shard_map/ppermute | solution.py:331
  38.9 7.2 %collective-permute-start.16 = (bf16[64,1792]{1,0:T(8,128)(2,1)S(1)}, bf16[64,1792]{1,0:T(8,128)(2,1)S(1)}, u32[]{:S(2)}, u32[]{:S(2)}) collective-permute-start(bf16[64,1792]{1,0:T(8,128)(2,1)S(1)} %get-tuple-element.114), channel_id=1, source_target_pairs={{0,4},{4,0},{8,12},{12,8},{1,5},{5,1},{9,13},{13,9},{2,6},{6,2},{1... | collective-permute-start | bytes 688136 | tf_op jit(solution)/shard_map/ppermute | solution.py:341
  42.6 1.6 %collective-permute-start.13 = (bf16[64,896]{1,0:T(8,128)(2,1)S(1)}, bf16[64,896]{1,0:T(8,128)(2,1)S(1)}, u32[]{:S(2)}, u32[]{:S(2)}) collective-permute-start(bf16[64,896]{1,0:T(8,128)(2,1)S(1)} %get-tuple-element.110.refs_1_), channel_id=1, source_target_pairs={{0,4},{4,0},{8,12},{12,8},{1,5},{5,1},{9,13},{13,9},{2,6},{6,2},{1... | collective-permute-start | bytes 344072 | tf_op jit(solution)/shard_map/ppermute | solution.py:353
  42.7 5.8 %collective-permute-start.14 = (bf16[64,896]{1,0:T(8,128)(2,1)S(1)}, bf16[64,896]{1,0:T(8,128)(2,1)S(1)}, u32[]{:S(2)}, u32[]{:S(2)}) collective-permute-start(bf16[64,896]{1,0:T(8,128)(2,1)S(1)} %get-tuple-element.110.refs_1_), channel_id=1, source_target_pairs={{0,8},{4,12},{8,0},{12,4},{1,9},{5,13},{9,1},{13,5},{2,10},{6,14},... | collective-permute-start | bytes 344072 | tf_op jit(solution)/shard_map/ppermute | solution.py:352
  46.3 2.8 %collective-permute-start.19 = (bf16[64,896]{1,0:T(8,128)(2,1)S(1)}, bf16[64,896]{1,0:T(8,128)(2,1)S(1)}, u32[]{:S(2)}, u32[]{:S(2)}) collective-permute-start(bf16[64,896]{1,0:T(8,128)(2,1)S(1)} %get-tuple-element.119.refs_1_), channel_id=1, source_target_pairs={{0,4},{4,0},{8,12},{12,8},{1,5},{5,1},{9,13},{13,9},{2,6},{6,2},{1... | collective-permute-start | bytes 344072 | tf_op jit(solution)/shard_map/ppermute | solution.py:353
  46.4 7.4 %collective-permute-start.22 = (bf16[64,896]{1,0:T(8,128)(2,1)S(1)}, bf16[64,896]{1,0:T(8,128)(2,1)S(1)}, u32[]{:S(2)}, u32[]{:S(2)}) collective-permute-start(bf16[64,896]{1,0:T(8,128)(2,1)S(1)} %get-tuple-element.119.refs_1_), channel_id=1, source_target_pairs={{0,8},{4,12},{8,0},{12,4},{1,9},{5,13},{9,1},{13,5},{2,10},{6,14},... | collective-permute-start | bytes 344072 | tf_op jit(solution)/shard_map/ppermute | solution.py:352
  48.5 2.0 %collective-permute-start.17 = (bf16[32,896]{1,0:T(8,128)(2,1)S(1)}, bf16[32,896]{1,0:T(8,128)(2,1)S(1)}, u32[]{:S(2)}, u32[]{:S(2)}) collective-permute-start(bf16[32,896]{1,0:T(8,128)(2,1)S(1)} %get-tuple-element.117), channel_id=1, source_target_pairs={{0,4},{4,0},{8,12},{12,8},{1,5},{5,1},{9,13},{13,9},{2,6},{6,2},{1... | collective-permute-start | bytes 172040 | tf_op jit(solution)/shard_map/ppermute | solution.py:364
  48.6 1.9 %collective-permute-start.18 = (bf16[32,896]{1,0:T(8,128)(2,1)S(1)}, bf16[32,896]{1,0:T(8,128)(2,1)S(1)}, u32[]{:S(2)}, u32[]{:S(2)}) collective-permute-start(bf16[32,896]{1,0:T(8,128)(2,1)S(1)} %get-tuple-element.118), channel_id=1, source_target_pairs={{0,4},{4,0},{8,12},{12,8},{1,5},{5,1},{9,13},{13,9},{2,6},{6,2},{1... | collective-permute-start | bytes 172040 | tf_op jit(solution)/shard_map/ppermute | solution.py:364
  51.9 9.1 %collective-permute-start.20 = (bf16[16,2048]{1,0:T(8,128)(2,1)S(1)}, bf16[16,2048]{1,0:T(8,128)(2,1)S(1)}, u32[]{:S(2)}, u32[]{:S(2)}) collective-permute-start(bf16[16,2048]{1,0:T(8,128)(2,1)S(1)} %get-tuple-element.123), channel_id=1, source_target_pairs={{0,3},{1,2},{2,1},{3,0},{4,7},{5,6},{6,5},{7,4},{8,11},{9,10},{10,... | collective-permute-start | bytes 196616 | tf_op jit(solution)/shard_map/ppermute | solution.py:375
  53.7 1.3 %collective-permute-start.23 = (bf16[32,896]{1,0:T(8,128)(2,1)S(1)}, bf16[32,896]{1,0:T(8,128)(2,1)S(1)}, u32[]{:S(2)}, u32[]{:S(2)}) collective-permute-start(bf16[32,896]{1,0:T(8,128)(2,1)S(1)} %get-tuple-element.128), channel_id=1, source_target_pairs={{0,4},{4,0},{8,12},{12,8},{1,5},{5,1},{9,13},{13,9},{2,6},{6,2},{1... | collective-permute-start | bytes 172040 | tf_op jit(solution)/shard_map/ppermute | solution.py:364
  53.8 1.4 %collective-permute-start.24 = (bf16[32,896]{1,0:T(8,128)(2,1)S(1)}, bf16[32,896]{1,0:T(8,128)(2,1)S(1)}, u32[]{:S(2)}, u32[]{:S(2)}) collective-permute-start(bf16[32,896]{1,0:T(8,128)(2,1)S(1)} %get-tuple-element.129), channel_id=1, source_target_pairs={{0,4},{4,0},{8,12},{12,8},{1,5},{5,1},{9,13},{13,9},{2,6},{6,2},{1... | collective-permute-start | bytes 172040 | tf_op jit(solution)/shard_map/ppermute | solution.py:364
  54.3 7.6 %collective-permute-start.21 = (bf16[16,2048]{1,0:T(8,128)(2,1)S(1)}, bf16[16,2048]{1,0:T(8,128)(2,1)S(1)}, u32[]{:S(2)}, u32[]{:S(2)}) collective-permute-start(bf16[16,2048]{1,0:T(8,128)(2,1)S(1)} %get-tuple-element.124), channel_id=1, source_target_pairs={{0,2},{1,3},{2,0},{3,1},{4,6},{5,7},{6,4},{7,5},{8,10},{9,11},{10,... | collective-permute-start | bytes 196616 | tf_op jit(solution)/shard_map/ppermute | solution.py:375
  56.6 6.9 %collective-permute-start.25 = (bf16[16,2048]{1,0:T(8,128)(2,1)S(1)}, bf16[16,2048]{1,0:T(8,128)(2,1)S(1)}, u32[]{:S(2)}, u32[]{:S(2)}) collective-permute-start(bf16[16,2048]{1,0:T(8,128)(2,1)S(1)} %get-tuple-element.132), channel_id=1, source_target_pairs={{0,3},{1,2},{2,1},{3,0},{4,7},{5,6},{6,5},{7,4},{8,11},{9,10},{10,... | collective-permute-start | bytes 196616 | tf_op jit(solution)/shard_map/ppermute | solution.py:375
  58.8 7.8 %collective-permute-start.26 = (bf16[16,2048]{1,0:T(8,128)(2,1)S(1)}, bf16[16,2048]{1,0:T(8,128)(2,1)S(1)}, u32[]{:S(2)}, u32[]{:S(2)}) collective-permute-start(bf16[16,2048]{1,0:T(8,128)(2,1)S(1)} %get-tuple-element.133), channel_id=1, source_target_pairs={{0,2},{1,3},{2,0},{3,1},{4,6},{5,7},{6,4},{7,5},{8,10},{9,11},{10,... | collective-permute-start | bytes 196616 | tf_op jit(solution)/shard_map/ppermute | solution.py:375
  59.9 6.7 %collective-permute-start.27 = (bf16[16,2048]{1,0:T(8,128)(2,1)S(1)}, bf16[16,2048]{1,0:T(8,128)(2,1)S(1)}, u32[]{:S(2)}, u32[]{:S(2)}) collective-permute-start(bf16[16,2048]{1,0:T(8,128)(2,1)S(1)} %get-tuple-element.134), channel_id=1, source_target_pairs={{0,1},{1,0},{2,3},{3,2},{4,5},{5,4},{6,7},{7,6},{8,9},{9,8},{10,11... | collective-permute-start | bytes 196616 | tf_op jit(solution)/shard_map/ppermute | solution.py:387
  61.1 6.1 %collective-permute-start.28 = (bf16[16,2048]{1,0:T(8,128)(2,1)S(1)}, bf16[16,2048]{1,0:T(8,128)(2,1)S(1)}, u32[]{:S(2)}, u32[]{:S(2)}) collective-permute-start(bf16[16,2048]{1,0:T(8,128)(2,1)S(1)} %get-tuple-element.135), channel_id=1, source_target_pairs={{0,1},{1,0},{2,3},{3,2},{4,5},{5,4},{6,7},{7,6},{8,9},{9,8},{10,11... | collective-permute-start | bytes 196616 | tf_op jit(solution)/shard_map/ppermute | solution.py:387
  67.3 1.9 %collective-permute-start.29 = (bf16[2,4,2048]{2,1,0:T(4,128)(2,1)S(1)}, bf16[2,4,2048]{2,1,0:T(4,128)(2,1)S(1)}, u32[]{:S(2)}, u32[]{:S(2)}) collective-permute-start(bf16[2,4,2048]{2,1,0:T(4,128)(2,1)S(1)} %get-tuple-element.138), channel_id=1, source_target_pairs={{0,4},{4,0},{8,12},{12,8},{1,5},{5,1},{9,13},{13,9},{2,6},{6,2},{1... | collective-permute-start | bytes 98312 | tf_op jit(solution)/shard_map/ppermute | solution.py:389
  67.4 4.0 %collective-permute-start.30 = (bf16[2,4,2048]{2,1,0:T(4,128)(2,1)S(1)}, bf16[2,4,2048]{2,1,0:T(4,128)(2,1)S(1)}, u32[]{:S(2)}, u32[]{:S(2)}) collective-permute-start(bf16[2,4,2048]{2,1,0:T(4,128)(2,1)S(1)} %get-tuple-element.139), channel_id=1, source_target_pairs={{0,8},{4,12},{8,0},{12,4},{1,9},{5,13},{9,1},{13,5},{2,10},{6,14},... | collective-permute-start | bytes 98312 | tf_op jit(solution)/shard_map/ppermute | solution.py:389
  68.6 3.3 %collective-permute-start.31 = (bf16[2,4,2048]{2,1,0:T(4,128)(2,1)S(1)}, bf16[2,4,2048]{2,1,0:T(4,128)(2,1)S(1)}, u32[]{:S(2)}, u32[]{:S(2)}) collective-permute-start(bf16[2,4,2048]{2,1,0:T(4,128)(2,1)S(1)} %get-tuple-element.140), channel_id=1, source_target_pairs={{0,12},{4,8},{8,4},{12,0},{1,13},{5,9},{9,5},{13,1},{2,14},{6,10},... | collective-permute-start | bytes 98312 | tf_op jit(solution)/shard_map/ppermute | solution.py:389
  (7 other events, 33.2 us)

commit v11 on v8

--- a/solution.py
+++ b/solution.py
@@ -304,9 +304,9 @@
     passed, token = run(after_body, (block,), (near_sent[0], near_sent[1]), token)
     near_sent.append(lax.ppermute(passed, "col", X1))
     token = bring(1, 0, token)
+    pick, token = run(pick_body, (like((steps * rows, steps * assign.shape[1])),), (counts, assign), token)
     passed, token = run(after_body, (block,), (far_sent[0], far_sent[1]), token)
     far_sent.append(lax.ppermute(passed, "col", X1))
-    pick, token = run(pick_body, (like((steps * rows, steps * assign.shape[1])),), (counts, assign), token)
     token = bring(0, 1, token)
     pieces = []
     for dz in range(4):

time: 70 us -> 70 us (level)
  transfers between devices with their start and end apart: 32 -> 32, of which waited for: 12 -> 11; matrix products, arithmetic and copies ran while one was open for 0% -> 0% of each run, Pallas kernels for 32% -> 32%
where the time goes in v11:
time: 70 us; the launch traced here: 69.8 us
  starting transfers between devices  30.9 us (44%)
  Pallas kernels  25.2 us (36%)
  waiting for transfers between devices  10.4 us (15%)
  local copies, waits for them, and re-layouts  3.01 us (4%)
    pallas_call x26, Pallas kernels, run(): pl.pallas_call(wrapped, out_shape=outs, in_specs=[spec or vmem] * count +...  25.2 us
    ppermute x2, waiting for transfers between devices, down_rest(): lax.ppermute(send2, 'col', X2)  5.21 us
    ppermute x1, starting transfers between devices, near_plan(): lax.ppermute(near_block, 'col', X3)  3.87 us
    ppermute x1, starting transfers between devices, near_plan(): lax.ppermute(far_block, 'col', X3)  3.67 us
    ppermute x2, starting transfers between devices, down_rest(): lax.ppermute(send3, 'col', X3)  3.53 us
    unnamed x14, local copies, waits for them, and re-layouts  3.01 us
    ppermute x2, starting transfers between devices, near_plan(): y, yd = (lax.ppermute(y, 'row', X2), lax.ppermute(yd, 'row', X3))  2.66 us
    ppermute x2, starting transfers between devices, down_rest(): lax.ppermute(send2, 'col', X2)  2.45 us
  transfers between devices with their start and end apart: 32, of which 11 were waited for; matrix products, arithmetic and copies ran while one was open for 0% of the time, Pallas kernels for 32%

profile of v11, /device:TPU:0, one launch (start us, length us, event | category | flops | bytes accessed | tf_op | source)
XLA Modules:
  0.0 69.8 jit_solution(9103115047855658219)
XLA Ops:
  0.0 0.9 %copy-done = bf16[2,8,8192]{2,1,0:T(8,128)(2,1)S(1)} copy-done((bf16[2,8,8192]{2,1,0:T(8,128)(2,1)S(1)}, bf16[2,8,8192]{2,1,0:T(8,128)(2,1)}, u32[]{:S(2)}) %copy-start) | copy-done | bytes 262168
  1.7 2.6 %collective-permute-start.1 = (bf16[2,8,2048]{2,1,0:T(8,128)(2,1)S(1)}, bf16[2,8,2048]{2,1,0:T(8,128)(2,1)S(1)}, u32[]{:S(2)}, u32[]{:S(2)}) collective-permute-start(bf16[2,8,2048]{2,1,0:T(8,128)(2,1)S(1)} %get-tuple-element.80), channel_id=1, source_target_pairs={{0,8},{4,12},{8,0},{12,4},{1,9},{5,13},{9,1},{13,5},{2,10},{6,14},... | collective-permute-start | bytes 196616 | tf_op jit(solution)/shard_map/ppermute | solution.py:289
  4.4 3.9 %collective-permute-start.5 = (bf16[32,2048]{1,0:T(8,128)(2,1)S(1)}, bf16[32,2048]{1,0:T(8,128)(2,1)S(1)}, u32[]{:S(2)}, u32[]{:S(2)}) collective-permute-start(bf16[32,2048]{1,0:T(8,128)(2,1)S(1)} %get-tuple-element.79.refs_0_), channel_id=1, source_target_pairs={{0,3},{1,2},{2,1},{3,0},{4,7},{5,6},{6,5},{7,4},{8,11},{9,10},{10,... | collective-permute-start | bytes 393224 | tf_op jit(solution)/shard_map/ppermute | solution.py:300
  8.3 3.7 %collective-permute-start.7 = (bf16[32,2048]{1,0:T(8,128)(2,1)S(1)}, bf16[32,2048]{1,0:T(8,128)(2,1)S(1)}, u32[]{:S(2)}, u32[]{:S(2)}) collective-permute-start(bf16[32,2048]{1,0:T(8,128)(2,1)S(1)} %get-tuple-element.83.refs_1_), channel_id=1, source_target_pairs={{0,3},{1,2},{2,1},{3,0},{4,7},{5,6},{6,5},{7,4},{8,11},{9,10},{10,... | collective-permute-start | bytes 393224 | tf_op jit(solution)/shard_map/ppermute | solution.py:302
  12.0 3.2 %shard_map.67 = (bf16[2048,1792]{1,0:T(8,128)(2,1)S(1)}, f32[8,128]{1,0:T(8,128)S(1)}) custom-call(bf16[2048,3584]{1,0:T(8,128)(2,1)} %refs_2_.1, bf16[2048,3584]{1,0:T(8,128)(2,1)} %refs_3_.1, f32[8,128]{1,0:T(8,128)S(1)} %get-tuple-element.84.refs_2_), custom_call_target="tpu_custom_call" | custom-call | bytes 1 | tf_op jit(solution)/shard_map/pallas_call | solution.py:41
  15.8 1.6 %collective-permute-start.6 = (bf16[32,2048]{1,0:T(8,128)(2,1)S(1)}, bf16[32,2048]{1,0:T(8,128)(2,1)S(1)}, u32[]{:S(2)}, u32[]{:S(2)}) collective-permute-start(bf16[32,2048]{1,0:T(8,128)(2,1)S(1)} %get-tuple-element.86), channel_id=1, source_target_pairs={{0,1},{1,0},{2,3},{3,2},{4,5},{5,4},{6,7},{7,6},{8,9},{9,8},{10,11... | collective-permute-start | bytes 393224 | tf_op jit(solution)/shard_map/ppermute | solution.py:305
  17.5 3.2 %shard_map.69 = (bf16[2048,1792]{1,0:T(8,128)(2,1)S(1)}, f32[8,128]{1,0:T(8,128)S(1)}) custom-call(bf16[2048,3584]{1,0:T(8,128)(2,1)} %refs_2_.1, bf16[2048,3584]{1,0:T(8,128)(2,1)} %refs_3_.1, f32[8,128]{1,0:T(8,128)S(1)} %get-tuple-element.87.refs_2_), custom_call_target="tpu_custom_call" | custom-call | bytes 1 | tf_op jit(solution)/shard_map/pallas_call | solution.py:41
  21.0 2.1 %collective-permute-start.8 = (bf16[32,2048]{1,0:T(8,128)(2,1)S(1)}, bf16[32,2048]{1,0:T(8,128)(2,1)S(1)}, u32[]{:S(2)}, u32[]{:S(2)}) collective-permute-start(bf16[32,2048]{1,0:T(8,128)(2,1)S(1)} %get-tuple-element.90), channel_id=1, source_target_pairs={{0,1},{1,0},{2,3},{3,2},{4,5},{5,4},{6,7},{7,6},{8,9},{9,8},{10,11... | collective-permute-start | bytes 393224 | tf_op jit(solution)/shard_map/ppermute | solution.py:309
  23.1 3.3 %shard_map.72 = (bf16[2048,1792]{1,0:T(8,128)(2,1)S(1)}, f32[8,128]{1,0:T(8,128)S(1)}) custom-call(bf16[2048,3584]{1,0:T(8,128)(2,1)} %refs_2_.1, bf16[2048,3584]{1,0:T(8,128)(2,1)} %refs_3_.1, f32[8,128]{1,0:T(8,128)S(1)} %get-tuple-element.93.refs_2_), custom_call_target="tpu_custom_call" | custom-call | bytes 1 | tf_op jit(solution)/shard_map/pallas_call | solution.py:41
  26.4 1.4 %shard_map.73 = (bf16[128,2048]{1,0:T(8,128)(2,1)S(1)}, bf16[64,1792]{1,0:T(8,128)(2,1)S(1)}, bf16[64,1792]{1,0:T(8,128)(2,1)S(1)}, f32[8,128]{1,0:T(8,128)S(1)}) custom-call(bf16[32,2048]{1,0:T(8,128)(2,1)S(1)} %get-tuple-element.79.refs_0_, bf16[32,2048]{1,0:T(8,128)(2,1)S(1)} %get-tuple-element.83.refs_1_, ...), custom_call_target="tpu_custom_call" | custom-call | bytes 1 | tf_op jit(solution)/shard_map/pallas_call | solution.py:41
  28.4 1.1 %shard_map.74 = (f32[128,1792]{1,0:T(8,128)S(1)}, f32[8,128]{1,0:T(8,128)S(1)}) custom-call(bf16[128,2048]{1,0:T(8,128)(2,1)S(1)} %get-tuple-element.95.refs_0_, bf16[2048,1792]{1,0:T(8,128)(2,1)S(1)} %get-tuple-element.97.refs_1_, f32[8,128]{1,0:T(8,128)S(1)} %get-tuple-element.98.refs_2_), custom_call_target="tpu_custom_call" | custom-call | bytes 1 | tf_op jit(solution)/shard_map/pallas_call | solution.py:41
  29.9 1.5 %collective-permute-start.11 = (bf16[64,1792]{1,0:T(8,128)(2,1)S(1)}, bf16[64,1792]{1,0:T(8,128)(2,1)S(1)}, u32[]{:S(2)}, u32[]{:S(2)}) collective-permute-start(bf16[64,1792]{1,0:T(8,128)(2,1)S(1)} %get-tuple-element.107), channel_id=1, source_target_pairs={{0,8},{4,12},{8,0},{12,4},{1,9},{5,13},{9,1},{13,5},{2,10},{6,14},... | collective-permute-start | bytes 688136 | tf_op jit(solution)/shard_map/ppermute | solution.py:329
  31.4 3.3 %shard_map.76 = (bf16[64,1792]{1,0:T(8,128)(2,1)S(1)}, bf16[64,1792]{1,0:T(8,128)(2,1)S(1)}, bf16[2048,1792]{1,0:T(8,128)(2,1)S(1)}, f32[8,128]{1,0:T(8,128)S(1)}) custom-call(bf16[128,2048]{1,0:T(8,128)(2,1)S(1)} %get-tuple-element.95.refs_0_, bf16[2048,1792]{1,0:T(8,128)(2,1)S(1)} %get-tuple-element.96.refs_1_, bf16[2048,3584]{1,0:T(8,128)(2,1)} %refs_2_.1, ...), custom_call_target="tpu_custom_call" | custom-call | bytes 1 | tf_op jit(solution)/shard_map/pallas_call | solution.py:41
  35.6 1.1 %shard_map.77 = (f32[128,1792]{1,0:T(8,128)S(1)}, f32[8,128]{1,0:T(8,128)S(1)}) custom-call(bf16[128,2048]{1,0:T(8,128)(2,1)S(1)} %get-tuple-element.95.refs_0_, bf16[2048,1792]{1,0:T(8,128)(2,1)S(1)} %get-tuple-element.104.refs_1_, f32[8,128]{1,0:T(8,128)S(1)} %get-tuple-element.105.refs_2_), custom_call_target="tpu_custom_call" | custom-call | bytes 1 | tf_op jit(solution)/shard_map/pallas_call | solution.py:41
  37.1 1.2 %slice-done.2 = s8[4194304]{0:T(1024)(128)(4,1)S(1)} async-done(((s8[14680064]{0:T(1024)(128)(4,1)}), s8[4194304]{0:T(1024)(128)(4,1)S(1)}, s32[]{:S(2)}) %slice-start.2) | async-done | bytes 4194328
  40.9 1.4 %shard_map.81 = (f32[64,2048]{1,0:T(8,128)S(1)}, f32[8,128]{1,0:T(8,128)S(1)}) custom-call(bf16[1792,2048]{1,0:T(8,128)(2,1)S(1)} %get-tuple-element.113.refs_0_, bf16[64,896]{1,0:T(8,128)(2,1)S(1)} %get-tuple-element.114.refs_1_, bf16[64,896]{1,0:T(8,128)(2,1)S(1)} %collective-permute-done.13.refs_2_, f32[8,128]{1,0:T(8,128)S(1)} %get-tuple-element.115.refs_3_), custom_call_target="tpu_custom_call" | custom-call | bytes 1 | tf_op jit(solution)/shard_map/pallas_call | solution.py:41
  42.3 0.6 collective-permute-done.15.refs_1_
  43.2 1.6 %collective-permute-start.22 = (bf16[64,896]{1,0:T(8,128)(2,1)S(1)}, bf16[64,896]{1,0:T(8,128)(2,1)S(1)}, u32[]{:S(2)}, u32[]{:S(2)}) collective-permute-start(bf16[64,896]{1,0:T(8,128)(2,1)S(1)} %get-tuple-element.123.refs_1_), channel_id=1, source_target_pairs={{0,8},{4,12},{8,0},{12,4},{1,9},{5,13},{9,1},{13,5},{2,10},{6,14},... | collective-permute-start | bytes 344072 | tf_op jit(solution)/shard_map/ppermute | solution.py:350
  45.9 1.4 %shard_map.84 = (f32[64,2048]{1,0:T(8,128)S(1)}, f32[8,128]{1,0:T(8,128)S(1)}) custom-call(bf16[1792,2048]{1,0:T(8,128)(2,1)S(1)} %get-tuple-element.113.refs_0_, bf16[64,896]{1,0:T(8,128)(2,1)S(1)} %get-tuple-element.123.refs_1_, bf16[64,896]{1,0:T(8,128)(2,1)S(1)} %collective-permute-done.19.refs_2_, f32[8,128]{1,0:T(8,128)S(1)} %get-tuple-element.124.refs_3_), custom_call_target="tpu_custom_call" | custom-call | bytes 1 | tf_op jit(solution)/shard_map/pallas_call | solution.py:41
  47.4 1.4 %shard_map.85 = (f32[16,2048]{1,0:T(8,128)S(1)}, bf16[16,2048]{1,0:T(8,128)(2,1)S(1)}, bf16[16,2048]{1,0:T(8,128)(2,1)S(1)}, bf16[16,2048]{1,0:T(8,128)(2,1)S(1)}, f32[8,128]{1,0:T(8,128)S(1)}) custom-call(bf16[1792,2048]{1,0:T(8,128)(2,1)S(1)} %get-tuple-element.112.refs_0_, f32[64,2048]{1,0:T(8,128)S(1)} %get-tuple-element.116.refs_1_, ...), custom_call_target="tpu_custom_call" | custom-call | bytes 1 | tf_op jit(solution)/shard_map/pallas_call | solution.py:41
  48.8 2.0 %collective-permute-start.20 = (bf16[16,2048]{1,0:T(8,128)(2,1)S(1)}, bf16[16,2048]{1,0:T(8,128)(2,1)S(1)}, u32[]{:S(2)}, u32[]{:S(2)}) collective-permute-start(bf16[16,2048]{1,0:T(8,128)(2,1)S(1)} %get-tuple-element.127), channel_id=1, source_target_pairs={{0,3},{1,2},{2,1},{3,0},{4,7},{5,6},{6,5},{7,4},{8,11},{9,10},{10,... | collective-permute-start | bytes 196616 | tf_op jit(solution)/shard_map/ppermute | solution.py:373
  51.3 1.3 %collective-permute-start.21 = (bf16[16,2048]{1,0:T(8,128)(2,1)S(1)}, bf16[16,2048]{1,0:T(8,128)(2,1)S(1)}, u32[]{:S(2)}, u32[]{:S(2)}) collective-permute-start(bf16[16,2048]{1,0:T(8,128)(2,1)S(1)} %get-tuple-element.128), channel_id=1, source_target_pairs={{0,2},{1,3},{2,0},{3,1},{4,6},{5,7},{6,4},{7,5},{8,10},{9,11},{10,... | collective-permute-start | bytes 196616 | tf_op jit(solution)/shard_map/ppermute | solution.py:373
  52.7 1.4 %shard_map.87 = (f32[16,2048]{1,0:T(8,128)S(1)}, bf16[16,2048]{1,0:T(8,128)(2,1)S(1)}, bf16[16,2048]{1,0:T(8,128)(2,1)S(1)}, bf16[16,2048]{1,0:T(8,128)(2,1)S(1)...) custom-call(bf16[1792,2048]{1,0:T(8,128)(2,1)S(1)} %get-tuple-element.112.refs_0_, ...), custom_call_target="tpu_custom_call" | custom-call | bytes 1 | tf_op jit(solution)/shard_map/pallas_call | solution.py:41
  54.1 1.6 %collective-permute-start.25 = (bf16[16,2048]{1,0:T(8,128)(2,1)S(1)}, bf16[16,2048]{1,0:T(8,128)(2,1)S(1)}, u32[]{:S(2)}, u32[]{:S(2)}) collective-permute-start(bf16[16,2048]{1,0:T(8,128)(2,1)S(1)} %get-tuple-element.136), channel_id=1, source_target_pairs={{0,3},{1,2},{2,1},{3,0},{4,7},{5,6},{6,5},{7,4},{8,11},{9,10},{10,... | collective-permute-start | bytes 196616 | tf_op jit(solution)/shard_map/ppermute | solution.py:373
  55.7 1.1 %collective-permute-start.26 = (bf16[16,2048]{1,0:T(8,128)(2,1)S(1)}, bf16[16,2048]{1,0:T(8,128)(2,1)S(1)}, u32[]{:S(2)}, u32[]{:S(2)}) collective-permute-start(bf16[16,2048]{1,0:T(8,128)(2,1)S(1)} %get-tuple-element.137), channel_id=1, source_target_pairs={{0,2},{1,3},{2,0},{3,1},{4,6},{5,7},{6,4},{7,5},{8,10},{9,11},{10,... | collective-permute-start | bytes 196616 | tf_op jit(solution)/shard_map/ppermute | solution.py:373
  56.8 1.7 %collective-permute-start.27 = (bf16[16,2048]{1,0:T(8,128)(2,1)S(1)}, bf16[16,2048]{1,0:T(8,128)(2,1)S(1)}, u32[]{:S(2)}, u32[]{:S(2)}) collective-permute-start(bf16[16,2048]{1,0:T(8,128)(2,1)S(1)} %get-tuple-element.138), channel_id=1, source_target_pairs={{0,1},{1,0},{2,3},{3,2},{4,5},{5,4},{6,7},{7,6},{8,9},{9,8},{10,11... | collective-permute-start | bytes 196616 | tf_op jit(solution)/shard_map/ppermute | solution.py:385
  58.8 2.3 %collective-permute-done.21.refs_2_ = bf16[16,2048]{1,0:T(8,128)(2,1)S(1)} collective-permute-done((bf16[16,2048]{1,0:T(8,128)(2,1)S(1)}, bf16[16,2048]{1,0:T(8,128)(2,1)S(1)}, u32[]{:S(2)}, u32[]{:S(2)}) %collective-permute-start.21) | collective-permute-done | bytes 65568 | tf_op jit(solution)/shard_map/ppermute | solution.py:373
  61.1 2.9 %collective-permute-done.26.refs_5_ = bf16[16,2048]{1,0:T(8,128)(2,1)S(1)} collective-permute-done((bf16[16,2048]{1,0:T(8,128)(2,1)S(1)}, bf16[16,2048]{1,0:T(8,128)(2,1)S(1)}, u32[]{:S(2)}, u32[]{:S(2)}) %collective-permute-start.26) | collective-permute-done | bytes 65568 | tf_op jit(solution)/shard_map/ppermute | solution.py:373
  64.6 1.2 %collective-permute-start.30 = (bf16[2,4,2048]{2,1,0:T(4,128)(2,1)S(1)}, bf16[2,4,2048]{2,1,0:T(4,128)(2,1)S(1)}, u32[]{:S(2)}, u32[]{:S(2)}) collective-permute-start(bf16[2,4,2048]{2,1,0:T(4,128)(2,1)S(1)} %get-tuple-element.143), channel_id=1, source_target_pairs={{0,8},{4,12},{8,0},{12,4},{1,9},{5,13},{9,1},{13,5},{2,10},{6,14},... | collective-permute-start | bytes 98312 | tf_op jit(solution)/shard_map/ppermute | solution.py:387
  65.8 0.7 collective-permute-start.31
  66.5 2.1 %collective-permute-done.30.refs_2_ = bf16[2,4,2048]{2,1,0:T(4,128)(2,1)S(1)} collective-permute-done((bf16[2,4,2048]{2,1,0:T(4,128)(2,1)S(1)}, bf16[2,4,2048]{2,1,0:T(4,128)(2,1)S(1)}, u32[]{:S(2)}, u32[]{:S(2)}) %collective-permute-start.30) | collective-permute-done | bytes 32800 | tf_op jit(solution)/shard_map/ppermute | solution.py:387
  69.1 0.7 shard_map.89
  (73 shorter events, 9.7 us)
Async XLA Ops:
  1.2 3.2 %collective-permute-start = (bf16[2,8,2048]{2,1,0:T(8,128)(2,1)S(1)}, bf16[2,8,2048]{2,1,0:T(8,128)(2,1)S(1)}, u32[]{:S(2)}, u32[]{:S(2)}) collective-permute-start(bf16[2,8,2048]{2,1,0:T(8,128)(2,1)S(1)} %get-tuple-element.77), channel_id=1, source_target_pairs={{0,4},{4,0},{8,12},{12,8},{1,5},{5,1},{9,13},{13,9},{2,6},{6,2},{1... | collective-permute-start | bytes 196616 | tf_op jit(solution)/shard_map/ppermute | solution.py:290
  1.7 6.6 %collective-permute-start.1 = (bf16[2,8,2048]{2,1,0:T(8,128)(2,1)S(1)}, bf16[2,8,2048]{2,1,0:T(8,128)(2,1)S(1)}, u32[]{:S(2)}, u32[]{:S(2)}) collective-permute-start(bf16[2,8,2048]{2,1,0:T(8,128)(2,1)S(1)} %get-tuple-element.80), channel_id=1, source_target_pairs={{0,8},{4,12},{8,0},{12,4},{1,9},{5,13},{9,1},{13,5},{2,10},{6,14},... | collective-permute-start | bytes 196616 | tf_op jit(solution)/shard_map/ppermute | solution.py:289
  4.3 4.0 %collective-permute-start.2 = (bf16[2,8,2048]{2,1,0:T(8,128)(2,1)S(1)}, bf16[2,8,2048]{2,1,0:T(8,128)(2,1)S(1)}, u32[]{:S(2)}, u32[]{:S(2)}) collective-permute-start(bf16[2,8,2048]{2,1,0:T(8,128)(2,1)S(1)} %get-tuple-element.81), channel_id=1, source_target_pairs={{0,12},{4,8},{8,4},{12,0},{1,13},{5,9},{9,5},{13,1},{2,14},{6,10},... | collective-permute-start | bytes 196616 | tf_op jit(solution)/shard_map/ppermute | solution.py:289
  4.4 10.8 %collective-permute-start.5 = (bf16[32,2048]{1,0:T(8,128)(2,1)S(1)}, bf16[32,2048]{1,0:T(8,128)(2,1)S(1)}, u32[]{:S(2)}, u32[]{:S(2)}) collective-permute-start(bf16[32,2048]{1,0:T(8,128)(2,1)S(1)} %get-tuple-element.79.refs_0_), channel_id=1, source_target_pairs={{0,3},{1,2},{2,1},{3,0},{4,7},{5,6},{6,5},{7,4},{8,11},{9,10},{10,... | collective-permute-start | bytes 393224 | tf_op jit(solution)/shard_map/ppermute | solution.py:300
  8.2 7.6 %collective-permute-start.3 = (bf16[32,2048]{1,0:T(8,128)(2,1)S(1)}, bf16[32,2048]{1,0:T(8,128)(2,1)S(1)}, u32[]{:S(2)}, u32[]{:S(2)}) collective-permute-start(bf16[32,2048]{1,0:T(8,128)(2,1)S(1)} %get-tuple-element.79.refs_0_), channel_id=1, source_target_pairs={{0,1},{1,0},{2,3},{3,2},{4,5},{5,4},{6,7},{7,6},{8,9},{9,8},{10,11... | collective-permute-start | bytes 393224 | tf_op jit(solution)/shard_map/ppermute | solution.py:300
  8.3 12.7 %collective-permute-start.7 = (bf16[32,2048]{1,0:T(8,128)(2,1)S(1)}, bf16[32,2048]{1,0:T(8,128)(2,1)S(1)}, u32[]{:S(2)}, u32[]{:S(2)}) collective-permute-start(bf16[32,2048]{1,0:T(8,128)(2,1)S(1)} %get-tuple-element.83.refs_1_), channel_id=1, source_target_pairs={{0,3},{1,2},{2,1},{3,0},{4,7},{5,6},{6,5},{7,4},{8,11},{9,10},{10,... | collective-permute-start | bytes 393224 | tf_op jit(solution)/shard_map/ppermute | solution.py:302
  12.0 9.0 %collective-permute-start.4 = (bf16[32,2048]{1,0:T(8,128)(2,1)S(1)}, bf16[32,2048]{1,0:T(8,128)(2,1)S(1)}, u32[]{:S(2)}, u32[]{:S(2)}) collective-permute-start(bf16[32,2048]{1,0:T(8,128)(2,1)S(1)} %get-tuple-element.83.refs_1_), channel_id=1, source_target_pairs={{0,1},{1,0},{2,3},{3,2},{4,5},{5,4},{6,7},{7,6},{8,9},{9,8},{10,11... | collective-permute-start | bytes 393224 | tf_op jit(solution)/shard_map/ppermute | solution.py:302
  15.8 10.6 %collective-permute-start.6 = (bf16[32,2048]{1,0:T(8,128)(2,1)S(1)}, bf16[32,2048]{1,0:T(8,128)(2,1)S(1)}, u32[]{:S(2)}, u32[]{:S(2)}) collective-permute-start(bf16[32,2048]{1,0:T(8,128)(2,1)S(1)} %get-tuple-element.86), channel_id=1, source_target_pairs={{0,1},{1,0},{2,3},{3,2},{4,5},{5,4},{6,7},{7,6},{8,9},{9,8},{10,11... | collective-permute-start | bytes 393224 | tf_op jit(solution)/shard_map/ppermute | solution.py:305
  21.0 5.4 %collective-permute-start.8 = (bf16[32,2048]{1,0:T(8,128)(2,1)S(1)}, bf16[32,2048]{1,0:T(8,128)(2,1)S(1)}, u32[]{:S(2)}, u32[]{:S(2)}) collective-permute-start(bf16[32,2048]{1,0:T(8,128)(2,1)S(1)} %get-tuple-element.90), channel_id=1, source_target_pairs={{0,1},{1,0},{2,3},{3,2},{4,5},{5,4},{6,7},{7,6},{8,9},{9,8},{10,11... | collective-permute-start | bytes 393224 | tf_op jit(solution)/shard_map/ppermute | solution.py:309
  27.9 1.7 %collective-permute-start.9 = (bf16[64,1792]{1,0:T(8,128)(2,1)S(1)}, bf16[64,1792]{1,0:T(8,128)(2,1)S(1)}, u32[]{:S(2)}, u32[]{:S(2)}) collective-permute-start(bf16[64,1792]{1,0:T(8,128)(2,1)S(1)} %get-tuple-element.100), channel_id=1, source_target_pairs={{0,4},{4,0},{8,12},{12,8},{1,5},{5,1},{9,13},{13,9},{2,6},{6,2},{1... | collective-permute-start | bytes 688136 | tf_op jit(solution)/shard_map/ppermute | solution.py:326
  27.9 1.8 %collective-permute-start.10 = (bf16[64,1792]{1,0:T(8,128)(2,1)S(1)}, bf16[64,1792]{1,0:T(8,128)(2,1)S(1)}, u32[]{:S(2)}, u32[]{:S(2)}) collective-permute-start(bf16[64,1792]{1,0:T(8,128)(2,1)S(1)} %get-tuple-element.101), channel_id=1, source_target_pairs={{0,4},{4,0},{8,12},{12,8},{1,5},{5,1},{9,13},{13,9},{2,6},{6,2},{1... | collective-permute-start | bytes 688136 | tf_op jit(solution)/shard_map/ppermute | solution.py:326
  29.9 9.5 %collective-permute-start.11 = (bf16[64,1792]{1,0:T(8,128)(2,1)S(1)}, bf16[64,1792]{1,0:T(8,128)(2,1)S(1)}, u32[]{:S(2)}, u32[]{:S(2)}) collective-permute-start(bf16[64,1792]{1,0:T(8,128)(2,1)S(1)} %get-tuple-element.107), channel_id=1, source_target_pairs={{0,8},{4,12},{8,0},{12,4},{1,9},{5,13},{9,1},{13,5},{2,10},{6,14},... | collective-permute-start | bytes 688136 | tf_op jit(solution)/shard_map/ppermute | solution.py:329
  34.8 4.6 %collective-permute-start.12 = (bf16[64,1792]{1,0:T(8,128)(2,1)S(1)}, bf16[64,1792]{1,0:T(8,128)(2,1)S(1)}, u32[]{:S(2)}, u32[]{:S(2)}) collective-permute-start(bf16[64,1792]{1,0:T(8,128)(2,1)S(1)} %get-tuple-element.108), channel_id=1, source_target_pairs={{0,4},{4,0},{8,12},{12,8},{1,5},{5,1},{9,13},{13,9},{2,6},{6,2},{1... | collective-permute-start | bytes 688136 | tf_op jit(solution)/shard_map/ppermute | solution.py:339
  34.9 8.1 %collective-permute-start.15 = (bf16[64,1792]{1,0:T(8,128)(2,1)S(1)}, bf16[64,1792]{1,0:T(8,128)(2,1)S(1)}, u32[]{:S(2)}, u32[]{:S(2)}) collective-permute-start(bf16[64,1792]{1,0:T(8,128)(2,1)S(1)} %get-tuple-element.117), channel_id=1, source_target_pairs={{0,8},{4,12},{8,0},{12,4},{1,9},{5,13},{9,1},{13,5},{2,10},{6,14},... | collective-permute-start | bytes 688136 | tf_op jit(solution)/shard_map/ppermute | solution.py:329
  35.5 7.5 %collective-permute-start.16 = (bf16[64,1792]{1,0:T(8,128)(2,1)S(1)}, bf16[64,1792]{1,0:T(8,128)(2,1)S(1)}, u32[]{:S(2)}, u32[]{:S(2)}) collective-permute-start(bf16[64,1792]{1,0:T(8,128)(2,1)S(1)} %get-tuple-element.118), channel_id=1, source_target_pairs={{0,4},{4,0},{8,12},{12,8},{1,5},{5,1},{9,13},{13,9},{2,6},{6,2},{1... | collective-permute-start | bytes 688136 | tf_op jit(solution)/shard_map/ppermute | solution.py:339
  39.5 1.4 %collective-permute-start.13 = (bf16[64,896]{1,0:T(8,128)(2,1)S(1)}, bf16[64,896]{1,0:T(8,128)(2,1)S(1)}, u32[]{:S(2)}, u32[]{:S(2)}) collective-permute-start(bf16[64,896]{1,0:T(8,128)(2,1)S(1)} %get-tuple-element.114.refs_1_), channel_id=1, source_target_pairs={{0,4},{4,0},{8,12},{12,8},{1,5},{5,1},{9,13},{13,9},{2,6},{6,2},{1... | collective-permute-start | bytes 344072 | tf_op jit(solution)/shard_map/ppermute | solution.py:351
  39.6 5.7 %collective-permute-start.14 = (bf16[64,896]{1,0:T(8,128)(2,1)S(1)}, bf16[64,896]{1,0:T(8,128)(2,1)S(1)}, u32[]{:S(2)}, u32[]{:S(2)}) collective-permute-start(bf16[64,896]{1,0:T(8,128)(2,1)S(1)} %get-tuple-element.114.refs_1_), channel_id=1, source_target_pairs={{0,8},{4,12},{8,0},{12,4},{1,9},{5,13},{9,1},{13,5},{2,10},{6,14},... | collective-permute-start | bytes 344072 | tf_op jit(solution)/shard_map/ppermute | solution.py:350
  43.1 2.8 %collective-permute-start.19 = (bf16[64,896]{1,0:T(8,128)(2,1)S(1)}, bf16[64,896]{1,0:T(8,128)(2,1)S(1)}, u32[]{:S(2)}, u32[]{:S(2)}) collective-permute-start(bf16[64,896]{1,0:T(8,128)(2,1)S(1)} %get-tuple-element.123.refs_1_), channel_id=1, source_target_pairs={{0,4},{4,0},{8,12},{12,8},{1,5},{5,1},{9,13},{13,9},{2,6},{6,2},{1... | collective-permute-start | bytes 344072 | tf_op jit(solution)/shard_map/ppermute | solution.py:351
  43.2 7.6 %collective-permute-start.22 = (bf16[64,896]{1,0:T(8,128)(2,1)S(1)}, bf16[64,896]{1,0:T(8,128)(2,1)S(1)}, u32[]{:S(2)}, u32[]{:S(2)}) collective-permute-start(bf16[64,896]{1,0:T(8,128)(2,1)S(1)} %get-tuple-element.123.refs_1_), channel_id=1, source_target_pairs={{0,8},{4,12},{8,0},{12,4},{1,9},{5,13},{9,1},{13,5},{2,10},{6,14},... | collective-permute-start | bytes 344072 | tf_op jit(solution)/shard_map/ppermute | solution.py:350
  45.3 2.0 %collective-permute-start.17 = (bf16[32,896]{1,0:T(8,128)(2,1)S(1)}, bf16[32,896]{1,0:T(8,128)(2,1)S(1)}, u32[]{:S(2)}, u32[]{:S(2)}) collective-permute-start(bf16[32,896]{1,0:T(8,128)(2,1)S(1)} %get-tuple-element.121), channel_id=1, source_target_pairs={{0,4},{4,0},{8,12},{12,8},{1,5},{5,1},{9,13},{13,9},{2,6},{6,2},{1... | collective-permute-start | bytes 172040 | tf_op jit(solution)/shard_map/ppermute | solution.py:362
  45.4 1.9 %collective-permute-start.18 = (bf16[32,896]{1,0:T(8,128)(2,1)S(1)}, bf16[32,896]{1,0:T(8,128)(2,1)S(1)}, u32[]{:S(2)}, u32[]{:S(2)}) collective-permute-start(bf16[32,896]{1,0:T(8,128)(2,1)S(1)} %get-tuple-element.122), channel_id=1, source_target_pairs={{0,4},{4,0},{8,12},{12,8},{1,5},{5,1},{9,13},{13,9},{2,6},{6,2},{1... | collective-permute-start | bytes 172040 | tf_op jit(solution)/shard_map/ppermute | solution.py:362
  48.8 9.7 %collective-permute-start.20 = (bf16[16,2048]{1,0:T(8,128)(2,1)S(1)}, bf16[16,2048]{1,0:T(8,128)(2,1)S(1)}, u32[]{:S(2)}, u32[]{:S(2)}) collective-permute-start(bf16[16,2048]{1,0:T(8,128)(2,1)S(1)} %get-tuple-element.127), channel_id=1, source_target_pairs={{0,3},{1,2},{2,1},{3,0},{4,7},{5,6},{6,5},{7,4},{8,11},{9,10},{10,... | collective-permute-start | bytes 196616 | tf_op jit(solution)/shard_map/ppermute | solution.py:373
  50.8 1.9 %collective-permute-start.23 = (bf16[32,896]{1,0:T(8,128)(2,1)S(1)}, bf16[32,896]{1,0:T(8,128)(2,1)S(1)}, u32[]{:S(2)}, u32[]{:S(2)}) collective-permute-start(bf16[32,896]{1,0:T(8,128)(2,1)S(1)} %get-tuple-element.132), channel_id=1, source_target_pairs={{0,4},{4,0},{8,12},{12,8},{1,5},{5,1},{9,13},{13,9},{2,6},{6,2},{1... | collective-permute-start | bytes 172040 | tf_op jit(solution)/shard_map/ppermute | solution.py:362
  50.8 1.8 %collective-permute-start.24 = (bf16[32,896]{1,0:T(8,128)(2,1)S(1)}, bf16[32,896]{1,0:T(8,128)(2,1)S(1)}, u32[]{:S(2)}, u32[]{:S(2)}) collective-permute-start(bf16[32,896]{1,0:T(8,128)(2,1)S(1)} %get-tuple-element.133), channel_id=1, source_target_pairs={{0,4},{4,0},{8,12},{12,8},{1,5},{5,1},{9,13},{13,9},{2,6},{6,2},{1... | collective-permute-start | bytes 172040 | tf_op jit(solution)/shard_map/ppermute | solution.py:362
  51.3 9.7 %collective-permute-start.21 = (bf16[16,2048]{1,0:T(8,128)(2,1)S(1)}, bf16[16,2048]{1,0:T(8,128)(2,1)S(1)}, u32[]{:S(2)}, u32[]{:S(2)}) collective-permute-start(bf16[16,2048]{1,0:T(8,128)(2,1)S(1)} %get-tuple-element.128), channel_id=1, source_target_pairs={{0,2},{1,3},{2,0},{3,1},{4,6},{5,7},{6,4},{7,5},{8,10},{9,11},{10,... | collective-permute-start | bytes 196616 | tf_op jit(solution)/shard_map/ppermute | solution.py:373
  54.1 7.0 %collective-permute-start.25 = (bf16[16,2048]{1,0:T(8,128)(2,1)S(1)}, bf16[16,2048]{1,0:T(8,128)(2,1)S(1)}, u32[]{:S(2)}, u32[]{:S(2)}) collective-permute-start(bf16[16,2048]{1,0:T(8,128)(2,1)S(1)} %get-tuple-element.136), channel_id=1, source_target_pairs={{0,3},{1,2},{2,1},{3,0},{4,7},{5,6},{6,5},{7,4},{8,11},{9,10},{10,... | collective-permute-start | bytes 196616 | tf_op jit(solution)/shard_map/ppermute | solution.py:373
  55.7 8.4 %collective-permute-start.26 = (bf16[16,2048]{1,0:T(8,128)(2,1)S(1)}, bf16[16,2048]{1,0:T(8,128)(2,1)S(1)}, u32[]{:S(2)}, u32[]{:S(2)}) collective-permute-start(bf16[16,2048]{1,0:T(8,128)(2,1)S(1)} %get-tuple-element.137), channel_id=1, source_target_pairs={{0,2},{1,3},{2,0},{3,1},{4,6},{5,7},{6,4},{7,5},{8,10},{9,11},{10,... | collective-permute-start | bytes 196616 | tf_op jit(solution)/shard_map/ppermute | solution.py:373
  56.8 7.2 %collective-permute-start.27 = (bf16[16,2048]{1,0:T(8,128)(2,1)S(1)}, bf16[16,2048]{1,0:T(8,128)(2,1)S(1)}, u32[]{:S(2)}, u32[]{:S(2)}) collective-permute-start(bf16[16,2048]{1,0:T(8,128)(2,1)S(1)} %get-tuple-element.138), channel_id=1, source_target_pairs={{0,1},{1,0},{2,3},{3,2},{4,5},{5,4},{6,7},{7,6},{8,9},{9,8},{10,11... | collective-permute-start | bytes 196616 | tf_op jit(solution)/shard_map/ppermute | solution.py:385
  58.5 5.8 %collective-permute-start.28 = (bf16[16,2048]{1,0:T(8,128)(2,1)S(1)}, bf16[16,2048]{1,0:T(8,128)(2,1)S(1)}, u32[]{:S(2)}, u32[]{:S(2)}) collective-permute-start(bf16[16,2048]{1,0:T(8,128)(2,1)S(1)} %get-tuple-element.139), channel_id=1, source_target_pairs={{0,1},{1,0},{2,3},{3,2},{4,5},{5,4},{6,7},{7,6},{8,9},{9,8},{10,11... | collective-permute-start | bytes 196616 | tf_op jit(solution)/shard_map/ppermute | solution.py:385
  64.5 1.9 %collective-permute-start.29 = (bf16[2,4,2048]{2,1,0:T(4,128)(2,1)S(1)}, bf16[2,4,2048]{2,1,0:T(4,128)(2,1)S(1)}, u32[]{:S(2)}, u32[]{:S(2)}) collective-permute-start(bf16[2,4,2048]{2,1,0:T(4,128)(2,1)S(1)} %get-tuple-element.142), channel_id=1, source_target_pairs={{0,4},{4,0},{8,12},{12,8},{1,5},{5,1},{9,13},{13,9},{2,6},{6,2},{1... | collective-permute-start | bytes 98312 | tf_op jit(solution)/shard_map/ppermute | solution.py:387
  64.6 4.0 %collective-permute-start.30 = (bf16[2,4,2048]{2,1,0:T(4,128)(2,1)S(1)}, bf16[2,4,2048]{2,1,0:T(4,128)(2,1)S(1)}, u32[]{:S(2)}, u32[]{:S(2)}) collective-permute-start(bf16[2,4,2048]{2,1,0:T(4,128)(2,1)S(1)} %get-tuple-element.143), channel_id=1, source_target_pairs={{0,8},{4,12},{8,0},{12,4},{1,9},{5,13},{9,1},{13,5},{2,10},{6,14},... | collective-permute-start | bytes 98312 | tf_op jit(solution)/shard_map/ppermute | solution.py:387
  65.8 3.3 %collective-permute-start.31 = (bf16[2,4,2048]{2,1,0:T(4,128)(2,1)S(1)}, bf16[2,4,2048]{2,1,0:T(4,128)(2,1)S(1)}, u32[]{:S(2)}, u32[]{:S(2)}) collective-permute-start(bf16[2,4,2048]{2,1,0:T(4,128)(2,1)S(1)} %get-tuple-element.144), channel_id=1, source_target_pairs={{0,12},{4,8},{8,4},{12,0},{1,13},{5,9},{9,5},{13,1},{2,14},{6,10},... | collective-permute-start | bytes 98312 | tf_op jit(solution)/shard_map/ppermute | solution.py:387
  (7 other events, 32.7 us)

commit v12 on v11

--- a/solution.py
+++ b/solution.py
@@ -378,8 +378,8 @@
     part0, token = down_part(0, token)
     token = activate(1, token)
     yd0, token = shared(0, token)
+    sums0, first, _, token = down_rest(0, part0, yd0, (), token)
     part1, token = down_part(1, token)
-    sums0, first, _, token = down_rest(0, part0, yd0, (), token)
     yd1, token = shared(1, token)
     sums1, second, passed, token = down_rest(1, part1, yd1, (first,), token)
     sums = sums0 + sums1 + [lax.ppermute(s, "col", X1) for s in (second, passed[0])]

time: 70 us -> 70.7 us (1.010)
    ppermute x2, waiting for transfers between devices: 5.21 us -> 2.48 us  [down_rest(): lax.ppermute(send2, 'col', X2)]
    ppermute x2, waiting for transfers between devices: 0.01 us -> 2 us  [down_rest(): lax.ppermute(send3, 'col', X3)]
    ppermute x4, waiting for transfers between devices: 0.01 us -> 0.9 us  [shared(): return (tuple((lax.ppermute(p, 'row', X1) for p in passed)), token)]
  transfers between devices with their start and end apart: 32 -> 32, of which waited for: 11 -> 14; matrix products, arithmetic and copies ran while one was open for 0% -> 0% of each run, Pallas kernels for 32% -> 32%
where the time goes in v12:
time: 70.7 us; the launch traced here: 70.5 us
  starting transfers between devices  30.9 us (44%)
  Pallas kernels  25.2 us (36%)
  waiting for transfers between devices  11.1 us (16%)
  local copies, waits for them, and re-layouts  3.01 us (4%)
    pallas_call x26, Pallas kernels, run(): pl.pallas_call(wrapped, out_shape=outs, in_specs=[spec or vmem] * count +...  25.2 us
    ppermute x1, starting transfers between devices, near_plan(): lax.ppermute(near_block, 'col', X3)  3.87 us
    ppermute x1, starting transfers between devices, near_plan(): lax.ppermute(far_block, 'col', X3)  3.67 us
    ppermute x2, starting transfers between devices, down_rest(): lax.ppermute(send3, 'col', X3)  3.54 us
    unnamed x14, local copies, waits for them, and re-layouts  3.01 us
    ppermute x2, starting transfers between devices, near_plan(): y, yd = (lax.ppermute(y, 'row', X2), lax.ppermute(yd, 'row', X3))  2.66 us
    ppermute x2, waiting for transfers between devices, down_rest(): lax.ppermute(send2, 'col', X2)  2.48 us
    ppermute x2, starting transfers between devices, down_rest(): lax.ppermute(send2, 'col', X2)  2.44 us
  transfers between devices with their start and end apart: 32, of which 14 were waited for; matrix products, arithmetic and copies ran while one was open for 0% of the time, Pallas kernels for 32%

profile of v12, /device:TPU:0, one launch (start us, length us, event | category | flops | bytes accessed | tf_op | source)
XLA Modules:
  0.0 70.5 jit_solution(16438690746568053869)
XLA Ops:
  0.0 0.9 %copy-done = bf16[2,8,8192]{2,1,0:T(8,128)(2,1)S(1)} copy-done((bf16[2,8,8192]{2,1,0:T(8,128)(2,1)S(1)}, bf16[2,8,8192]{2,1,0:T(8,128)(2,1)}, u32[]{:S(2)}) %copy-start) | copy-done | bytes 262168
  1.7 2.6 %collective-permute-start.1 = (bf16[2,8,2048]{2,1,0:T(8,128)(2,1)S(1)}, bf16[2,8,2048]{2,1,0:T(8,128)(2,1)S(1)}, u32[]{:S(2)}, u32[]{:S(2)}) collective-permute-start(bf16[2,8,2048]{2,1,0:T(8,128)(2,1)S(1)} %get-tuple-element.80), channel_id=1, source_target_pairs={{0,8},{4,12},{8,0},{12,4},{1,9},{5,13},{9,1},{13,5},{2,10},{6,14},... | collective-permute-start | bytes 196616 | tf_op jit(solution)/shard_map/ppermute | solution.py:289
  4.4 3.9 %collective-permute-start.5 = (bf16[32,2048]{1,0:T(8,128)(2,1)S(1)}, bf16[32,2048]{1,0:T(8,128)(2,1)S(1)}, u32[]{:S(2)}, u32[]{:S(2)}) collective-permute-start(bf16[32,2048]{1,0:T(8,128)(2,1)S(1)} %get-tuple-element.79.refs_0_), channel_id=1, source_target_pairs={{0,3},{1,2},{2,1},{3,0},{4,7},{5,6},{6,5},{7,4},{8,11},{9,10},{10,... | collective-permute-start | bytes 393224 | tf_op jit(solution)/shard_map/ppermute | solution.py:300
  8.3 3.7 %collective-permute-start.7 = (bf16[32,2048]{1,0:T(8,128)(2,1)S(1)}, bf16[32,2048]{1,0:T(8,128)(2,1)S(1)}, u32[]{:S(2)}, u32[]{:S(2)}) collective-permute-start(bf16[32,2048]{1,0:T(8,128)(2,1)S(1)} %get-tuple-element.83.refs_1_), channel_id=1, source_target_pairs={{0,3},{1,2},{2,1},{3,0},{4,7},{5,6},{6,5},{7,4},{8,11},{9,10},{10,... | collective-permute-start | bytes 393224 | tf_op jit(solution)/shard_map/ppermute | solution.py:302
  12.0 3.2 %shard_map.67 = (bf16[2048,1792]{1,0:T(8,128)(2,1)S(1)}, f32[8,128]{1,0:T(8,128)S(1)}) custom-call(bf16[2048,3584]{1,0:T(8,128)(2,1)} %refs_2_.1, bf16[2048,3584]{1,0:T(8,128)(2,1)} %refs_3_.1, f32[8,128]{1,0:T(8,128)S(1)} %get-tuple-element.84.refs_2_), custom_call_target="tpu_custom_call" | custom-call | bytes 1 | tf_op jit(solution)/shard_map/pallas_call | solution.py:41
  15.8 1.6 %collective-permute-start.6 = (bf16[32,2048]{1,0:T(8,128)(2,1)S(1)}, bf16[32,2048]{1,0:T(8,128)(2,1)S(1)}, u32[]{:S(2)}, u32[]{:S(2)}) collective-permute-start(bf16[32,2048]{1,0:T(8,128)(2,1)S(1)} %get-tuple-element.86), channel_id=1, source_target_pairs={{0,1},{1,0},{2,3},{3,2},{4,5},{5,4},{6,7},{7,6},{8,9},{9,8},{10,11... | collective-permute-start | bytes 393224 | tf_op jit(solution)/shard_map/ppermute | solution.py:305
  17.5 3.2 %shard_map.69 = (bf16[2048,1792]{1,0:T(8,128)(2,1)S(1)}, f32[8,128]{1,0:T(8,128)S(1)}) custom-call(bf16[2048,3584]{1,0:T(8,128)(2,1)} %refs_2_.1, bf16[2048,3584]{1,0:T(8,128)(2,1)} %refs_3_.1, f32[8,128]{1,0:T(8,128)S(1)} %get-tuple-element.87.refs_2_), custom_call_target="tpu_custom_call" | custom-call | bytes 1 | tf_op jit(solution)/shard_map/pallas_call | solution.py:41
  21.0 2.1 %collective-permute-start.8 = (bf16[32,2048]{1,0:T(8,128)(2,1)S(1)}, bf16[32,2048]{1,0:T(8,128)(2,1)S(1)}, u32[]{:S(2)}, u32[]{:S(2)}) collective-permute-start(bf16[32,2048]{1,0:T(8,128)(2,1)S(1)} %get-tuple-element.90), channel_id=1, source_target_pairs={{0,1},{1,0},{2,3},{3,2},{4,5},{5,4},{6,7},{7,6},{8,9},{9,8},{10,11... | collective-permute-start | bytes 393224 | tf_op jit(solution)/shard_map/ppermute | solution.py:309
  23.1 3.3 %shard_map.72 = (bf16[2048,1792]{1,0:T(8,128)(2,1)S(1)}, f32[8,128]{1,0:T(8,128)S(1)}) custom-call(bf16[2048,3584]{1,0:T(8,128)(2,1)} %refs_2_.1, bf16[2048,3584]{1,0:T(8,128)(2,1)} %refs_3_.1, f32[8,128]{1,0:T(8,128)S(1)} %get-tuple-element.93.refs_2_), custom_call_target="tpu_custom_call" | custom-call | bytes 1 | tf_op jit(solution)/shard_map/pallas_call | solution.py:41
  26.4 1.4 %shard_map.73 = (bf16[128,2048]{1,0:T(8,128)(2,1)S(1)}, bf16[64,1792]{1,0:T(8,128)(2,1)S(1)}, bf16[64,1792]{1,0:T(8,128)(2,1)S(1)}, f32[8,128]{1,0:T(8,128)S(1)}) custom-call(bf16[32,2048]{1,0:T(8,128)(2,1)S(1)} %get-tuple-element.79.refs_0_, bf16[32,2048]{1,0:T(8,128)(2,1)S(1)} %get-tuple-element.83.refs_1_, ...), custom_call_target="tpu_custom_call" | custom-call | bytes 1 | tf_op jit(solution)/shard_map/pallas_call | solution.py:41
  28.4 1.1 %shard_map.74 = (f32[128,1792]{1,0:T(8,128)S(1)}, f32[8,128]{1,0:T(8,128)S(1)}) custom-call(bf16[128,2048]{1,0:T(8,128)(2,1)S(1)} %get-tuple-element.95.refs_0_, bf16[2048,1792]{1,0:T(8,128)(2,1)S(1)} %get-tuple-element.97.refs_1_, f32[8,128]{1,0:T(8,128)S(1)} %get-tuple-element.98.refs_2_), custom_call_target="tpu_custom_call" | custom-call | bytes 1 | tf_op jit(solution)/shard_map/pallas_call | solution.py:41
  29.9 1.5 %collective-permute-start.11 = (bf16[64,1792]{1,0:T(8,128)(2,1)S(1)}, bf16[64,1792]{1,0:T(8,128)(2,1)S(1)}, u32[]{:S(2)}, u32[]{:S(2)}) collective-permute-start(bf16[64,1792]{1,0:T(8,128)(2,1)S(1)} %get-tuple-element.107), channel_id=1, source_target_pairs={{0,8},{4,12},{8,0},{12,4},{1,9},{5,13},{9,1},{13,5},{2,10},{6,14},... | collective-permute-start | bytes 688136 | tf_op jit(solution)/shard_map/ppermute | solution.py:329
  31.4 3.3 %shard_map.76 = (bf16[64,1792]{1,0:T(8,128)(2,1)S(1)}, bf16[64,1792]{1,0:T(8,128)(2,1)S(1)}, bf16[2048,1792]{1,0:T(8,128)(2,1)S(1)}, f32[8,128]{1,0:T(8,128)S(1)}) custom-call(bf16[128,2048]{1,0:T(8,128)(2,1)S(1)} %get-tuple-element.95.refs_0_, bf16[2048,1792]{1,0:T(8,128)(2,1)S(1)} %get-tuple-element.96.refs_1_, bf16[2048,3584]{1,0:T(8,128)(2,1)} %refs_2_.1, ...), custom_call_target="tpu_custom_call" | custom-call | bytes 1 | tf_op jit(solution)/shard_map/pallas_call | solution.py:41
  35.6 1.1 %shard_map.77 = (f32[128,1792]{1,0:T(8,128)S(1)}, f32[8,128]{1,0:T(8,128)S(1)}) custom-call(bf16[128,2048]{1,0:T(8,128)(2,1)S(1)} %get-tuple-element.95.refs_0_, bf16[2048,1792]{1,0:T(8,128)(2,1)S(1)} %get-tuple-element.104.refs_1_, f32[8,128]{1,0:T(8,128)S(1)} %get-tuple-element.105.refs_2_), custom_call_target="tpu_custom_call" | custom-call | bytes 1 | tf_op jit(solution)/shard_map/pallas_call | solution.py:41
  37.1 1.2 %slice-done.2 = s8[4194304]{0:T(1024)(128)(4,1)S(1)} async-done(((s8[14680064]{0:T(1024)(128)(4,1)}), s8[4194304]{0:T(1024)(128)(4,1)S(1)}, s32[]{:S(2)}) %slice-start.2) | async-done | bytes 4194328
  40.9 1.4 %shard_map.81 = (f32[64,2048]{1,0:T(8,128)S(1)}, f32[8,128]{1,0:T(8,128)S(1)}) custom-call(bf16[1792,2048]{1,0:T(8,128)(2,1)S(1)} %get-tuple-element.113.refs_0_, bf16[64,896]{1,0:T(8,128)(2,1)S(1)} %get-tuple-element.114.refs_1_, bf16[64,896]{1,0:T(8,128)(2,1)S(1)} %collective-permute-done.13.refs_2_, f32[8,128]{1,0:T(8,128)S(1)} %get-tuple-element.115.refs_3_), custom_call_target="tpu_custom_call" | custom-call | bytes 1 | tf_op jit(solution)/shard_map/pallas_call | solution.py:41
  43.2 1.6 %collective-permute-start.22 = (bf16[64,896]{1,0:T(8,128)(2,1)S(1)}, bf16[64,896]{1,0:T(8,128)(2,1)S(1)}, u32[]{:S(2)}, u32[]{:S(2)}) collective-permute-start(bf16[64,896]{1,0:T(8,128)(2,1)S(1)} %get-tuple-element.127.refs_1_), channel_id=1, source_target_pairs={{0,8},{4,12},{8,0},{12,4},{1,9},{5,13},{9,1},{13,5},{2,10},{6,14},... | collective-permute-start | bytes 344072 | tf_op jit(solution)/shard_map/ppermute | solution.py:350
  45.9 0.7 %collective-permute-done.17.refs_3_ = bf16[32,896]{1,0:T(8,128)(2,1)S(1)} collective-permute-done((bf16[32,896]{1,0:T(8,128)(2,1)S(1)}, bf16[32,896]{1,0:T(8,128)(2,1)S(1)}, u32[]{:S(2)}, u32[]{:S(2)}) %collective-permute-start.17) | collective-permute-done | bytes 57376 | tf_op jit(solution)/shard_map/ppermute | solution.py:362
  46.8 1.4 %shard_map.84 = (f32[16,2048]{1,0:T(8,128)S(1)}, bf16[16,2048]{1,0:T(8,128)(2,1)S(1)}, bf16[16,2048]{1,0:T(8,128)(2,1)S(1)}, bf16[16,2048]{1,0:T(8,128)(2,1)S(1)}, f32[8,128]{1,0:T(8,128)S(1)}) custom-call(bf16[1792,2048]{1,0:T(8,128)(2,1)S(1)} %get-tuple-element.112.refs_0_, f32[64,2048]{1,0:T(8,128)S(1)} %get-tuple-element.116.refs_1_, ...), custom_call_target="tpu_custom_call" | custom-call | bytes 1 | tf_op jit(solution)/shard_map/pallas_call | solution.py:41
  48.2 1.9 %collective-permute-start.19 = (bf16[16,2048]{1,0:T(8,128)(2,1)S(1)}, bf16[16,2048]{1,0:T(8,128)(2,1)S(1)}, u32[]{:S(2)}, u32[]{:S(2)}) collective-permute-start(bf16[16,2048]{1,0:T(8,128)(2,1)S(1)} %get-tuple-element.125), channel_id=1, source_target_pairs={{0,3},{1,2},{2,1},{3,0},{4,7},{5,6},{6,5},{7,4},{8,11},{9,10},{10,... | collective-permute-start | bytes 196616 | tf_op jit(solution)/shard_map/ppermute | solution.py:373
  50.2 1.4 %shard_map.85 = (f32[64,2048]{1,0:T(8,128)S(1)}, f32[8,128]{1,0:T(8,128)S(1)}) custom-call(bf16[1792,2048]{1,0:T(8,128)(2,1)S(1)} %get-tuple-element.113.refs_0_, bf16[64,896]{1,0:T(8,128)(2,1)S(1)} %get-tuple-element.127.refs_1_, bf16[64,896]{1,0:T(8,128)(2,1)S(1)} %collective-permute-done.21.refs_2_, f32[8,128]{1,0:T(8,128)S(1)} %get-tuple-element.128.refs_3_), custom_call_target="tpu_custom_call" | custom-call | bytes 1 | tf_op jit(solution)/shard_map/pallas_call | solution.py:41
  52.2 1.3 %collective-permute-start.20 = (bf16[16,2048]{1,0:T(8,128)(2,1)S(1)}, bf16[16,2048]{1,0:T(8,128)(2,1)S(1)}, u32[]{:S(2)}, u32[]{:S(2)}) collective-permute-start(bf16[16,2048]{1,0:T(8,128)(2,1)S(1)} %get-tuple-element.126), channel_id=1, source_target_pairs={{0,2},{1,3},{2,0},{3,1},{4,6},{5,7},{6,4},{7,5},{8,10},{9,11},{10,... | collective-permute-start | bytes 196616 | tf_op jit(solution)/shard_map/ppermute | solution.py:373
  53.5 1.4 %shard_map.87 = (f32[16,2048]{1,0:T(8,128)S(1)}, bf16[16,2048]{1,0:T(8,128)(2,1)S(1)}, bf16[16,2048]{1,0:T(8,128)(2,1)S(1)}, bf16[16,2048]{1,0:T(8,128)(2,1)S(1)...) custom-call(bf16[1792,2048]{1,0:T(8,128)(2,1)S(1)} %get-tuple-element.112.refs_0_, ...), custom_call_target="tpu_custom_call" | custom-call | bytes 1 | tf_op jit(solution)/shard_map/pallas_call | solution.py:41
  54.9 1.6 %collective-permute-start.25 = (bf16[16,2048]{1,0:T(8,128)(2,1)S(1)}, bf16[16,2048]{1,0:T(8,128)(2,1)S(1)}, u32[]{:S(2)}, u32[]{:S(2)}) collective-permute-start(bf16[16,2048]{1,0:T(8,128)(2,1)S(1)} %get-tuple-element.136), channel_id=1, source_target_pairs={{0,3},{1,2},{2,1},{3,0},{4,7},{5,6},{6,5},{7,4},{8,11},{9,10},{10,... | collective-permute-start | bytes 196616 | tf_op jit(solution)/shard_map/ppermute | solution.py:373
  56.5 1.1 %collective-permute-start.26 = (bf16[16,2048]{1,0:T(8,128)(2,1)S(1)}, bf16[16,2048]{1,0:T(8,128)(2,1)S(1)}, u32[]{:S(2)}, u32[]{:S(2)}) collective-permute-start(bf16[16,2048]{1,0:T(8,128)(2,1)S(1)} %get-tuple-element.137), channel_id=1, source_target_pairs={{0,2},{1,3},{2,0},{3,1},{4,6},{5,7},{6,4},{7,5},{8,10},{9,11},{10,... | collective-permute-start | bytes 196616 | tf_op jit(solution)/shard_map/ppermute | solution.py:373
  57.7 1.7 %collective-permute-start.27 = (bf16[16,2048]{1,0:T(8,128)(2,1)S(1)}, bf16[16,2048]{1,0:T(8,128)(2,1)S(1)}, u32[]{:S(2)}, u32[]{:S(2)}) collective-permute-start(bf16[16,2048]{1,0:T(8,128)(2,1)S(1)} %get-tuple-element.138), channel_id=1, source_target_pairs={{0,1},{1,0},{2,3},{3,2},{4,5},{5,4},{6,7},{7,6},{8,9},{9,8},{10,11... | collective-permute-start | bytes 196616 | tf_op jit(solution)/shard_map/ppermute | solution.py:385
  59.7 2.0 %collective-permute-done.25.refs_4_ = bf16[16,2048]{1,0:T(8,128)(2,1)S(1)} collective-permute-done((bf16[16,2048]{1,0:T(8,128)(2,1)S(1)}, bf16[16,2048]{1,0:T(8,128)(2,1)S(1)}, u32[]{:S(2)}, u32[]{:S(2)}) %collective-permute-start.25) | collective-permute-done | bytes 65568 | tf_op jit(solution)/shard_map/ppermute | solution.py:373
  61.7 2.5 %collective-permute-done.26.refs_5_ = bf16[16,2048]{1,0:T(8,128)(2,1)S(1)} collective-permute-done((bf16[16,2048]{1,0:T(8,128)(2,1)S(1)}, bf16[16,2048]{1,0:T(8,128)(2,1)S(1)}, u32[]{:S(2)}, u32[]{:S(2)}) %collective-permute-start.26) | collective-permute-done | bytes 65568 | tf_op jit(solution)/shard_map/ppermute | solution.py:373
  64.4 0.7 collective-permute-done.28.refs_7_
  65.3 1.2 %collective-permute-start.30 = (bf16[2,4,2048]{2,1,0:T(4,128)(2,1)S(1)}, bf16[2,4,2048]{2,1,0:T(4,128)(2,1)S(1)}, u32[]{:S(2)}, u32[]{:S(2)}) collective-permute-start(bf16[2,4,2048]{2,1,0:T(4,128)(2,1)S(1)} %get-tuple-element.143), channel_id=1, source_target_pairs={{0,8},{4,12},{8,0},{12,4},{1,9},{5,13},{9,1},{13,5},{2,10},{6,14},... | collective-permute-start | bytes 98312 | tf_op jit(solution)/shard_map/ppermute | solution.py:387
  67.2 2.1 %collective-permute-done.30.refs_2_ = bf16[2,4,2048]{2,1,0:T(4,128)(2,1)S(1)} collective-permute-done((bf16[2,4,2048]{2,1,0:T(4,128)(2,1)S(1)}, bf16[2,4,2048]{2,1,0:T(4,128)(2,1)S(1)}, u32[]{:S(2)}, u32[]{:S(2)}) %collective-permute-start.30) | collective-permute-done | bytes 32800 | tf_op jit(solution)/shard_map/ppermute | solution.py:387
  69.9 0.7 shard_map.89
  (73 shorter events, 11.0 us)
Async XLA Ops:
  1.2 3.2 %collective-permute-start = (bf16[2,8,2048]{2,1,0:T(8,128)(2,1)S(1)}, bf16[2,8,2048]{2,1,0:T(8,128)(2,1)S(1)}, u32[]{:S(2)}, u32[]{:S(2)}) collective-permute-start(bf16[2,8,2048]{2,1,0:T(8,128)(2,1)S(1)} %get-tuple-element.77), channel_id=1, source_target_pairs={{0,4},{4,0},{8,12},{12,8},{1,5},{5,1},{9,13},{13,9},{2,6},{6,2},{1... | collective-permute-start | bytes 196616 | tf_op jit(solution)/shard_map/ppermute | solution.py:290
  1.7 6.6 %collective-permute-start.1 = (bf16[2,8,2048]{2,1,0:T(8,128)(2,1)S(1)}, bf16[2,8,2048]{2,1,0:T(8,128)(2,1)S(1)}, u32[]{:S(2)}, u32[]{:S(2)}) collective-permute-start(bf16[2,8,2048]{2,1,0:T(8,128)(2,1)S(1)} %get-tuple-element.80), channel_id=1, source_target_pairs={{0,8},{4,12},{8,0},{12,4},{1,9},{5,13},{9,1},{13,5},{2,10},{6,14},... | collective-permute-start | bytes 196616 | tf_op jit(solution)/shard_map/ppermute | solution.py:289
  4.3 4.0 %collective-permute-start.2 = (bf16[2,8,2048]{2,1,0:T(8,128)(2,1)S(1)}, bf16[2,8,2048]{2,1,0:T(8,128)(2,1)S(1)}, u32[]{:S(2)}, u32[]{:S(2)}) collective-permute-start(bf16[2,8,2048]{2,1,0:T(8,128)(2,1)S(1)} %get-tuple-element.81), channel_id=1, source_target_pairs={{0,12},{4,8},{8,4},{12,0},{1,13},{5,9},{9,5},{13,1},{2,14},{6,10},... | collective-permute-start | bytes 196616 | tf_op jit(solution)/shard_map/ppermute | solution.py:289
  4.4 10.8 %collective-permute-start.5 = (bf16[32,2048]{1,0:T(8,128)(2,1)S(1)}, bf16[32,2048]{1,0:T(8,128)(2,1)S(1)}, u32[]{:S(2)}, u32[]{:S(2)}) collective-permute-start(bf16[32,2048]{1,0:T(8,128)(2,1)S(1)} %get-tuple-element.79.refs_0_), channel_id=1, source_target_pairs={{0,3},{1,2},{2,1},{3,0},{4,7},{5,6},{6,5},{7,4},{8,11},{9,10},{10,... | collective-permute-start | bytes 393224 | tf_op jit(solution)/shard_map/ppermute | solution.py:300
  8.2 7.6 %collective-permute-start.3 = (bf16[32,2048]{1,0:T(8,128)(2,1)S(1)}, bf16[32,2048]{1,0:T(8,128)(2,1)S(1)}, u32[]{:S(2)}, u32[]{:S(2)}) collective-permute-start(bf16[32,2048]{1,0:T(8,128)(2,1)S(1)} %get-tuple-element.79.refs_0_), channel_id=1, source_target_pairs={{0,1},{1,0},{2,3},{3,2},{4,5},{5,4},{6,7},{7,6},{8,9},{9,8},{10,11... | collective-permute-start | bytes 393224 | tf_op jit(solution)/shard_map/ppermute | solution.py:300
  8.3 12.7 %collective-permute-start.7 = (bf16[32,2048]{1,0:T(8,128)(2,1)S(1)}, bf16[32,2048]{1,0:T(8,128)(2,1)S(1)}, u32[]{:S(2)}, u32[]{:S(2)}) collective-permute-start(bf16[32,2048]{1,0:T(8,128)(2,1)S(1)} %get-tuple-element.83.refs_1_), channel_id=1, source_target_pairs={{0,3},{1,2},{2,1},{3,0},{4,7},{5,6},{6,5},{7,4},{8,11},{9,10},{10,... | collective-permute-start | bytes 393224 | tf_op jit(solution)/shard_map/ppermute | solution.py:302
  12.0 9.0 %collective-permute-start.4 = (bf16[32,2048]{1,0:T(8,128)(2,1)S(1)}, bf16[32,2048]{1,0:T(8,128)(2,1)S(1)}, u32[]{:S(2)}, u32[]{:S(2)}) collective-permute-start(bf16[32,2048]{1,0:T(8,128)(2,1)S(1)} %get-tuple-element.83.refs_1_), channel_id=1, source_target_pairs={{0,1},{1,0},{2,3},{3,2},{4,5},{5,4},{6,7},{7,6},{8,9},{9,8},{10,11... | collective-permute-start | bytes 393224 | tf_op jit(solution)/shard_map/ppermute | solution.py:302
  15.8 10.6 %collective-permute-start.6 = (bf16[32,2048]{1,0:T(8,128)(2,1)S(1)}, bf16[32,2048]{1,0:T(8,128)(2,1)S(1)}, u32[]{:S(2)}, u32[]{:S(2)}) collective-permute-start(bf16[32,2048]{1,0:T(8,128)(2,1)S(1)} %get-tuple-element.86), channel_id=1, source_target_pairs={{0,1},{1,0},{2,3},{3,2},{4,5},{5,4},{6,7},{7,6},{8,9},{9,8},{10,11... | collective-permute-start | bytes 393224 | tf_op jit(solution)/shard_map/ppermute | solution.py:305
  21.0 5.4 %collective-permute-start.8 = (bf16[32,2048]{1,0:T(8,128)(2,1)S(1)}, bf16[32,2048]{1,0:T(8,128)(2,1)S(1)}, u32[]{:S(2)}, u32[]{:S(2)}) collective-permute-start(bf16[32,2048]{1,0:T(8,128)(2,1)S(1)} %get-tuple-element.90), channel_id=1, source_target_pairs={{0,1},{1,0},{2,3},{3,2},{4,5},{5,4},{6,7},{7,6},{8,9},{9,8},{10,11... | collective-permute-start | bytes 393224 | tf_op jit(solution)/shard_map/ppermute | solution.py:309
  27.9 1.7 %collective-permute-start.9 = (bf16[64,1792]{1,0:T(8,128)(2,1)S(1)}, bf16[64,1792]{1,0:T(8,128)(2,1)S(1)}, u32[]{:S(2)}, u32[]{:S(2)}) collective-permute-start(bf16[64,1792]{1,0:T(8,128)(2,1)S(1)} %get-tuple-element.100), channel_id=1, source_target_pairs={{0,4},{4,0},{8,12},{12,8},{1,5},{5,1},{9,13},{13,9},{2,6},{6,2},{1... | collective-permute-start | bytes 688136 | tf_op jit(solution)/shard_map/ppermute | solution.py:326
  27.9 1.8 %collective-permute-start.10 = (bf16[64,1792]{1,0:T(8,128)(2,1)S(1)}, bf16[64,1792]{1,0:T(8,128)(2,1)S(1)}, u32[]{:S(2)}, u32[]{:S(2)}) collective-permute-start(bf16[64,1792]{1,0:T(8,128)(2,1)S(1)} %get-tuple-element.101), channel_id=1, source_target_pairs={{0,4},{4,0},{8,12},{12,8},{1,5},{5,1},{9,13},{13,9},{2,6},{6,2},{1... | collective-permute-start | bytes 688136 | tf_op jit(solution)/shard_map/ppermute | solution.py:326
  29.9 9.5 %collective-permute-start.11 = (bf16[64,1792]{1,0:T(8,128)(2,1)S(1)}, bf16[64,1792]{1,0:T(8,128)(2,1)S(1)}, u32[]{:S(2)}, u32[]{:S(2)}) collective-permute-start(bf16[64,1792]{1,0:T(8,128)(2,1)S(1)} %get-tuple-element.107), channel_id=1, source_target_pairs={{0,8},{4,12},{8,0},{12,4},{1,9},{5,13},{9,1},{13,5},{2,10},{6,14},... | collective-permute-start | bytes 688136 | tf_op jit(solution)/shard_map/ppermute | solution.py:329
  34.8 4.6 %collective-permute-start.12 = (bf16[64,1792]{1,0:T(8,128)(2,1)S(1)}, bf16[64,1792]{1,0:T(8,128)(2,1)S(1)}, u32[]{:S(2)}, u32[]{:S(2)}) collective-permute-start(bf16[64,1792]{1,0:T(8,128)(2,1)S(1)} %get-tuple-element.108), channel_id=1, source_target_pairs={{0,4},{4,0},{8,12},{12,8},{1,5},{5,1},{9,13},{13,9},{2,6},{6,2},{1... | collective-permute-start | bytes 688136 | tf_op jit(solution)/shard_map/ppermute | solution.py:339
  34.9 8.1 %collective-permute-start.15 = (bf16[64,1792]{1,0:T(8,128)(2,1)S(1)}, bf16[64,1792]{1,0:T(8,128)(2,1)S(1)}, u32[]{:S(2)}, u32[]{:S(2)}) collective-permute-start(bf16[64,1792]{1,0:T(8,128)(2,1)S(1)} %get-tuple-element.117), channel_id=1, source_target_pairs={{0,8},{4,12},{8,0},{12,4},{1,9},{5,13},{9,1},{13,5},{2,10},{6,14},... | collective-permute-start | bytes 688136 | tf_op jit(solution)/shard_map/ppermute | solution.py:329
  35.5 7.5 %collective-permute-start.16 = (bf16[64,1792]{1,0:T(8,128)(2,1)S(1)}, bf16[64,1792]{1,0:T(8,128)(2,1)S(1)}, u32[]{:S(2)}, u32[]{:S(2)}) collective-permute-start(bf16[64,1792]{1,0:T(8,128)(2,1)S(1)} %get-tuple-element.118), channel_id=1, source_target_pairs={{0,4},{4,0},{8,12},{12,8},{1,5},{5,1},{9,13},{13,9},{2,6},{6,2},{1... | collective-permute-start | bytes 688136 | tf_op jit(solution)/shard_map/ppermute | solution.py:339
  39.5 1.4 %collective-permute-start.13 = (bf16[64,896]{1,0:T(8,128)(2,1)S(1)}, bf16[64,896]{1,0:T(8,128)(2,1)S(1)}, u32[]{:S(2)}, u32[]{:S(2)}) collective-permute-start(bf16[64,896]{1,0:T(8,128)(2,1)S(1)} %get-tuple-element.114.refs_1_), channel_id=1, source_target_pairs={{0,4},{4,0},{8,12},{12,8},{1,5},{5,1},{9,13},{13,9},{2,6},{6,2},{1... | collective-permute-start | bytes 344072 | tf_op jit(solution)/shard_map/ppermute | solution.py:351
  39.6 5.7 %collective-permute-start.14 = (bf16[64,896]{1,0:T(8,128)(2,1)S(1)}, bf16[64,896]{1,0:T(8,128)(2,1)S(1)}, u32[]{:S(2)}, u32[]{:S(2)}) collective-permute-start(bf16[64,896]{1,0:T(8,128)(2,1)S(1)} %get-tuple-element.114.refs_1_), channel_id=1, source_target_pairs={{0,8},{4,12},{8,0},{12,4},{1,9},{5,13},{9,1},{13,5},{2,10},{6,14},... | collective-permute-start | bytes 344072 | tf_op jit(solution)/shard_map/ppermute | solution.py:350
  43.1 7.1 %collective-permute-start.21 = (bf16[64,896]{1,0:T(8,128)(2,1)S(1)}, bf16[64,896]{1,0:T(8,128)(2,1)S(1)}, u32[]{:S(2)}, u32[]{:S(2)}) collective-permute-start(bf16[64,896]{1,0:T(8,128)(2,1)S(1)} %get-tuple-element.127.refs_1_), channel_id=1, source_target_pairs={{0,4},{4,0},{8,12},{12,8},{1,5},{5,1},{9,13},{13,9},{2,6},{6,2},{1... | collective-permute-start | bytes 344072 | tf_op jit(solution)/shard_map/ppermute | solution.py:351
  43.2 8.4 %collective-permute-start.22 = (bf16[64,896]{1,0:T(8,128)(2,1)S(1)}, bf16[64,896]{1,0:T(8,128)(2,1)S(1)}, u32[]{:S(2)}, u32[]{:S(2)}) collective-permute-start(bf16[64,896]{1,0:T(8,128)(2,1)S(1)} %get-tuple-element.127.refs_1_), channel_id=1, source_target_pairs={{0,8},{4,12},{8,0},{12,4},{1,9},{5,13},{9,1},{13,5},{2,10},{6,14},... | collective-permute-start | bytes 344072 | tf_op jit(solution)/shard_map/ppermute | solution.py:350
  45.3 1.3 %collective-permute-start.17 = (bf16[32,896]{1,0:T(8,128)(2,1)S(1)}, bf16[32,896]{1,0:T(8,128)(2,1)S(1)}, u32[]{:S(2)}, u32[]{:S(2)}) collective-permute-start(bf16[32,896]{1,0:T(8,128)(2,1)S(1)} %get-tuple-element.121), channel_id=1, source_target_pairs={{0,4},{4,0},{8,12},{12,8},{1,5},{5,1},{9,13},{13,9},{2,6},{6,2},{1... | collective-permute-start | bytes 172040 | tf_op jit(solution)/shard_map/ppermute | solution.py:362
  45.4 1.4 %collective-permute-start.18 = (bf16[32,896]{1,0:T(8,128)(2,1)S(1)}, bf16[32,896]{1,0:T(8,128)(2,1)S(1)}, u32[]{:S(2)}, u32[]{:S(2)}) collective-permute-start(bf16[32,896]{1,0:T(8,128)(2,1)S(1)} %get-tuple-element.122), channel_id=1, source_target_pairs={{0,4},{4,0},{8,12},{12,8},{1,5},{5,1},{9,13},{13,9},{2,6},{6,2},{1... | collective-permute-start | bytes 172040 | tf_op jit(solution)/shard_map/ppermute | solution.py:362
  48.2 11.2 %collective-permute-start.19 = (bf16[16,2048]{1,0:T(8,128)(2,1)S(1)}, bf16[16,2048]{1,0:T(8,128)(2,1)S(1)}, u32[]{:S(2)}, u32[]{:S(2)}) collective-permute-start(bf16[16,2048]{1,0:T(8,128)(2,1)S(1)} %get-tuple-element.125), channel_id=1, source_target_pairs={{0,3},{1,2},{2,1},{3,0},{4,7},{5,6},{6,5},{7,4},{8,11},{9,10},{10,... | collective-permute-start | bytes 196616 | tf_op jit(solution)/shard_map/ppermute | solution.py:373
  51.6 1.9 %collective-permute-start.23 = (bf16[32,896]{1,0:T(8,128)(2,1)S(1)}, bf16[32,896]{1,0:T(8,128)(2,1)S(1)}, u32[]{:S(2)}, u32[]{:S(2)}) collective-permute-start(bf16[32,896]{1,0:T(8,128)(2,1)S(1)} %get-tuple-element.132), channel_id=1, source_target_pairs={{0,4},{4,0},{8,12},{12,8},{1,5},{5,1},{9,13},{13,9},{2,6},{6,2},{1... | collective-permute-start | bytes 172040 | tf_op jit(solution)/shard_map/ppermute | solution.py:362
  51.8 1.8 %collective-permute-start.24 = (bf16[32,896]{1,0:T(8,128)(2,1)S(1)}, bf16[32,896]{1,0:T(8,128)(2,1)S(1)}, u32[]{:S(2)}, u32[]{:S(2)}) collective-permute-start(bf16[32,896]{1,0:T(8,128)(2,1)S(1)} %get-tuple-element.133), channel_id=1, source_target_pairs={{0,4},{4,0},{8,12},{12,8},{1,5},{5,1},{9,13},{13,9},{2,6},{6,2},{1... | collective-permute-start | bytes 172040 | tf_op jit(solution)/shard_map/ppermute | solution.py:362
  52.2 7.5 %collective-permute-start.20 = (bf16[16,2048]{1,0:T(8,128)(2,1)S(1)}, bf16[16,2048]{1,0:T(8,128)(2,1)S(1)}, u32[]{:S(2)}, u32[]{:S(2)}) collective-permute-start(bf16[16,2048]{1,0:T(8,128)(2,1)S(1)} %get-tuple-element.126), channel_id=1, source_target_pairs={{0,2},{1,3},{2,0},{3,1},{4,6},{5,7},{6,4},{7,5},{8,10},{9,11},{10,... | collective-permute-start | bytes 196616 | tf_op jit(solution)/shard_map/ppermute | solution.py:373
  54.9 6.8 %collective-permute-start.25 = (bf16[16,2048]{1,0:T(8,128)(2,1)S(1)}, bf16[16,2048]{1,0:T(8,128)(2,1)S(1)}, u32[]{:S(2)}, u32[]{:S(2)}) collective-permute-start(bf16[16,2048]{1,0:T(8,128)(2,1)S(1)} %get-tuple-element.136), channel_id=1, source_target_pairs={{0,3},{1,2},{2,1},{3,0},{4,7},{5,6},{6,5},{7,4},{8,11},{9,10},{10,... | collective-permute-start | bytes 196616 | tf_op jit(solution)/shard_map/ppermute | solution.py:373
  56.5 7.6 %collective-permute-start.26 = (bf16[16,2048]{1,0:T(8,128)(2,1)S(1)}, bf16[16,2048]{1,0:T(8,128)(2,1)S(1)}, u32[]{:S(2)}, u32[]{:S(2)}) collective-permute-start(bf16[16,2048]{1,0:T(8,128)(2,1)S(1)} %get-tuple-element.137), channel_id=1, source_target_pairs={{0,2},{1,3},{2,0},{3,1},{4,6},{5,7},{6,4},{7,5},{8,10},{9,11},{10,... | collective-permute-start | bytes 196616 | tf_op jit(solution)/shard_map/ppermute | solution.py:373
  57.7 6.7 %collective-permute-start.27 = (bf16[16,2048]{1,0:T(8,128)(2,1)S(1)}, bf16[16,2048]{1,0:T(8,128)(2,1)S(1)}, u32[]{:S(2)}, u32[]{:S(2)}) collective-permute-start(bf16[16,2048]{1,0:T(8,128)(2,1)S(1)} %get-tuple-element.138), channel_id=1, source_target_pairs={{0,1},{1,0},{2,3},{3,2},{4,5},{5,4},{6,7},{7,6},{8,9},{9,8},{10,11... | collective-permute-start | bytes 196616 | tf_op jit(solution)/shard_map/ppermute | solution.py:385
  59.4 5.7 %collective-permute-start.28 = (bf16[16,2048]{1,0:T(8,128)(2,1)S(1)}, bf16[16,2048]{1,0:T(8,128)(2,1)S(1)}, u32[]{:S(2)}, u32[]{:S(2)}) collective-permute-start(bf16[16,2048]{1,0:T(8,128)(2,1)S(1)} %get-tuple-element.139), channel_id=1, source_target_pairs={{0,1},{1,0},{2,3},{3,2},{4,5},{5,4},{6,7},{7,6},{8,9},{9,8},{10,11... | collective-permute-start | bytes 196616 | tf_op jit(solution)/shard_map/ppermute | solution.py:385
  65.2 1.9 %collective-permute-start.29 = (bf16[2,4,2048]{2,1,0:T(4,128)(2,1)S(1)}, bf16[2,4,2048]{2,1,0:T(4,128)(2,1)S(1)}, u32[]{:S(2)}, u32[]{:S(2)}) collective-permute-start(bf16[2,4,2048]{2,1,0:T(4,128)(2,1)S(1)} %get-tuple-element.142), channel_id=1, source_target_pairs={{0,4},{4,0},{8,12},{12,8},{1,5},{5,1},{9,13},{13,9},{2,6},{6,2},{1... | collective-permute-start | bytes 98312 | tf_op jit(solution)/shard_map/ppermute | solution.py:387
  65.3 4.0 %collective-permute-start.30 = (bf16[2,4,2048]{2,1,0:T(4,128)(2,1)S(1)}, bf16[2,4,2048]{2,1,0:T(4,128)(2,1)S(1)}, u32[]{:S(2)}, u32[]{:S(2)}) collective-permute-start(bf16[2,4,2048]{2,1,0:T(4,128)(2,1)S(1)} %get-tuple-element.143), channel_id=1, source_target_pairs={{0,8},{4,12},{8,0},{12,4},{1,9},{5,13},{9,1},{13,5},{2,10},{6,14},... | collective-permute-start | bytes 98312 | tf_op jit(solution)/shard_map/ppermute | solution.py:387
  66.5 3.3 %collective-permute-start.31 = (bf16[2,4,2048]{2,1,0:T(4,128)(2,1)S(1)}, bf16[2,4,2048]{2,1,0:T(4,128)(2,1)S(1)}, u32[]{:S(2)}, u32[]{:S(2)}) collective-permute-start(bf16[2,4,2048]{2,1,0:T(4,128)(2,1)S(1)} %get-tuple-element.144), channel_id=1, source_target_pairs={{0,12},{4,8},{8,4},{12,0},{1,13},{5,9},{9,5},{13,1},{2,14},{6,10},... | collective-permute-start | bytes 98312 | tf_op jit(solution)/shard_map/ppermute | solution.py:387
  (7 other events, 32.7 us)
